TPU v7x, 32 devices: a whole 2x2x4 slice. The times are simulated.
32 devices in a mesh: cell: 8 (over z, y), sensor: 4 (over x, core).
Axes of the slice: x: 2, y: 2, z: 4, core: 2. Of those that a mesh axis runs over, the one named last changes fastest.
Arguments:
- kernel: bfloat16 [2, 65, 256, 2048], P(None, None, 'sensor', 'cell'), may hold values from -3 to 3
- observed: float32 [64, 256], P(None, 'sensor'), may hold values from -6 to 6
- start_model: float32 [64, 2048], P(None, 'cell'), may hold values from -6 to 6
- start_multiplier: float32 [4, 64, 2048], P(None, None, 'cell'), may hold values from -1.8 to 1.8
- neighbours: int32 [4, 2048], P(None, 'cell'), may hold values from 0 to 2047, as said below
- tile_of_cell: int32 [2048], P('cell'), may hold values from 0 to 63
- tile_weight: float32 [64], replicated, may hold values from 0.3 to 3
Outputs:
- estimate: float32 [64, 2048], P(None, 'cell')
- auxiliary: float32 [4, 64, 2048], P(None, None, 'cell')
- multiplier: float32 [4, 64, 2048], P(None, None, 'cell')
Inputs may be any that keep to these rules, and one draw needn't show every extreme that they name: The cells form a grid of 16 rows of 128 cells, numbered row by row. neighbours[k, c] is c itself or the cell beside c: c + 1 for k = 0 and c - 1 for k = 1 within the same row, c - 128 for k = 2 and c + 128 for k = 3. Where neighbours[k, c] = c' differs from c, neighbours[k xor 1, c'] = c.
All inputs are finite; a program needn't handle non-finite values.
Results may differ from a plain program's by a relative error of at most 0.00092.
Values sent between devices are 32-bit elements; how exact they have to be, the bound alone decides.
No kernel may reach another device: no remote copies, remote signals or barrier semaphores. Data moves between devices by JAX's collectives and lax.ppermute only.
A program may use at most 64 MiB of HBM per device.

v0:
```python
import functools

import jax
import jax.numpy as jnp
import numpy as np
from jax import lax
from jax.experimental import pallas as pl
from jax.experimental.pallas import tpu as pltpu
from jax.sharding import PartitionSpec as P

COLS = 128
LANES = 128
GROUP = 8
SHRINK_SCALE = 0.4
TINY = 1e-06
VMEM = pltpu.VMEM
HBM = pltpu.HBM


def tables(times, freqs):
    padded = 2 * times
    groups = -(-freqs // GROUP)
    plain = np.zeros((16 * groups, times), np.float64)
    weighted = np.zeros((16 * groups, times), np.float64)
    for f in range(freqs):
        phase = 2.0 * np.pi * ((f * np.arange(times)) % padded) / padded
        weight = (1.0 if f in (0, freqs - 1) else 2.0) / padded
        row = 16 * (f // GROUP) + f % GROUP
        plain[row], plain[row + GROUP] = np.cos(phase), -np.sin(phase)
        weighted[row], weighted[row + GROUP] = weight * np.cos(phase), -weight * np.sin(phase)
    return plain.astype(np.float32), weighted.astype(np.float32)


def exact(left, right):
    return jnp.dot(left, right, precision=lax.Precision.HIGHEST, preferred_element_type=jnp.float32)


def turned(rows):
    return jnp.concatenate([-rows[GROUP:], rows[:GROUP]], axis=0)


def dot_nt(left, right):
    return lax.dot_general(left, right, (((1,), (1,)), ((), ())), preferred_element_type=jnp.float32)


def dot_nn(left, right):
    return jnp.dot(left, right, preferred_element_type=jnp.float32)


def slab(kernel_ref, part, group):
    freqs, sensors, cells = kernel_ref.shape[1:]
    count = min(GROUP, freqs - group * GROUP)
    block = kernel_ref[part, group * GROUP : group * GROUP + count]
    return block.reshape(count * sensors, cells)


def own_block(width, sensors):
    row = lax.broadcasted_iota(jnp.int32, (16, width), 0) % GROUP
    lane = lax.broadcasted_iota(jnp.int32, (16, width), 1) // sensors
    return row == lane


def fold(wide):
    total = functools.reduce(
        lambda a, b: a + b, [wide[:, i : i + LANES] for i in range(0, wide.shape[1], LANES)]
    )
    return total + pltpu.roll(total, LANES // 2, 1)


def forward(field, kernel_ref, plain, weighted_t, arrived=None):
    freqs, sensors = kernel_ref.shape[1:3]
    times = field.shape[0]
    spectra = exact(plain, field)
    rows = []
    for group in range(plain.shape[0] // 16):
        part = spectra[16 * group : 16 * group + 16]
        if arrived is not None:
            arrived(group)
        re_slab, im_slab = slab(kernel_ref, 0, group), slab(kernel_ref, 1, group)
        out = dot_nt(part.astype(jnp.bfloat16), re_slab) + dot_nt(turned(part).astype(jnp.bfloat16), im_slab)
        width = out.shape[1]
        out = jnp.where(own_block(width, sensors), out, 0.0)
        if width < LANES:
            out = jnp.concatenate([out, jnp.zeros((16, LANES - width), jnp.float32)], axis=1)
        rows.append(fold(out))
    series = exact(weighted_t, jnp.concatenate(rows, axis=0))
    left = lax.broadcasted_iota(jnp.int32, (times // 2, LANES), 1) < sensors
    return jnp.where(left, series[: times // 2], series[times // 2 :])


def unpacked(packed, sensors):
    other = pltpu.roll(packed, sensors, 1)
    left = lax.broadcasted_iota(jnp.int32, packed.shape, 1) < sensors
    return jnp.concatenate([jnp.where(left, packed, other), jnp.where(left, other, packed)], axis=0)


def adjoint(residual, kernel_ref, plain_t, weighted, halves):
    freqs, sensors, cells = kernel_ref.shape[1:]
    spectra = exact(weighted, residual)
    rows = []
    for group in range(weighted.shape[0] // 16):
        part = spectra[16 * group : 16 * group + 16]
        count = min(GROUP, freqs - group * GROUP)
        width = count * sensors
        re_slab, im_slab = slab(kernel_ref, 0, group), slab(kernel_ref, 1, group)
        wide = jnp.concatenate([part] * (-(-width // LANES)), axis=1)[:, :width]
        wide = jnp.where(own_block(width, sensors), wide, 0.0)
        total = None
        for _ in range(halves):
            re_left = wide.astype(jnp.bfloat16)
            rounded = re_left.astype(jnp.float32)
            out = dot_nn(re_left, re_slab) - dot_nn(turned(rounded).astype(jnp.bfloat16), im_slab)
            total = out if total is None else total + out
            wide = wide - rounded
        rows.append(total)
    return exact(plain_t, jnp.concatenate(rows, axis=0))


def strip(array, row):
    return array[..., row * COLS : (row + 1) * COLS]


def jumps(field, above, below, linked):
    count = field.shape[1] // COLS
    out = []
    for direction in range(4):
        strips = []
        for row in range(count):
            here = strip(field, row)
            if direction == 0:
                there = pltpu.roll(here, COLS - 1, 1)
            elif direction == 1:
                there = pltpu.roll(here, 1, 1)
            elif direction == 2:
                there = above if row == 0 else strip(field, row - 1)
            else:
                there = below if row == count - 1 else strip(field, row + 1)
            strips.append(strip(linked[direction : direction + 1], row) * (there - here))
        out.append(strips)
    return out


def gathered_jumps(values, above, below, linked):
    count = len(values[0])
    out = []
    for row in range(count):
        arriving = (
            pltpu.roll(values[1][row], COLS - 1, 1),
            pltpu.roll(values[0][row], 1, 1),
            above if row == 0 else values[3][row - 1],
            below if row == count - 1 else values[2][row + 1],
        )
        total = None
        for direction in range(4):
            term = strip(linked[direction : direction + 1], row) * (arriving[direction] - values[direction][row])
            total = term if total is None else total + term
        out.append(total)
    return jnp.concatenate(out, axis=1)


def shrunk(shifted, threshold):
    return shifted - jnp.clip(shifted, -threshold, threshold)


def tree_sum(parts):
    parts = list(parts)
    while len(parts) > 1:
        parts = [parts[i] + parts[i + 1] if i + 1 < len(parts) else parts[i] for i in range(0, len(parts), 2)]
    return parts[0]


def square_sum(array):
    return jnp.sum(array * array)


def block_of(scalar, rows=8):
    return jnp.full((rows, LANES), scalar, jnp.float32)


def call(body, out_shapes, *operands, scratch=(), inputs=None):
    single = isinstance(out_shapes, tuple)
    shapes = [out_shapes] if single else list(out_shapes)
    shapes = [s if isinstance(s, jax.ShapeDtypeStruct) else jax.ShapeDtypeStruct(s, jnp.float32) for s in shapes]
    out = pl.pallas_call(
        body,
        out_shape=shapes,
        in_specs=[pl.BlockSpec(memory_space=space) for space in inputs or [VMEM] * len(operands)],
        out_specs=[pl.BlockSpec(memory_space=VMEM)] * len(shapes),
        scratch_shapes=list(scratch),
        compiler_params=pltpu.CompilerParams(vmem_limit_bytes=24 * 2**20),
    )(*operands)
    return out[0] if single else out


def first_forward_body(
    field, kernel, start_multiplier, neighbours, tile_of_cell, tile_weight, plain, weighted_t,
    out, kept, above, below, threshold, linked,
    field_here, plain_here, weighted_here, neighbours_here, tiles_here, sems,
):
    freqs = kernel.shape[1]
    times, cells = field.shape
    copies = []

    def load(source, target):
        copy = pltpu.make_async_copy(source, target, sems.at[len(copies)])
        copy.start()
        copies.append(copy)
        return copy

    first = [load(field, field_here), load(plain, plain_here), load(weighted_t, weighted_here)]
    head, tail = pl.ds(0, COLS), pl.ds(cells - COLS, COLS)
    rows, more = pl.ds(0, times), pl.ds(times, times)
    small = [load(neighbours, neighbours_here), load(tile_of_cell, tiles_here)]
    small += [load(field.at[:, tail], above.at[rows]), load(field.at[:, head], below.at[rows])]
    small += [load(start_multiplier.at[3, :, tail], above.at[more])]
    small += [load(start_multiplier.at[2, :, head], below.at[more])]
    large = []
    for group in range(plain.shape[0] // 16):
        start = group * GROUP
        for part in range(2):
            at = (part, pl.ds(start, min(GROUP, freqs - start)))
            large.append(load(kernel.at[at], kept.at[at]))

    for copy in first:
        copy.wait()

    def arrived(group):
        large[2 * group].wait()
        large[2 * group + 1].wait()

    out[...] = forward(field_here[...], kept, plain_here[...], weighted_here[...], arrived)

    for copy in small:
        copy.wait()
    cell = lax.broadcasted_iota(jnp.int32, (4, cells), 1) + lax.axis_index("cell") * cells
    linked[0:4, :] = jnp.where(neighbours_here[...] != cell, 1.0, 0.0)
    linked[4:8, :] = jnp.zeros((4, cells), jnp.float32)
    tiles = jnp.broadcast_to(tiles_here[...], (8, cells))
    weights = jnp.zeros((8, cells), jnp.float32)
    for tile in range(tile_weight.shape[0]):
        weights = jnp.where(tiles == tile, tile_weight[tile], weights)
    limit = SHRINK_SCALE * weights
    threshold[...] = limit
    above[2 * times :, :] = limit[:, cells - COLS :]
    below[2 * times :, :] = limit[:, :COLS]


def forward_body(field, kernel, plain, weighted_t, out):
    out[...] = forward(field[...], kernel, plain[...], weighted_t[...])


def summed(parts):
    return tree_sum([part[...] for part in parts])


def first_adjoint_body(count, *refs):
    observed, kernel, plain_t, weighted, out = refs[count:]
    predicted = unpacked(summed(refs[:count]), kernel.shape[2])
    out[...] = adjoint(predicted - observed[...], kernel, plain_t[...], weighted[...], 1)


def edge_rows(field, first, last):
    first[...] = strip(field, 0)
    last[...] = strip(field, field.shape[1] // COLS - 1)


def first_gradient_body(count, *refs):
    start_multiplier, above, below, linked, adjoint_out, gradient, first, last = refs[count:]
    times, cells = adjoint_out.shape
    total = summed(refs[:count])
    values = [[strip(start_multiplier[k], r) for r in range(cells // COLS)] for k in range(4)]
    back = gathered_jumps(values, above[times : 2 * times], below[times : 2 * times], linked[...])
    adjoint_out[...] = total
    field = total + back
    gradient[...] = field
    edge_rows(field, first, last)


def norms_body(packed, gradient, above, linked, out):
    field = gradient[...]
    squares = []
    for row in range(field.shape[1] // COLS):
        here = strip(field, row)
        beside = above[...] if row == 0 else strip(field, row - 1)
        east = strip(linked[0:1], row) * (pltpu.roll(here, COLS - 1, 1) - here)
        north = strip(linked[2:3], row) * (beside - here)
        squares.append(east * east + north * north)
    half = packed.shape[0]
    out[:half, :] = packed[...]
    out[half : half + 8, :] = block_of(square_sum(field))
    out[half + 8 :, :] = block_of(2.0 * jnp.sum(tree_sum(squares)))


def second_adjoint_body(count, *refs):
    kernel, plain_t, weighted, out, norms = refs[count:]
    times = plain_t.shape[0]
    total = summed(refs[:count])
    packed = total[: times // 2]
    out[:times, :] = adjoint(unpacked(packed, kernel.shape[2]), kernel, plain_t[...], weighted[...], 2)
    out[times:, :] = jnp.full((out.shape[0] - times, out.shape[1]), square_sum(packed), jnp.float32)
    norms[...] = total[times // 2 :]


def second_gradient_body(count, *refs):
    (norms, adjoint_in, gradient_in, model, start_multiplier, threshold, above, below, grad_above, grad_below,
     linked_ref, model_out, jumps_out, multiplier_out, gradient_out, first, last) = refs[count:]
    times, cells = model.shape
    total = summed(refs[:count])
    step = norms[0, 0] / (total[times, 0] + norms[8, 0] + TINY)
    linked = linked_ref[...]
    field, gradient = model[...], gradient_in[...]
    rows = cells // COLS
    field_jumps = jumps(field, above[:times], below[:times], linked)
    grad_jumps = jumps(gradient, grad_above[...], grad_below[...], linked)

    def advance(model_jumps, old_multiplier, limit):
        shifted = model_jumps + old_multiplier
        auxiliary = shrunk(shifted, limit)
        multiplier = shifted - auxiliary
        return multiplier, model_jumps - auxiliary + multiplier

    penalties, new_jumps = [], []
    for k in range(4):
        penalties.append([])
        new_jumps.append([])
        for r in range(rows):
            new = field_jumps[k][r] - step * grad_jumps[k][r]
            multiplier, penalty = advance(new, strip(start_multiplier[k], r), strip(threshold[0:1], r))
            jumps_out[k, :, r * COLS : (r + 1) * COLS] = new
            multiplier_out[k, :, r * COLS : (r + 1) * COLS] = multiplier
            penalties[k].append(penalty)
            new_jumps[k].append(new)
    _, beside_above = advance(-new_jumps[2][0], above[times : 2 * times], above[2 * times : 2 * times + 1])
    _, beside_below = advance(-new_jumps[3][-1], below[times : 2 * times], below[2 * times : 2 * times + 1])
    back = gathered_jumps(penalties, beside_above, beside_below, linked)
    model_out[...] = field - step * gradient
    new_gradient = adjoint_in[...] - step * total[:times] + back
    gradient_out[...] = new_gradient
    edge_rows(new_gradient, first, last)


def response_body(count, *refs):
    out, norms = refs[count:]
    total = summed(refs[:count])
    half = total.shape[0] - 16
    out[...] = block_of(square_sum(total[:half]))
    norms[...] = total[half:]


def finish_body(count, *refs):
    (norms, gradient_in, model, model_jumps, multiplier, threshold, above, below, linked,
     estimate_out, auxiliary_out, multiplier_out) = refs[count:]
    step = norms[0, 0] / (summed(refs[:count])[0, 0] + norms[8, 0] + TINY)
    gradient = gradient_in[...]
    estimate_out[...] = model[...] - step * gradient
    grad_jumps = jumps(gradient, above[...], below[...], linked[...])
    for k in range(4):
        for r in range(gradient.shape[1] // COLS):
            at = slice(r * COLS, (r + 1) * COLS)
            shifted = model_jumps[k, :, at] - step * grad_jumps[k][r] + multiplier[k, :, at]
            auxiliary = shrunk(shifted, threshold[0:1, at])
            auxiliary_out[k, :, at] = auxiliary
            multiplier_out[k, :, at] = shifted - auxiliary


def parts_of(array, axis, *radices):
    count = lax.axis_size(axis)
    if count & (count - 1):
        return [lax.psum(array, axis)]
    stages, left = [], count
    for radix in radices:
        if left > 1 and left % radix == 0:
            stages.append(radix)
            left //= radix
    while left > 1:
        stages.append(2)
        left //= 2
    parts, stride = [array], 1
    for radix in stages:
        total = tree_sum(parts)
        parts = [total] + [
            lax.ppermute(total, axis, [(i, i ^ (k * stride)) for i in range(count)]) for k in range(1, radix)
        ]
        stride *= radix
    return parts


def from_above(last):
    count = lax.axis_size("cell")
    return lax.ppermute(last, "cell", [(i, i + 1) for i in range(count - 1)])


def from_below(first):
    count = lax.axis_size("cell")
    return lax.ppermute(first, "cell", [(i + 1, i) for i in range(count - 1)])


def per_device(kernel, observed, start_model, start_multiplier, neighbours, tile_of_cell, tile_weight):
    times, cells = start_model.shape
    freqs, sensors = kernel.shape[1:3]
    plain, weighted = tables(times, freqs)
    plain_t, weighted_t = jnp.asarray(plain.T.copy()), jnp.asarray(weighted.T.copy())
    plain, weighted = jnp.asarray(plain), jnp.asarray(weighted)
    observed_twice = jnp.concatenate([observed, observed], axis=1)
    half = times // 2
    packed, field, row, wide = (half, 2 * sensors), (times, cells), (times, COLS), (4, times, cells)

    part, kept, above, below, threshold, linked = call(
        first_forward_body,
        [packed, jax.ShapeDtypeStruct(kernel.shape, kernel.dtype), (2 * times + 8, COLS), (2 * times + 8, COLS),
         (8, cells), (8, cells)],
        start_model, kernel, start_multiplier, neighbours, tile_of_cell[None, :], tile_weight, plain, weighted_t,
        scratch=[
            VMEM(start_model.shape, jnp.float32), VMEM(plain.shape, jnp.float32), VMEM(weighted_t.shape, jnp.float32),
            VMEM(neighbours.shape, jnp.int32), VMEM((1, cells), jnp.int32),
            pltpu.SemaphoreType.DMA((9 + 2 * (plain.shape[0] // 16),)),
        ],
        inputs=[HBM] * 5 + [pltpu.SMEM] + [HBM] * 2,
    )
    parts = parts_of(part, "cell", 2, 2, 2)
    above, below = from_above(above), from_below(below)
    back = call(
        functools.partial(first_adjoint_body, len(parts)), field, *parts, observed_twice, kept, plain_t, weighted
    )
    parts = parts_of(back, "sensor", 2, 2)
    adjoint_one, gradient, edge_first, edge_last = call(
        functools.partial(first_gradient_body, len(parts)), [field, field, row, row],
        *parts, start_multiplier, above, below, linked,
    )

    def response_and_norms(gradient, edge_last, *radices):
        beside = from_above(edge_last)
        part = call(forward_body, packed, gradient, kept, plain, weighted_t)
        sent = call(norms_body, (half + 16, LANES), part, gradient, beside, linked)
        return parts_of(sent, "cell", *radices), beside

    parts, grad_above = response_and_norms(gradient, edge_last, 2, 4)
    grad_below = from_below(edge_first)
    back, norms = call(
        functools.partial(second_adjoint_body, len(parts)), [(times + 8, cells), (16, LANES)],
        *parts, kept, plain_t, weighted,
    )
    parts = parts_of(back, "sensor", 4)
    model, model_jumps, multiplier, gradient, edge_first, edge_last = call(
        functools.partial(second_gradient_body, len(parts)), [field, wide, wide, field, row, row],
        *parts, norms, adjoint_one, gradient, start_model, start_multiplier, threshold, above, below,
        grad_above, grad_below, linked,
    )
    parts, grad_above = response_and_norms(gradient, edge_last, 4, 2)
    grad_below = from_below(edge_first)
    square, norms = call(functools.partial(response_body, len(parts)), [(8, LANES), (16, LANES)], *parts)
    parts = parts_of(square, "sensor", 2, 2)
    return tuple(
        call(
            functools.partial(finish_body, len(parts)), [field, wide, wide],
            *parts, norms, gradient, model, model_jumps, multiplier, threshold, grad_above, grad_below, linked,
        )
    )


def solution(mesh):
    in_specs = (
        P(None, None, "sensor", "cell"),
        P(None, "sensor"),
        P(None, "cell"),
        P(None, None, "cell"),
        P(None, "cell"),
        P("cell"),
        P(),
    )
    out_specs = (P(None, "cell"), P(None, None, "cell"), P(None, None, "cell"))
    return jax.shard_map(
        per_device, mesh=mesh, in_specs=in_specs, out_specs=out_specs, check_vma=False
    )
```

profile of v0, /device:TPU:0, one launch (start us, length us, event | category | flops | bytes accessed | tf_op | source)
XLA Modules:
  0.0 92.6 jit_solution(15190566575024593139)
XLA Ops:
  0.6 2.2 %copy-done = bf16[2,65,64,256]{3,2,1,0:T(8,128)(2,1)S(1)} copy-done((bf16[2,65,64,256]{3,2,1,0:T(8,128)(2,1)S(1)}, bf16[2,65,64,256]{3,2,1,0:T(8,128)(2,1)}, u32[]{:S(2)}) %copy-start) | copy-done | bytes 4259864
  8.4 6.0 %shard_map.130 = (f32[32,128]{1,0:T(8,128)S(1)}, bf16[2,65,64,256]{3,2,1,0:T(8,128)(2,1)S(1)}, f32[136,128]{1,0:T(8,128)S(1)}, f32[136,128]{1,0:T(8,128)S(1)}, f...) custom-call(f32[64,256]{1,0:T(8,128)S(1)} %copy-done.7, bf16[2,65,64,256]{3,2,1,0:T(8,128)(2,1)S(1)} %copy-done, ...), custom_call_target="tpu_custom_call" | custom-call | tf_op jit(solution)/shard_map/pallas_call | solution.py:184
  14.4 3.0 %collective-permute-start = (f32[32,128]{1,0:T(8,128)S(1)}, f32[32,128]{1,0:T(8,128)S(1)}, u32[]{:S(2)}, u32[]{:S(2)}) collective-permute-start(f32[32,128]{1,0:T(8,128)S(1)} %get-tuple-element.23), channel_id=1, source_target_pairs={{0,4},{4,0},{8,12},{12,8},{16,20},{20,16},{24,28},{28,24},{1,5},{5... | collective-permute-start | bytes 49160 | tf_op jit(solution)/shard_map/ppermute | solution.py:382
  17.4 1.7 %collective-permute-done = f32[32,128]{1,0:T(8,128)S(1)} collective-permute-done((f32[32,128]{1,0:T(8,128)S(1)}, f32[32,128]{1,0:T(8,128)S(1)}, u32[]{:S(2)}, u32[]{:S(2)}) %collective-permute-start) | collective-permute-done | bytes 16416 | tf_op jit(solution)/shard_map/ppermute | solution.py:382
  19.1 2.1 %collective-permute-start.1 = (f32[32,128]{1,0:T(8,128)S(1)}, f32[32,128]{1,0:T(8,128)S(1)}, u32[]{:S(2)}, u32[]{:S(2)}) collective-permute-start(f32[32,128]{1,0:T(8,128)S(1)} %add.24), channel_id=1, source_target_pairs={{0,8},{4,12},{8,0},{12,4},{16,24},{20,28},{24,16},{28,20},{1,9},{5... | collective-permute-start | bytes 49160 | tf_op jit(solution)/shard_map/ppermute | solution.py:382
  21.2 1.7 %collective-permute-done.1 = f32[32,128]{1,0:T(8,128)S(1)} collective-permute-done((f32[32,128]{1,0:T(8,128)S(1)}, f32[32,128]{1,0:T(8,128)S(1)}, u32[]{:S(2)}, u32[]{:S(2)}) %collective-permute-start.1) | collective-permute-done | bytes 16416 | tf_op jit(solution)/shard_map/ppermute | solution.py:382
  22.9 3.0 %collective-permute-start.2 = (f32[32,128]{1,0:T(8,128)S(1)}, f32[32,128]{1,0:T(8,128)S(1)}, u32[]{:S(2)}, u32[]{:S(2)}) collective-permute-start(f32[32,128]{1,0:T(8,128)S(1)} %add.25.refs_0_), channel_id=1, source_target_pairs={{0,16},{4,20},{8,24},{12,28},{16,0},{20,4},{24,8},{28,12},{1,17},{... | collective-permute-start | bytes 49160 | tf_op jit(solution)/shard_map/ppermute | solution.py:382
  26.0 1.6 %collective-permute-done.2.refs_1_ = f32[32,128]{1,0:T(8,128)S(1)} collective-permute-done((f32[32,128]{1,0:T(8,128)S(1)}, f32[32,128]{1,0:T(8,128)S(1)}, u32[]{:S(2)}, u32[]{:S(2)}) %collective-permute-start.2) | collective-permute-done | bytes 16416 | tf_op jit(solution)/shard_map/ppermute | solution.py:382
  29.0 3.8 %collective-permute-start.5 = (f32[136,128]{1,0:T(8,128)S(1)}, f32[136,128]{1,0:T(8,128)S(1)}, u32[]{:S(2)}, u32[]{:S(2)}) collective-permute-start(f32[136,128]{1,0:T(8,128)S(1)} %get-tuple-element.25), channel_id=1, source_target_pairs={{0,4},{4,8},{8,12},{12,16},{16,20},{20,24},{24,28},{1,5},{5,9},{9,... | collective-permute-start | bytes 208904 | tf_op jit(solution)/shard_map/ppermute | solution.py:390
  35.7 3.3 %collective-permute-done.6.refs_4_.refs_11_ = f32[136,128]{1,0:T(8,128)S(1)} collective-permute-done((f32[136,128]{1,0:T(8,128)S(1)}, f32[136,128]{1,0:T(8,128)S(1)}, u32[]{:S(2)}, u32[]{:S(2)}) %collective-permute-start.6) | collective-permute-done | bytes 69664 | tf_op jit(solution)/shard_map/ppermute | solution.py:395
  39.1 4.3 %collective-permute-start.7 = (f32[64,128]{1,0:T(8,128)S(1)}, f32[64,128]{1,0:T(8,128)S(1)}, u32[]{:S(2)}, u32[]{:S(2)}) collective-permute-start(f32[64,128]{1,0:T(8,128)S(1)} %get-tuple-element.29), channel_id=1, source_target_pairs={{0,4},{4,8},{8,12},{12,16},{16,20},{20,24},{24,28},{1,5},{5,9},{9,... | collective-permute-start | bytes 98312 | tf_op jit(solution)/shard_map/ppermute | solution.py:390
  43.5 1.7 %shard_map.133.packed = f32[32,128]{1,0:T(8,128)S(1)} custom-call(f32[64,256]{1,0:T(8,128)S(1)} %get-tuple-element.28.field.gradient.refs_6_, bf16[2,65,64,256]{3,2,1,0:T(8,128)(2,1)S(1)} %get-tuple-element.24.refs_3_.kernel.refs_4_, f32[144,64]{1,0:T(8,128)S(1)} %copy-done.3, f32[64,144]{1,0:T(8,128)S(1)} %copy-done.4), custom_call_target="tpu_custom_call" | custom-call | tf_op jit(solution)/shard_map/pallas_call | solution.py:184
  45.4 2.2 %collective-permute-start.8 = (f32[48,128]{1,0:T(8,128)S(1)}, f32[48,128]{1,0:T(8,128)S(1)}, u32[]{:S(2)}, u32[]{:S(2)}) collective-permute-start(f32[48,128]{1,0:T(8,128)S(1)} %shard_map.134), channel_id=1, source_target_pairs={{0,4},{4,0},{8,12},{12,8},{16,20},{20,16},{24,28},{28,24},{1,5},{5... | collective-permute-start | bytes 73736 | tf_op jit(solution)/shard_map/ppermute | solution.py:382
  47.6 1.8 %collective-permute-done.8 = f32[48,128]{1,0:T(8,128)S(1)} collective-permute-done((f32[48,128]{1,0:T(8,128)S(1)}, f32[48,128]{1,0:T(8,128)S(1)}, u32[]{:S(2)}, u32[]{:S(2)}) %collective-permute-start.8) | collective-permute-done | bytes 24608 | tf_op jit(solution)/shard_map/ppermute | solution.py:382
  49.4 5.6 %collective-permute-start.11 = (f32[48,128]{1,0:T(8,128)S(1)}, f32[48,128]{1,0:T(8,128)S(1)}, u32[]{:S(2)}, u32[]{:S(2)}) collective-permute-start(f32[48,128]{1,0:T(8,128)S(1)} %add.27.refs_0_), channel_id=1, source_target_pairs={{0,24},{4,28},{8,16},{12,20},{16,8},{20,12},{24,0},{28,4},{1,25},{... | collective-permute-start | bytes 73736 | tf_op jit(solution)/shard_map/ppermute | solution.py:382
  56.9 2.9 %collective-permute-done.10.refs_2_ = f32[48,128]{1,0:T(8,128)S(1)} collective-permute-done((f32[48,128]{1,0:T(8,128)S(1)}, f32[48,128]{1,0:T(8,128)S(1)}, u32[]{:S(2)}, u32[]{:S(2)}) %collective-permute-start.10) | collective-permute-done | bytes 24608 | tf_op jit(solution)/shard_map/ppermute | solution.py:382
  59.8 1.7 %shard_map.135 = (f32[72,256]{1,0:T(8,128)S(1)}, f32[16,128]{1,0:T(8,128)S(1)}) custom-call(f32[48,128]{1,0:T(8,128)S(1)} %add.27.refs_0_, f32[48,128]{1,0:T(8,128)S(1)} %collective-permute-done.9.refs_1_, f32[48,128]{1,0:T(8,128)S(1)} %collective-permute-done.10.refs_2_, f32[48,128]{1,0:T(8,128)S(1)} %collective-permute-done.11.refs_3_, ...), custom_call_target="tpu_custom_call" | custom-call | tf_op jit(solution)/shard_map/pallas_call | solution.py:184
  64.8 4.5 %collective-permute-done.15.refs_13_ = f32[64,128]{1,0:T(8,128)S(1)} collective-permute-done((f32[64,128]{1,0:T(8,128)S(1)}, f32[64,128]{1,0:T(8,128)S(1)}, u32[]{:S(2)}, u32[]{:S(2)}) %collective-permute-start.15) | collective-permute-done | bytes 32800 | tf_op jit(solution)/shard_map/ppermute | solution.py:395
  69.6 2.8 %collective-permute-start.16 = (f32[64,128]{1,0:T(8,128)S(1)}, f32[64,128]{1,0:T(8,128)S(1)}, u32[]{:S(2)}, u32[]{:S(2)}) collective-permute-start(f32[64,128]{1,0:T(8,128)S(1)} %get-tuple-element.36), channel_id=1, source_target_pairs={{0,4},{4,8},{8,12},{12,16},{16,20},{20,24},{24,28},{1,5},{5,9},{9,... | collective-permute-start | bytes 98312 | tf_op jit(solution)/shard_map/ppermute | solution.py:390
  72.4 1.7 %shard_map.137.packed = f32[32,128]{1,0:T(8,128)S(1)} custom-call(f32[64,256]{1,0:T(8,128)S(1)} %get-tuple-element.35.field.gradient.refs_3_, bf16[2,65,64,256]{3,2,1,0:T(8,128)(2,1)S(1)} %get-tuple-element.24.refs_3_.kernel.refs_4_, f32[144,64]{1,0:T(8,128)S(1)} %copy-done.3, f32[64,144]{1,0:T(8,128)S(1)} %copy-done.4), custom_call_target="tpu_custom_call" | custom-call | tf_op jit(solution)/shard_map/pallas_call | solution.py:184
  74.4 2.8 %collective-permute-start.19 = (f32[48,128]{1,0:T(8,128)S(1)}, f32[48,128]{1,0:T(8,128)S(1)}, u32[]{:S(2)}, u32[]{:S(2)}) collective-permute-start(f32[48,128]{1,0:T(8,128)S(1)} %shard_map.138), channel_id=1, source_target_pairs={{0,12},{4,8},{8,4},{12,0},{16,28},{20,24},{24,20},{28,16},{1,13},{... | collective-permute-start | bytes 73736 | tf_op jit(solution)/shard_map/ppermute | solution.py:382
  79.2 1.8 %collective-permute-done.18 = f32[48,128]{1,0:T(8,128)S(1)} collective-permute-done((f32[48,128]{1,0:T(8,128)S(1)}, f32[48,128]{1,0:T(8,128)S(1)}, u32[]{:S(2)}, u32[]{:S(2)}) %collective-permute-start.18) | collective-permute-done | bytes 24608 | tf_op jit(solution)/shard_map/ppermute | solution.py:382
  81.9 2.1 %collective-permute-start.20 = (f32[48,128]{1,0:T(8,128)S(1)}, f32[48,128]{1,0:T(8,128)S(1)}, u32[]{:S(2)}, u32[]{:S(2)}) collective-permute-start(f32[48,128]{1,0:T(8,128)S(1)} %add_add_fusion.refs_0_), channel_id=1, source_target_pairs={{0,16},{4,20},{8,24},{12,28},{16,0},{20,4},{24,8},{28,12},{1,17},{... | collective-permute-start | bytes 73736 | tf_op jit(solution)/shard_map/ppermute | solution.py:382
  89.8 1.9 %collective-permute-done.22.refs_1_ = f32[8,128]{1,0:T(8,128)S(1)} collective-permute-done((f32[8,128]{1,0:T(8,128)S(1)}, f32[8,128]{1,0:T(8,128)S(1)}, u32[]{:S(2)}, u32[]{:S(2)}) %collective-permute-start.22) | collective-permute-done | bytes 4128 | tf_op jit(solution)/shard_map/ppermute | solution.py:382
  (68 shorter events, 25.3 us)
Async XLA Ops:
  14.4 4.8 %collective-permute-start = (f32[32,128]{1,0:T(8,128)S(1)}, f32[32,128]{1,0:T(8,128)S(1)}, u32[]{:S(2)}, u32[]{:S(2)}) collective-permute-start(f32[32,128]{1,0:T(8,128)S(1)} %get-tuple-element.23), channel_id=1, source_target_pairs={{0,4},{4,0},{8,12},{12,8},{16,20},{20,16},{24,28},{28,24},{1,5},{5... | collective-permute-start | bytes 49160 | tf_op jit(solution)/shard_map/ppermute | solution.py:382
  19.1 3.8 %collective-permute-start.1 = (f32[32,128]{1,0:T(8,128)S(1)}, f32[32,128]{1,0:T(8,128)S(1)}, u32[]{:S(2)}, u32[]{:S(2)}) collective-permute-start(f32[32,128]{1,0:T(8,128)S(1)} %add.24), channel_id=1, source_target_pairs={{0,8},{4,12},{8,0},{12,4},{16,24},{20,28},{24,16},{28,20},{1,9},{5... | collective-permute-start | bytes 49160 | tf_op jit(solution)/shard_map/ppermute | solution.py:382
  22.9 4.8 %collective-permute-start.2 = (f32[32,128]{1,0:T(8,128)S(1)}, f32[32,128]{1,0:T(8,128)S(1)}, u32[]{:S(2)}, u32[]{:S(2)}) collective-permute-start(f32[32,128]{1,0:T(8,128)S(1)} %add.25.refs_0_), channel_id=1, source_target_pairs={{0,16},{4,20},{8,24},{12,28},{16,0},{20,4},{24,8},{28,12},{1,17},{... | collective-permute-start | bytes 49160 | tf_op jit(solution)/shard_map/ppermute | solution.py:382
  28.9 5.2 %collective-permute-start.3 = (f32[64,256]{1,0:T(8,128)S(1)}, f32[64,256]{1,0:T(8,128)S(1)}, u32[]{:S(2)}, u32[]{:S(2)}) collective-permute-start(f32[64,256]{1,0:T(8,128)S(1)} %shard_map.131), channel_id=1, source_target_pairs={{0,1},{1,0},{2,3},{3,2},{4,5},{5,4},{6,7},{7,6},{8,9},{9,8},{10,11... | collective-permute-start | bytes 196616 | tf_op jit(solution)/shard_map/ppermute | solution.py:382
  29.0 6.7 %collective-permute-start.5 = (f32[136,128]{1,0:T(8,128)S(1)}, f32[136,128]{1,0:T(8,128)S(1)}, u32[]{:S(2)}, u32[]{:S(2)}) collective-permute-start(f32[136,128]{1,0:T(8,128)S(1)} %get-tuple-element.25), channel_id=1, source_target_pairs={{0,4},{4,8},{8,12},{12,16},{16,20},{20,24},{24,28},{1,5},{5,9},{9,... | collective-permute-start | bytes 208904 | tf_op jit(solution)/shard_map/ppermute | solution.py:390
  32.8 6.2 %collective-permute-start.6 = (f32[136,128]{1,0:T(8,128)S(1)}, f32[136,128]{1,0:T(8,128)S(1)}, u32[]{:S(2)}, u32[]{:S(2)}) collective-permute-start(f32[136,128]{1,0:T(8,128)S(1)} %get-tuple-element.26), channel_id=1, source_target_pairs={{4,0},{8,4},{12,8},{16,12},{20,16},{24,20},{28,24},{5,1},{9,5},{13... | collective-permute-start | bytes 208904 | tf_op jit(solution)/shard_map/ppermute | solution.py:395
  34.1 4.9 %collective-permute-start.4 = (f32[64,256]{1,0:T(8,128)S(1)}, f32[64,256]{1,0:T(8,128)S(1)}, u32[]{:S(2)}, u32[]{:S(2)}) collective-permute-start(f32[64,256]{1,0:T(8,128)S(1)} %add.26.refs_0_), channel_id=1, source_target_pairs={{0,2},{1,3},{2,0},{3,1},{4,6},{5,7},{6,4},{7,5},{8,10},{9,11},{10,... | collective-permute-start | bytes 196616 | tf_op jit(solution)/shard_map/ppermute | solution.py:382
  39.1 6.1 %collective-permute-start.7 = (f32[64,128]{1,0:T(8,128)S(1)}, f32[64,128]{1,0:T(8,128)S(1)}, u32[]{:S(2)}, u32[]{:S(2)}) collective-permute-start(f32[64,128]{1,0:T(8,128)S(1)} %get-tuple-element.29), channel_id=1, source_target_pairs={{0,4},{4,8},{8,12},{12,16},{16,20},{20,24},{24,28},{1,5},{5,9},{9,... | collective-permute-start | bytes 98312 | tf_op jit(solution)/shard_map/ppermute | solution.py:390
  45.4 4.0 %collective-permute-start.8 = (f32[48,128]{1,0:T(8,128)S(1)}, f32[48,128]{1,0:T(8,128)S(1)}, u32[]{:S(2)}, u32[]{:S(2)}) collective-permute-start(f32[48,128]{1,0:T(8,128)S(1)} %shard_map.134), channel_id=1, source_target_pairs={{0,4},{4,0},{8,12},{12,8},{16,20},{20,16},{24,28},{28,24},{1,5},{5... | collective-permute-start | bytes 73736 | tf_op jit(solution)/shard_map/ppermute | solution.py:382
  49.4 7.4 %collective-permute-start.11 = (f32[48,128]{1,0:T(8,128)S(1)}, f32[48,128]{1,0:T(8,128)S(1)}, u32[]{:S(2)}, u32[]{:S(2)}) collective-permute-start(f32[48,128]{1,0:T(8,128)S(1)} %add.27.refs_0_), channel_id=1, source_target_pairs={{0,24},{4,28},{8,16},{12,20},{16,8},{20,12},{24,0},{28,4},{1,25},{... | collective-permute-start | bytes 73736 | tf_op jit(solution)/shard_map/ppermute | solution.py:382
  55.1 4.7 %collective-permute-start.10 = (f32[48,128]{1,0:T(8,128)S(1)}, f32[48,128]{1,0:T(8,128)S(1)}, u32[]{:S(2)}, u32[]{:S(2)}) collective-permute-start(f32[48,128]{1,0:T(8,128)S(1)} %add.27.refs_0_), channel_id=1, source_target_pairs={{0,16},{4,20},{8,24},{12,28},{16,0},{20,4},{24,8},{28,12},{1,17},{... | collective-permute-start | bytes 73736 | tf_op jit(solution)/shard_map/ppermute | solution.py:382
  55.1 4.7 %collective-permute-start.9 = (f32[48,128]{1,0:T(8,128)S(1)}, f32[48,128]{1,0:T(8,128)S(1)}, u32[]{:S(2)}, u32[]{:S(2)}) collective-permute-start(f32[48,128]{1,0:T(8,128)S(1)} %add.27.refs_0_), channel_id=1, source_target_pairs={{0,8},{4,12},{8,0},{12,4},{16,24},{20,28},{24,16},{28,20},{1,9},{5... | collective-permute-start | bytes 73736 | tf_op jit(solution)/shard_map/ppermute | solution.py:382
  61.5 7.7 %collective-permute-start.14 = (f32[72,256]{1,0:T(8,128)S(1)}, f32[72,256]{1,0:T(8,128)S(1)}, u32[]{:S(2)}, u32[]{:S(2)}) collective-permute-start(f32[72,256]{1,0:T(8,128)S(1)} %get-tuple-element.30.refs_0_), channel_id=1, source_target_pairs={{0,3},{1,2},{2,1},{3,0},{4,7},{5,6},{6,5},{7,4},{8,11},{9,10},{10,... | collective-permute-start | bytes 221192 | tf_op jit(solution)/shard_map/ppermute | solution.py:382
  61.6 7.7 %collective-permute-start.13 = (f32[72,256]{1,0:T(8,128)S(1)}, f32[72,256]{1,0:T(8,128)S(1)}, u32[]{:S(2)}, u32[]{:S(2)}) collective-permute-start(f32[72,256]{1,0:T(8,128)S(1)} %get-tuple-element.30.refs_0_), channel_id=1, source_target_pairs={{0,2},{1,3},{2,0},{3,1},{4,6},{5,7},{6,4},{7,5},{8,10},{9,11},{10,... | collective-permute-start | bytes 221192 | tf_op jit(solution)/shard_map/ppermute | solution.py:382
  63.2 6.1 %collective-permute-start.12 = (f32[72,256]{1,0:T(8,128)S(1)}, f32[72,256]{1,0:T(8,128)S(1)}, u32[]{:S(2)}, u32[]{:S(2)}) collective-permute-start(f32[72,256]{1,0:T(8,128)S(1)} %get-tuple-element.30.refs_0_), channel_id=1, source_target_pairs={{0,1},{1,0},{2,3},{3,2},{4,5},{5,4},{6,7},{7,6},{8,9},{9,8},{10,11... | collective-permute-start | bytes 221192 | tf_op jit(solution)/shard_map/ppermute | solution.py:382
  63.5 5.8 %collective-permute-start.15 = (f32[64,128]{1,0:T(8,128)S(1)}, f32[64,128]{1,0:T(8,128)S(1)}, u32[]{:S(2)}, u32[]{:S(2)}) collective-permute-start(f32[64,128]{1,0:T(8,128)S(1)} %get-tuple-element.34), channel_id=1, source_target_pairs={{4,0},{8,4},{12,8},{16,12},{20,16},{24,20},{28,24},{5,1},{9,5},{13... | collective-permute-start | bytes 98312 | tf_op jit(solution)/shard_map/ppermute | solution.py:395
  69.6 4.6 %collective-permute-start.16 = (f32[64,128]{1,0:T(8,128)S(1)}, f32[64,128]{1,0:T(8,128)S(1)}, u32[]{:S(2)}, u32[]{:S(2)}) collective-permute-start(f32[64,128]{1,0:T(8,128)S(1)} %get-tuple-element.36), channel_id=1, source_target_pairs={{0,4},{4,8},{8,12},{12,16},{16,20},{20,24},{24,28},{1,5},{5,9},{9,... | collective-permute-start | bytes 98312 | tf_op jit(solution)/shard_map/ppermute | solution.py:390
  74.4 4.8 %collective-permute-start.19 = (f32[48,128]{1,0:T(8,128)S(1)}, f32[48,128]{1,0:T(8,128)S(1)}, u32[]{:S(2)}, u32[]{:S(2)}) collective-permute-start(f32[48,128]{1,0:T(8,128)S(1)} %shard_map.138), channel_id=1, source_target_pairs={{0,12},{4,8},{8,4},{12,0},{16,28},{20,24},{24,20},{28,16},{1,13},{... | collective-permute-start | bytes 73736 | tf_op jit(solution)/shard_map/ppermute | solution.py:382
  77.2 3.8 %collective-permute-start.18 = (f32[48,128]{1,0:T(8,128)S(1)}, f32[48,128]{1,0:T(8,128)S(1)}, u32[]{:S(2)}, u32[]{:S(2)}) collective-permute-start(f32[48,128]{1,0:T(8,128)S(1)} %shard_map.138), channel_id=1, source_target_pairs={{0,8},{4,12},{8,0},{12,4},{16,24},{20,28},{24,16},{28,20},{1,9},{5... | collective-permute-start | bytes 73736 | tf_op jit(solution)/shard_map/ppermute | solution.py:382
  78.0 3.8 %collective-permute-start.17 = (f32[48,128]{1,0:T(8,128)S(1)}, f32[48,128]{1,0:T(8,128)S(1)}, u32[]{:S(2)}, u32[]{:S(2)}) collective-permute-start(f32[48,128]{1,0:T(8,128)S(1)} %shard_map.138), channel_id=1, source_target_pairs={{0,4},{4,0},{8,12},{12,8},{16,20},{20,16},{24,28},{28,24},{1,5},{5... | collective-permute-start | bytes 73736 | tf_op jit(solution)/shard_map/ppermute | solution.py:382
  81.9 4.8 %collective-permute-start.20 = (f32[48,128]{1,0:T(8,128)S(1)}, f32[48,128]{1,0:T(8,128)S(1)}, u32[]{:S(2)}, u32[]{:S(2)}) collective-permute-start(f32[48,128]{1,0:T(8,128)S(1)} %add_add_fusion.refs_0_), channel_id=1, source_target_pairs={{0,16},{4,20},{8,24},{12,28},{16,0},{20,4},{24,8},{28,12},{1,17},{... | collective-permute-start | bytes 73736 | tf_op jit(solution)/shard_map/ppermute | solution.py:382
  84.0 5.8 %collective-permute-start.23 = (f32[64,128]{1,0:T(8,128)S(1)}, f32[64,128]{1,0:T(8,128)S(1)}, u32[]{:S(2)}, u32[]{:S(2)}) collective-permute-start(f32[64,128]{1,0:T(8,128)S(1)} %get-tuple-element.42), channel_id=1, source_target_pairs={{4,0},{8,4},{12,8},{16,12},{20,16},{24,20},{28,24},{5,1},{9,5},{13... | collective-permute-start | bytes 98312 | tf_op jit(solution)/shard_map/ppermute | solution.py:395
  86.8 1.2 %collective-permute-start.21 = (f32[8,128]{1,0:T(8,128)S(1)}, f32[8,128]{1,0:T(8,128)S(1)}, u32[]{:S(2)}, u32[]{:S(2)}) collective-permute-start(f32[8,128]{1,0:T(8,128)S(1)} %get-tuple-element.37), channel_id=1, source_target_pairs={{0,1},{1,0},{2,3},{3,2},{4,5},{5,4},{6,7},{7,6},{8,9},{9,8},{10,11... | collective-permute-start | bytes 12296 | tf_op jit(solution)/shard_map/ppermute | solution.py:382
  88.0 3.6 %collective-permute-start.22 = (f32[8,128]{1,0:T(8,128)S(1)}, f32[8,128]{1,0:T(8,128)S(1)}, u32[]{:S(2)}, u32[]{:S(2)}) collective-permute-start(f32[8,128]{1,0:T(8,128)S(1)} %add.31.refs_0_), channel_id=1, source_target_pairs={{0,2},{1,3},{2,0},{3,1},{4,6},{5,7},{6,4},{7,5},{8,10},{9,11},{10,... | collective-permute-start | bytes 12296 | tf_op jit(solution)/shard_map/ppermute | solution.py:382
  (13 other events, 120.4 us)
where the time goes:
time: 93.1 us; the launch traced here: 92.6 us
  starting transfers between devices  42.2 us (45%)
  waiting for transfers between devices  27.3 us (29%)
  Pallas kernels  14.4 us (15%)
  local copies, waits for them, and re-layouts  7.75 us (8%)
    ppermute x18, starting transfers between devices, parts_of(): lax.ppermute(total, axis, [(i, i ^ k * stride) for i in range(count)])  27.5 us
    ppermute x18, waiting for transfers between devices, parts_of(): lax.ppermute(total, axis, [(i, i ^ k * stride) for i in range(count)])  19.2 us
    pallas_call x11, Pallas kernels, call(): pl.pallas_call(body, out_shape=shapes, in_specs=[pl.BlockSpec(memory_spac...  14.4 us
    ppermute x3, starting transfers between devices, from_above(): return lax.ppermute(last, 'cell', [(i, i + 1) for i in range(count - 1)])  10.9 us
    ppermute x3, waiting for transfers between devices, from_below(): return lax.ppermute(first, 'cell', [(i + 1, i) for i in range(count - 1)])  8.07 us
    unnamed x26, local copies, waits for them, and re-layouts  7.75 us
    ppermute x3, starting transfers between devices, from_below(): return lax.ppermute(first, 'cell', [(i + 1, i) for i in range(count - 1)])  3.85 us
  transfers between devices with their start and end apart: 24, of which 15 were waited for; matrix products, arithmetic and copies ran while one was open for 0% of the time, Pallas kernels for 4%

commit v1 on v0

--- a/solution.py
+++ b/solution.py
@@ -177,14 +177,14 @@
     return jnp.full((rows, LANES), scalar, jnp.float32)
 
 
-def call(body, out_shapes, *operands, scratch=(), inputs=None):
+def call(body, out_shapes, *operands, scratch=(), inputs=VMEM):
     single = isinstance(out_shapes, tuple)
     shapes = [out_shapes] if single else list(out_shapes)
     shapes = [s if isinstance(s, jax.ShapeDtypeStruct) else jax.ShapeDtypeStruct(s, jnp.float32) for s in shapes]
     out = pl.pallas_call(
         body,
         out_shape=shapes,
-        in_specs=[pl.BlockSpec(memory_space=space) for space in inputs or [VMEM] * len(operands)],
+        in_specs=[pl.BlockSpec(memory_space=inputs)] * len(operands),
         out_specs=[pl.BlockSpec(memory_space=VMEM)] * len(shapes),
         scratch_shapes=list(scratch),
         compiler_params=pltpu.CompilerParams(vmem_limit_bytes=24 * 2**20),
@@ -192,11 +192,36 @@
     return out[0] if single else out
 
 
-def first_forward_body(
-    field, kernel, start_multiplier, neighbours, tile_of_cell, tile_weight, plain, weighted_t,
-    out, kept, above, below, threshold, linked,
-    field_here, plain_here, weighted_here, neighbours_here, tiles_here, sems,
-):
+def summed(parts):
+    return tree_sum([part[...] for part in parts])
+
+
+def below_first():
+    return lax.rem(lax.axis_index("cell") + lax.axis_index("sensor"), 2) == 0
+
+
+def edges(head, tail):
+    first = below_first()
+    return jnp.where(first, tail, head), jnp.where(first, head, tail)
+
+
+def beside(hop_one, hop_two):
+    first = below_first()
+    return jnp.where(first, hop_two, hop_one), jnp.where(first, hop_one, hop_two)
+
+
+def rows_of(scalars):
+    row = lax.broadcasted_iota(jnp.int32, (8, LANES), 0)
+    out = jnp.zeros((8, LANES), jnp.float32)
+    for i, scalar in enumerate(scalars):
+        out = jnp.where(row == i, scalar, out)
+    return out
+
+
+def first_forward_body(*refs):
+    loaded, (sent, edge, threshold, linked), kept, sems = refs[:10], refs[10:14], refs[14:24], refs[24]
+    kernel, kernel_here = loaded[0], kept[0]
+    field, multiplier, neighbours, tile_of_cell, tile_weight, plain, weighted_t = kept[1:8]
     freqs = kernel.shape[1]
     times, cells = field.shape
     copies = []
@@ -207,111 +232,140 @@
         copies.append(copy)
         return copy
 
-    first = [load(field, field_here), load(plain, plain_here), load(weighted_t, weighted_here)]
-    head, tail = pl.ds(0, COLS), pl.ds(cells - COLS, COLS)
-    rows, more = pl.ds(0, times), pl.ds(times, times)
-    small = [load(neighbours, neighbours_here), load(tile_of_cell, tiles_here)]
-    small += [load(field.at[:, tail], above.at[rows]), load(field.at[:, head], below.at[rows])]
-    small += [load(start_multiplier.at[3, :, tail], above.at[more])]
-    small += [load(start_multiplier.at[2, :, head], below.at[more])]
+    early = [load(loaded[i], kept[i]) for i in (1, 6, 7)]
+    small = [load(loaded[i], kept[i]) for i in (3, 4, 5, 2)]
     large = []
     for group in range(plain.shape[0] // 16):
         start = group * GROUP
         for part in range(2):
             at = (part, pl.ds(start, min(GROUP, freqs - start)))
-            large.append(load(kernel.at[at], kept.at[at]))
-
-    for copy in first:
+            large.append(load(kernel.at[at], kernel_here.at[at]))
+    late = [load(loaded[i], kept[i]) for i in (8, 9)]
+
+    for copy in early:
         copy.wait()
 
     def arrived(group):
         large[2 * group].wait()
         large[2 * group + 1].wait()
 
-    out[...] = forward(field_here[...], kept, plain_here[...], weighted_here[...], arrived)
+    half = times // 2
+    sent[:half, :] = forward(field[...], kernel_here, plain[...], weighted_t[...], arrived)
 
     for copy in small:
         copy.wait()
     cell = lax.broadcasted_iota(jnp.int32, (4, cells), 1) + lax.axis_index("cell") * cells
-    linked[0:4, :] = jnp.where(neighbours_here[...] != cell, 1.0, 0.0)
+    linked[0:4, :] = jnp.where(neighbours[...] != cell, 1.0, 0.0)
     linked[4:8, :] = jnp.zeros((4, cells), jnp.float32)
-    tiles = jnp.broadcast_to(tiles_here[...], (8, cells))
+    tiles = jnp.broadcast_to(tile_of_cell[...], (8, cells))
     weights = jnp.zeros((8, cells), jnp.float32)
-    for tile in range(tile_weight.shape[0]):
-        weights = jnp.where(tiles == tile, tile_weight[tile], weights)
+    for tile in range(tile_weight.shape[1]):
+        weight = jnp.broadcast_to(tile_weight[0:1, tile : tile + 1], (8, cells))
+        weights = jnp.where(tiles == tile, weight, weights)
     limit = SHRINK_SCALE * weights
     threshold[...] = limit
-    above[2 * times :, :] = limit[:, cells - COLS :]
-    below[2 * times :, :] = limit[:, :COLS]
-
-
-def forward_body(field, kernel, plain, weighted_t, out):
-    out[...] = forward(field[...], kernel, plain[...], weighted_t[...])
-
-
-def summed(parts):
-    return tree_sum([part[...] for part in parts])
+    bottom = cells // COLS - 1
+    pairs = (
+        (strip(field, 0), strip(field, bottom)),
+        (strip(multiplier[2], 0), strip(multiplier[3], bottom)),
+        (strip(limit, 0), strip(limit, bottom)),
+    )
+    for (head, tail), start in zip(pairs, (0, times, 2 * times)):
+        one, two = edges(head, tail)
+        sent[half + start : half + start + head.shape[0], :] = one
+        edge[start : start + head.shape[0], :] = two
+    for copy in late:
+        copy.wait()
+
+
+def first_merge_body(sent, came, edge, out):
+    half = sent.shape[0] - edge.shape[0]
+    out[:half, :] = sent[:half, :] + came[:half, :]
+    out[half:, :] = edge[...]
 
 
 def first_adjoint_body(count, *refs):
     observed, kernel, plain_t, weighted, out = refs[count:]
     predicted = unpacked(summed(refs[:count]), kernel.shape[2])
-    out[...] = adjoint(predicted - observed[...], kernel, plain_t[...], weighted[...], 1)
-
-
-def edge_rows(field, first, last):
-    first[...] = strip(field, 0)
-    last[...] = strip(field, field.shape[1] // COLS - 1)
+    residual = predicted - jnp.concatenate([observed[...], observed[...]], axis=1)
+    out[...] = adjoint(residual, kernel, plain_t[...], weighted[...], 1)
+
+
+def response_of(field, kernel, plain, weighted_t, linked, sent, edge):
+    half = field.shape[0] // 2
+    rows = field.shape[1] // COLS
+    one, two = edges(strip(field, 0), strip(field, rows - 1))
+    squares = []
+    for row in range(rows):
+        here = strip(field, row)
+        east = strip(linked[0:1], row) * (pltpu.roll(here, COLS - 1, 1) - here)
+        squares.append(east * east)
+        if row > 0:
+            north = strip(linked[2:3], row) * (strip(field, row - 1) - here)
+            squares.append(north * north)
+    sent[:half, :] = forward(field, kernel, plain[...], weighted_t[...])
+    sent[half : half + 8, :] = rows_of([square_sum(field), 2.0 * jnp.sum(tree_sum(squares))])
+    sent[half + 8 :, :] = one
+    edge[...] = two
+
+
+def merge_body(sent, came, edge, linked, out):
+    cells = linked.shape[1]
+    top = sent.shape[0] - edge.shape[0]
+    mask = jnp.where(below_first(), linked[3:4, cells - COLS :], linked[2:3, :COLS])
+    across = mask * (came[top:, :] - sent[top:, :])
+    out[: top - 8, :] = sent[: top - 8, :] + came[: top - 8, :]
+    out[top - 8 : top, :] = (
+        sent[top - 8 : top, :] + came[top - 8 : top, :] + rows_of([0.0, 0.0, 2.0 * square_sum(across)])
+    )
+    out[top:, :] = edge[...]
 
 
 def first_gradient_body(count, *refs):
-    start_multiplier, above, below, linked, adjoint_out, gradient, first, last = refs[count:]
+    (start_multiplier, one, two, linked_ref, kernel, plain, weighted_t,
+     adjoint_out, gradient, sent, edge) = refs[count:]
     times, cells = adjoint_out.shape
+    half = times // 2
+    linked = linked_ref[...]
     total = summed(refs[:count])
     values = [[strip(start_multiplier[k], r) for r in range(cells // COLS)] for k in range(4)]
-    back = gathered_jumps(values, above[times : 2 * times], below[times : 2 * times], linked[...])
+    above, below = beside(one[half + times : half + 2 * times, :], two[half + times : half + 2 * times, :])
+    field = total + gathered_jumps(values, above, below, linked)
     adjoint_out[...] = total
-    field = total + back
     gradient[...] = field
-    edge_rows(field, first, last)
-
-
-def norms_body(packed, gradient, above, linked, out):
-    field = gradient[...]
-    squares = []
-    for row in range(field.shape[1] // COLS):
-        here = strip(field, row)
-        beside = above[...] if row == 0 else strip(field, row - 1)
-        east = strip(linked[0:1], row) * (pltpu.roll(here, COLS - 1, 1) - here)
-        north = strip(linked[2:3], row) * (beside - here)
-        squares.append(east * east + north * north)
-    half = packed.shape[0]
-    out[:half, :] = packed[...]
-    out[half : half + 8, :] = block_of(square_sum(field))
-    out[half + 8 :, :] = block_of(2.0 * jnp.sum(tree_sum(squares)))
+    response_of(field, kernel, plain, weighted_t, linked, sent, edge)
 
 
 def second_adjoint_body(count, *refs):
     kernel, plain_t, weighted, out, norms = refs[count:]
     times = plain_t.shape[0]
+    half = times // 2
     total = summed(refs[:count])
-    packed = total[: times // 2]
+    packed, squares = total[:half], total[half : half + 8]
     out[:times, :] = adjoint(unpacked(packed, kernel.shape[2]), kernel, plain_t[...], weighted[...], 2)
-    out[times:, :] = jnp.full((out.shape[0] - times, out.shape[1]), square_sum(packed), jnp.float32)
-    norms[...] = total[times // 2 :]
+    across = squares[2:3, :] * (2.0 / lax.axis_size("sensor"))
+    scalars = rows_of([square_sum(packed), across])
+    out[times:, :] = jnp.concatenate([scalars] * (out.shape[1] // LANES), axis=1)
+    norms[...] = squares
+
+
+def step_of(norms, scalars):
+    return norms[0, 0] / (scalars[0, 0] + (norms[1, 0] + scalars[1, 0]) + TINY)
 
 
 def second_gradient_body(count, *refs):
-    (norms, adjoint_in, gradient_in, model, start_multiplier, threshold, above, below, grad_above, grad_below,
-     linked_ref, model_out, jumps_out, multiplier_out, gradient_out, first, last) = refs[count:]
+    (norms, adjoint_in, gradient_in, model, start_multiplier, threshold, one, two, grad_one, grad_two, linked_ref,
+     kernel, plain, weighted_t, model_out, jumps_out, multiplier_out, gradient_out, sent, edge) = refs[count:]
     times, cells = model.shape
+    half = times // 2
     total = summed(refs[:count])
-    step = norms[0, 0] / (total[times, 0] + norms[8, 0] + TINY)
+    step = step_of(norms, total[times:])
     linked = linked_ref[...]
     field, gradient = model[...], gradient_in[...]
     rows = cells // COLS
+    above, below = beside(one[half:, :], two[half:, :])
     field_jumps = jumps(field, above[:times], below[:times], linked)
-    grad_jumps = jumps(gradient, grad_above[...], grad_below[...], linked)
+    grad_jumps = jumps(gradient, *beside(grad_one[half + 8 :, :], grad_two[half + 8 :, :]), linked)
 
     def advance(model_jumps, old_multiplier, limit):
         shifted = model_jumps + old_multiplier
@@ -336,24 +390,25 @@
     model_out[...] = field - step * gradient
     new_gradient = adjoint_in[...] - step * total[:times] + back
     gradient_out[...] = new_gradient
-    edge_rows(new_gradient, first, last)
+    response_of(new_gradient, kernel, plain, weighted_t, linked, sent, edge)
 
 
 def response_body(count, *refs):
     out, norms = refs[count:]
     total = summed(refs[:count])
-    half = total.shape[0] - 16
-    out[...] = block_of(square_sum(total[:half]))
-    norms[...] = total[half:]
+    packed, squares = total[:-8], total[-8:]
+    out[...] = rows_of([square_sum(packed), squares[2:3, :] * (2.0 / lax.axis_size("sensor"))])
+    norms[...] = squares
 
 
 def finish_body(count, *refs):
-    (norms, gradient_in, model, model_jumps, multiplier, threshold, above, below, linked,
+    (norms, gradient_in, model, model_jumps, multiplier, threshold, grad_one, grad_two, linked,
      estimate_out, auxiliary_out, multiplier_out) = refs[count:]
-    step = norms[0, 0] / (summed(refs[:count])[0, 0] + norms[8, 0] + TINY)
+    step = step_of(norms, summed(refs[:count]))
+    half = gradient_in.shape[0] // 2
     gradient = gradient_in[...]
     estimate_out[...] = model[...] - step * gradient
-    grad_jumps = jumps(gradient, above[...], below[...], linked[...])
+    grad_jumps = jumps(gradient, *beside(grad_one[half + 8 :, :], grad_two[half + 8 :, :]), linked[...])
     for k in range(4):
         for r in range(gradient.shape[1] // COLS):
             at = slice(r * COLS, (r + 1) * COLS)
@@ -363,10 +418,8 @@
             multiplier_out[k, :, at] = shifted - auxiliary
 
 
-def parts_of(array, axis, *radices):
-    count = lax.axis_size(axis)
-    if count & (count - 1):
-        return [lax.psum(array, axis)]
+def sensor_parts(array, *radices):
+    count = lax.axis_size("sensor")
     stages, left = [], count
     for radix in radices:
         if left > 1 and left % radix == 0:
@@ -379,81 +432,87 @@
     for radix in stages:
         total = tree_sum(parts)
         parts = [total] + [
-            lax.ppermute(total, axis, [(i, i ^ (k * stride)) for i in range(count)]) for k in range(1, radix)
+            lax.ppermute(total, "sensor", [(i, i ^ (k * stride)) for i in range(count)]) for k in range(1, radix)
         ]
         stride *= radix
     return parts
 
 
-def from_above(last):
-    count = lax.axis_size("cell")
-    return lax.ppermute(last, "cell", [(i, i + 1) for i in range(count - 1)])
-
-
-def from_below(first):
-    count = lax.axis_size("cell")
-    return lax.ppermute(first, "cell", [(i + 1, i) for i in range(count - 1)])
+def neighbour_hop(array, second):
+    cells, sensors = lax.axis_size("cell"), lax.axis_size("sensor")
+    pairs = []
+    for cell in range(cells):
+        for sensor in range(sensors):
+            down = ((cell + sensor) % 2 == 0) != second
+            other = (cell + (1 if down else -1)) % cells
+            pairs.append((cell * sensors + sensor, other * sensors + sensor))
+    return lax.ppermute(array, ("cell", "sensor"), pairs)
+
+
+def cell_parts(sent, merge, rows):
+    one = neighbour_hop(sent, False)
+    sent = merge(one)
+    two = neighbour_hop(sent, True)
+    parts = [sent[:rows], two[:rows]]
+    count, shift = lax.axis_size("cell"), 4
+    while shift < count:
+        total = parts[0] + parts[1]
+        parts = [total, lax.ppermute(total, "cell", [((i + shift) % count, i) for i in range(count)])]
+        shift *= 2
+    return parts, one, two
 
 
 def per_device(kernel, observed, start_model, start_multiplier, neighbours, tile_of_cell, tile_weight):
     times, cells = start_model.shape
     freqs, sensors = kernel.shape[1:3]
     plain, weighted = tables(times, freqs)
-    plain_t, weighted_t = jnp.asarray(plain.T.copy()), jnp.asarray(weighted.T.copy())
-    plain, weighted = jnp.asarray(plain), jnp.asarray(weighted)
-    observed_twice = jnp.concatenate([observed, observed], axis=1)
     half = times // 2
-    packed, field, row, wide = (half, 2 * sensors), (times, cells), (times, COLS), (4, times, cells)
-
-    part, kept, above, below, threshold, linked = call(
+    field, row, wide = (times, cells), (times, COLS), (4, times, cells)
+
+    loads = [
+        kernel, start_model, start_multiplier, neighbours, tile_of_cell[None, :], tile_weight[None, :],
+        jnp.asarray(plain), jnp.asarray(weighted.T.copy()), jnp.asarray(plain.T.copy()), jnp.asarray(weighted),
+    ]
+    sent, edge, threshold, linked, kernel, start_model, start_multiplier, _, _, _, plain, weighted_t, plain_t, weighted = call(
         first_forward_body,
-        [packed, jax.ShapeDtypeStruct(kernel.shape, kernel.dtype), (2 * times + 8, COLS), (2 * times + 8, COLS),
-         (8, cells), (8, cells)],
-        start_model, kernel, start_multiplier, neighbours, tile_of_cell[None, :], tile_weight, plain, weighted_t,
-        scratch=[
-            VMEM(start_model.shape, jnp.float32), VMEM(plain.shape, jnp.float32), VMEM(weighted_t.shape, jnp.float32),
-            VMEM(neighbours.shape, jnp.int32), VMEM((1, cells), jnp.int32),
-            pltpu.SemaphoreType.DMA((9 + 2 * (plain.shape[0] // 16),)),
-        ],
-        inputs=[HBM] * 5 + [pltpu.SMEM] + [HBM] * 2,
-    )
-    parts = parts_of(part, "cell", 2, 2, 2)
-    above, below = from_above(above), from_below(below)
-    back = call(
-        functools.partial(first_adjoint_body, len(parts)), field, *parts, observed_twice, kept, plain_t, weighted
-    )
-    parts = parts_of(back, "sensor", 2, 2)
-    adjoint_one, gradient, edge_first, edge_last = call(
-        functools.partial(first_gradient_body, len(parts)), [field, field, row, row],
-        *parts, start_multiplier, above, below, linked,
-    )
-
-    def response_and_norms(gradient, edge_last, *radices):
-        beside = from_above(edge_last)
-        part = call(forward_body, packed, gradient, kept, plain, weighted_t)
-        sent = call(norms_body, (half + 16, LANES), part, gradient, beside, linked)
-        return parts_of(sent, "cell", *radices), beside
-
-    parts, grad_above = response_and_norms(gradient, edge_last, 2, 4)
-    grad_below = from_below(edge_first)
+        [(half + 2 * times + 8, LANES), (2 * times + 8, LANES), (8, cells), (8, cells)]
+        + [jax.ShapeDtypeStruct(a.shape, a.dtype) for a in loads],
+        *[pltpu.with_memory_space_constraint(a, HBM) for a in loads],
+        scratch=[pltpu.SemaphoreType.DMA((9 + 2 * (plain.shape[0] // 16),))],
+        inputs=HBM,
+    )
+    parts, one, two = cell_parts(
+        sent, lambda came: call(first_merge_body, (half + 2 * times + 8, LANES), sent, came, edge), half
+    )
+    back = call(functools.partial(first_adjoint_body, len(parts)), field, *parts, observed, kernel, plain_t, weighted)
+    parts = sensor_parts(back, 2, 2)
+    message, side = (half + 8 + times, LANES), (times, LANES)
+    adjoint_one, gradient, sent, edge = call(
+        functools.partial(first_gradient_body, len(parts)), [field, field, message, side],
+        *parts, start_multiplier, one, two, linked, kernel, plain, weighted_t,
+    )
+    parts, grad_one, grad_two = cell_parts(
+        sent, lambda came: call(merge_body, message, sent, came, edge, linked), half + 8
+    )
     back, norms = call(
-        functools.partial(second_adjoint_body, len(parts)), [(times + 8, cells), (16, LANES)],
-        *parts, kept, plain_t, weighted,
-    )
-    parts = parts_of(back, "sensor", 4)
-    model, model_jumps, multiplier, gradient, edge_first, edge_last = call(
-        functools.partial(second_gradient_body, len(parts)), [field, wide, wide, field, row, row],
-        *parts, norms, adjoint_one, gradient, start_model, start_multiplier, threshold, above, below,
-        grad_above, grad_below, linked,
-    )
-    parts, grad_above = response_and_norms(gradient, edge_last, 4, 2)
-    grad_below = from_below(edge_first)
-    square, norms = call(functools.partial(response_body, len(parts)), [(8, LANES), (16, LANES)], *parts)
-    parts = parts_of(square, "sensor", 2, 2)
+        functools.partial(second_adjoint_body, len(parts)), [(times + 8, cells), (8, LANES)],
+        *parts, kernel, plain_t, weighted,
+    )
+    parts = sensor_parts(back, 4)
+    model, model_jumps, multiplier, gradient, sent, edge = call(
+        functools.partial(second_gradient_body, len(parts)), [field, wide, wide, field, message, side],
+        *parts, norms, adjoint_one, gradient, start_model, start_multiplier, threshold, one, two, grad_one, grad_two,
+        linked, kernel, plain, weighted_t,
+    )
+    parts, grad_one, grad_two = cell_parts(
+        sent, lambda came: call(merge_body, message, sent, came, edge, linked), half + 8
+    )
+    square, norms = call(functools.partial(response_body, len(parts)), [(8, LANES), (8, LANES)], *parts)
+    parts = sensor_parts(square, 2, 2)
     return tuple(
         call(
             functools.partial(finish_body, len(parts)), [field, wide, wide],
-            *parts, norms, gradient, model, model_jumps, multiplier, threshold, grad_above, grad_below, linked,
+            *parts, norms, gradient, model, model_jumps, multiplier, threshold, grad_one, grad_two, linked,
         )
     )
 

time: 93.1 us -> 81.7 us (0.88)
  starting transfers between devices: 42.2 us -> 23.9 us
  waiting for transfers between devices: 27.3 us -> 42.2 us
  local copies, waits for them, and re-layouts: 7.75 us -> 0.01 us
    ppermute x24 -> x16, starting transfers between devices: 42.2 us -> 23.9 us  [the longest x6 18 us: neighbour_hop(): return lax.ppermute(array, ('cell', 'sensor'), pairs)]
    ppermute x24 -> x16, waiting for transfers between devices: 27.3 us -> 42.2 us  [the longest x6 17.2 us: neighbour_hop(): return lax.ppermute(array, ('cell', 'sensor'), pairs)]
    unnamed x26 -> x2, local copies, waits for them, and re-layouts: 7.75 us -> 0.01 us
    pallas_call x11 -> x10, Pallas kernels: 14.4 us -> 14.7 us  [call(): pl.pallas_call(body, out_shape=shapes, in_specs=[pl.BlockSpec(memory_spac...]
  transfers between devices with their start and end apart: 24 -> 16, of which waited for: 15 -> 15; matrix products, arithmetic and copies ran while one was open for 0% -> 0% of each run, Pallas kernels for 4% -> 0%
where the time goes in v1:
time: 81.7 us; the launch traced here: 81.6 us
  waiting for transfers between devices  42.2 us (52%)
  starting transfers between devices  23.9 us (29%)
  Pallas kernels  14.7 us (18%)
    ppermute x6, starting transfers between devices, neighbour_hop(): return lax.ppermute(array, ('cell', 'sensor'), pairs)  18 us
    ppermute x6, waiting for transfers between devices, neighbour_hop(): return lax.ppermute(array, ('cell', 'sensor'), pairs)  17.2 us
    pallas_call x10, Pallas kernels, call(): pl.pallas_call(body, out_shape=shapes, in_specs=[pl.BlockSpec(memory_spac...  14.7 us
    ppermute x3, waiting for transfers between devices, cell_parts(): lax.ppermute(total, 'cell', [((i + shift) % count, i) for i in range(coun...  12.5 us
    ppermute x7, waiting for transfers between devices, sensor_parts(): lax.ppermute(total, 'sensor', [(i, i ^ k * stride) for i in range(count)])  12.4 us
    ppermute x7, starting transfers between devices, sensor_parts(): lax.ppermute(total, 'sensor', [(i, i ^ k * stride) for i in range(count)])  4.25 us
    ppermute x3, starting transfers between devices, cell_parts(): lax.ppermute(total, 'cell', [((i + shift) % count, i) for i in range(coun...  1.64 us
  transfers between devices with their start and end apart: 16, of which 15 were waited for; matrix products, arithmetic and copies ran while one was open for 0% of the time, Pallas kernels for 0%

profile of v1, /device:TPU:0, one launch (start us, length us, event | category | flops | bytes accessed | tf_op | source)
XLA Modules:
  0.0 81.6 jit_solution(18352431014545509344)
XLA Ops:
  0.6 6.4 %shard_map.130 = (f32[168,128]{1,0:T(8,128)S(1)}, f32[136,128]{1,0:T(8,128)S(1)}, f32[8,256]{1,0:T(8,128)S(1)}, f32[8,256]{1,0:T(8,128)S(1)}, bf16[2,65,64,256]{...) custom-call(bf16[2,65,64,256]{3,2,1,0:T(8,128)(2,1)} %refs_0_.1, ...), custom_call_target="tpu_custom_call" | custom-call | tf_op jit(solution)/shard_map/pallas_call | solution.py:184
  7.1 3.0 %collective-permute-start = (f32[168,128]{1,0:T(8,128)S(1)}, f32[168,128]{1,0:T(8,128)S(1)}, u32[]{:S(2)}, u32[]{:S(2)}) collective-permute-start(f32[168,128]{1,0:T(8,128)S(1)} %get-tuple-element.28.sent), channel_id=1, source_target_pairs={{0,4},{1,29},{2,6},{3,31},{4,0},{5,9},{6,2},{7,11},{8,12},{9,5},{1... | collective-permute-start | bytes 258056 | tf_op jit(solution)/shard_map/ppermute | solution.py:449
  10.1 2.7 %collective-permute-done.came.refs_3_.refs_10_ = f32[168,128]{1,0:T(8,128)S(1)} collective-permute-done((f32[168,128]{1,0:T(8,128)S(1)}, f32[168,128]{1,0:T(8,128)S(1)}, u32[]{:S(2)}, u32[]{:S(2)}) %collective-permute-start) | collective-permute-done | bytes 86048 | tf_op jit(solution)/shard_map/ppermute | solution.py:449
  12.8 4.9 %collective-permute-start.1 = (f32[168,128]{1,0:T(8,128)S(1)}, f32[168,128]{1,0:T(8,128)S(1)}, u32[]{:S(2)}, u32[]{:S(2)}) collective-permute-start(f32[168,128]{1,0:T(8,128)S(1)} %shard_map.131), channel_id=1, source_target_pairs={{0,28},{1,5},{2,30},{3,7},{4,8},{5,1},{6,10},{7,3},{8,4},{9,13},{1... | collective-permute-start | bytes 258056 | tf_op jit(solution)/shard_map/ppermute | solution.py:449
  17.7 2.5 %collective-permute-done.1.refs_4_.refs_11_ = f32[168,128]{1,0:T(8,128)S(1)} collective-permute-done((f32[168,128]{1,0:T(8,128)S(1)}, f32[168,128]{1,0:T(8,128)S(1)}, u32[]{:S(2)}, u32[]{:S(2)}) %collective-permute-start.1) | collective-permute-done | bytes 86048 | tf_op jit(solution)/shard_map/ppermute | solution.py:449
  20.2 1.6 %collective-permute-start.2 = (f32[32,128]{1,0:T(8,128)S(1)}, f32[32,128]{1,0:T(8,128)S(1)}, u32[]{:S(2)}, u32[]{:S(2)}) collective-permute-start(f32[32,128]{1,0:T(8,128)S(1)} %slice_add_fusion.2.refs_0_), channel_id=1, source_target_pairs={{16,0},{20,4},{24,8},{28,12},{0,16},{4,20},{8,24},{12,28},{17,1},{... | collective-permute-start | bytes 49160 | tf_op jit(solution)/shard_map/ppermute | solution.py:460
  21.8 3.2 %collective-permute-done.2.refs_1_ = f32[32,128]{1,0:T(8,128)S(1)} collective-permute-done((f32[32,128]{1,0:T(8,128)S(1)}, f32[32,128]{1,0:T(8,128)S(1)}, u32[]{:S(2)}, u32[]{:S(2)}) %collective-permute-start.2) | collective-permute-done | bytes 16416 | tf_op jit(solution)/shard_map/ppermute | solution.py:460
  27.6 1.6 %collective-permute-start.4 = (f32[64,256]{1,0:T(8,128)S(1)}, f32[64,256]{1,0:T(8,128)S(1)}, u32[]{:S(2)}, u32[]{:S(2)}) collective-permute-start(f32[64,256]{1,0:T(8,128)S(1)} %add.16.refs_0_), channel_id=1, source_target_pairs={{0,2},{1,3},{2,0},{3,1},{4,6},{5,7},{6,4},{7,5},{8,10},{9,11},{10,... | collective-permute-start | bytes 196616 | tf_op jit(solution)/shard_map/ppermute | solution.py:435
  29.2 2.7 %collective-permute-done.4.refs_1_ = f32[64,256]{1,0:T(8,128)S(1)} collective-permute-done((f32[64,256]{1,0:T(8,128)S(1)}, f32[64,256]{1,0:T(8,128)S(1)}, u32[]{:S(2)}, u32[]{:S(2)}) %collective-permute-start.4) | collective-permute-done | bytes 65568 | tf_op jit(solution)/shard_map/ppermute | solution.py:435
  31.9 1.9 %shard_map.133 = (f32[64,256]{1,0:T(8,128)S(1)}, f32[64,256]{1,0:T(8,128)S(1)}, f32[104,128]{1,0:T(8,128)S(1)}, f32[64,128]{1,0:T(8,128)S(1)}) custom-call(f32[64,256]{1,0:T(8,128)S(1)} %add.16.refs_0_, f32[64,256]{1,0:T(8,128)S(1)} %collective-permute-done.4.refs_1_, f32[4,64,256]{2,1,0:T(8,128)S(1)} %get-tuple-element.33.refs_2_.refs_8_, ...), custom_call_target="tpu_custom_call" | custom-call | tf_op jit(solution)/shard_map/pallas_call | solution.py:184
  34.2 3.7 %collective-permute-done.5.came.refs_12_ = f32[104,128]{1,0:T(8,128)S(1)} collective-permute-done((f32[104,128]{1,0:T(8,128)S(1)}, f32[104,128]{1,0:T(8,128)S(1)}, u32[]{:S(2)}, u32[]{:S(2)}) %collective-permute-start.5) | collective-permute-done | bytes 53280 | tf_op jit(solution)/shard_map/ppermute | solution.py:449
  38.1 4.8 %collective-permute-start.6 = (f32[104,128]{1,0:T(8,128)S(1)}, f32[104,128]{1,0:T(8,128)S(1)}, u32[]{:S(2)}, u32[]{:S(2)}) collective-permute-start(f32[104,128]{1,0:T(8,128)S(1)} %shard_map.134), channel_id=1, source_target_pairs={{0,28},{1,5},{2,30},{3,7},{4,8},{5,1},{6,10},{7,3},{8,4},{9,13},{1... | collective-permute-start | bytes 159752 | tf_op jit(solution)/shard_map/ppermute | solution.py:449
  42.9 2.1 %collective-permute-done.6.refs_13_ = f32[104,128]{1,0:T(8,128)S(1)} collective-permute-done((f32[104,128]{1,0:T(8,128)S(1)}, f32[104,128]{1,0:T(8,128)S(1)}, u32[]{:S(2)}, u32[]{:S(2)}) %collective-permute-start.6) | collective-permute-done | bytes 53280 | tf_op jit(solution)/shard_map/ppermute | solution.py:449
  45.0 4.7 %collective-permute-done.7.refs_1_ = f32[40,128]{1,0:T(8,128)S(1)} collective-permute-done((f32[40,128]{1,0:T(8,128)S(1)}, f32[40,128]{1,0:T(8,128)S(1)}, u32[]{:S(2)}, u32[]{:S(2)}) %collective-permute-start.7) | collective-permute-done | bytes 20512 | tf_op jit(solution)/shard_map/ppermute | solution.py:460
  49.7 1.7 %shard_map.135 = (f32[72,256]{1,0:T(8,128)S(1)}, f32[8,128]{1,0:T(8,128)S(1)}) custom-call(f32[40,128]{1,0:T(8,128)S(1)} %slice_add_fusion.1.refs_0_, f32[40,128]{1,0:T(8,128)S(1)} %collective-permute-done.7.refs_1_, bf16[2,65,64,256]{3,2,1,0:T(8,128)(2,1)S(1)} %get-tuple-element.30.refs_3_.refs_6_.refs_2_.refs_15_, ...), custom_call_target="tpu_custom_call" | custom-call | tf_op jit(solution)/shard_map/pallas_call | solution.py:184
  51.5 1.6 %collective-permute-start.9 = (f32[72,256]{1,0:T(8,128)S(1)}, f32[72,256]{1,0:T(8,128)S(1)}, u32[]{:S(2)}, u32[]{:S(2)}) collective-permute-start(f32[72,256]{1,0:T(8,128)S(1)} %get-tuple-element.39.refs_0_), channel_id=1, source_target_pairs={{0,2},{1,3},{2,0},{3,1},{4,6},{5,7},{6,4},{7,5},{8,10},{9,11},{10,... | collective-permute-start | bytes 221192 | tf_op jit(solution)/shard_map/ppermute | solution.py:435
  53.3 2.6 %collective-permute-done.10.refs_3_ = f32[72,256]{1,0:T(8,128)S(1)} collective-permute-done((f32[72,256]{1,0:T(8,128)S(1)}, f32[72,256]{1,0:T(8,128)S(1)}, u32[]{:S(2)}, u32[]{:S(2)}) %collective-permute-start.10) | collective-permute-done | bytes 73760 | tf_op jit(solution)/shard_map/ppermute | solution.py:435
  55.9 1.7 %collective-permute-done.9.refs_2_ = f32[72,256]{1,0:T(8,128)S(1)} collective-permute-done((f32[72,256]{1,0:T(8,128)S(1)}, f32[72,256]{1,0:T(8,128)S(1)}, u32[]{:S(2)}, u32[]{:S(2)}) %collective-permute-start.9) | collective-permute-done | bytes 73760 | tf_op jit(solution)/shard_map/ppermute | solution.py:435
  57.6 2.0 %shard_map.136 = (f32[64,256]{1,0:T(8,128)S(1)}, f32[4,64,256]{2,1,0:T(8,128)S(1)}, f32[4,64,256]{2,1,0:T(8,128)S(1)}, f32[64,256]{1,0:T(8,128)S(1)}, f32[104,128]{1,0:T(8,128)S(1)}, /*index=5*/f32[64,128]{1,0:T(8,128)S(1)}) custom-call(f32[72,256]{1,0:T(8,128)S(1)} %get-tuple-element.39.refs_0_, f32[72,256]{1,0:T(8,128)S(1)} %collective-permute-done.8.refs_1_, ...), custom_call_target="tpu_custom_call" | custom-call | tf_op jit(solution)/shard_map/pallas_call | solution.py:184
  59.8 4.1 %collective-permute-done.11.came.refs_8_ = f32[104,128]{1,0:T(8,128)S(1)} collective-permute-done((f32[104,128]{1,0:T(8,128)S(1)}, f32[104,128]{1,0:T(8,128)S(1)}, u32[]{:S(2)}, u32[]{:S(2)}) %collective-permute-start.11) | collective-permute-done | bytes 53280 | tf_op jit(solution)/shard_map/ppermute | solution.py:449
  64.0 4.8 %collective-permute-start.12 = (f32[104,128]{1,0:T(8,128)S(1)}, f32[104,128]{1,0:T(8,128)S(1)}, u32[]{:S(2)}, u32[]{:S(2)}) collective-permute-start(f32[104,128]{1,0:T(8,128)S(1)} %shard_map.137), channel_id=1, source_target_pairs={{0,28},{1,5},{2,30},{3,7},{4,8},{5,1},{6,10},{7,3},{8,4},{9,13},{1... | collective-permute-start | bytes 159752 | tf_op jit(solution)/shard_map/ppermute | solution.py:449
  68.8 2.1 %collective-permute-done.12.refs_9_ = f32[104,128]{1,0:T(8,128)S(1)} collective-permute-done((f32[104,128]{1,0:T(8,128)S(1)}, f32[104,128]{1,0:T(8,128)S(1)}, u32[]{:S(2)}, u32[]{:S(2)}) %collective-permute-start.12) | collective-permute-done | bytes 53280 | tf_op jit(solution)/shard_map/ppermute | solution.py:449
  70.9 4.7 %collective-permute-done.13.refs_1_ = f32[40,128]{1,0:T(8,128)S(1)} collective-permute-done((f32[40,128]{1,0:T(8,128)S(1)}, f32[40,128]{1,0:T(8,128)S(1)}, u32[]{:S(2)}, u32[]{:S(2)}) %collective-permute-start.13) | collective-permute-done | bytes 20512 | tf_op jit(solution)/shard_map/ppermute | solution.py:460
  77.6 3.0 %collective-permute-done.15.refs_1_ = f32[8,128]{1,0:T(8,128)S(1)} collective-permute-done((f32[8,128]{1,0:T(8,128)S(1)}, f32[8,128]{1,0:T(8,128)S(1)}, u32[]{:S(2)}, u32[]{:S(2)}) %collective-permute-start.15) | collective-permute-done | bytes 4128 | tf_op jit(solution)/shard_map/ppermute | solution.py:435
  (25 shorter events, 6.6 us)
Async XLA Ops:
  0.6 24.4 %copy-start = (f32[64,64]{1,0:T(8,128)S(1)}, f32[64,64]{1,0:T(8,128)}, u32[]{:S(2)}) copy-start(f32[64,64]{1,0:T(8,128)} %refs_2_.3) | copy-start | bytes 49156
  7.1 5.7 %collective-permute-start = (f32[168,128]{1,0:T(8,128)S(1)}, f32[168,128]{1,0:T(8,128)S(1)}, u32[]{:S(2)}, u32[]{:S(2)}) collective-permute-start(f32[168,128]{1,0:T(8,128)S(1)} %get-tuple-element.28.sent), channel_id=1, source_target_pairs={{0,4},{1,29},{2,6},{3,31},{4,0},{5,9},{6,2},{7,11},{8,12},{9,5},{1... | collective-permute-start | bytes 258056 | tf_op jit(solution)/shard_map/ppermute | solution.py:449
  12.8 7.4 %collective-permute-start.1 = (f32[168,128]{1,0:T(8,128)S(1)}, f32[168,128]{1,0:T(8,128)S(1)}, u32[]{:S(2)}, u32[]{:S(2)}) collective-permute-start(f32[168,128]{1,0:T(8,128)S(1)} %shard_map.131), channel_id=1, source_target_pairs={{0,28},{1,5},{2,30},{3,7},{4,8},{5,1},{6,10},{7,3},{8,4},{9,13},{1... | collective-permute-start | bytes 258056 | tf_op jit(solution)/shard_map/ppermute | solution.py:449
  20.2 4.8 %collective-permute-start.2 = (f32[32,128]{1,0:T(8,128)S(1)}, f32[32,128]{1,0:T(8,128)S(1)}, u32[]{:S(2)}, u32[]{:S(2)}) collective-permute-start(f32[32,128]{1,0:T(8,128)S(1)} %slice_add_fusion.2.refs_0_), channel_id=1, source_target_pairs={{16,0},{20,4},{24,8},{28,12},{0,16},{4,20},{8,24},{12,28},{17,1},{... | collective-permute-start | bytes 49160 | tf_op jit(solution)/shard_map/ppermute | solution.py:460
  26.2 1.3 %collective-permute-start.3 = (f32[64,256]{1,0:T(8,128)S(1)}, f32[64,256]{1,0:T(8,128)S(1)}, u32[]{:S(2)}, u32[]{:S(2)}) collective-permute-start(f32[64,256]{1,0:T(8,128)S(1)} %shard_map.132), channel_id=1, source_target_pairs={{0,1},{1,0},{2,3},{3,2},{4,5},{5,4},{6,7},{7,6},{8,9},{9,8},{10,11... | collective-permute-start | bytes 196616 | tf_op jit(solution)/shard_map/ppermute | solution.py:435
  27.6 4.3 %collective-permute-start.4 = (f32[64,256]{1,0:T(8,128)S(1)}, f32[64,256]{1,0:T(8,128)S(1)}, u32[]{:S(2)}, u32[]{:S(2)}) collective-permute-start(f32[64,256]{1,0:T(8,128)S(1)} %add.16.refs_0_), channel_id=1, source_target_pairs={{0,2},{1,3},{2,0},{3,1},{4,6},{5,7},{6,4},{7,5},{8,10},{9,11},{10,... | collective-permute-start | bytes 196616 | tf_op jit(solution)/shard_map/ppermute | solution.py:435
  33.8 4.2 %collective-permute-start.5 = (f32[104,128]{1,0:T(8,128)S(1)}, f32[104,128]{1,0:T(8,128)S(1)}, u32[]{:S(2)}, u32[]{:S(2)}) collective-permute-start(f32[104,128]{1,0:T(8,128)S(1)} %get-tuple-element.37.sent), channel_id=1, source_target_pairs={{0,4},{1,29},{2,6},{3,31},{4,0},{5,9},{6,2},{7,11},{8,12},{9,5},{1... | collective-permute-start | bytes 159752 | tf_op jit(solution)/shard_map/ppermute | solution.py:449
  38.1 6.9 %collective-permute-start.6 = (f32[104,128]{1,0:T(8,128)S(1)}, f32[104,128]{1,0:T(8,128)S(1)}, u32[]{:S(2)}, u32[]{:S(2)}) collective-permute-start(f32[104,128]{1,0:T(8,128)S(1)} %shard_map.134), channel_id=1, source_target_pairs={{0,28},{1,5},{2,30},{3,7},{4,8},{5,1},{6,10},{7,3},{8,4},{9,13},{1... | collective-permute-start | bytes 159752 | tf_op jit(solution)/shard_map/ppermute | solution.py:449
  45.0 4.7 %collective-permute-start.7 = (f32[40,128]{1,0:T(8,128)S(1)}, f32[40,128]{1,0:T(8,128)S(1)}, u32[]{:S(2)}, u32[]{:S(2)}) collective-permute-start(f32[40,128]{1,0:T(8,128)S(1)} %slice_add_fusion.1.refs_0_), channel_id=1, source_target_pairs={{16,0},{20,4},{24,8},{28,12},{0,16},{4,20},{8,24},{12,28},{17,1},{... | collective-permute-start | bytes 61448 | tf_op jit(solution)/shard_map/ppermute | solution.py:460
  51.4 4.5 %collective-permute-start.10 = (f32[72,256]{1,0:T(8,128)S(1)}, f32[72,256]{1,0:T(8,128)S(1)}, u32[]{:S(2)}, u32[]{:S(2)}) collective-permute-start(f32[72,256]{1,0:T(8,128)S(1)} %get-tuple-element.39.refs_0_), channel_id=1, source_target_pairs={{0,3},{1,2},{2,1},{3,0},{4,7},{5,6},{6,5},{7,4},{8,11},{9,10},{10,... | collective-permute-start | bytes 221192 | tf_op jit(solution)/shard_map/ppermute | solution.py:435
  51.5 6.1 %collective-permute-start.9 = (f32[72,256]{1,0:T(8,128)S(1)}, f32[72,256]{1,0:T(8,128)S(1)}, u32[]{:S(2)}, u32[]{:S(2)}) collective-permute-start(f32[72,256]{1,0:T(8,128)S(1)} %get-tuple-element.39.refs_0_), channel_id=1, source_target_pairs={{0,2},{1,3},{2,0},{3,1},{4,6},{5,7},{6,4},{7,5},{8,10},{9,11},{10,... | collective-permute-start | bytes 221192 | tf_op jit(solution)/shard_map/ppermute | solution.py:435
  53.1 4.5 %collective-permute-start.8 = (f32[72,256]{1,0:T(8,128)S(1)}, f32[72,256]{1,0:T(8,128)S(1)}, u32[]{:S(2)}, u32[]{:S(2)}) collective-permute-start(f32[72,256]{1,0:T(8,128)S(1)} %get-tuple-element.39.refs_0_), channel_id=1, source_target_pairs={{0,1},{1,0},{2,3},{3,2},{4,5},{5,4},{6,7},{7,6},{8,9},{9,8},{10,11... | collective-permute-start | bytes 221192 | tf_op jit(solution)/shard_map/ppermute | solution.py:435
  59.7 4.2 %collective-permute-start.11 = (f32[104,128]{1,0:T(8,128)S(1)}, f32[104,128]{1,0:T(8,128)S(1)}, u32[]{:S(2)}, u32[]{:S(2)}) collective-permute-start(f32[104,128]{1,0:T(8,128)S(1)} %get-tuple-element.45.sent), channel_id=1, source_target_pairs={{0,4},{1,29},{2,6},{3,31},{4,0},{5,9},{6,2},{7,11},{8,12},{9,5},{1... | collective-permute-start | bytes 159752 | tf_op jit(solution)/shard_map/ppermute | solution.py:449
  64.0 6.9 %collective-permute-start.12 = (f32[104,128]{1,0:T(8,128)S(1)}, f32[104,128]{1,0:T(8,128)S(1)}, u32[]{:S(2)}, u32[]{:S(2)}) collective-permute-start(f32[104,128]{1,0:T(8,128)S(1)} %shard_map.137), channel_id=1, source_target_pairs={{0,28},{1,5},{2,30},{3,7},{4,8},{5,1},{6,10},{7,3},{8,4},{9,13},{1... | collective-permute-start | bytes 159752 | tf_op jit(solution)/shard_map/ppermute | solution.py:449
  70.9 4.7 %collective-permute-start.13 = (f32[40,128]{1,0:T(8,128)S(1)}, f32[40,128]{1,0:T(8,128)S(1)}, u32[]{:S(2)}, u32[]{:S(2)}) collective-permute-start(f32[40,128]{1,0:T(8,128)S(1)} %slice_add_fusion.refs_0_), channel_id=1, source_target_pairs={{16,0},{20,4},{24,8},{28,12},{0,16},{4,20},{8,24},{12,28},{17,1},{... | collective-permute-start | bytes 61448 | tf_op jit(solution)/shard_map/ppermute | solution.py:460
  75.7 1.2 %collective-permute-start.14 = (f32[8,128]{1,0:T(8,128)S(1)}, f32[8,128]{1,0:T(8,128)S(1)}, u32[]{:S(2)}, u32[]{:S(2)}) collective-permute-start(f32[8,128]{1,0:T(8,128)S(1)} %get-tuple-element.47), channel_id=1, source_target_pairs={{0,1},{1,0},{2,3},{3,2},{4,5},{5,4},{6,7},{7,6},{8,9},{9,8},{10,11... | collective-permute-start | bytes 12296 | tf_op jit(solution)/shard_map/ppermute | solution.py:435
  77.0 3.6 %collective-permute-start.15 = (f32[8,128]{1,0:T(8,128)S(1)}, f32[8,128]{1,0:T(8,128)S(1)}, u32[]{:S(2)}, u32[]{:S(2)}) collective-permute-start(f32[8,128]{1,0:T(8,128)S(1)} %add.19.refs_0_), channel_id=1, source_target_pairs={{0,2},{1,3},{2,0},{3,1},{4,6},{5,7},{6,4},{7,5},{8,10},{9,11},{10,... | collective-permute-start | bytes 12296 | tf_op jit(solution)/shard_map/ppermute | solution.py:435

commit v2 on v1

--- a/solution.py
+++ b/solution.py
@@ -11,6 +11,7 @@
 COLS = 128
 LANES = 128
 GROUP = 8
+CHUNK = 16
 SHRINK_SCALE = 0.4
 TINY = 1e-06
 VMEM = pltpu.VMEM
@@ -67,12 +68,14 @@
     return total + pltpu.roll(total, LANES // 2, 1)
 
 
-def forward(field, kernel_ref, plain, weighted_t, arrived=None):
+def forward(field, kernel_ref, plain, weighted_t):
+    return forward_of(exact(plain, field), kernel_ref, weighted_t, field.shape[0])
+
+
+def forward_of(spectra, kernel_ref, weighted_t, times, arrived=None):
     freqs, sensors = kernel_ref.shape[1:3]
-    times = field.shape[0]
-    spectra = exact(plain, field)
     rows = []
-    for group in range(plain.shape[0] // 16):
+    for group in range(spectra.shape[0] // 16):
         part = spectra[16 * group : 16 * group + 16]
         if arrived is not None:
             arrived(group)
@@ -196,18 +199,18 @@
     return tree_sum([part[...] for part in parts])
 
 
-def below_first():
-    return lax.rem(lax.axis_index("cell") + lax.axis_index("sensor"), 2) == 0
+def is_even():
+    return lax.rem(lax.axis_index("cell"), 2) == 0
 
 
 def edges(head, tail):
-    first = below_first()
-    return jnp.where(first, tail, head), jnp.where(first, head, tail)
-
-
-def beside(hop_one, hop_two):
-    first = below_first()
-    return jnp.where(first, hop_two, hop_one), jnp.where(first, hop_one, hop_two)
+    even = is_even()
+    return jnp.where(even, tail, head), jnp.where(even, head, tail)
+
+
+def beside(partner, other):
+    even = is_even()
+    return jnp.where(even, other, partner), jnp.where(even, partner, other)
 
 
 def rows_of(scalars):
@@ -224,6 +227,7 @@
     field, multiplier, neighbours, tile_of_cell, tile_weight, plain, weighted_t = kept[1:8]
     freqs = kernel.shape[1]
     times, cells = field.shape
+    half = times // 2
     copies = []
 
     def load(source, target):
@@ -232,28 +236,18 @@
         copies.append(copy)
         return copy
 
-    early = [load(loaded[i], kept[i]) for i in (1, 6, 7)]
-    small = [load(loaded[i], kept[i]) for i in (3, 4, 5, 2)]
+    early = [load(loaded[i], kept[i]) for i in (1, 6)]
     large = []
-    for group in range(plain.shape[0] // 16):
-        start = group * GROUP
-        for part in range(2):
-            at = (part, pl.ds(start, min(GROUP, freqs - start)))
-            large.append(load(kernel.at[at], kernel_here.at[at]))
-    late = [load(loaded[i], kept[i]) for i in (8, 9)]
-
+    for start in range(0, freqs, CHUNK):
+        at = (slice(None), pl.ds(start, min(CHUNK, freqs - start)))
+        large.append(load(kernel.at[at], kernel_here.at[at]))
+    small = [load(loaded[i], kept[i]) for i in (3, 4, 5, 2, 7, 8, 9)]
     for copy in early:
         copy.wait()
-
-    def arrived(group):
-        large[2 * group].wait()
-        large[2 * group + 1].wait()
-
-    half = times // 2
-    sent[:half, :] = forward(field[...], kernel_here, plain[...], weighted_t[...], arrived)
-
+    spectra = exact(plain[...], field[...])
     for copy in small:
         copy.wait()
+
     cell = lax.broadcasted_iota(jnp.int32, (4, cells), 1) + lax.axis_index("cell") * cells
     linked[0:4, :] = jnp.where(neighbours[...] != cell, 1.0, 0.0)
     linked[4:8, :] = jnp.zeros((4, cells), jnp.float32)
@@ -274,14 +268,12 @@
         one, two = edges(head, tail)
         sent[half + start : half + start + head.shape[0], :] = one
         edge[start : start + head.shape[0], :] = two
-    for copy in late:
-        copy.wait()
-
-
-def first_merge_body(sent, came, edge, out):
-    half = sent.shape[0] - edge.shape[0]
-    out[:half, :] = sent[:half, :] + came[:half, :]
-    out[half:, :] = edge[...]
+
+    def arrived(group):
+        if group * GROUP % CHUNK == 0:
+            large[group * GROUP // CHUNK].wait()
+
+    sent[:half, :] = forward_of(spectra, kernel_here, weighted_t[...], times, arrived)
 
 
 def first_adjoint_body(count, *refs):
@@ -309,16 +301,15 @@
     edge[...] = two
 
 
-def merge_body(sent, came, edge, linked, out):
+def merge_body(sent, came, edge, other, linked, out):
     cells = linked.shape[1]
-    top = sent.shape[0] - edge.shape[0]
-    mask = jnp.where(below_first(), linked[3:4, cells - COLS :], linked[2:3, :COLS])
-    across = mask * (came[top:, :] - sent[top:, :])
+    top = out.shape[0]
+    to_partner, to_other = edges(linked[2:3, :COLS], linked[3:4, cells - COLS :])
+    across = to_partner * (came[top:, :] - sent[top:, :])
+    beyond = to_other * (other[...] - edge[...])
     out[: top - 8, :] = sent[: top - 8, :] + came[: top - 8, :]
-    out[top - 8 : top, :] = (
-        sent[top - 8 : top, :] + came[top - 8 : top, :] + rows_of([0.0, 0.0, 2.0 * square_sum(across)])
-    )
-    out[top:, :] = edge[...]
+    boundary = 2.0 * jnp.sum(across * across + beyond * beyond)
+    out[top - 8 :, :] = sent[top - 8 : top, :] + came[top - 8 : top, :] + rows_of([0.0, boundary])
 
 
 def first_gradient_body(count, *refs):
@@ -329,7 +320,7 @@
     linked = linked_ref[...]
     total = summed(refs[:count])
     values = [[strip(start_multiplier[k], r) for r in range(cells // COLS)] for k in range(4)]
-    above, below = beside(one[half + times : half + 2 * times, :], two[half + times : half + 2 * times, :])
+    above, below = beside(one[half + times : half + 2 * times, :], two[times : 2 * times, :])
     field = total + gathered_jumps(values, above, below, linked)
     adjoint_out[...] = total
     gradient[...] = field
@@ -343,14 +334,12 @@
     total = summed(refs[:count])
     packed, squares = total[:half], total[half : half + 8]
     out[:times, :] = adjoint(unpacked(packed, kernel.shape[2]), kernel, plain_t[...], weighted[...], 2)
-    across = squares[2:3, :] * (2.0 / lax.axis_size("sensor"))
-    scalars = rows_of([square_sum(packed), across])
-    out[times:, :] = jnp.concatenate([scalars] * (out.shape[1] // LANES), axis=1)
+    out[times:, :] = jnp.full((8, out.shape[1]), square_sum(packed), jnp.float32)
     norms[...] = squares
 
 
 def step_of(norms, scalars):
-    return norms[0, 0] / (scalars[0, 0] + (norms[1, 0] + scalars[1, 0]) + TINY)
+    return norms[0, 0] / (scalars[0, 0] + norms[1, 0] + TINY)
 
 
 def second_gradient_body(count, *refs):
@@ -363,9 +352,9 @@
     linked = linked_ref[...]
     field, gradient = model[...], gradient_in[...]
     rows = cells // COLS
-    above, below = beside(one[half:, :], two[half:, :])
+    above, below = beside(one[half:, :], two[...])
     field_jumps = jumps(field, above[:times], below[:times], linked)
-    grad_jumps = jumps(gradient, *beside(grad_one[half + 8 :, :], grad_two[half + 8 :, :]), linked)
+    grad_jumps = jumps(gradient, *beside(grad_one[half + 8 :, :], grad_two[...]), linked)
 
     def advance(model_jumps, old_multiplier, limit):
         shifted = model_jumps + old_multiplier
@@ -397,7 +386,7 @@
     out, norms = refs[count:]
     total = summed(refs[:count])
     packed, squares = total[:-8], total[-8:]
-    out[...] = rows_of([square_sum(packed), squares[2:3, :] * (2.0 / lax.axis_size("sensor"))])
+    out[...] = jnp.full((8, LANES), square_sum(packed), jnp.float32)
     norms[...] = squares
 
 
@@ -408,7 +397,7 @@
     half = gradient_in.shape[0] // 2
     gradient = gradient_in[...]
     estimate_out[...] = model[...] - step * gradient
-    grad_jumps = jumps(gradient, *beside(grad_one[half + 8 :, :], grad_two[half + 8 :, :]), linked[...])
+    grad_jumps = jumps(gradient, *beside(grad_one[half + 8 :, :], grad_two[...]), linked[...])
     for k in range(4):
         for r in range(gradient.shape[1] // COLS):
             at = slice(r * COLS, (r + 1) * COLS)
@@ -418,48 +407,44 @@
             multiplier_out[k, :, at] = shifted - auxiliary
 
 
-def sensor_parts(array, *radices):
-    count = lax.axis_size("sensor")
-    stages, left = [], count
+def stages_of(count, *radices):
+    stages = []
     for radix in radices:
-        if left > 1 and left % radix == 0:
+        if count > 1 and count % radix == 0:
             stages.append(radix)
-            left //= radix
-    while left > 1:
+            count //= radix
+    while count > 1:
         stages.append(2)
-        left //= 2
-    parts, stride = [array], 1
+        count //= 2
+    return stages
+
+
+def summing(parts, axis, stride, stages):
+    count = lax.axis_size(axis)
     for radix in stages:
         total = tree_sum(parts)
         parts = [total] + [
-            lax.ppermute(total, "sensor", [(i, i ^ (k * stride)) for i in range(count)]) for k in range(1, radix)
+            lax.ppermute(total, axis, [(i, i ^ (k * stride)) for i in range(count)]) for k in range(1, radix)
         ]
         stride *= radix
     return parts
 
 
-def neighbour_hop(array, second):
-    cells, sensors = lax.axis_size("cell"), lax.axis_size("sensor")
-    pairs = []
-    for cell in range(cells):
-        for sensor in range(sensors):
-            down = ((cell + sensor) % 2 == 0) != second
-            other = (cell + (1 if down else -1)) % cells
-            pairs.append((cell * sensors + sensor, other * sensors + sensor))
-    return lax.ppermute(array, ("cell", "sensor"), pairs)
-
-
-def cell_parts(sent, merge, rows):
-    one = neighbour_hop(sent, False)
-    sent = merge(one)
-    two = neighbour_hop(sent, True)
-    parts = [sent[:rows], two[:rows]]
-    count, shift = lax.axis_size("cell"), 4
-    while shift < count:
-        total = parts[0] + parts[1]
-        parts = [total, lax.ppermute(total, "cell", [((i + shift) % count, i) for i in range(count)])]
-        shift *= 2
-    return parts, one, two
+def sensor_parts(array, *radices):
+    return summing([array], "sensor", 1, stages_of(lax.axis_size("sensor"), *radices))
+
+
+def cell_parts(merged):
+    return summing([merged], "cell", 2, stages_of(lax.axis_size("cell") // 2, 4, 4))
+
+
+def from_partner(array):
+    return lax.ppermute(array, "cell", [(i, i ^ 1) for i in range(lax.axis_size("cell"))])
+
+
+def from_other(array):
+    inner = range(1, lax.axis_size("cell") - 1)
+    return lax.ppermute(array, "cell", [(i, i + 1 if i % 2 else i - 1) for i in inner])
 
 
 def per_device(kernel, observed, start_model, start_multiplier, neighbours, tile_of_cell, tile_weight):
@@ -478,12 +463,13 @@
         [(half + 2 * times + 8, LANES), (2 * times + 8, LANES), (8, cells), (8, cells)]
         + [jax.ShapeDtypeStruct(a.shape, a.dtype) for a in loads],
         *[pltpu.with_memory_space_constraint(a, HBM) for a in loads],
-        scratch=[pltpu.SemaphoreType.DMA((9 + 2 * (plain.shape[0] // 16),))],
+        scratch=[pltpu.SemaphoreType.DMA((9 + -(-freqs // CHUNK),))],
         inputs=HBM,
     )
-    parts, one, two = cell_parts(
-        sent, lambda came: call(first_merge_body, (half + 2 * times + 8, LANES), sent, came, edge), half
-    )
+    one = from_partner(sent)
+    merged, edge = lax.optimization_barrier((sent[:half] + one[:half], edge))
+    parts = cell_parts(merged)
+    two = from_other(edge)
     back = call(functools.partial(first_adjoint_body, len(parts)), field, *parts, observed, kernel, plain_t, weighted)
     parts = sensor_parts(back, 2, 2)
     message, side = (half + 8 + times, LANES), (times, LANES)
@@ -491,9 +477,8 @@
         functools.partial(first_gradient_body, len(parts)), [field, field, message, side],
         *parts, start_multiplier, one, two, linked, kernel, plain, weighted_t,
     )
-    parts, grad_one, grad_two = cell_parts(
-        sent, lambda came: call(merge_body, message, sent, came, edge, linked), half + 8
-    )
+    grad_one, grad_two = from_partner(sent), from_other(edge)
+    parts = cell_parts(call(merge_body, (half + 8, LANES), sent, grad_one, edge, grad_two, linked))
     back, norms = call(
         functools.partial(second_adjoint_body, len(parts)), [(times + 8, cells), (8, LANES)],
         *parts, kernel, plain_t, weighted,
@@ -504,11 +489,10 @@
         *parts, norms, adjoint_one, gradient, start_model, start_multiplier, threshold, one, two, grad_one, grad_two,
         linked, kernel, plain, weighted_t,
     )
-    parts, grad_one, grad_two = cell_parts(
-        sent, lambda came: call(merge_body, message, sent, came, edge, linked), half + 8
-    )
+    grad_one, grad_two = from_partner(sent), from_other(edge)
+    parts = cell_parts(call(merge_body, (half + 8, LANES), sent, grad_one, edge, grad_two, linked))
     square, norms = call(functools.partial(response_body, len(parts)), [(8, LANES), (8, LANES)], *parts)
-    parts = sensor_parts(square, 2, 2)
+    parts = sensor_parts(square, 4)
     return tuple(
         call(
             functools.partial(finish_body, len(parts)), [field, wide, wide],

time: 81.7 us -> 75.1 us (0.919)
  waiting for transfers between devices: 42.2 us -> 28 us
  starting transfers between devices: 23.9 us -> 32.7 us
  Pallas kernels: 14.7 us -> 13.4 us
    ppermute x16 -> x23, waiting for transfers between devices: 42.2 us -> 28 us  [the longest x17 21.3 us: summing(): lax.ppermute(total, axis, [(i, i ^ k * stride) for i in range(count)])]
    ppermute x16 -> x23, starting transfers between devices: 23.9 us -> 32.7 us  [the longest x17 23.5 us: summing(): lax.ppermute(total, axis, [(i, i ^ k * stride) for i in range(count)])]
    pallas_call x10 -> x9, Pallas kernels: 14.7 us -> 13.4 us  [call(): pl.pallas_call(body, out_shape=shapes, in_specs=[pl.BlockSpec(memory_spac...]
  transfers between devices with their start and end apart: 16 -> 23, of which waited for: 15 -> 16; matrix products, arithmetic and copies ran while one was open for 0% -> 0% of each run, Pallas kernels for 0% -> 0%
where the time goes in v2:
time: 75.1 us; the launch traced here: 74.9 us
  starting transfers between devices  32.7 us (44%)
  waiting for transfers between devices  28 us (37%)
  Pallas kernels  13.4 us (18%)
  between operations  0.78 us (1%)
    ppermute x17, starting transfers between devices, summing(): lax.ppermute(total, axis, [(i, i ^ k * stride) for i in range(count)])  23.5 us
    ppermute x17, waiting for transfers between devices, summing(): lax.ppermute(total, axis, [(i, i ^ k * stride) for i in range(count)])  21.3 us
    pallas_call x9, Pallas kernels, call(): pl.pallas_call(body, out_shape=shapes, in_specs=[pl.BlockSpec(memory_spac...  13.4 us
    ppermute x3, starting transfers between devices, from_partner(): lax.ppermute(array, 'cell', [(i, i ^ 1) for i in range(lax.axis_size('cel...  7.2 us
    ppermute x3, waiting for transfers between devices, from_partner(): lax.ppermute(array, 'cell', [(i, i ^ 1) for i in range(lax.axis_size('cel...  6.7 us
    ppermute x3, starting transfers between devices, from_other(): lax.ppermute(array, 'cell', [(i, i + 1 if i % 2 else i - 1) for i in inner])  1.97 us
  transfers between devices with their start and end apart: 23, of which 16 were waited for; matrix products, arithmetic and copies ran while one was open for 0% of the time, Pallas kernels for 0%

profile of v2, /device:TPU:0, one launch (start us, length us, event | category | flops | bytes accessed | tf_op | source)
XLA Modules:
  0.0 74.9 jit_solution(8787264707637636328)
XLA Ops:
  0.6 5.1 %shard_map.130 = (f32[168,128]{1,0:T(8,128)S(1)}, f32[136,128]{1,0:T(8,128)S(1)}, f32[8,256]{1,0:T(8,128)S(1)}, f32[8,256]{1,0:T(8,128)S(1)}, bf16[2,65,64,256]{...) custom-call(bf16[2,65,64,256]{3,2,1,0:T(8,128)(2,1)} %refs_0_.1, ...), custom_call_target="tpu_custom_call" | custom-call | tf_op jit(solution)/shard_map/pallas_call | solution.py:187
  5.8 3.0 %collective-permute-start = (f32[168,128]{1,0:T(8,128)S(1)}, f32[168,128]{1,0:T(8,128)S(1)}, u32[]{:S(2)}, u32[]{:S(2)}) collective-permute-start(f32[168,128]{1,0:T(8,128)S(1)} %get-tuple-element.30), channel_id=1, source_target_pairs={{0,4},{4,0},{8,12},{12,8},{16,20},{20,16},{24,28},{28,24},{1,5},{5... | collective-permute-start | bytes 258056 | tf_op jit(solution)/shard_map/ppermute | solution.py:442
  8.8 2.5 %collective-permute-done.refs_3_.refs_10_ = f32[168,128]{1,0:T(8,128)S(1)} collective-permute-done((f32[168,128]{1,0:T(8,128)S(1)}, f32[168,128]{1,0:T(8,128)S(1)}, u32[]{:S(2)}, u32[]{:S(2)}) %collective-permute-start) | collective-permute-done | bytes 86048 | tf_op jit(solution)/shard_map/ppermute | solution.py:442
  11.4 4.0 %collective-permute-start.3 = (f32[32,128]{1,0:T(8,128)S(1)}, f32[32,128]{1,0:T(8,128)S(1)}, u32[]{:S(2)}, u32[]{:S(2)}) collective-permute-start(f32[32,128]{1,0:T(8,128)S(1)} %slice_add_fusion.refs_0_), channel_id=1, source_target_pairs={{0,24},{4,28},{8,16},{12,20},{16,8},{20,12},{24,0},{28,4},{1,25},{... | collective-permute-start | bytes 49160 | tf_op jit(solution)/shard_map/ppermute | solution.py:427
  17.1 2.9 %collective-permute-done.2.refs_2_ = f32[32,128]{1,0:T(8,128)S(1)} collective-permute-done((f32[32,128]{1,0:T(8,128)S(1)}, f32[32,128]{1,0:T(8,128)S(1)}, u32[]{:S(2)}, u32[]{:S(2)}) %collective-permute-start.2) | collective-permute-done | bytes 16416 | tf_op jit(solution)/shard_map/ppermute | solution.py:427
  20.0 1.3 %shard_map.131 = f32[64,256]{1,0:T(8,128)S(1)} custom-call(f32[32,128]{1,0:T(8,128)S(1)} %slice_add_fusion.refs_0_, f32[32,128]{1,0:T(8,128)S(1)} %collective-permute-done.1.refs_1_, f32[32,128]{1,0:T(8,128)S(1)} %collective-permute-done.2.refs_2_, f32[32,128]{1,0:T(8,128)S(1)} %collective-permute-done.3.refs_3_, f32[64,64]{1,0:T(8,128)S(1)} %copy-done, ...), custom_call_target="tpu_custom_call" | custom-call | tf_op jit(solution)/shard_map/pallas_call | solution.py:187
  22.6 1.6 %collective-permute-start.5 = (f32[64,256]{1,0:T(8,128)S(1)}, f32[64,256]{1,0:T(8,128)S(1)}, u32[]{:S(2)}, u32[]{:S(2)}) collective-permute-start(f32[64,256]{1,0:T(8,128)S(1)} %add.7.refs_0_), channel_id=1, source_target_pairs={{0,2},{1,3},{2,0},{3,1},{4,6},{5,7},{6,4},{7,5},{8,10},{9,11},{10,... | collective-permute-start | bytes 196616 | tf_op jit(solution)/shard_map/ppermute | solution.py:427
  24.2 2.8 %collective-permute-done.5.refs_1_ = f32[64,256]{1,0:T(8,128)S(1)} collective-permute-done((f32[64,256]{1,0:T(8,128)S(1)}, f32[64,256]{1,0:T(8,128)S(1)}, u32[]{:S(2)}, u32[]{:S(2)}) %collective-permute-start.5) | collective-permute-done | bytes 65568 | tf_op jit(solution)/shard_map/ppermute | solution.py:427
  27.0 1.8 %shard_map.132 = (f32[64,256]{1,0:T(8,128)S(1)}, f32[64,256]{1,0:T(8,128)S(1)}, f32[104,128]{1,0:T(8,128)S(1)}, f32[64,128]{1,0:T(8,128)S(1)}) custom-call(f32[64,256]{1,0:T(8,128)S(1)} %add.7.refs_0_, f32[64,256]{1,0:T(8,128)S(1)} %collective-permute-done.5.refs_1_, f32[4,64,256]{2,1,0:T(8,128)S(1)} %get-tuple-element.36.refs_2_.refs_8_, ...), custom_call_target="tpu_custom_call" | custom-call | tf_op jit(solution)/shard_map/pallas_call | solution.py:187
  28.8 3.4 %collective-permute-start.7 = (f32[104,128]{1,0:T(8,128)S(1)}, f32[104,128]{1,0:T(8,128)S(1)}, u32[]{:S(2)}, u32[]{:S(2)}) collective-permute-start(f32[104,128]{1,0:T(8,128)S(1)} %get-tuple-element.41.sent), channel_id=1, source_target_pairs={{0,4},{4,0},{8,12},{12,8},{16,20},{20,16},{24,28},{28,24},{1,5},{5... | collective-permute-start | bytes 159752 | tf_op jit(solution)/shard_map/ppermute | solution.py:442
  32.9 1.4 %collective-permute-done.7.came.refs_12_ = f32[104,128]{1,0:T(8,128)S(1)} collective-permute-done((f32[104,128]{1,0:T(8,128)S(1)}, f32[104,128]{1,0:T(8,128)S(1)}, u32[]{:S(2)}, u32[]{:S(2)}) %collective-permute-start.7) | collective-permute-done | bytes 53280 | tf_op jit(solution)/shard_map/ppermute | solution.py:442
  34.4 6.5 %collective-permute-start.11 = (f32[40,128]{1,0:T(8,128)S(1)}, f32[40,128]{1,0:T(8,128)S(1)}, u32[]{:S(2)}, u32[]{:S(2)}) collective-permute-start(f32[40,128]{1,0:T(8,128)S(1)} %shard_map.133.refs_0_), channel_id=1, source_target_pairs={{0,24},{4,28},{8,16},{12,20},{16,8},{20,12},{24,0},{28,4},{1,25},{... | collective-permute-start | bytes 61448 | tf_op jit(solution)/shard_map/ppermute | solution.py:427
  41.0 1.3 %collective-permute-start.10 = (f32[40,128]{1,0:T(8,128)S(1)}, f32[40,128]{1,0:T(8,128)S(1)}, u32[]{:S(2)}, u32[]{:S(2)}) collective-permute-start(f32[40,128]{1,0:T(8,128)S(1)} %shard_map.133.refs_0_), channel_id=1, source_target_pairs={{0,16},{4,20},{8,24},{12,28},{16,0},{20,4},{24,8},{28,12},{1,17},{... | collective-permute-start | bytes 61448 | tf_op jit(solution)/shard_map/ppermute | solution.py:427
  42.8 2.8 %collective-permute-done.10.refs_2_ = f32[40,128]{1,0:T(8,128)S(1)} collective-permute-done((f32[40,128]{1,0:T(8,128)S(1)}, f32[40,128]{1,0:T(8,128)S(1)}, u32[]{:S(2)}, u32[]{:S(2)}) %collective-permute-start.10) | collective-permute-done | bytes 20512 | tf_op jit(solution)/shard_map/ppermute | solution.py:427
  46.0 1.7 %shard_map.134 = (f32[72,256]{1,0:T(8,128)S(1)}, f32[8,128]{1,0:T(8,128)S(1)}) custom-call(f32[40,128]{1,0:T(8,128)S(1)} %shard_map.133.refs_0_, f32[40,128]{1,0:T(8,128)S(1)} %collective-permute-done.9.refs_1_, f32[40,128]{1,0:T(8,128)S(1)} %collective-permute-done.10.refs_2_, f32[40,128]{1,0:T(8,128)S(1)} %collective-permute-done.11.refs_3_, ...), custom_call_target="tpu_custom_call" | custom-call | tf_op jit(solution)/shard_map/pallas_call | solution.py:187
  47.8 1.6 %collective-permute-start.13 = (f32[72,256]{1,0:T(8,128)S(1)}, f32[72,256]{1,0:T(8,128)S(1)}, u32[]{:S(2)}, u32[]{:S(2)}) collective-permute-start(f32[72,256]{1,0:T(8,128)S(1)} %get-tuple-element.43.refs_0_), channel_id=1, source_target_pairs={{0,2},{1,3},{2,0},{3,1},{4,6},{5,7},{6,4},{7,5},{8,10},{9,11},{10,... | collective-permute-start | bytes 221192 | tf_op jit(solution)/shard_map/ppermute | solution.py:427
  49.7 2.7 %collective-permute-done.14.refs_3_ = f32[72,256]{1,0:T(8,128)S(1)} collective-permute-done((f32[72,256]{1,0:T(8,128)S(1)}, f32[72,256]{1,0:T(8,128)S(1)}, u32[]{:S(2)}, u32[]{:S(2)}) %collective-permute-start.14) | collective-permute-done | bytes 73760 | tf_op jit(solution)/shard_map/ppermute | solution.py:427
  52.3 1.6 %collective-permute-done.13.refs_2_ = f32[72,256]{1,0:T(8,128)S(1)} collective-permute-done((f32[72,256]{1,0:T(8,128)S(1)}, f32[72,256]{1,0:T(8,128)S(1)}, u32[]{:S(2)}, u32[]{:S(2)}) %collective-permute-start.13) | collective-permute-done | bytes 73760 | tf_op jit(solution)/shard_map/ppermute | solution.py:427
  54.0 2.0 %shard_map.135 = (f32[64,256]{1,0:T(8,128)S(1)}, f32[4,64,256]{2,1,0:T(8,128)S(1)}, f32[4,64,256]{2,1,0:T(8,128)S(1)}, f32[64,256]{1,0:T(8,128)S(1)}, f32[104,128]{1,0:T(8,128)S(1)}, /*index=5*/f32[64,128]{1,0:T(8,128)S(1)}) custom-call(f32[72,256]{1,0:T(8,128)S(1)} %get-tuple-element.43.refs_0_, f32[72,256]{1,0:T(8,128)S(1)} %collective-permute-done.12.refs_1_, ...), custom_call_target="tpu_custom_call" | custom-call | tf_op jit(solution)/shard_map/pallas_call | solution.py:187
  57.5 2.7 %collective-permute-done.15.came.refs_10_ = f32[104,128]{1,0:T(8,128)S(1)} collective-permute-done((f32[104,128]{1,0:T(8,128)S(1)}, f32[104,128]{1,0:T(8,128)S(1)}, u32[]{:S(2)}, u32[]{:S(2)}) %collective-permute-start.15) | collective-permute-done | bytes 53280 | tf_op jit(solution)/shard_map/ppermute | solution.py:442
  60.4 5.0 %collective-permute-start.19 = (f32[40,128]{1,0:T(8,128)S(1)}, f32[40,128]{1,0:T(8,128)S(1)}, u32[]{:S(2)}, u32[]{:S(2)}) collective-permute-start(f32[40,128]{1,0:T(8,128)S(1)} %shard_map.136.refs_0_), channel_id=1, source_target_pairs={{0,24},{4,28},{8,16},{12,20},{16,8},{20,12},{24,0},{28,4},{1,25},{... | collective-permute-start | bytes 61448 | tf_op jit(solution)/shard_map/ppermute | solution.py:427
  66.0 1.3 %collective-permute-done.19.refs_3_ = f32[40,128]{1,0:T(8,128)S(1)} collective-permute-done((f32[40,128]{1,0:T(8,128)S(1)}, f32[40,128]{1,0:T(8,128)S(1)}, u32[]{:S(2)}, u32[]{:S(2)}) %collective-permute-start.19) | collective-permute-done | bytes 20512 | tf_op jit(solution)/shard_map/ppermute | solution.py:427
  67.2 2.8 %collective-permute-done.18.refs_2_ = f32[40,128]{1,0:T(8,128)S(1)} collective-permute-done((f32[40,128]{1,0:T(8,128)S(1)}, f32[40,128]{1,0:T(8,128)S(1)}, u32[]{:S(2)}, u32[]{:S(2)}) %collective-permute-start.18) | collective-permute-done | bytes 20512 | tf_op jit(solution)/shard_map/ppermute | solution.py:427
  70.8 1.3 %collective-permute-start.20 = (f32[8,128]{1,0:T(8,128)S(1)}, f32[8,128]{1,0:T(8,128)S(1)}, u32[]{:S(2)}, u32[]{:S(2)}) collective-permute-start(f32[8,128]{1,0:T(8,128)S(1)} %get-tuple-element.51.refs_0_), channel_id=1, source_target_pairs={{0,1},{1,0},{2,3},{3,2},{4,5},{5,4},{6,7},{7,6},{8,9},{9,8},{10,11... | collective-permute-start | bytes 12296 | tf_op jit(solution)/shard_map/ppermute | solution.py:427
  (35 shorter events, 11.0 us)
Async XLA Ops:
  0.6 19.4 %copy-start = (f32[64,64]{1,0:T(8,128)S(1)}, f32[64,64]{1,0:T(8,128)}, u32[]{:S(2)}) copy-start(f32[64,64]{1,0:T(8,128)} %refs_4_.1) | copy-start | bytes 49156
  5.8 5.6 %collective-permute-start = (f32[168,128]{1,0:T(8,128)S(1)}, f32[168,128]{1,0:T(8,128)S(1)}, u32[]{:S(2)}, u32[]{:S(2)}) collective-permute-start(f32[168,128]{1,0:T(8,128)S(1)} %get-tuple-element.30), channel_id=1, source_target_pairs={{0,4},{4,0},{8,12},{12,8},{16,20},{20,16},{24,28},{28,24},{1,5},{5... | collective-permute-start | bytes 258056 | tf_op jit(solution)/shard_map/ppermute | solution.py:442
  11.4 5.8 %collective-permute-start.3 = (f32[32,128]{1,0:T(8,128)S(1)}, f32[32,128]{1,0:T(8,128)S(1)}, u32[]{:S(2)}, u32[]{:S(2)}) collective-permute-start(f32[32,128]{1,0:T(8,128)S(1)} %slice_add_fusion.refs_0_), channel_id=1, source_target_pairs={{0,24},{4,28},{8,16},{12,20},{16,8},{20,12},{24,0},{28,4},{1,25},{... | collective-permute-start | bytes 49160 | tf_op jit(solution)/shard_map/ppermute | solution.py:427
  15.4 4.6 %collective-permute-start.2 = (f32[32,128]{1,0:T(8,128)S(1)}, f32[32,128]{1,0:T(8,128)S(1)}, u32[]{:S(2)}, u32[]{:S(2)}) collective-permute-start(f32[32,128]{1,0:T(8,128)S(1)} %slice_add_fusion.refs_0_), channel_id=1, source_target_pairs={{0,16},{4,20},{8,24},{12,28},{16,0},{20,4},{24,8},{28,12},{1,17},{... | collective-permute-start | bytes 49160 | tf_op jit(solution)/shard_map/ppermute | solution.py:427
  15.4 4.6 %collective-permute-start.1 = (f32[32,128]{1,0:T(8,128)S(1)}, f32[32,128]{1,0:T(8,128)S(1)}, u32[]{:S(2)}, u32[]{:S(2)}) collective-permute-start(f32[32,128]{1,0:T(8,128)S(1)} %slice_add_fusion.refs_0_), channel_id=1, source_target_pairs={{0,8},{4,12},{8,0},{12,4},{16,24},{20,28},{24,16},{28,20},{1,9},{5... | collective-permute-start | bytes 49160 | tf_op jit(solution)/shard_map/ppermute | solution.py:427
  21.3 1.3 %collective-permute-start.4 = (f32[64,256]{1,0:T(8,128)S(1)}, f32[64,256]{1,0:T(8,128)S(1)}, u32[]{:S(2)}, u32[]{:S(2)}) collective-permute-start(f32[64,256]{1,0:T(8,128)S(1)} %shard_map.131), channel_id=1, source_target_pairs={{0,1},{1,0},{2,3},{3,2},{4,5},{5,4},{6,7},{7,6},{8,9},{9,8},{10,11... | collective-permute-start | bytes 196616 | tf_op jit(solution)/shard_map/ppermute | solution.py:427
  21.4 2.8 %collective-permute-start.6 = (f32[136,128]{1,0:T(8,128)S(1)}, f32[136,128]{1,0:T(8,128)S(1)}, u32[]{:S(2)}, u32[]{:S(2)}) collective-permute-start(f32[136,128]{1,0:T(8,128)S(1)} %get-tuple-element.37), channel_id=1, source_target_pairs={{4,8},{8,4},{12,16},{16,12},{20,24},{24,20},{5,9},{9,5},{13,17},{1... | collective-permute-start | bytes 208904 | tf_op jit(solution)/shard_map/ppermute | solution.py:447
  22.6 4.3 %collective-permute-start.5 = (f32[64,256]{1,0:T(8,128)S(1)}, f32[64,256]{1,0:T(8,128)S(1)}, u32[]{:S(2)}, u32[]{:S(2)}) collective-permute-start(f32[64,256]{1,0:T(8,128)S(1)} %add.7.refs_0_), channel_id=1, source_target_pairs={{0,2},{1,3},{2,0},{3,1},{4,6},{5,7},{6,4},{7,5},{8,10},{9,11},{10,... | collective-permute-start | bytes 196616 | tf_op jit(solution)/shard_map/ppermute | solution.py:427
  28.8 5.5 %collective-permute-start.7 = (f32[104,128]{1,0:T(8,128)S(1)}, f32[104,128]{1,0:T(8,128)S(1)}, u32[]{:S(2)}, u32[]{:S(2)}) collective-permute-start(f32[104,128]{1,0:T(8,128)S(1)} %get-tuple-element.41.sent), channel_id=1, source_target_pairs={{0,4},{4,0},{8,12},{12,8},{16,20},{20,16},{24,28},{28,24},{1,5},{5... | collective-permute-start | bytes 159752 | tf_op jit(solution)/shard_map/ppermute | solution.py:442
  32.2 0.7 collective-permute-start.8
  34.4 8.4 %collective-permute-start.11 = (f32[40,128]{1,0:T(8,128)S(1)}, f32[40,128]{1,0:T(8,128)S(1)}, u32[]{:S(2)}, u32[]{:S(2)}) collective-permute-start(f32[40,128]{1,0:T(8,128)S(1)} %shard_map.133.refs_0_), channel_id=1, source_target_pairs={{0,24},{4,28},{8,16},{12,20},{16,8},{20,12},{24,0},{28,4},{1,25},{... | collective-permute-start | bytes 61448 | tf_op jit(solution)/shard_map/ppermute | solution.py:427
  41.0 4.7 %collective-permute-start.10 = (f32[40,128]{1,0:T(8,128)S(1)}, f32[40,128]{1,0:T(8,128)S(1)}, u32[]{:S(2)}, u32[]{:S(2)}) collective-permute-start(f32[40,128]{1,0:T(8,128)S(1)} %shard_map.133.refs_0_), channel_id=1, source_target_pairs={{0,16},{4,20},{8,24},{12,28},{16,0},{20,4},{24,8},{28,12},{1,17},{... | collective-permute-start | bytes 61448 | tf_op jit(solution)/shard_map/ppermute | solution.py:427
  42.2 3.8 %collective-permute-start.9 = (f32[40,128]{1,0:T(8,128)S(1)}, f32[40,128]{1,0:T(8,128)S(1)}, u32[]{:S(2)}, u32[]{:S(2)}) collective-permute-start(f32[40,128]{1,0:T(8,128)S(1)} %shard_map.133.refs_0_), channel_id=1, source_target_pairs={{0,8},{4,12},{8,0},{12,4},{16,24},{20,28},{24,16},{28,20},{1,9},{5... | collective-permute-start | bytes 61448 | tf_op jit(solution)/shard_map/ppermute | solution.py:427
  47.7 4.6 %collective-permute-start.14 = (f32[72,256]{1,0:T(8,128)S(1)}, f32[72,256]{1,0:T(8,128)S(1)}, u32[]{:S(2)}, u32[]{:S(2)}) collective-permute-start(f32[72,256]{1,0:T(8,128)S(1)} %get-tuple-element.43.refs_0_), channel_id=1, source_target_pairs={{0,3},{1,2},{2,1},{3,0},{4,7},{5,6},{6,5},{7,4},{8,11},{9,10},{10,... | collective-permute-start | bytes 221192 | tf_op jit(solution)/shard_map/ppermute | solution.py:427
  47.8 6.1 %collective-permute-start.13 = (f32[72,256]{1,0:T(8,128)S(1)}, f32[72,256]{1,0:T(8,128)S(1)}, u32[]{:S(2)}, u32[]{:S(2)}) collective-permute-start(f32[72,256]{1,0:T(8,128)S(1)} %get-tuple-element.43.refs_0_), channel_id=1, source_target_pairs={{0,2},{1,3},{2,0},{3,1},{4,6},{5,7},{6,4},{7,5},{8,10},{9,11},{10,... | collective-permute-start | bytes 221192 | tf_op jit(solution)/shard_map/ppermute | solution.py:427
  49.4 4.6 %collective-permute-start.12 = (f32[72,256]{1,0:T(8,128)S(1)}, f32[72,256]{1,0:T(8,128)S(1)}, u32[]{:S(2)}, u32[]{:S(2)}) collective-permute-start(f32[72,256]{1,0:T(8,128)S(1)} %get-tuple-element.43.refs_0_), channel_id=1, source_target_pairs={{0,1},{1,0},{2,3},{3,2},{4,5},{5,4},{6,7},{7,6},{8,9},{9,8},{10,11... | collective-permute-start | bytes 221192 | tf_op jit(solution)/shard_map/ppermute | solution.py:427
  56.0 4.2 %collective-permute-start.15 = (f32[104,128]{1,0:T(8,128)S(1)}, f32[104,128]{1,0:T(8,128)S(1)}, u32[]{:S(2)}, u32[]{:S(2)}) collective-permute-start(f32[104,128]{1,0:T(8,128)S(1)} %get-tuple-element.49.sent), channel_id=1, source_target_pairs={{0,4},{4,0},{8,12},{12,8},{16,20},{20,16},{24,28},{28,24},{1,5},{5... | collective-permute-start | bytes 159752 | tf_op jit(solution)/shard_map/ppermute | solution.py:442
  56.8 0.7 collective-permute-start.16
  60.4 6.9 %collective-permute-start.19 = (f32[40,128]{1,0:T(8,128)S(1)}, f32[40,128]{1,0:T(8,128)S(1)}, u32[]{:S(2)}, u32[]{:S(2)}) collective-permute-start(f32[40,128]{1,0:T(8,128)S(1)} %shard_map.136.refs_0_), channel_id=1, source_target_pairs={{0,24},{4,28},{8,16},{12,20},{16,8},{20,12},{24,0},{28,4},{1,25},{... | collective-permute-start | bytes 61448 | tf_op jit(solution)/shard_map/ppermute | solution.py:427
  65.3 4.7 %collective-permute-start.18 = (f32[40,128]{1,0:T(8,128)S(1)}, f32[40,128]{1,0:T(8,128)S(1)}, u32[]{:S(2)}, u32[]{:S(2)}) collective-permute-start(f32[40,128]{1,0:T(8,128)S(1)} %shard_map.136.refs_0_), channel_id=1, source_target_pairs={{0,16},{4,20},{8,24},{12,28},{16,0},{20,4},{24,8},{28,12},{1,17},{... | collective-permute-start | bytes 61448 | tf_op jit(solution)/shard_map/ppermute | solution.py:427
  65.7 4.3 %collective-permute-start.17 = (f32[40,128]{1,0:T(8,128)S(1)}, f32[40,128]{1,0:T(8,128)S(1)}, u32[]{:S(2)}, u32[]{:S(2)}) collective-permute-start(f32[40,128]{1,0:T(8,128)S(1)} %shard_map.136.refs_0_), channel_id=1, source_target_pairs={{0,8},{4,12},{8,0},{12,4},{16,24},{20,28},{24,16},{28,20},{1,9},{5... | collective-permute-start | bytes 61448 | tf_op jit(solution)/shard_map/ppermute | solution.py:427
  70.1 3.1 %collective-permute-start.22 = (f32[8,128]{1,0:T(8,128)S(1)}, f32[8,128]{1,0:T(8,128)S(1)}, u32[]{:S(2)}, u32[]{:S(2)}) collective-permute-start(f32[8,128]{1,0:T(8,128)S(1)} %get-tuple-element.51.refs_0_), channel_id=1, source_target_pairs={{0,3},{1,2},{2,1},{3,0},{4,7},{5,6},{6,5},{7,4},{8,11},{9,10},{10,... | collective-permute-start | bytes 12296 | tf_op jit(solution)/shard_map/ppermute | solution.py:427
  70.2 3.7 %collective-permute-start.21 = (f32[8,128]{1,0:T(8,128)S(1)}, f32[8,128]{1,0:T(8,128)S(1)}, u32[]{:S(2)}, u32[]{:S(2)}) collective-permute-start(f32[8,128]{1,0:T(8,128)S(1)} %get-tuple-element.51.refs_0_), channel_id=1, source_target_pairs={{0,2},{1,3},{2,0},{3,1},{4,6},{5,7},{6,4},{7,5},{8,10},{9,11},{10,... | collective-permute-start | bytes 12296 | tf_op jit(solution)/shard_map/ppermute | solution.py:427
  70.8 3.1 %collective-permute-start.20 = (f32[8,128]{1,0:T(8,128)S(1)}, f32[8,128]{1,0:T(8,128)S(1)}, u32[]{:S(2)}, u32[]{:S(2)}) collective-permute-start(f32[8,128]{1,0:T(8,128)S(1)} %get-tuple-element.51.refs_0_), channel_id=1, source_target_pairs={{0,1},{1,0},{2,3},{3,2},{4,5},{5,4},{6,7},{7,6},{8,9},{9,8},{10,11... | collective-permute-start | bytes 12296 | tf_op jit(solution)/shard_map/ppermute | solution.py:427

commit v3 on v2

--- a/solution.py
+++ b/solution.py
@@ -11,7 +11,7 @@
 COLS = 128
 LANES = 128
 GROUP = 8
-CHUNK = 16
+IN_FLIGHT = 4
 SHRINK_SCALE = 0.4
 TINY = 1e-06
 VMEM = pltpu.VMEM
@@ -69,11 +69,11 @@
 
 
 def forward(field, kernel_ref, plain, weighted_t):
-    return forward_of(exact(plain, field), kernel_ref, weighted_t, field.shape[0])
-
-
-def forward_of(spectra, kernel_ref, weighted_t, times, arrived=None):
-    freqs, sensors = kernel_ref.shape[1:3]
+    return packed_series(forward_rows(exact(plain, field), kernel_ref), weighted_t, kernel_ref.shape[2])
+
+
+def forward_rows(spectra, kernel_ref, arrived=None):
+    sensors = kernel_ref.shape[2]
     rows = []
     for group in range(spectra.shape[0] // 16):
         part = spectra[16 * group : 16 * group + 16]
@@ -86,7 +86,12 @@
         if width < LANES:
             out = jnp.concatenate([out, jnp.zeros((16, LANES - width), jnp.float32)], axis=1)
         rows.append(fold(out))
-    series = exact(weighted_t, jnp.concatenate(rows, axis=0))
+    return jnp.concatenate(rows, axis=0)
+
+
+def packed_series(rows, weighted_t, sensors):
+    times = weighted_t.shape[0]
+    series = exact(weighted_t, rows)
     left = lax.broadcasted_iota(jnp.int32, (times // 2, LANES), 1) < sensors
     return jnp.where(left, series[: times // 2], series[times // 2 :])
 
@@ -213,6 +218,22 @@
     return jnp.where(even, other, partner), jnp.where(even, partner, other)
 
 
+def is_odd():
+    return lax.rem(lax.axis_index("sensor"), 2) == 1
+
+
+def spread(rows):
+    upper = -(-rows.shape[0] // 16) * 8
+    lower = rows[upper:]
+    if lower.shape[0] < upper:
+        lower = jnp.concatenate([lower, jnp.zeros((upper - lower.shape[0], LANES), rows.dtype)])
+    return jnp.concatenate([rows[:upper], lower], axis=1)
+
+
+def gathered(wide, count):
+    return jnp.concatenate([wide[:, :LANES], wide[: count - wide.shape[0], LANES:]])
+
+
 def rows_of(scalars):
     row = lax.broadcasted_iota(jnp.int32, (8, LANES), 0)
     out = jnp.zeros((8, LANES), jnp.float32)
@@ -237,25 +258,37 @@
         return copy
 
     early = [load(loaded[i], kept[i]) for i in (1, 6)]
+    starts = list(range(0, freqs, GROUP))
     large = []
-    for start in range(0, freqs, CHUNK):
-        at = (slice(None), pl.ds(start, min(CHUNK, freqs - start)))
-        large.append(load(kernel.at[at], kernel_here.at[at]))
+
+    def load_group():
+        if len(large) < len(starts):
+            start = starts[len(large)]
+            at = (slice(None), pl.ds(start, min(GROUP, freqs - start)))
+            large.append(load(kernel.at[at], kernel_here.at[at]))
+
+    for _ in range(IN_FLIGHT):
+        load_group()
     small = [load(loaded[i], kept[i]) for i in (3, 4, 5, 2, 7, 8, 9)]
     for copy in early:
         copy.wait()
     spectra = exact(plain[...], field[...])
+
+    def arrived(group):
+        large[group].wait()
+        load_group()
+
+    rows = forward_rows(spectra, kernel_here, arrived)
     for copy in small:
         copy.wait()
+    sent[:half, :] = packed_series(rows, weighted_t[...], kernel.shape[2])
 
     cell = lax.broadcasted_iota(jnp.int32, (4, cells), 1) + lax.axis_index("cell") * cells
     linked[0:4, :] = jnp.where(neighbours[...] != cell, 1.0, 0.0)
     linked[4:8, :] = jnp.zeros((4, cells), jnp.float32)
-    tiles = jnp.broadcast_to(tile_of_cell[...], (8, cells))
-    weights = jnp.zeros((8, cells), jnp.float32)
-    for tile in range(tile_weight.shape[1]):
-        weight = jnp.broadcast_to(tile_weight[0:1, tile : tile + 1], (8, cells))
-        weights = jnp.where(tiles == tile, weight, weights)
+    tile = lax.broadcasted_iota(jnp.int32, (tile_weight.shape[1], cells), 0)
+    chosen = jnp.where(tile == tile_of_cell[...], 1.0, 0.0)
+    weights = exact(jnp.broadcast_to(tile_weight[...], (8, tile_weight.shape[1])), chosen)
     limit = SHRINK_SCALE * weights
     threshold[...] = limit
     bottom = cells // COLS - 1
@@ -269,18 +302,14 @@
         sent[half + start : half + start + head.shape[0], :] = one
         edge[start : start + head.shape[0], :] = two
 
-    def arrived(group):
-        if group * GROUP % CHUNK == 0:
-            large[group * GROUP // CHUNK].wait()
-
-    sent[:half, :] = forward_of(spectra, kernel_here, weighted_t[...], times, arrived)
-
 
 def first_adjoint_body(count, *refs):
-    observed, kernel, plain_t, weighted, out = refs[count:]
+    observed, two, kernel, plain_t, weighted, out = refs[count:]
+    times = observed.shape[0]
     predicted = unpacked(summed(refs[:count]), kernel.shape[2])
     residual = predicted - jnp.concatenate([observed[...], observed[...]], axis=1)
-    out[...] = adjoint(residual, kernel, plain_t[...], weighted[...], 1)
+    out[:times, :] = adjoint(residual, kernel, plain_t[...], weighted[...], 1)
+    out[times:, :] = spread(two[...])
 
 
 def response_of(field, kernel, plain, weighted_t, linked, sent, edge):
@@ -308,15 +337,17 @@
     across = to_partner * (came[top:, :] - sent[top:, :])
     beyond = to_other * (other[...] - edge[...])
     out[: top - 8, :] = sent[: top - 8, :] + came[: top - 8, :]
-    boundary = 2.0 * jnp.sum(across * across + beyond * beyond)
-    out[top - 8 :, :] = sent[top - 8 : top, :] + came[top - 8 : top, :] + rows_of([0.0, boundary])
+    boundary = 2.0 * square_sum(jnp.where(is_odd(), beyond, across))
+    out[top - 8 :, :] = sent[top - 8 : top, :] + came[top - 8 : top, :] + rows_of([0.0, 0.0, boundary])
 
 
 def first_gradient_body(count, *refs):
-    (start_multiplier, one, two, linked_ref, kernel, plain, weighted_t,
-     adjoint_out, gradient, sent, edge) = refs[count:]
+    (start_multiplier, one, two, passed, linked_ref, kernel, plain, weighted_t,
+     adjoint_out, gradient, sent, edge, two_out) = refs[count:]
     times, cells = adjoint_out.shape
     half = times // 2
+    two = jnp.where(is_odd(), two[...], gathered(passed[times:, :], two.shape[0]))
+    two_out[...] = two
     linked = linked_ref[...]
     total = summed(refs[:count])
     values = [[strip(start_multiplier[k], r) for r in range(cells // COLS)] for k in range(4)]
@@ -328,22 +359,24 @@
 
 
 def second_adjoint_body(count, *refs):
-    kernel, plain_t, weighted, out, norms = refs[count:]
+    two, kernel, plain_t, weighted, out, norms = refs[count:]
     times = plain_t.shape[0]
     half = times // 2
     total = summed(refs[:count])
     packed, squares = total[:half], total[half : half + 8]
     out[:times, :] = adjoint(unpacked(packed, kernel.shape[2]), kernel, plain_t[...], weighted[...], 2)
-    out[times:, :] = jnp.full((8, out.shape[1]), square_sum(packed), jnp.float32)
+    scalars = rows_of([square_sum(packed), squares[2:3, :] * (2.0 / lax.axis_size("sensor"))])
+    out[times : times + 8, :] = jnp.concatenate([scalars] * (out.shape[1] // LANES), axis=1)
+    out[times + 8 :, :] = spread(two[...])
     norms[...] = squares
 
 
 def step_of(norms, scalars):
-    return norms[0, 0] / (scalars[0, 0] + norms[1, 0] + TINY)
+    return norms[0, 0] / (scalars[0, 0] + (norms[1, 0] + scalars[1, 0]) + TINY)
 
 
 def second_gradient_body(count, *refs):
-    (norms, adjoint_in, gradient_in, model, start_multiplier, threshold, one, two, grad_one, grad_two, linked_ref,
+    (norms, adjoint_in, gradient_in, model, start_multiplier, threshold, one, two, grad_one, grad_two, passed, linked_ref,
      kernel, plain, weighted_t, model_out, jumps_out, multiplier_out, gradient_out, sent, edge) = refs[count:]
     times, cells = model.shape
     half = times // 2
@@ -354,7 +387,8 @@
     rows = cells // COLS
     above, below = beside(one[half:, :], two[...])
     field_jumps = jumps(field, above[:times], below[:times], linked)
-    grad_jumps = jumps(gradient, *beside(grad_one[half + 8 :, :], grad_two[...]), linked)
+    grad_two = jnp.where(is_odd(), grad_two[...], gathered(passed[times + 8 :, :], times))
+    grad_jumps = jumps(gradient, *beside(grad_one[half + 8 :, :], grad_two), linked)
 
     def advance(model_jumps, old_multiplier, limit):
         shifted = model_jumps + old_multiplier
@@ -383,21 +417,25 @@
 
 
 def response_body(count, *refs):
-    out, norms = refs[count:]
+    two, out, passing, norms = refs[count:]
     total = summed(refs[:count])
     packed, squares = total[:-8], total[-8:]
-    out[...] = jnp.full((8, LANES), square_sum(packed), jnp.float32)
+    scalars = rows_of([square_sum(packed), squares[2:3, :] * (2.0 / lax.axis_size("sensor"))])
+    out[...] = scalars
+    passing[:8, :] = scalars
+    passing[8:, :] = two[...]
     norms[...] = squares
 
 
 def finish_body(count, *refs):
-    (norms, gradient_in, model, model_jumps, multiplier, threshold, grad_one, grad_two, linked,
+    (norms, gradient_in, model, model_jumps, multiplier, threshold, grad_one, grad_two, passed, linked,
      estimate_out, auxiliary_out, multiplier_out) = refs[count:]
-    step = step_of(norms, summed(refs[:count]))
+    step = step_of(norms, tree_sum([part[:8, :] for part in refs[:count]]))
+    grad_two = jnp.where(is_odd(), grad_two[...], passed[8:, :])
     half = gradient_in.shape[0] // 2
     gradient = gradient_in[...]
     estimate_out[...] = model[...] - step * gradient
-    grad_jumps = jumps(gradient, *beside(grad_one[half + 8 :, :], grad_two[...]), linked[...])
+    grad_jumps = jumps(gradient, *beside(grad_one[half + 8 :, :], grad_two), linked[...])
     for k in range(4):
         for r in range(gradient.shape[1] // COLS):
             at = slice(r * COLS, (r + 1) * COLS)
@@ -430,8 +468,14 @@
     return parts
 
 
-def sensor_parts(array, *radices):
-    return summing([array], "sensor", 1, stages_of(lax.axis_size("sensor"), *radices))
+def sensor_hop(array):
+    return lax.ppermute(array, "sensor", [(i, i ^ 1) for i in range(lax.axis_size("sensor"))])
+
+
+def sensor_parts(array, rows):
+    passed = sensor_hop(array)
+    total = array[:rows] + passed[:rows]
+    return summing([total], "sensor", 2, stages_of(lax.axis_size("sensor") // 2, 2)), passed
 
 
 def cell_parts(merged):
@@ -443,8 +487,13 @@
 
 
 def from_other(array):
-    inner = range(1, lax.axis_size("cell") - 1)
-    return lax.ppermute(array, "cell", [(i, i + 1 if i % 2 else i - 1) for i in inner])
+    sensors = lax.axis_size("sensor")
+    pairs = [
+        (i * sensors + s, (i + 1 if i % 2 else i - 1) * sensors + s)
+        for i in range(1, lax.axis_size("cell") - 1)
+        for s in range(1, sensors, 2)
+    ]
+    return lax.ppermute(array, ("cell", "sensor"), pairs)
 
 
 def per_device(kernel, observed, start_model, start_multiplier, neighbours, tile_of_cell, tile_weight):
@@ -463,40 +512,52 @@
         [(half + 2 * times + 8, LANES), (2 * times + 8, LANES), (8, cells), (8, cells)]
         + [jax.ShapeDtypeStruct(a.shape, a.dtype) for a in loads],
         *[pltpu.with_memory_space_constraint(a, HBM) for a in loads],
-        scratch=[pltpu.SemaphoreType.DMA((9 + -(-freqs // CHUNK),))],
+        scratch=[pltpu.SemaphoreType.DMA((9 + -(-freqs // GROUP),))],
         inputs=HBM,
     )
     one = from_partner(sent)
     merged, edge = lax.optimization_barrier((sent[:half] + one[:half], edge))
     parts = cell_parts(merged)
     two = from_other(edge)
-    back = call(functools.partial(first_adjoint_body, len(parts)), field, *parts, observed, kernel, plain_t, weighted)
-    parts = sensor_parts(back, 2, 2)
-    message, side = (half + 8 + times, LANES), (times, LANES)
-    adjoint_one, gradient, sent, edge = call(
-        functools.partial(first_gradient_body, len(parts)), [field, field, message, side],
-        *parts, start_multiplier, one, two, linked, kernel, plain, weighted_t,
+    message, side, shared = (half + 8 + times, LANES), (times, LANES), (2 * times + 8, LANES)
+    back = call(
+        functools.partial(first_adjoint_body, len(parts)), (2 * times + 8, cells),
+        *parts, observed, two, kernel, plain_t, weighted,
+    )
+    parts, passed = sensor_parts(back, times)
+    adjoint_one, gradient, sent, edge, two = call(
+        functools.partial(first_gradient_body, len(parts)), [field, field, message, side, shared],
+        *parts, start_multiplier, one, two, passed, linked, kernel, plain, weighted_t,
     )
     grad_one, grad_two = from_partner(sent), from_other(edge)
     parts = cell_parts(call(merge_body, (half + 8, LANES), sent, grad_one, edge, grad_two, linked))
     back, norms = call(
-        functools.partial(second_adjoint_body, len(parts)), [(times + 8, cells), (8, LANES)],
-        *parts, kernel, plain_t, weighted,
-    )
-    parts = sensor_parts(back, 4)
+        functools.partial(second_adjoint_body, len(parts)), [(times + 8 + half, cells), (8, LANES)],
+        *parts, grad_two, kernel, plain_t, weighted,
+    )
+    parts, passed = sensor_parts(back, times + 8)
     model, model_jumps, multiplier, gradient, sent, edge = call(
         functools.partial(second_gradient_body, len(parts)), [field, wide, wide, field, message, side],
         *parts, norms, adjoint_one, gradient, start_model, start_multiplier, threshold, one, two, grad_one, grad_two,
-        linked, kernel, plain, weighted_t,
+        passed, linked, kernel, plain, weighted_t,
     )
     grad_one, grad_two = from_partner(sent), from_other(edge)
     parts = cell_parts(call(merge_body, (half + 8, LANES), sent, grad_one, edge, grad_two, linked))
-    square, norms = call(functools.partial(response_body, len(parts)), [(8, LANES), (8, LANES)], *parts)
-    parts = sensor_parts(square, 4)
+    scalars, passing, norms = call(
+        functools.partial(response_body, len(parts)), [(8, LANES), (8 + times, LANES), (8, LANES)], *parts, grad_two
+    )
+    passed = sensor_hop(passing)
+    sensor_count = lax.axis_size("sensor")
+    if sensor_count <= 4:
+        parts = [scalars, passed] + [
+            lax.ppermute(scalars, "sensor", [(i, i ^ k) for i in range(sensor_count)]) for k in range(2, sensor_count)
+        ]
+    else:
+        parts = summing([scalars + passed[:8]], "sensor", 2, stages_of(sensor_count // 2, 2))
     return tuple(
         call(
             functools.partial(finish_body, len(parts)), [field, wide, wide],
-            *parts, norms, gradient, model, model_jumps, multiplier, threshold, grad_one, grad_two, linked,
+            *parts, norms, gradient, model, model_jumps, multiplier, threshold, grad_one, grad_two, passed, linked,
         )
     )
 

time: 75.1 us -> 69.3 us (0.923)
  starting transfers between devices: 32.7 us -> 27.1 us
  waiting for transfers between devices: 28 us -> 27 us
  Pallas kernels: 13.4 us -> 14.2 us
    ppermute x17 -> x11, starting transfers between devices: 23.5 us -> 16.8 us  [summing(): lax.ppermute(total, axis, [(i, i ^ k * stride) for i in range(count)])]
    ppermute x17 -> x11, waiting for transfers between devices: 21.3 us -> 14.6 us  [summing(): lax.ppermute(total, axis, [(i, i ^ k * stride) for i in range(count)])]
    ppermute x3 -> x8, waiting for transfers between devices: 0.01 us -> 5.63 us  [the longest x2 3.07 us: per_device(): lax.ppermute(scalars, 'sensor', [(i, i ^ k) for i in range(sensor_count)])]
    ppermute x3 -> x8, starting transfers between devices: 1.97 us -> 4.44 us  [the longest x2 2.06 us: per_device(): lax.ppermute(scalars, 'sensor', [(i, i ^ k) for i in range(sensor_count)])]
    ppermute x3, starting transfers between devices: 7.2 us -> 5.88 us  [from_partner(): lax.ppermute(array, 'cell', [(i, i ^ 1) for i in range(lax.axis_size('cel...]
    pallas_call x9, Pallas kernels: 13.4 us -> 14.2 us  [call(): pl.pallas_call(body, out_shape=shapes, in_specs=[pl.BlockSpec(memory_spac...]
  transfers between devices with their start and end apart: 23 -> 22, of which waited for: 16 -> 16; matrix products, arithmetic and copies ran while one was open for 0% -> 0% of each run, Pallas kernels for 0% -> 0%
where the time goes in v3:
time: 69.3 us; the launch traced here: 69.1 us
  starting transfers between devices  27.1 us (39%)
  waiting for transfers between devices  27 us (39%)
  Pallas kernels  14.2 us (20%)
  between operations  0.77 us (1%)
    ppermute x11, starting transfers between devices, summing(): lax.ppermute(total, axis, [(i, i ^ k * stride) for i in range(count)])  16.8 us
    ppermute x11, waiting for transfers between devices, summing(): lax.ppermute(total, axis, [(i, i ^ k * stride) for i in range(count)])  14.6 us
    pallas_call x9, Pallas kernels, call(): pl.pallas_call(body, out_shape=shapes, in_specs=[pl.BlockSpec(memory_spac...  14.2 us
    ppermute x3, waiting for transfers between devices, from_partner(): lax.ppermute(array, 'cell', [(i, i ^ 1) for i in range(lax.axis_size('cel...  6.74 us
    ppermute x3, starting transfers between devices, from_partner(): lax.ppermute(array, 'cell', [(i, i ^ 1) for i in range(lax.axis_size('cel...  5.88 us
    ppermute x2, waiting for transfers between devices, per_device(): lax.ppermute(scalars, 'sensor', [(i, i ^ k) for i in range(sensor_count)])  3.07 us
    ppermute x3, waiting for transfers between devices, sensor_hop(): lax.ppermute(array, 'sensor', [(i, i ^ 1) for i in range(lax.axis_size('s...  2.55 us
    ppermute x2, starting transfers between devices, per_device(): lax.ppermute(scalars, 'sensor', [(i, i ^ k) for i in range(sensor_count)])  2.06 us
  transfers between devices with their start and end apart: 22, of which 16 were waited for; matrix products, arithmetic and copies ran while one was open for 0% of the time, Pallas kernels for 0%

profile of v3, /device:TPU:0, one launch (start us, length us, event | category | flops | bytes accessed | tf_op | source)
XLA Modules:
  0.0 69.1 jit_solution(17064029618115774210)
XLA Ops:
  0.6 5.9 %shard_map.130 = (f32[168,128]{1,0:T(8,128)S(1)}, f32[136,128]{1,0:T(8,128)S(1)}, f32[8,256]{1,0:T(8,128)S(1)}, f32[8,256]{1,0:T(8,128)S(1)}, bf16[2,65,64,256]{...) custom-call(bf16[2,65,64,256]{3,2,1,0:T(8,128)(2,1)} %refs_0_.1, ...), custom_call_target="tpu_custom_call" | custom-call | tf_op jit(solution)/shard_map/pallas_call | solution.py:192
  6.6 3.0 %collective-permute-start = (f32[168,128]{1,0:T(8,128)S(1)}, f32[168,128]{1,0:T(8,128)S(1)}, u32[]{:S(2)}, u32[]{:S(2)}) collective-permute-start(f32[168,128]{1,0:T(8,128)S(1)} %get-tuple-element.32), channel_id=1, source_target_pairs={{0,4},{4,0},{8,12},{12,8},{16,20},{20,16},{24,28},{28,24},{1,5},{5... | collective-permute-start | bytes 258056 | tf_op jit(solution)/shard_map/ppermute | solution.py:486
  9.6 2.5 %collective-permute-done.refs_3_.refs_8_ = f32[168,128]{1,0:T(8,128)S(1)} collective-permute-done((f32[168,128]{1,0:T(8,128)S(1)}, f32[168,128]{1,0:T(8,128)S(1)}, u32[]{:S(2)}, u32[]{:S(2)}) %collective-permute-start) | collective-permute-done | bytes 86048 | tf_op jit(solution)/shard_map/ppermute | solution.py:486
  12.8 4.1 %collective-permute-start.3 = (f32[32,128]{1,0:T(8,128)S(1)}, f32[32,128]{1,0:T(8,128)S(1)}, u32[]{:S(2)}, u32[]{:S(2)}) collective-permute-start(f32[32,128]{1,0:T(8,128)S(1)} %slice_add_fusion.2.refs_0_), channel_id=1, source_target_pairs={{0,24},{4,28},{8,16},{12,20},{16,8},{20,12},{24,0},{28,4},{1,25},{... | collective-permute-start | bytes 49160 | tf_op jit(solution)/shard_map/ppermute | solution.py:465
  18.7 2.8 %collective-permute-done.2.refs_2_ = f32[32,128]{1,0:T(8,128)S(1)} collective-permute-done((f32[32,128]{1,0:T(8,128)S(1)}, f32[32,128]{1,0:T(8,128)S(1)}, u32[]{:S(2)}, u32[]{:S(2)}) %collective-permute-start.2) | collective-permute-done | bytes 16416 | tf_op jit(solution)/shard_map/ppermute | solution.py:465
  22.9 1.3 %collective-permute-done.5.refs_5_ = f32[136,256]{1,0:T(8,128)S(1)} collective-permute-done((f32[136,256]{1,0:T(8,128)S(1)}, f32[136,256]{1,0:T(8,128)S(1)}, u32[]{:S(2)}, u32[]{:S(2)}) %collective-permute-start.5) | collective-permute-done | bytes 139296 | tf_op jit(solution)/shard_map/ppermute | solution.py:472
  24.3 1.6 %collective-permute-start.6 = (f32[64,256]{1,0:T(8,128)S(1)}, f32[64,256]{1,0:T(8,128)S(1)}, u32[]{:S(2)}, u32[]{:S(2)}) collective-permute-start(f32[64,256]{1,0:T(8,128)S(1)} %slice_add_fusion.1.refs_0_), channel_id=1, source_target_pairs={{0,2},{1,3},{2,0},{3,1},{4,6},{5,7},{6,4},{7,5},{8,10},{9,11},{10,... | collective-permute-start | bytes 196616 | tf_op jit(solution)/shard_map/ppermute | solution.py:465
  25.8 2.8 %collective-permute-done.6.refs_1_ = f32[64,256]{1,0:T(8,128)S(1)} collective-permute-done((f32[64,256]{1,0:T(8,128)S(1)}, f32[64,256]{1,0:T(8,128)S(1)}, u32[]{:S(2)}, u32[]{:S(2)}) %collective-permute-start.6) | collective-permute-done | bytes 65568 | tf_op jit(solution)/shard_map/ppermute | solution.py:465
  28.6 1.9 %shard_map.132 = (f32[64,256]{1,0:T(8,128)S(1)}, f32[64,256]{1,0:T(8,128)S(1)}, f32[104,128]{1,0:T(8,128)S(1)}, f32[64,128]{1,0:T(8,128)S(1)}, f32[136,128]{1,0:T(8,128)S(1)}) custom-call(f32[64,256]{1,0:T(8,128)S(1)} %slice_add_fusion.1.refs_0_, f32[64,256]{1,0:T(8,128)S(1)} %collective-permute-done.6.refs_1_, ...), custom_call_target="tpu_custom_call" | custom-call | tf_op jit(solution)/shard_map/pallas_call | solution.py:192
  30.5 1.6 %collective-permute-start.7 = (f32[104,128]{1,0:T(8,128)S(1)}, f32[104,128]{1,0:T(8,128)S(1)}, u32[]{:S(2)}, u32[]{:S(2)}) collective-permute-start(f32[104,128]{1,0:T(8,128)S(1)} %get-tuple-element.43.sent), channel_id=1, source_target_pairs={{0,4},{4,0},{8,12},{12,8},{16,20},{20,16},{24,28},{28,24},{1,5},{5... | collective-permute-start | bytes 159752 | tf_op jit(solution)/shard_map/ppermute | solution.py:486
  32.7 1.9 %collective-permute-done.7.came.refs_10_ = f32[104,128]{1,0:T(8,128)S(1)} collective-permute-done((f32[104,128]{1,0:T(8,128)S(1)}, f32[104,128]{1,0:T(8,128)S(1)}, u32[]{:S(2)}, u32[]{:S(2)}) %collective-permute-start.7) | collective-permute-done | bytes 53280 | tf_op jit(solution)/shard_map/ppermute | solution.py:486
  34.8 1.5 %collective-permute-start.11 = (f32[40,128]{1,0:T(8,128)S(1)}, f32[40,128]{1,0:T(8,128)S(1)}, u32[]{:S(2)}, u32[]{:S(2)}) collective-permute-start(f32[40,128]{1,0:T(8,128)S(1)} %shard_map.133.refs_0_), channel_id=1, source_target_pairs={{0,24},{4,28},{8,16},{12,20},{16,8},{20,12},{24,0},{28,4},{1,25},{... | collective-permute-start | bytes 61448 | tf_op jit(solution)/shard_map/ppermute | solution.py:465
  37.0 2.3 %collective-permute-start.9 = (f32[40,128]{1,0:T(8,128)S(1)}, f32[40,128]{1,0:T(8,128)S(1)}, u32[]{:S(2)}, u32[]{:S(2)}) collective-permute-start(f32[40,128]{1,0:T(8,128)S(1)} %shard_map.133.refs_0_), channel_id=1, source_target_pairs={{0,8},{4,12},{8,0},{12,4},{16,24},{20,28},{24,16},{28,20},{1,9},{5... | collective-permute-start | bytes 61448 | tf_op jit(solution)/shard_map/ppermute | solution.py:465
  41.6 1.7 %shard_map.134 = (f32[104,256]{1,0:T(8,128)S(1)}, f32[8,128]{1,0:T(8,128)S(1)}) custom-call(f32[40,128]{1,0:T(8,128)S(1)} %shard_map.133.refs_0_, f32[40,128]{1,0:T(8,128)S(1)} %collective-permute-done.9.refs_1_, f32[40,128]{1,0:T(8,128)S(1)} %collective-permute-done.10.refs_2_, f32[40,128]{1,0:T(8,128)S(1)} %collective-permute-done.11.refs_3_, ...), custom_call_target="tpu_custom_call" | custom-call | tf_op jit(solution)/shard_map/pallas_call | solution.py:192
  44.7 1.6 %collective-permute-start.13 = (f32[72,256]{1,0:T(8,128)S(1)}, f32[72,256]{1,0:T(8,128)S(1)}, u32[]{:S(2)}, u32[]{:S(2)}) collective-permute-start(f32[72,256]{1,0:T(8,128)S(1)} %slice_add_fusion.refs_0_), channel_id=1, source_target_pairs={{0,2},{1,3},{2,0},{3,1},{4,6},{5,7},{6,4},{7,5},{8,10},{9,11},{10,... | collective-permute-start | bytes 221192 | tf_op jit(solution)/shard_map/ppermute | solution.py:465
  46.3 2.9 %collective-permute-done.13.refs_1_ = f32[72,256]{1,0:T(8,128)S(1)} collective-permute-done((f32[72,256]{1,0:T(8,128)S(1)}, f32[72,256]{1,0:T(8,128)S(1)}, u32[]{:S(2)}, u32[]{:S(2)}) %collective-permute-start.13) | collective-permute-done | bytes 73760 | tf_op jit(solution)/shard_map/ppermute | solution.py:465
  49.1 2.0 %shard_map.135 = (f32[64,256]{1,0:T(8,128)S(1)}, f32[4,64,256]{2,1,0:T(8,128)S(1)}, f32[4,64,256]{2,1,0:T(8,128)S(1)}, f32[64,256]{1,0:T(8,128)S(1)}, f32[104,128]{1,0:T(8,128)S(1)}, /*index=5*/f32[64,128]{1,0:T(8,128)S(1)}) custom-call(f32[72,256]{1,0:T(8,128)S(1)} %slice_add_fusion.refs_0_, f32[72,256]{1,0:T(8,128)S(1)} %collective-permute-done.13.refs_1_, ...), custom_call_target="tpu_custom_call" | custom-call | tf_op jit(solution)/shard_map/pallas_call | solution.py:192
  51.2 1.3 %collective-permute-start.14 = (f32[104,128]{1,0:T(8,128)S(1)}, f32[104,128]{1,0:T(8,128)S(1)}, u32[]{:S(2)}, u32[]{:S(2)}) collective-permute-start(f32[104,128]{1,0:T(8,128)S(1)} %get-tuple-element.52.sent), channel_id=1, source_target_pairs={{0,4},{4,0},{8,12},{12,8},{16,20},{20,16},{24,28},{28,24},{1,5},{5... | collective-permute-start | bytes 159752 | tf_op jit(solution)/shard_map/ppermute | solution.py:486
  53.1 2.3 %collective-permute-done.14.came.refs_10_ = f32[104,128]{1,0:T(8,128)S(1)} collective-permute-done((f32[104,128]{1,0:T(8,128)S(1)}, f32[104,128]{1,0:T(8,128)S(1)}, u32[]{:S(2)}, u32[]{:S(2)}) %collective-permute-start.14) | collective-permute-done | bytes 53280 | tf_op jit(solution)/shard_map/ppermute | solution.py:486
  55.5 2.3 %collective-permute-start.18 = (f32[40,128]{1,0:T(8,128)S(1)}, f32[40,128]{1,0:T(8,128)S(1)}, u32[]{:S(2)}, u32[]{:S(2)}) collective-permute-start(f32[40,128]{1,0:T(8,128)S(1)} %shard_map.136.refs_0_), channel_id=1, source_target_pairs={{0,24},{4,28},{8,16},{12,20},{16,8},{20,12},{24,0},{28,4},{1,25},{... | collective-permute-start | bytes 61448 | tf_op jit(solution)/shard_map/ppermute | solution.py:465
  58.5 1.5 %collective-permute-start.16 = (f32[40,128]{1,0:T(8,128)S(1)}, f32[40,128]{1,0:T(8,128)S(1)}, u32[]{:S(2)}, u32[]{:S(2)}) collective-permute-start(f32[40,128]{1,0:T(8,128)S(1)} %shard_map.136.refs_0_), channel_id=1, source_target_pairs={{0,8},{4,12},{8,0},{12,4},{16,24},{20,28},{24,16},{28,20},{1,9},{5... | collective-permute-start | bytes 61448 | tf_op jit(solution)/shard_map/ppermute | solution.py:465
  61.2 1.5 %collective-permute-done.17.refs_2_ = f32[40,128]{1,0:T(8,128)S(1)} collective-permute-done((f32[40,128]{1,0:T(8,128)S(1)}, f32[40,128]{1,0:T(8,128)S(1)}, u32[]{:S(2)}, u32[]{:S(2)}) %collective-permute-start.17) | collective-permute-done | bytes 20512 | tf_op jit(solution)/shard_map/ppermute | solution.py:465
  63.0 1.5 %collective-permute-start.21 = (f32[8,128]{1,0:T(8,128)S(1)}, f32[8,128]{1,0:T(8,128)S(1)}, u32[]{:S(2)}, u32[]{:S(2)}) collective-permute-start(f32[8,128]{1,0:T(8,128)S(1)} %get-tuple-element.54.refs_0_), channel_id=1, source_target_pairs={{0,3},{1,2},{2,1},{3,0},{4,7},{5,6},{6,5},{7,4},{8,11},{9,10},{10,... | collective-permute-start | bytes 12296 | tf_op jit(solution)/shard_map/ppermute | solution.py:553
  66.0 2.1 %collective-permute-done.20.refs_2_ = f32[8,128]{1,0:T(8,128)S(1)} collective-permute-done((f32[8,128]{1,0:T(8,128)S(1)}, f32[8,128]{1,0:T(8,128)S(1)}, u32[]{:S(2)}, u32[]{:S(2)}) %collective-permute-start.20) | collective-permute-done | bytes 4128 | tf_op jit(solution)/shard_map/ppermute | solution.py:553
  (34 shorter events, 14.4 us)
Async XLA Ops:
  0.6 20.9 %copy-start = (f32[64,64]{1,0:T(8,128)S(1)}, f32[64,64]{1,0:T(8,128)}, u32[]{:S(2)}) copy-start(f32[64,64]{1,0:T(8,128)} %refs_4_.1) | copy-start | bytes 49156
  6.6 5.6 %collective-permute-start = (f32[168,128]{1,0:T(8,128)S(1)}, f32[168,128]{1,0:T(8,128)S(1)}, u32[]{:S(2)}, u32[]{:S(2)}) collective-permute-start(f32[168,128]{1,0:T(8,128)S(1)} %get-tuple-element.32), channel_id=1, source_target_pairs={{0,4},{4,0},{8,12},{12,8},{16,20},{20,16},{24,28},{28,24},{1,5},{5... | collective-permute-start | bytes 258056 | tf_op jit(solution)/shard_map/ppermute | solution.py:486
  12.2 9.4 %collective-permute-start.4 = (f32[136,128]{1,0:T(8,128)S(1)}, f32[136,128]{1,0:T(8,128)S(1)}, u32[]{:S(2)}, u32[]{:S(2)}) collective-permute-start(f32[136,128]{1,0:T(8,128)S(1)} %get-tuple-element.35), channel_id=1, source_target_pairs={{5,9},{7,11},{9,5},{11,7},{13,17},{15,19},{17,13},{19,15},{21,25},... | collective-permute-start | bytes 208904 | tf_op jit(solution)/shard_map/ppermute | solution.py:496
  12.8 5.9 %collective-permute-start.3 = (f32[32,128]{1,0:T(8,128)S(1)}, f32[32,128]{1,0:T(8,128)S(1)}, u32[]{:S(2)}, u32[]{:S(2)}) collective-permute-start(f32[32,128]{1,0:T(8,128)S(1)} %slice_add_fusion.2.refs_0_), channel_id=1, source_target_pairs={{0,24},{4,28},{8,16},{12,20},{16,8},{20,12},{24,0},{28,4},{1,25},{... | collective-permute-start | bytes 49160 | tf_op jit(solution)/shard_map/ppermute | solution.py:465
  16.9 4.6 %collective-permute-start.2 = (f32[32,128]{1,0:T(8,128)S(1)}, f32[32,128]{1,0:T(8,128)S(1)}, u32[]{:S(2)}, u32[]{:S(2)}) collective-permute-start(f32[32,128]{1,0:T(8,128)S(1)} %slice_add_fusion.2.refs_0_), channel_id=1, source_target_pairs={{0,16},{4,20},{8,24},{12,28},{16,0},{20,4},{24,8},{28,12},{1,17},{... | collective-permute-start | bytes 49160 | tf_op jit(solution)/shard_map/ppermute | solution.py:465
  16.9 4.6 %collective-permute-start.1 = (f32[32,128]{1,0:T(8,128)S(1)}, f32[32,128]{1,0:T(8,128)S(1)}, u32[]{:S(2)}, u32[]{:S(2)}) collective-permute-start(f32[32,128]{1,0:T(8,128)S(1)} %slice_add_fusion.2.refs_0_), channel_id=1, source_target_pairs={{0,8},{4,12},{8,0},{12,4},{16,24},{20,28},{24,16},{28,20},{1,9},{5... | collective-permute-start | bytes 49160 | tf_op jit(solution)/shard_map/ppermute | solution.py:465
  22.8 1.4 %collective-permute-start.5 = (f32[136,256]{1,0:T(8,128)S(1)}, f32[136,256]{1,0:T(8,128)S(1)}, u32[]{:S(2)}, u32[]{:S(2)}) collective-permute-start(f32[136,256]{1,0:T(8,128)S(1)} %shard_map.131), channel_id=1, source_target_pairs={{0,1},{1,0},{2,3},{3,2},{4,5},{5,4},{6,7},{7,6},{8,9},{9,8},{10,11... | collective-permute-start | bytes 417800 | tf_op jit(solution)/shard_map/ppermute | solution.py:472
  24.3 4.3 %collective-permute-start.6 = (f32[64,256]{1,0:T(8,128)S(1)}, f32[64,256]{1,0:T(8,128)S(1)}, u32[]{:S(2)}, u32[]{:S(2)}) collective-permute-start(f32[64,256]{1,0:T(8,128)S(1)} %slice_add_fusion.1.refs_0_), channel_id=1, source_target_pairs={{0,2},{1,3},{2,0},{3,1},{4,6},{5,7},{6,4},{7,5},{8,10},{9,11},{10,... | collective-permute-start | bytes 196616 | tf_op jit(solution)/shard_map/ppermute | solution.py:465
  30.5 4.2 %collective-permute-start.7 = (f32[104,128]{1,0:T(8,128)S(1)}, f32[104,128]{1,0:T(8,128)S(1)}, u32[]{:S(2)}, u32[]{:S(2)}) collective-permute-start(f32[104,128]{1,0:T(8,128)S(1)} %get-tuple-element.43.sent), channel_id=1, source_target_pairs={{0,4},{4,0},{8,12},{12,8},{16,20},{20,16},{24,28},{28,24},{1,5},{5... | collective-permute-start | bytes 159752 | tf_op jit(solution)/shard_map/ppermute | solution.py:486
  32.1 0.7 collective-permute-start.8
  34.8 5.6 %collective-permute-start.11 = (f32[40,128]{1,0:T(8,128)S(1)}, f32[40,128]{1,0:T(8,128)S(1)}, u32[]{:S(2)}, u32[]{:S(2)}) collective-permute-start(f32[40,128]{1,0:T(8,128)S(1)} %shard_map.133.refs_0_), channel_id=1, source_target_pairs={{0,24},{4,28},{8,16},{12,20},{16,8},{20,12},{24,0},{28,4},{1,25},{... | collective-permute-start | bytes 61448 | tf_op jit(solution)/shard_map/ppermute | solution.py:465
  36.4 4.8 %collective-permute-start.10 = (f32[40,128]{1,0:T(8,128)S(1)}, f32[40,128]{1,0:T(8,128)S(1)}, u32[]{:S(2)}, u32[]{:S(2)}) collective-permute-start(f32[40,128]{1,0:T(8,128)S(1)} %shard_map.133.refs_0_), channel_id=1, source_target_pairs={{0,16},{4,20},{8,24},{12,28},{16,0},{20,4},{24,8},{28,12},{1,17},{... | collective-permute-start | bytes 61448 | tf_op jit(solution)/shard_map/ppermute | solution.py:465
  37.0 4.6 %collective-permute-start.9 = (f32[40,128]{1,0:T(8,128)S(1)}, f32[40,128]{1,0:T(8,128)S(1)}, u32[]{:S(2)}, u32[]{:S(2)}) collective-permute-start(f32[40,128]{1,0:T(8,128)S(1)} %shard_map.133.refs_0_), channel_id=1, source_target_pairs={{0,8},{4,12},{8,0},{12,4},{16,24},{20,28},{24,16},{28,20},{1,9},{5... | collective-permute-start | bytes 61448 | tf_op jit(solution)/shard_map/ppermute | solution.py:465
  43.3 1.4 %collective-permute-start.12 = (f32[104,256]{1,0:T(8,128)S(1)}, f32[104,256]{1,0:T(8,128)S(1)}, u32[]{:S(2)}, u32[]{:S(2)}) collective-permute-start(f32[104,256]{1,0:T(8,128)S(1)} %get-tuple-element.45), channel_id=1, source_target_pairs={{0,1},{1,0},{2,3},{3,2},{4,5},{5,4},{6,7},{7,6},{8,9},{9,8},{10,11... | collective-permute-start | bytes 319496 | tf_op jit(solution)/shard_map/ppermute | solution.py:472
  44.7 4.4 %collective-permute-start.13 = (f32[72,256]{1,0:T(8,128)S(1)}, f32[72,256]{1,0:T(8,128)S(1)}, u32[]{:S(2)}, u32[]{:S(2)}) collective-permute-start(f32[72,256]{1,0:T(8,128)S(1)} %slice_add_fusion.refs_0_), channel_id=1, source_target_pairs={{0,2},{1,3},{2,0},{3,1},{4,6},{5,7},{6,4},{7,5},{8,10},{9,11},{10,... | collective-permute-start | bytes 221192 | tf_op jit(solution)/shard_map/ppermute | solution.py:465
  51.2 4.2 %collective-permute-start.14 = (f32[104,128]{1,0:T(8,128)S(1)}, f32[104,128]{1,0:T(8,128)S(1)}, u32[]{:S(2)}, u32[]{:S(2)}) collective-permute-start(f32[104,128]{1,0:T(8,128)S(1)} %get-tuple-element.52.sent), channel_id=1, source_target_pairs={{0,4},{4,0},{8,12},{12,8},{16,20},{20,16},{24,28},{28,24},{1,5},{5... | collective-permute-start | bytes 159752 | tf_op jit(solution)/shard_map/ppermute | solution.py:486
  52.4 0.7 collective-permute-start.15
  55.5 5.7 %collective-permute-start.18 = (f32[40,128]{1,0:T(8,128)S(1)}, f32[40,128]{1,0:T(8,128)S(1)}, u32[]{:S(2)}, u32[]{:S(2)}) collective-permute-start(f32[40,128]{1,0:T(8,128)S(1)} %shard_map.136.refs_0_), channel_id=1, source_target_pairs={{0,24},{4,28},{8,16},{12,20},{16,8},{20,12},{24,0},{28,4},{1,25},{... | collective-permute-start | bytes 61448 | tf_op jit(solution)/shard_map/ppermute | solution.py:465
  57.9 4.8 %collective-permute-start.17 = (f32[40,128]{1,0:T(8,128)S(1)}, f32[40,128]{1,0:T(8,128)S(1)}, u32[]{:S(2)}, u32[]{:S(2)}) collective-permute-start(f32[40,128]{1,0:T(8,128)S(1)} %shard_map.136.refs_0_), channel_id=1, source_target_pairs={{0,16},{4,20},{8,24},{12,28},{16,0},{20,4},{24,8},{28,12},{1,17},{... | collective-permute-start | bytes 61448 | tf_op jit(solution)/shard_map/ppermute | solution.py:465
  58.5 4.2 %collective-permute-start.16 = (f32[40,128]{1,0:T(8,128)S(1)}, f32[40,128]{1,0:T(8,128)S(1)}, u32[]{:S(2)}, u32[]{:S(2)}) collective-permute-start(f32[40,128]{1,0:T(8,128)S(1)} %shard_map.136.refs_0_), channel_id=1, source_target_pairs={{0,8},{4,12},{8,0},{12,4},{16,24},{20,28},{24,16},{28,20},{1,9},{5... | collective-permute-start | bytes 61448 | tf_op jit(solution)/shard_map/ppermute | solution.py:465
  62.8 5.3 %collective-permute-start.19 = (f32[72,128]{1,0:T(8,128)S(1)}, f32[72,128]{1,0:T(8,128)S(1)}, u32[]{:S(2)}, u32[]{:S(2)}) collective-permute-start(f32[72,128]{1,0:T(8,128)S(1)} %get-tuple-element.55), channel_id=1, source_target_pairs={{0,1},{1,0},{2,3},{3,2},{4,5},{5,4},{6,7},{7,6},{8,9},{9,8},{10,11... | collective-permute-start | bytes 110600 | tf_op jit(solution)/shard_map/ppermute | solution.py:472
  63.0 3.0 %collective-permute-start.21 = (f32[8,128]{1,0:T(8,128)S(1)}, f32[8,128]{1,0:T(8,128)S(1)}, u32[]{:S(2)}, u32[]{:S(2)}) collective-permute-start(f32[8,128]{1,0:T(8,128)S(1)} %get-tuple-element.54.refs_0_), channel_id=1, source_target_pairs={{0,3},{1,2},{2,1},{3,0},{4,7},{5,6},{6,5},{7,4},{8,11},{9,10},{10,... | collective-permute-start | bytes 12296 | tf_op jit(solution)/shard_map/ppermute | solution.py:553
  64.5 3.6 %collective-permute-start.20 = (f32[8,128]{1,0:T(8,128)S(1)}, f32[8,128]{1,0:T(8,128)S(1)}, u32[]{:S(2)}, u32[]{:S(2)}) collective-permute-start(f32[8,128]{1,0:T(8,128)S(1)} %get-tuple-element.54.refs_0_), channel_id=1, source_target_pairs={{0,2},{1,3},{2,0},{3,1},{4,6},{5,7},{6,4},{7,5},{8,10},{9,11},{10,... | collective-permute-start | bytes 12296 | tf_op jit(solution)/shard_map/ppermute | solution.py:553

commit v4 on v3

--- a/solution.py
+++ b/solution.py
@@ -11,7 +11,7 @@
 COLS = 128
 LANES = 128
 GROUP = 8
-IN_FLIGHT = 4
+CHUNK = 24
 SHRINK_SCALE = 0.4
 TINY = 1e-06
 VMEM = pltpu.VMEM
@@ -32,12 +32,21 @@
     return plain.astype(np.float32), weighted.astype(np.float32)
 
 
-def exact(left, right):
-    return jnp.dot(left, right, precision=lax.Precision.HIGHEST, preferred_element_type=jnp.float32)
+def table_terms(table):
+    high = table.astype(jnp.bfloat16)
+    low = (table - high.astype(np.float32)).astype(jnp.bfloat16)
+    return np.concatenate([high, high, low], axis=1)
+
+
+def table_dot(terms, values):
+    high = values.astype(jnp.bfloat16)
+    low = (values - high.astype(jnp.float32)).astype(jnp.bfloat16)
+    return dot_nn(terms, jnp.concatenate([high, low, high], axis=0))
 
 
 def turned(rows):
-    return jnp.concatenate([-rows[GROUP:], rows[:GROUP]], axis=0)
+    rows = rows.astype(jnp.float32)
+    return jnp.concatenate([-rows[GROUP:], rows[:GROUP]], axis=0).astype(jnp.bfloat16)
 
 
 def dot_nt(left, right):
@@ -69,7 +78,7 @@
 
 
 def forward(field, kernel_ref, plain, weighted_t):
-    return packed_series(forward_rows(exact(plain, field), kernel_ref), weighted_t, kernel_ref.shape[2])
+    return packed_series(forward_rows(table_dot(plain, field), kernel_ref), weighted_t, kernel_ref.shape[2])
 
 
 def forward_rows(spectra, kernel_ref, arrived=None):
@@ -80,7 +89,7 @@
         if arrived is not None:
             arrived(group)
         re_slab, im_slab = slab(kernel_ref, 0, group), slab(kernel_ref, 1, group)
-        out = dot_nt(part.astype(jnp.bfloat16), re_slab) + dot_nt(turned(part).astype(jnp.bfloat16), im_slab)
+        out = dot_nt(part.astype(jnp.bfloat16), re_slab) + dot_nt(turned(part), im_slab)
         width = out.shape[1]
         out = jnp.where(own_block(width, sensors), out, 0.0)
         if width < LANES:
@@ -91,7 +100,7 @@
 
 def packed_series(rows, weighted_t, sensors):
     times = weighted_t.shape[0]
-    series = exact(weighted_t, rows)
+    series = table_dot(weighted_t, rows)
     left = lax.broadcasted_iota(jnp.int32, (times // 2, LANES), 1) < sensors
     return jnp.where(left, series[: times // 2], series[times // 2 :])
 
@@ -104,7 +113,7 @@
 
 def adjoint(residual, kernel_ref, plain_t, weighted, halves):
     freqs, sensors, cells = kernel_ref.shape[1:]
-    spectra = exact(weighted, residual)
+    spectra = table_dot(weighted, residual)
     rows = []
     for group in range(weighted.shape[0] // 16):
         part = spectra[16 * group : 16 * group + 16]
@@ -113,15 +122,15 @@
         re_slab, im_slab = slab(kernel_ref, 0, group), slab(kernel_ref, 1, group)
         wide = jnp.concatenate([part] * (-(-width // LANES)), axis=1)[:, :width]
         wide = jnp.where(own_block(width, sensors), wide, 0.0)
-        total = None
+        terms = []
         for _ in range(halves):
-            re_left = wide.astype(jnp.bfloat16)
-            rounded = re_left.astype(jnp.float32)
-            out = dot_nn(re_left, re_slab) - dot_nn(turned(rounded).astype(jnp.bfloat16), im_slab)
-            total = out if total is None else total + out
-            wide = wide - rounded
-        rows.append(total)
-    return exact(plain_t, jnp.concatenate(rows, axis=0))
+            terms.append(wide.astype(jnp.bfloat16))
+            wide = wide - terms[-1].astype(jnp.float32)
+        left = jnp.concatenate(terms, axis=0)
+        swapped = jnp.concatenate([turned(term) for term in terms], axis=0)
+        out = dot_nn(left, re_slab) - dot_nn(swapped, im_slab)
+        rows.append(tree_sum([out[16 * i : 16 * i + 16] for i in range(halves)]))
+    return table_dot(plain_t, jnp.concatenate(rows, axis=0))
 
 
 def strip(array, row):
@@ -245,7 +254,8 @@
 def first_forward_body(*refs):
     loaded, (sent, edge, threshold, linked), kept, sems = refs[:10], refs[10:14], refs[14:24], refs[24]
     kernel, kernel_here = loaded[0], kept[0]
-    field, multiplier, neighbours, tile_of_cell, tile_weight, plain, weighted_t = kept[1:8]
+    field, multiplier, plain, weighted_t = kept[1:5]
+    neighbours, tile_of_cell, tile_weight = kept[7:]
     freqs = kernel.shape[1]
     times, cells = field.shape
     half = times // 2
@@ -257,38 +267,29 @@
         copies.append(copy)
         return copy
 
-    early = [load(loaded[i], kept[i]) for i in (1, 6)]
-    starts = list(range(0, freqs, GROUP))
+    early = [load(loaded[i], kept[i]) for i in (1, 3)]
     large = []
-
-    def load_group():
-        if len(large) < len(starts):
-            start = starts[len(large)]
-            at = (slice(None), pl.ds(start, min(GROUP, freqs - start)))
-            large.append(load(kernel.at[at], kernel_here.at[at]))
-
-    for _ in range(IN_FLIGHT):
-        load_group()
-    small = [load(loaded[i], kept[i]) for i in (3, 4, 5, 2, 7, 8, 9)]
+    for start in range(0, freqs, CHUNK):
+        at = (slice(None), pl.ds(start, min(CHUNK, freqs - start)))
+        large.append(load(kernel.at[at], kernel_here.at[at]))
+        if start == 0:
+            small = [load(loaded[i], kept[i]) for i in (7, 8, 9, 2, 4)]
+    late = [load(loaded[i], kept[i]) for i in (5, 6)]
     for copy in early:
         copy.wait()
-    spectra = exact(plain[...], field[...])
-
-    def arrived(group):
-        large[group].wait()
-        load_group()
-
-    rows = forward_rows(spectra, kernel_here, arrived)
+    spectra = table_dot(plain[...], field[...])
     for copy in small:
         copy.wait()
-    sent[:half, :] = packed_series(rows, weighted_t[...], kernel.shape[2])
 
     cell = lax.broadcasted_iota(jnp.int32, (4, cells), 1) + lax.axis_index("cell") * cells
     linked[0:4, :] = jnp.where(neighbours[...] != cell, 1.0, 0.0)
     linked[4:8, :] = jnp.zeros((4, cells), jnp.float32)
     tile = lax.broadcasted_iota(jnp.int32, (tile_weight.shape[1], cells), 0)
     chosen = jnp.where(tile == tile_of_cell[...], 1.0, 0.0)
-    weights = exact(jnp.broadcast_to(tile_weight[...], (8, tile_weight.shape[1])), chosen)
+    weights = jnp.dot(
+        jnp.broadcast_to(tile_weight[...], (8, tile_weight.shape[1])), chosen,
+        precision=lax.Precision.HIGHEST, preferred_element_type=jnp.float32,
+    )
     limit = SHRINK_SCALE * weights
     threshold[...] = limit
     bottom = cells // COLS - 1
@@ -301,6 +302,15 @@
         one, two = edges(head, tail)
         sent[half + start : half + start + head.shape[0], :] = one
         edge[start : start + head.shape[0], :] = two
+
+    def arrived(group):
+        if group * GROUP % CHUNK == 0:
+            large[group * GROUP // CHUNK].wait()
+
+    rows = forward_rows(spectra, kernel_here, arrived)
+    sent[:half, :] = packed_series(rows, weighted_t[...], kernel.shape[2])
+    for copy in late:
+        copy.wait()
 
 
 def first_adjoint_body(count, *refs):
@@ -417,21 +427,18 @@
 
 
 def response_body(count, *refs):
-    two, out, passing, norms = refs[count:]
+    out, norms = refs[count:]
     total = summed(refs[:count])
     packed, squares = total[:-8], total[-8:]
-    scalars = rows_of([square_sum(packed), squares[2:3, :] * (2.0 / lax.axis_size("sensor"))])
-    out[...] = scalars
-    passing[:8, :] = scalars
-    passing[8:, :] = two[...]
+    out[...] = rows_of([square_sum(packed), squares[2:3, :] * (2.0 / lax.axis_size("sensor"))])
     norms[...] = squares
 
 
 def finish_body(count, *refs):
     (norms, gradient_in, model, model_jumps, multiplier, threshold, grad_one, grad_two, passed, linked,
      estimate_out, auxiliary_out, multiplier_out) = refs[count:]
-    step = step_of(norms, tree_sum([part[:8, :] for part in refs[:count]]))
-    grad_two = jnp.where(is_odd(), grad_two[...], passed[8:, :])
+    step = step_of(norms, summed(refs[:count]))
+    grad_two = jnp.where(is_odd(), grad_two[...], passed[...])
     half = gradient_in.shape[0] // 2
     gradient = gradient_in[...]
     estimate_out[...] = model[...] - step * gradient
@@ -500,25 +507,27 @@
     times, cells = start_model.shape
     freqs, sensors = kernel.shape[1:3]
     plain, weighted = tables(times, freqs)
+    plain, plain_t, weighted, weighted_t = (
+        jnp.asarray(table_terms(t)) for t in (plain, plain.T, weighted, weighted.T)
+    )
     half = times // 2
     field, row, wide = (times, cells), (times, COLS), (4, times, cells)
 
     loads = [
-        kernel, start_model, start_multiplier, neighbours, tile_of_cell[None, :], tile_weight[None, :],
-        jnp.asarray(plain), jnp.asarray(weighted.T.copy()), jnp.asarray(plain.T.copy()), jnp.asarray(weighted),
+        kernel, start_model, start_multiplier, plain, weighted_t, plain_t, weighted,
+        neighbours, tile_of_cell[None, :], tile_weight[None, :],
     ]
-    sent, edge, threshold, linked, kernel, start_model, start_multiplier, _, _, _, plain, weighted_t, plain_t, weighted = call(
+    sent, edge, threshold, linked, kernel, start_model, start_multiplier, plain, weighted_t, plain_t, weighted = call(
         first_forward_body,
         [(half + 2 * times + 8, LANES), (2 * times + 8, LANES), (8, cells), (8, cells)]
-        + [jax.ShapeDtypeStruct(a.shape, a.dtype) for a in loads],
+        + [jax.ShapeDtypeStruct(a.shape, a.dtype) for a in loads[:7]],
         *[pltpu.with_memory_space_constraint(a, HBM) for a in loads],
-        scratch=[pltpu.SemaphoreType.DMA((9 + -(-freqs // GROUP),))],
+        scratch=[VMEM(a.shape, a.dtype) for a in loads[7:]] + [pltpu.SemaphoreType.DMA((9 + -(-freqs // CHUNK),))],
         inputs=HBM,
     )
     one = from_partner(sent)
-    merged, edge = lax.optimization_barrier((sent[:half] + one[:half], edge))
-    parts = cell_parts(merged)
     two = from_other(edge)
+    parts = cell_parts(sent[:half] + one[:half])
     message, side, shared = (half + 8 + times, LANES), (times, LANES), (2 * times + 8, LANES)
     back = call(
         functools.partial(first_adjoint_body, len(parts)), (2 * times + 8, cells),
@@ -543,17 +552,9 @@
     )
     grad_one, grad_two = from_partner(sent), from_other(edge)
     parts = cell_parts(call(merge_body, (half + 8, LANES), sent, grad_one, edge, grad_two, linked))
-    scalars, passing, norms = call(
-        functools.partial(response_body, len(parts)), [(8, LANES), (8 + times, LANES), (8, LANES)], *parts, grad_two
-    )
-    passed = sensor_hop(passing)
-    sensor_count = lax.axis_size("sensor")
-    if sensor_count <= 4:
-        parts = [scalars, passed] + [
-            lax.ppermute(scalars, "sensor", [(i, i ^ k) for i in range(sensor_count)]) for k in range(2, sensor_count)
-        ]
-    else:
-        parts = summing([scalars + passed[:8]], "sensor", 2, stages_of(sensor_count // 2, 2))
+    passed = sensor_hop(lax.optimization_barrier((grad_two, parts[-1]))[0])
+    scalars, norms = call(functools.partial(response_body, len(parts)), [(8, LANES), (8, LANES)], *parts)
+    parts = summing([scalars], "sensor", 1, stages_of(lax.axis_size("sensor"), 4, 4))
     return tuple(
         call(
             functools.partial(finish_body, len(parts)), [field, wide, wide],

time: 69.3 us -> 67.4 us (0.973)
  Pallas kernels: 14.2 us -> 10.8 us
  waiting for transfers between devices: 27 us -> 28.2 us
    ppermute x11 -> x14, waiting for transfers between devices: 14.6 us -> 19.5 us  [summing(): lax.ppermute(total, axis, [(i, i ^ k * stride) for i in range(count)])]
    pallas_call x9, Pallas kernels: 14.2 us -> 10.8 us  [call(): pl.pallas_call(body, out_shape=shapes, in_specs=[pl.BlockSpec(memory_spac...]
    ppermute x2 -> x0, waiting for transfers between devices: 3.07 us -> none  [per_device(): lax.ppermute(scalars, 'sensor', [(i, i ^ k) for i in range(sensor_count)])]
    ppermute x11 -> x14, starting transfers between devices: 16.8 us -> 19.4 us  [summing(): lax.ppermute(total, axis, [(i, i ^ k * stride) for i in range(count)])]
    ppermute x2 -> x0, starting transfers between devices: 2.06 us -> none  [per_device(): lax.ppermute(scalars, 'sensor', [(i, i ^ k) for i in range(sensor_count)])]
  transfers between devices with their start and end apart: 22 -> 23, of which waited for: 16 -> 17; matrix products, arithmetic and copies ran while one was open for 0% -> 0% of each run, Pallas kernels for 0% -> 0%
where the time goes in v4:
time: 67.4 us; the launch traced here: 67.2 us
  waiting for transfers between devices  28.2 us (42%)
  starting transfers between devices  27.4 us (41%)
  Pallas kernels  10.8 us (16%)
  between operations  0.76 us (1%)
    ppermute x14, waiting for transfers between devices, summing(): lax.ppermute(total, axis, [(i, i ^ k * stride) for i in range(count)])  19.5 us
    ppermute x14, starting transfers between devices, summing(): lax.ppermute(total, axis, [(i, i ^ k * stride) for i in range(count)])  19.4 us
    pallas_call x9, Pallas kernels, call(): pl.pallas_call(body, out_shape=shapes, in_specs=[pl.BlockSpec(memory_spac...  10.8 us
    ppermute x3, waiting for transfers between devices, from_partner(): lax.ppermute(array, 'cell', [(i, i ^ 1) for i in range(lax.axis_size('cel...  6.17 us
    ppermute x3, starting transfers between devices, from_partner(): lax.ppermute(array, 'cell', [(i, i ^ 1) for i in range(lax.axis_size('cel...  5.79 us
    ppermute x3, waiting for transfers between devices, sensor_hop(): lax.ppermute(array, 'sensor', [(i, i ^ 1) for i in range(lax.axis_size('s...  2.55 us
    ppermute x3, starting transfers between devices, from_other(): return lax.ppermute(array, ('cell', 'sensor'), pairs)  1.96 us
  transfers between devices with their start and end apart: 23, of which 17 were waited for; matrix products, arithmetic and copies ran while one was open for 0% of the time, Pallas kernels for 0%

profile of v4, /device:TPU:0, one launch (start us, length us, event | category | flops | bytes accessed | tf_op | source)
XLA Modules:
  0.0 67.2 jit_solution(853426801861870381)
XLA Ops:
  0.6 3.7 %shard_map.130 = (f32[168,128]{1,0:T(8,128)S(1)}, f32[136,128]{1,0:T(8,128)S(1)}, f32[8,256]{1,0:T(8,128)S(1)}, f32[8,256]{1,0:T(8,128)S(1)}, bf16[2,65,64,256]{...) custom-call(bf16[2,65,64,256]{3,2,1,0:T(8,128)(2,1)} %refs_0_.1, ...), custom_call_target="tpu_custom_call" | custom-call | tf_op jit(solution)/shard_map/pallas_call | solution.py:201
  4.3 3.0 %collective-permute-start = (f32[168,128]{1,0:T(8,128)S(1)}, f32[168,128]{1,0:T(8,128)S(1)}, u32[]{:S(2)}, u32[]{:S(2)}) collective-permute-start(f32[168,128]{1,0:T(8,128)S(1)} %get-tuple-element.30), channel_id=1, source_target_pairs={{0,4},{4,0},{8,12},{12,8},{16,20},{20,16},{24,28},{28,24},{1,5},{5... | collective-permute-start | bytes 258056 | tf_op jit(solution)/shard_map/ppermute | solution.py:493
  8.0 1.9 %collective-permute-done.refs_3_.refs_8_ = f32[168,128]{1,0:T(8,128)S(1)} collective-permute-done((f32[168,128]{1,0:T(8,128)S(1)}, f32[168,128]{1,0:T(8,128)S(1)}, u32[]{:S(2)}, u32[]{:S(2)}) %collective-permute-start) | collective-permute-done | bytes 86048 | tf_op jit(solution)/shard_map/ppermute | solution.py:493
  9.9 4.0 %collective-permute-start.3 = (f32[32,128]{1,0:T(8,128)S(1)}, f32[32,128]{1,0:T(8,128)S(1)}, u32[]{:S(2)}, u32[]{:S(2)}) collective-permute-start(f32[32,128]{1,0:T(8,128)S(1)} %slice_add_fusion.2.refs_0_), channel_id=1, source_target_pairs={{0,24},{4,28},{8,16},{12,20},{16,8},{20,12},{24,0},{28,4},{1,25},{... | collective-permute-start | bytes 49160 | tf_op jit(solution)/shard_map/ppermute | solution.py:472
  15.7 2.9 %collective-permute-done.2.refs_2_ = f32[32,128]{1,0:T(8,128)S(1)} collective-permute-done((f32[32,128]{1,0:T(8,128)S(1)}, f32[32,128]{1,0:T(8,128)S(1)}, u32[]{:S(2)}, u32[]{:S(2)}) %collective-permute-start.2) | collective-permute-done | bytes 16416 | tf_op jit(solution)/shard_map/ppermute | solution.py:472
  19.7 1.3 %collective-permute-done.5.refs_5_ = f32[136,256]{1,0:T(8,128)S(1)} collective-permute-done((f32[136,256]{1,0:T(8,128)S(1)}, f32[136,256]{1,0:T(8,128)S(1)}, u32[]{:S(2)}, u32[]{:S(2)}) %collective-permute-start.5) | collective-permute-done | bytes 139296 | tf_op jit(solution)/shard_map/ppermute | solution.py:479
  21.1 1.6 %collective-permute-start.6 = (f32[64,256]{1,0:T(8,128)S(1)}, f32[64,256]{1,0:T(8,128)S(1)}, u32[]{:S(2)}, u32[]{:S(2)}) collective-permute-start(f32[64,256]{1,0:T(8,128)S(1)} %slice_add_fusion.1.refs_0_), channel_id=1, source_target_pairs={{0,2},{1,3},{2,0},{3,1},{4,6},{5,7},{6,4},{7,5},{8,10},{9,11},{10,... | collective-permute-start | bytes 196616 | tf_op jit(solution)/shard_map/ppermute | solution.py:472
  22.7 2.8 %collective-permute-done.6.refs_1_ = f32[64,256]{1,0:T(8,128)S(1)} collective-permute-done((f32[64,256]{1,0:T(8,128)S(1)}, f32[64,256]{1,0:T(8,128)S(1)}, u32[]{:S(2)}, u32[]{:S(2)}) %collective-permute-start.6) | collective-permute-done | bytes 65568 | tf_op jit(solution)/shard_map/ppermute | solution.py:472
  25.4 1.7 %shard_map.132 = (f32[64,256]{1,0:T(8,128)S(1)}, f32[64,256]{1,0:T(8,128)S(1)}, f32[104,128]{1,0:T(8,128)S(1)}, f32[64,128]{1,0:T(8,128)S(1)}, f32[136,128]{1,0:T(8,128)S(1)}) custom-call(f32[64,256]{1,0:T(8,128)S(1)} %slice_add_fusion.1.refs_0_, f32[64,256]{1,0:T(8,128)S(1)} %collective-permute-done.6.refs_1_, ...), custom_call_target="tpu_custom_call" | custom-call | tf_op jit(solution)/shard_map/pallas_call | solution.py:201
  27.1 1.6 %collective-permute-start.7 = (f32[104,128]{1,0:T(8,128)S(1)}, f32[104,128]{1,0:T(8,128)S(1)}, u32[]{:S(2)}, u32[]{:S(2)}) collective-permute-start(f32[104,128]{1,0:T(8,128)S(1)} %get-tuple-element.39.sent), channel_id=1, source_target_pairs={{0,4},{4,0},{8,12},{12,8},{16,20},{20,16},{24,28},{28,24},{1,5},{5... | collective-permute-start | bytes 159752 | tf_op jit(solution)/shard_map/ppermute | solution.py:493
  29.3 1.9 %collective-permute-done.7.came.refs_10_ = f32[104,128]{1,0:T(8,128)S(1)} collective-permute-done((f32[104,128]{1,0:T(8,128)S(1)}, f32[104,128]{1,0:T(8,128)S(1)}, u32[]{:S(2)}, u32[]{:S(2)}) %collective-permute-start.7) | collective-permute-done | bytes 53280 | tf_op jit(solution)/shard_map/ppermute | solution.py:493
  31.4 1.5 %collective-permute-start.11 = (f32[40,128]{1,0:T(8,128)S(1)}, f32[40,128]{1,0:T(8,128)S(1)}, u32[]{:S(2)}, u32[]{:S(2)}) collective-permute-start(f32[40,128]{1,0:T(8,128)S(1)} %shard_map.133.refs_0_), channel_id=1, source_target_pairs={{0,24},{4,28},{8,16},{12,20},{16,8},{20,12},{24,0},{28,4},{1,25},{... | collective-permute-start | bytes 61448 | tf_op jit(solution)/shard_map/ppermute | solution.py:472
  33.6 2.3 %collective-permute-start.9 = (f32[40,128]{1,0:T(8,128)S(1)}, f32[40,128]{1,0:T(8,128)S(1)}, u32[]{:S(2)}, u32[]{:S(2)}) collective-permute-start(f32[40,128]{1,0:T(8,128)S(1)} %shard_map.133.refs_0_), channel_id=1, source_target_pairs={{0,8},{4,12},{8,0},{12,4},{16,24},{20,28},{24,16},{28,20},{1,9},{5... | collective-permute-start | bytes 61448 | tf_op jit(solution)/shard_map/ppermute | solution.py:472
  35.9 1.2 %collective-permute-done.11.refs_3_ = f32[40,128]{1,0:T(8,128)S(1)} collective-permute-done((f32[40,128]{1,0:T(8,128)S(1)}, f32[40,128]{1,0:T(8,128)S(1)}, u32[]{:S(2)}, u32[]{:S(2)}) %collective-permute-start.11) | collective-permute-done | bytes 20512 | tf_op jit(solution)/shard_map/ppermute | solution.py:472
  39.6 1.2 %collective-permute-done.12.refs_12_ = f32[104,256]{1,0:T(8,128)S(1)} collective-permute-done((f32[104,256]{1,0:T(8,128)S(1)}, f32[104,256]{1,0:T(8,128)S(1)}, u32[]{:S(2)}, u32[]{:S(2)}) %collective-permute-start.12) | collective-permute-done | bytes 106528 | tf_op jit(solution)/shard_map/ppermute | solution.py:479
  40.8 1.6 %collective-permute-start.13 = (f32[72,256]{1,0:T(8,128)S(1)}, f32[72,256]{1,0:T(8,128)S(1)}, u32[]{:S(2)}, u32[]{:S(2)}) collective-permute-start(f32[72,256]{1,0:T(8,128)S(1)} %slice_add_fusion.refs_0_), channel_id=1, source_target_pairs={{0,2},{1,3},{2,0},{3,1},{4,6},{5,7},{6,4},{7,5},{8,10},{9,11},{10,... | collective-permute-start | bytes 221192 | tf_op jit(solution)/shard_map/ppermute | solution.py:472
  42.4 2.9 %collective-permute-done.13.refs_1_ = f32[72,256]{1,0:T(8,128)S(1)} collective-permute-done((f32[72,256]{1,0:T(8,128)S(1)}, f32[72,256]{1,0:T(8,128)S(1)}, u32[]{:S(2)}, u32[]{:S(2)}) %collective-permute-start.13) | collective-permute-done | bytes 73760 | tf_op jit(solution)/shard_map/ppermute | solution.py:472
  45.3 1.8 %shard_map.135 = (f32[64,256]{1,0:T(8,128)S(1)}, f32[4,64,256]{2,1,0:T(8,128)S(1)}, f32[4,64,256]{2,1,0:T(8,128)S(1)}, f32[64,256]{1,0:T(8,128)S(1)}, f32[104,128]{1,0:T(8,128)S(1)}, /*index=5*/f32[64,128]{1,0:T(8,128)S(1)}) custom-call(f32[72,256]{1,0:T(8,128)S(1)} %slice_add_fusion.refs_0_, f32[72,256]{1,0:T(8,128)S(1)} %collective-permute-done.13.refs_1_, ...), custom_call_target="tpu_custom_call" | custom-call | tf_op jit(solution)/shard_map/pallas_call | solution.py:201
  47.1 1.2 %collective-permute-start.14 = (f32[104,128]{1,0:T(8,128)S(1)}, f32[104,128]{1,0:T(8,128)S(1)}, u32[]{:S(2)}, u32[]{:S(2)}) collective-permute-start(f32[104,128]{1,0:T(8,128)S(1)} %get-tuple-element.48.sent), channel_id=1, source_target_pairs={{0,4},{4,0},{8,12},{12,8},{16,20},{20,16},{24,28},{28,24},{1,5},{5... | collective-permute-start | bytes 159752 | tf_op jit(solution)/shard_map/ppermute | solution.py:493
  48.9 2.4 %collective-permute-done.14.came.refs_10_ = f32[104,128]{1,0:T(8,128)S(1)} collective-permute-done((f32[104,128]{1,0:T(8,128)S(1)}, f32[104,128]{1,0:T(8,128)S(1)}, u32[]{:S(2)}, u32[]{:S(2)}) %collective-permute-start.14) | collective-permute-done | bytes 53280 | tf_op jit(solution)/shard_map/ppermute | solution.py:493
  51.4 2.2 %collective-permute-start.18 = (f32[40,128]{1,0:T(8,128)S(1)}, f32[40,128]{1,0:T(8,128)S(1)}, u32[]{:S(2)}, u32[]{:S(2)}) collective-permute-start(f32[40,128]{1,0:T(8,128)S(1)} %shard_map.136.refs_0_), channel_id=1, source_target_pairs={{0,24},{4,28},{8,16},{12,20},{16,8},{20,12},{24,0},{28,4},{1,25},{... | collective-permute-start | bytes 61448 | tf_op jit(solution)/shard_map/ppermute | solution.py:472
  53.7 3.4 %collective-permute-done.18.refs_3_ = f32[40,128]{1,0:T(8,128)S(1)} collective-permute-done((f32[40,128]{1,0:T(8,128)S(1)}, f32[40,128]{1,0:T(8,128)S(1)}, u32[]{:S(2)}, u32[]{:S(2)}) %collective-permute-start.18) | collective-permute-done | bytes 20512 | tf_op jit(solution)/shard_map/ppermute | solution.py:472
  57.2 2.9 %collective-permute-start.16 = (f32[40,128]{1,0:T(8,128)S(1)}, f32[40,128]{1,0:T(8,128)S(1)}, u32[]{:S(2)}, u32[]{:S(2)}) collective-permute-start(f32[40,128]{1,0:T(8,128)S(1)} %shard_map.136.refs_0_), channel_id=1, source_target_pairs={{0,8},{4,12},{8,0},{12,4},{16,24},{20,28},{24,16},{28,20},{1,9},{5... | collective-permute-start | bytes 61448 | tf_op jit(solution)/shard_map/ppermute | solution.py:472
  60.1 1.7 %collective-permute-done.17.refs_2_ = f32[40,128]{1,0:T(8,128)S(1)} collective-permute-done((f32[40,128]{1,0:T(8,128)S(1)}, f32[40,128]{1,0:T(8,128)S(1)}, u32[]{:S(2)}, u32[]{:S(2)}) %collective-permute-start.17) | collective-permute-done | bytes 20512 | tf_op jit(solution)/shard_map/ppermute | solution.py:472
  (36 shorter events, 13.8 us)
Async XLA Ops:
  0.6 18.0 %copy-start = (f32[64,64]{1,0:T(8,128)S(1)}, f32[64,64]{1,0:T(8,128)}, u32[]{:S(2)}) copy-start(f32[64,64]{1,0:T(8,128)} %refs_4_.2) | copy-start | bytes 49156
  4.3 5.6 %collective-permute-start = (f32[168,128]{1,0:T(8,128)S(1)}, f32[168,128]{1,0:T(8,128)S(1)}, u32[]{:S(2)}, u32[]{:S(2)}) collective-permute-start(f32[168,128]{1,0:T(8,128)S(1)} %get-tuple-element.30), channel_id=1, source_target_pairs={{0,4},{4,0},{8,12},{12,8},{16,20},{20,16},{24,28},{28,24},{1,5},{5... | collective-permute-start | bytes 258056 | tf_op jit(solution)/shard_map/ppermute | solution.py:493
  7.4 7.2 %collective-permute-start.4 = (f32[136,128]{1,0:T(8,128)S(1)}, f32[136,128]{1,0:T(8,128)S(1)}, u32[]{:S(2)}, u32[]{:S(2)}) collective-permute-start(f32[136,128]{1,0:T(8,128)S(1)} %get-tuple-element.31), channel_id=1, source_target_pairs={{5,9},{7,11},{9,5},{11,7},{13,17},{15,19},{17,13},{19,15},{21,25},... | collective-permute-start | bytes 208904 | tf_op jit(solution)/shard_map/ppermute | solution.py:503
  9.9 5.8 %collective-permute-start.3 = (f32[32,128]{1,0:T(8,128)S(1)}, f32[32,128]{1,0:T(8,128)S(1)}, u32[]{:S(2)}, u32[]{:S(2)}) collective-permute-start(f32[32,128]{1,0:T(8,128)S(1)} %slice_add_fusion.2.refs_0_), channel_id=1, source_target_pairs={{0,24},{4,28},{8,16},{12,20},{16,8},{20,12},{24,0},{28,4},{1,25},{... | collective-permute-start | bytes 49160 | tf_op jit(solution)/shard_map/ppermute | solution.py:472
  14.0 4.6 %collective-permute-start.2 = (f32[32,128]{1,0:T(8,128)S(1)}, f32[32,128]{1,0:T(8,128)S(1)}, u32[]{:S(2)}, u32[]{:S(2)}) collective-permute-start(f32[32,128]{1,0:T(8,128)S(1)} %slice_add_fusion.2.refs_0_), channel_id=1, source_target_pairs={{0,16},{4,20},{8,24},{12,28},{16,0},{20,4},{24,8},{28,12},{1,17},{... | collective-permute-start | bytes 49160 | tf_op jit(solution)/shard_map/ppermute | solution.py:472
  14.0 4.6 %collective-permute-start.1 = (f32[32,128]{1,0:T(8,128)S(1)}, f32[32,128]{1,0:T(8,128)S(1)}, u32[]{:S(2)}, u32[]{:S(2)}) collective-permute-start(f32[32,128]{1,0:T(8,128)S(1)} %slice_add_fusion.2.refs_0_), channel_id=1, source_target_pairs={{0,8},{4,12},{8,0},{12,4},{16,24},{20,28},{24,16},{28,20},{1,9},{5... | collective-permute-start | bytes 49160 | tf_op jit(solution)/shard_map/ppermute | solution.py:472
  19.7 1.4 %collective-permute-start.5 = (f32[136,256]{1,0:T(8,128)S(1)}, f32[136,256]{1,0:T(8,128)S(1)}, u32[]{:S(2)}, u32[]{:S(2)}) collective-permute-start(f32[136,256]{1,0:T(8,128)S(1)} %shard_map.131), channel_id=1, source_target_pairs={{0,1},{1,0},{2,3},{3,2},{4,5},{5,4},{6,7},{7,6},{8,9},{9,8},{10,11... | collective-permute-start | bytes 417800 | tf_op jit(solution)/shard_map/ppermute | solution.py:479
  21.1 4.3 %collective-permute-start.6 = (f32[64,256]{1,0:T(8,128)S(1)}, f32[64,256]{1,0:T(8,128)S(1)}, u32[]{:S(2)}, u32[]{:S(2)}) collective-permute-start(f32[64,256]{1,0:T(8,128)S(1)} %slice_add_fusion.1.refs_0_), channel_id=1, source_target_pairs={{0,2},{1,3},{2,0},{3,1},{4,6},{5,7},{6,4},{7,5},{8,10},{9,11},{10,... | collective-permute-start | bytes 196616 | tf_op jit(solution)/shard_map/ppermute | solution.py:472
  27.1 4.2 %collective-permute-start.7 = (f32[104,128]{1,0:T(8,128)S(1)}, f32[104,128]{1,0:T(8,128)S(1)}, u32[]{:S(2)}, u32[]{:S(2)}) collective-permute-start(f32[104,128]{1,0:T(8,128)S(1)} %get-tuple-element.39.sent), channel_id=1, source_target_pairs={{0,4},{4,0},{8,12},{12,8},{16,20},{20,16},{24,28},{28,24},{1,5},{5... | collective-permute-start | bytes 159752 | tf_op jit(solution)/shard_map/ppermute | solution.py:493
  28.7 0.7 collective-permute-start.8
  31.4 5.6 %collective-permute-start.11 = (f32[40,128]{1,0:T(8,128)S(1)}, f32[40,128]{1,0:T(8,128)S(1)}, u32[]{:S(2)}, u32[]{:S(2)}) collective-permute-start(f32[40,128]{1,0:T(8,128)S(1)} %shard_map.133.refs_0_), channel_id=1, source_target_pairs={{0,24},{4,28},{8,16},{12,20},{16,8},{20,12},{24,0},{28,4},{1,25},{... | collective-permute-start | bytes 61448 | tf_op jit(solution)/shard_map/ppermute | solution.py:472
  33.0 4.7 %collective-permute-start.10 = (f32[40,128]{1,0:T(8,128)S(1)}, f32[40,128]{1,0:T(8,128)S(1)}, u32[]{:S(2)}, u32[]{:S(2)}) collective-permute-start(f32[40,128]{1,0:T(8,128)S(1)} %shard_map.133.refs_0_), channel_id=1, source_target_pairs={{0,16},{4,20},{8,24},{12,28},{16,0},{20,4},{24,8},{28,12},{1,17},{... | collective-permute-start | bytes 61448 | tf_op jit(solution)/shard_map/ppermute | solution.py:472
  33.6 4.7 %collective-permute-start.9 = (f32[40,128]{1,0:T(8,128)S(1)}, f32[40,128]{1,0:T(8,128)S(1)}, u32[]{:S(2)}, u32[]{:S(2)}) collective-permute-start(f32[40,128]{1,0:T(8,128)S(1)} %shard_map.133.refs_0_), channel_id=1, source_target_pairs={{0,8},{4,12},{8,0},{12,4},{16,24},{20,28},{24,16},{28,20},{1,9},{5... | collective-permute-start | bytes 61448 | tf_op jit(solution)/shard_map/ppermute | solution.py:472
  39.4 1.4 %collective-permute-start.12 = (f32[104,256]{1,0:T(8,128)S(1)}, f32[104,256]{1,0:T(8,128)S(1)}, u32[]{:S(2)}, u32[]{:S(2)}) collective-permute-start(f32[104,256]{1,0:T(8,128)S(1)} %get-tuple-element.41), channel_id=1, source_target_pairs={{0,1},{1,0},{2,3},{3,2},{4,5},{5,4},{6,7},{7,6},{8,9},{9,8},{10,11... | collective-permute-start | bytes 319496 | tf_op jit(solution)/shard_map/ppermute | solution.py:479
  40.8 4.4 %collective-permute-start.13 = (f32[72,256]{1,0:T(8,128)S(1)}, f32[72,256]{1,0:T(8,128)S(1)}, u32[]{:S(2)}, u32[]{:S(2)}) collective-permute-start(f32[72,256]{1,0:T(8,128)S(1)} %slice_add_fusion.refs_0_), channel_id=1, source_target_pairs={{0,2},{1,3},{2,0},{3,1},{4,6},{5,7},{6,4},{7,5},{8,10},{9,11},{10,... | collective-permute-start | bytes 221192 | tf_op jit(solution)/shard_map/ppermute | solution.py:472
  47.1 4.2 %collective-permute-start.14 = (f32[104,128]{1,0:T(8,128)S(1)}, f32[104,128]{1,0:T(8,128)S(1)}, u32[]{:S(2)}, u32[]{:S(2)}) collective-permute-start(f32[104,128]{1,0:T(8,128)S(1)} %get-tuple-element.48.sent), channel_id=1, source_target_pairs={{0,4},{4,0},{8,12},{12,8},{16,20},{20,16},{24,28},{28,24},{1,5},{5... | collective-permute-start | bytes 159752 | tf_op jit(solution)/shard_map/ppermute | solution.py:493
  48.3 0.7 collective-permute-start.15
  51.4 5.6 %collective-permute-start.18 = (f32[40,128]{1,0:T(8,128)S(1)}, f32[40,128]{1,0:T(8,128)S(1)}, u32[]{:S(2)}, u32[]{:S(2)}) collective-permute-start(f32[40,128]{1,0:T(8,128)S(1)} %shard_map.136.refs_0_), channel_id=1, source_target_pairs={{0,24},{4,28},{8,16},{12,20},{16,8},{20,12},{24,0},{28,4},{1,25},{... | collective-permute-start | bytes 61448 | tf_op jit(solution)/shard_map/ppermute | solution.py:472
  57.1 9.2 %collective-permute-start.22 = (f32[64,128]{1,0:T(8,128)S(1)}, f32[64,128]{1,0:T(8,128)S(1)}, u32[]{:S(2)}, u32[]{:S(2)}) collective-permute-start(f32[64,128]{1,0:T(8,128)S(1)} %collective-permute-done.15.other.refs_11_), channel_id=1, source_target_pairs={{0,1},{1,0},{2,3},{3,2},{4,5},{5,4},{6,7},{7,6},{8,9},{9,8},{10,11... | collective-permute-start | bytes 98312 | tf_op jit(solution)/shard_map/ppermute | solution.py:479
  57.1 4.7 %collective-permute-start.17 = (f32[40,128]{1,0:T(8,128)S(1)}, f32[40,128]{1,0:T(8,128)S(1)}, u32[]{:S(2)}, u32[]{:S(2)}) collective-permute-start(f32[40,128]{1,0:T(8,128)S(1)} %shard_map.136.refs_0_), channel_id=1, source_target_pairs={{0,16},{4,20},{8,24},{12,28},{16,0},{20,4},{24,8},{28,12},{1,17},{... | collective-permute-start | bytes 61448 | tf_op jit(solution)/shard_map/ppermute | solution.py:472
  57.2 4.8 %collective-permute-start.16 = (f32[40,128]{1,0:T(8,128)S(1)}, f32[40,128]{1,0:T(8,128)S(1)}, u32[]{:S(2)}, u32[]{:S(2)}) collective-permute-start(f32[40,128]{1,0:T(8,128)S(1)} %shard_map.136.refs_0_), channel_id=1, source_target_pairs={{0,8},{4,12},{8,0},{12,4},{16,24},{20,28},{24,16},{28,20},{1,9},{5... | collective-permute-start | bytes 61448 | tf_op jit(solution)/shard_map/ppermute | solution.py:472
  62.1 3.1 %collective-permute-start.21 = (f32[8,128]{1,0:T(8,128)S(1)}, f32[8,128]{1,0:T(8,128)S(1)}, u32[]{:S(2)}, u32[]{:S(2)}) collective-permute-start(f32[8,128]{1,0:T(8,128)S(1)} %get-tuple-element.50.refs_0_), channel_id=1, source_target_pairs={{0,3},{1,2},{2,1},{3,0},{4,7},{5,6},{6,5},{7,4},{8,11},{9,10},{10,... | collective-permute-start | bytes 12296 | tf_op jit(solution)/shard_map/ppermute | solution.py:472
  62.7 3.6 %collective-permute-start.20 = (f32[8,128]{1,0:T(8,128)S(1)}, f32[8,128]{1,0:T(8,128)S(1)}, u32[]{:S(2)}, u32[]{:S(2)}) collective-permute-start(f32[8,128]{1,0:T(8,128)S(1)} %get-tuple-element.50.refs_0_), channel_id=1, source_target_pairs={{0,2},{1,3},{2,0},{3,1},{4,6},{5,7},{6,4},{7,5},{8,10},{9,11},{10,... | collective-permute-start | bytes 12296 | tf_op jit(solution)/shard_map/ppermute | solution.py:472
  63.8 2.5 %collective-permute-start.19 = (f32[8,128]{1,0:T(8,128)S(1)}, f32[8,128]{1,0:T(8,128)S(1)}, u32[]{:S(2)}, u32[]{:S(2)}) collective-permute-start(f32[8,128]{1,0:T(8,128)S(1)} %get-tuple-element.50.refs_0_), channel_id=1, source_target_pairs={{0,1},{1,0},{2,3},{3,2},{4,5},{5,4},{6,7},{7,6},{8,9},{9,8},{10,11... | collective-permute-start | bytes 12296 | tf_op jit(solution)/shard_map/ppermute | solution.py:472

commit v5 on v4

--- a/solution.py
+++ b/solution.py
@@ -194,7 +194,7 @@
     return jnp.full((rows, LANES), scalar, jnp.float32)
 
 
-def call(body, out_shapes, *operands, scratch=(), inputs=VMEM):
+def call(body, out_shapes, *operands, scratch=(), inputs=VMEM, outputs=VMEM):
     single = isinstance(out_shapes, tuple)
     shapes = [out_shapes] if single else list(out_shapes)
     shapes = [s if isinstance(s, jax.ShapeDtypeStruct) else jax.ShapeDtypeStruct(s, jnp.float32) for s in shapes]
@@ -202,7 +202,7 @@
         body,
         out_shape=shapes,
         in_specs=[pl.BlockSpec(memory_space=inputs)] * len(operands),
-        out_specs=[pl.BlockSpec(memory_space=VMEM)] * len(shapes),
+        out_specs=[pl.BlockSpec(memory_space=outputs)] * len(shapes),
         scratch_shapes=list(scratch),
         compiler_params=pltpu.CompilerParams(vmem_limit_bytes=24 * 2**20),
     )(*operands)
@@ -436,20 +436,32 @@
 
 def finish_body(count, *refs):
     (norms, gradient_in, model, model_jumps, multiplier, threshold, grad_one, grad_two, passed, linked,
-     estimate_out, auxiliary_out, multiplier_out) = refs[count:]
+     estimate_out, auxiliary_out, multiplier_out, estimate_here, auxiliary_here, multiplier_here, sems) = refs[count:]
     step = step_of(norms, summed(refs[:count]))
     grad_two = jnp.where(is_odd(), grad_two[...], passed[...])
     half = gradient_in.shape[0] // 2
     gradient = gradient_in[...]
-    estimate_out[...] = model[...] - step * gradient
+    copies = []
+
+    def store(source, target):
+        copy = pltpu.make_async_copy(source, target, sems.at[len(copies)])
+        copy.start()
+        copies.append(copy)
+
+    estimate_here[...] = model[...] - step * gradient
+    store(estimate_here, estimate_out)
     grad_jumps = jumps(gradient, *beside(grad_one[half + 8 :, :], grad_two), linked[...])
     for k in range(4):
         for r in range(gradient.shape[1] // COLS):
             at = slice(r * COLS, (r + 1) * COLS)
             shifted = model_jumps[k, :, at] - step * grad_jumps[k][r] + multiplier[k, :, at]
             auxiliary = shrunk(shifted, threshold[0:1, at])
-            auxiliary_out[k, :, at] = auxiliary
-            multiplier_out[k, :, at] = shifted - auxiliary
+            auxiliary_here[k, :, at] = auxiliary
+            multiplier_here[k, :, at] = shifted - auxiliary
+        store(auxiliary_here.at[k], auxiliary_out.at[k])
+        store(multiplier_here.at[k], multiplier_out.at[k])
+    for copy in copies:
+        copy.wait()
 
 
 def stages_of(count, *radices):
@@ -552,13 +564,15 @@
     )
     grad_one, grad_two = from_partner(sent), from_other(edge)
     parts = cell_parts(call(merge_body, (half + 8, LANES), sent, grad_one, edge, grad_two, linked))
-    passed = sensor_hop(lax.optimization_barrier((grad_two, parts[-1]))[0])
     scalars, norms = call(functools.partial(response_body, len(parts)), [(8, LANES), (8, LANES)], *parts)
+    passed = sensor_hop(lax.optimization_barrier((grad_two, norms))[0])
     parts = summing([scalars], "sensor", 1, stages_of(lax.axis_size("sensor"), 4, 4))
     return tuple(
         call(
             functools.partial(finish_body, len(parts)), [field, wide, wide],
             *parts, norms, gradient, model, model_jumps, multiplier, threshold, grad_one, grad_two, passed, linked,
+            scratch=[VMEM(shape, jnp.float32) for shape in (field, wide, wide)] + [pltpu.SemaphoreType.DMA((9,))],
+            outputs=HBM,
         )
     )
 

time: 67.4 us -> 65.1 us (0.966)
  waiting for transfers between devices: 28.2 us -> 26.4 us
    ppermute x14, waiting for transfers between devices: 19.5 us -> 17.7 us  [summing(): lax.ppermute(total, axis, [(i, i ^ k * stride) for i in range(count)])]
    ppermute x14, starting transfers between devices: 19.4 us -> 18.8 us  [summing(): lax.ppermute(total, axis, [(i, i ^ k * stride) for i in range(count)])]
  transfers between devices with their start and end apart: 23 -> 23, of which waited for: 17 -> 16; matrix products, arithmetic and copies ran while one was open for 0% -> 0% of each run, Pallas kernels for 0% -> 0%
where the time goes in v5:
time: 65.1 us; the launch traced here: 65 us
  starting transfers between devices  26.9 us (41%)
  waiting for transfers between devices  26.4 us (41%)
  Pallas kernels  10.8 us (17%)
  between operations  0.76 us (1%)
    ppermute x14, starting transfers between devices, summing(): lax.ppermute(total, axis, [(i, i ^ k * stride) for i in range(count)])  18.8 us
    ppermute x14, waiting for transfers between devices, summing(): lax.ppermute(total, axis, [(i, i ^ k * stride) for i in range(count)])  17.7 us
    pallas_call x9, Pallas kernels, call(): pl.pallas_call(body, out_shape=shapes, in_specs=[pl.BlockSpec(memory_spac...  10.8 us
    ppermute x3, waiting for transfers between devices, from_partner(): lax.ppermute(array, 'cell', [(i, i ^ 1) for i in range(lax.axis_size('cel...  6.17 us
    ppermute x3, starting transfers between devices, from_partner(): lax.ppermute(array, 'cell', [(i, i ^ 1) for i in range(lax.axis_size('cel...  5.79 us
    ppermute x3, waiting for transfers between devices, sensor_hop(): lax.ppermute(array, 'sensor', [(i, i ^ 1) for i in range(lax.axis_size('s...  2.55 us
    ppermute x3, starting transfers between devices, from_other(): return lax.ppermute(array, ('cell', 'sensor'), pairs)  1.96 us
  transfers between devices with their start and end apart: 23, of which 16 were waited for; matrix products, arithmetic and copies ran while one was open for 0% of the time, Pallas kernels for 0%

profile of v5, /device:TPU:0, one launch (start us, length us, event | category | flops | bytes accessed | tf_op | source)
XLA Modules:
  0.0 65.0 jit_solution(14488152351782450820)
XLA Ops:
  0.6 3.7 %shard_map.130 = (f32[168,128]{1,0:T(8,128)S(1)}, f32[136,128]{1,0:T(8,128)S(1)}, f32[8,256]{1,0:T(8,128)S(1)}, f32[8,256]{1,0:T(8,128)S(1)}, bf16[2,65,64,256]{...) custom-call(bf16[2,65,64,256]{3,2,1,0:T(8,128)(2,1)} %refs_0_.1, ...), custom_call_target="tpu_custom_call" | custom-call | tf_op jit(solution)/shard_map/pallas_call | solution.py:201
  4.3 3.0 %collective-permute-start = (f32[168,128]{1,0:T(8,128)S(1)}, f32[168,128]{1,0:T(8,128)S(1)}, u32[]{:S(2)}, u32[]{:S(2)}) collective-permute-start(f32[168,128]{1,0:T(8,128)S(1)} %get-tuple-element.30), channel_id=1, source_target_pairs={{0,4},{4,0},{8,12},{12,8},{16,20},{20,16},{24,28},{28,24},{1,5},{5... | collective-permute-start | bytes 258056 | tf_op jit(solution)/shard_map/ppermute | solution.py:505
  8.0 1.9 %collective-permute-done.refs_3_.refs_8_ = f32[168,128]{1,0:T(8,128)S(1)} collective-permute-done((f32[168,128]{1,0:T(8,128)S(1)}, f32[168,128]{1,0:T(8,128)S(1)}, u32[]{:S(2)}, u32[]{:S(2)}) %collective-permute-start) | collective-permute-done | bytes 86048 | tf_op jit(solution)/shard_map/ppermute | solution.py:505
  9.9 4.0 %collective-permute-start.3 = (f32[32,128]{1,0:T(8,128)S(1)}, f32[32,128]{1,0:T(8,128)S(1)}, u32[]{:S(2)}, u32[]{:S(2)}) collective-permute-start(f32[32,128]{1,0:T(8,128)S(1)} %slice_add_fusion.2.refs_0_), channel_id=1, source_target_pairs={{0,24},{4,28},{8,16},{12,20},{16,8},{20,12},{24,0},{28,4},{1,25},{... | collective-permute-start | bytes 49160 | tf_op jit(solution)/shard_map/ppermute | solution.py:484
  15.7 2.9 %collective-permute-done.2.refs_2_ = f32[32,128]{1,0:T(8,128)S(1)} collective-permute-done((f32[32,128]{1,0:T(8,128)S(1)}, f32[32,128]{1,0:T(8,128)S(1)}, u32[]{:S(2)}, u32[]{:S(2)}) %collective-permute-start.2) | collective-permute-done | bytes 16416 | tf_op jit(solution)/shard_map/ppermute | solution.py:484
  19.7 1.3 %collective-permute-done.5.refs_5_ = f32[136,256]{1,0:T(8,128)S(1)} collective-permute-done((f32[136,256]{1,0:T(8,128)S(1)}, f32[136,256]{1,0:T(8,128)S(1)}, u32[]{:S(2)}, u32[]{:S(2)}) %collective-permute-start.5) | collective-permute-done | bytes 139296 | tf_op jit(solution)/shard_map/ppermute | solution.py:491
  21.1 1.6 %collective-permute-start.6 = (f32[64,256]{1,0:T(8,128)S(1)}, f32[64,256]{1,0:T(8,128)S(1)}, u32[]{:S(2)}, u32[]{:S(2)}) collective-permute-start(f32[64,256]{1,0:T(8,128)S(1)} %slice_add_fusion.1.refs_0_), channel_id=1, source_target_pairs={{0,2},{1,3},{2,0},{3,1},{4,6},{5,7},{6,4},{7,5},{8,10},{9,11},{10,... | collective-permute-start | bytes 196616 | tf_op jit(solution)/shard_map/ppermute | solution.py:484
  22.7 2.8 %collective-permute-done.6.refs_1_ = f32[64,256]{1,0:T(8,128)S(1)} collective-permute-done((f32[64,256]{1,0:T(8,128)S(1)}, f32[64,256]{1,0:T(8,128)S(1)}, u32[]{:S(2)}, u32[]{:S(2)}) %collective-permute-start.6) | collective-permute-done | bytes 65568 | tf_op jit(solution)/shard_map/ppermute | solution.py:484
  25.4 1.7 %shard_map.132 = (f32[64,256]{1,0:T(8,128)S(1)}, f32[64,256]{1,0:T(8,128)S(1)}, f32[104,128]{1,0:T(8,128)S(1)}, f32[64,128]{1,0:T(8,128)S(1)}, f32[136,128]{1,0:T(8,128)S(1)}) custom-call(f32[64,256]{1,0:T(8,128)S(1)} %slice_add_fusion.1.refs_0_, f32[64,256]{1,0:T(8,128)S(1)} %collective-permute-done.6.refs_1_, ...), custom_call_target="tpu_custom_call" | custom-call | tf_op jit(solution)/shard_map/pallas_call | solution.py:201
  27.1 1.6 %collective-permute-start.7 = (f32[104,128]{1,0:T(8,128)S(1)}, f32[104,128]{1,0:T(8,128)S(1)}, u32[]{:S(2)}, u32[]{:S(2)}) collective-permute-start(f32[104,128]{1,0:T(8,128)S(1)} %get-tuple-element.39.sent), channel_id=1, source_target_pairs={{0,4},{4,0},{8,12},{12,8},{16,20},{20,16},{24,28},{28,24},{1,5},{5... | collective-permute-start | bytes 159752 | tf_op jit(solution)/shard_map/ppermute | solution.py:505
  29.3 1.9 %collective-permute-done.7.came.refs_10_ = f32[104,128]{1,0:T(8,128)S(1)} collective-permute-done((f32[104,128]{1,0:T(8,128)S(1)}, f32[104,128]{1,0:T(8,128)S(1)}, u32[]{:S(2)}, u32[]{:S(2)}) %collective-permute-start.7) | collective-permute-done | bytes 53280 | tf_op jit(solution)/shard_map/ppermute | solution.py:505
  31.4 1.5 %collective-permute-start.11 = (f32[40,128]{1,0:T(8,128)S(1)}, f32[40,128]{1,0:T(8,128)S(1)}, u32[]{:S(2)}, u32[]{:S(2)}) collective-permute-start(f32[40,128]{1,0:T(8,128)S(1)} %shard_map.133.refs_0_), channel_id=1, source_target_pairs={{0,24},{4,28},{8,16},{12,20},{16,8},{20,12},{24,0},{28,4},{1,25},{... | collective-permute-start | bytes 61448 | tf_op jit(solution)/shard_map/ppermute | solution.py:484
  33.6 2.3 %collective-permute-start.9 = (f32[40,128]{1,0:T(8,128)S(1)}, f32[40,128]{1,0:T(8,128)S(1)}, u32[]{:S(2)}, u32[]{:S(2)}) collective-permute-start(f32[40,128]{1,0:T(8,128)S(1)} %shard_map.133.refs_0_), channel_id=1, source_target_pairs={{0,8},{4,12},{8,0},{12,4},{16,24},{20,28},{24,16},{28,20},{1,9},{5... | collective-permute-start | bytes 61448 | tf_op jit(solution)/shard_map/ppermute | solution.py:484
  35.9 1.2 %collective-permute-done.11.refs_3_ = f32[40,128]{1,0:T(8,128)S(1)} collective-permute-done((f32[40,128]{1,0:T(8,128)S(1)}, f32[40,128]{1,0:T(8,128)S(1)}, u32[]{:S(2)}, u32[]{:S(2)}) %collective-permute-start.11) | collective-permute-done | bytes 20512 | tf_op jit(solution)/shard_map/ppermute | solution.py:484
  39.6 1.2 %collective-permute-done.12.refs_12_ = f32[104,256]{1,0:T(8,128)S(1)} collective-permute-done((f32[104,256]{1,0:T(8,128)S(1)}, f32[104,256]{1,0:T(8,128)S(1)}, u32[]{:S(2)}, u32[]{:S(2)}) %collective-permute-start.12) | collective-permute-done | bytes 106528 | tf_op jit(solution)/shard_map/ppermute | solution.py:491
  40.8 1.6 %collective-permute-start.13 = (f32[72,256]{1,0:T(8,128)S(1)}, f32[72,256]{1,0:T(8,128)S(1)}, u32[]{:S(2)}, u32[]{:S(2)}) collective-permute-start(f32[72,256]{1,0:T(8,128)S(1)} %slice_add_fusion.refs_0_), channel_id=1, source_target_pairs={{0,2},{1,3},{2,0},{3,1},{4,6},{5,7},{6,4},{7,5},{8,10},{9,11},{10,... | collective-permute-start | bytes 221192 | tf_op jit(solution)/shard_map/ppermute | solution.py:484
  42.4 2.9 %collective-permute-done.13.refs_1_ = f32[72,256]{1,0:T(8,128)S(1)} collective-permute-done((f32[72,256]{1,0:T(8,128)S(1)}, f32[72,256]{1,0:T(8,128)S(1)}, u32[]{:S(2)}, u32[]{:S(2)}) %collective-permute-start.13) | collective-permute-done | bytes 73760 | tf_op jit(solution)/shard_map/ppermute | solution.py:484
  45.3 1.8 %shard_map.135 = (f32[64,256]{1,0:T(8,128)S(1)}, f32[4,64,256]{2,1,0:T(8,128)S(1)}, f32[4,64,256]{2,1,0:T(8,128)S(1)}, f32[64,256]{1,0:T(8,128)S(1)}, f32[104,128]{1,0:T(8,128)S(1)}, /*index=5*/f32[64,128]{1,0:T(8,128)S(1)}) custom-call(f32[72,256]{1,0:T(8,128)S(1)} %slice_add_fusion.refs_0_, f32[72,256]{1,0:T(8,128)S(1)} %collective-permute-done.13.refs_1_, ...), custom_call_target="tpu_custom_call" | custom-call | tf_op jit(solution)/shard_map/pallas_call | solution.py:201
  48.9 2.4 %collective-permute-done.14.came.refs_10_ = f32[104,128]{1,0:T(8,128)S(1)} collective-permute-done((f32[104,128]{1,0:T(8,128)S(1)}, f32[104,128]{1,0:T(8,128)S(1)}, u32[]{:S(2)}, u32[]{:S(2)}) %collective-permute-start.14) | collective-permute-done | bytes 53280 | tf_op jit(solution)/shard_map/ppermute | solution.py:505
  51.4 2.2 %collective-permute-start.18 = (f32[40,128]{1,0:T(8,128)S(1)}, f32[40,128]{1,0:T(8,128)S(1)}, u32[]{:S(2)}, u32[]{:S(2)}) collective-permute-start(f32[40,128]{1,0:T(8,128)S(1)} %shard_map.136.refs_0_), channel_id=1, source_target_pairs={{0,24},{4,28},{8,16},{12,20},{16,8},{20,12},{24,0},{28,4},{1,25},{... | collective-permute-start | bytes 61448 | tf_op jit(solution)/shard_map/ppermute | solution.py:484
  54.3 1.5 %collective-permute-start.16 = (f32[40,128]{1,0:T(8,128)S(1)}, f32[40,128]{1,0:T(8,128)S(1)}, u32[]{:S(2)}, u32[]{:S(2)}) collective-permute-start(f32[40,128]{1,0:T(8,128)S(1)} %shard_map.136.refs_0_), channel_id=1, source_target_pairs={{0,8},{4,12},{8,0},{12,4},{16,24},{20,28},{24,16},{28,20},{1,9},{5... | collective-permute-start | bytes 61448 | tf_op jit(solution)/shard_map/ppermute | solution.py:484
  57.1 1.4 %collective-permute-done.17.refs_2_ = f32[40,128]{1,0:T(8,128)S(1)} collective-permute-done((f32[40,128]{1,0:T(8,128)S(1)}, f32[40,128]{1,0:T(8,128)S(1)}, u32[]{:S(2)}, u32[]{:S(2)}) %collective-permute-start.17) | collective-permute-done | bytes 20512 | tf_op jit(solution)/shard_map/ppermute | solution.py:484
  58.8 1.5 %collective-permute-start.21 = (f32[8,128]{1,0:T(8,128)S(1)}, f32[8,128]{1,0:T(8,128)S(1)}, u32[]{:S(2)}, u32[]{:S(2)}) collective-permute-start(f32[8,128]{1,0:T(8,128)S(1)} %get-tuple-element.50.refs_0_), channel_id=1, source_target_pairs={{0,3},{1,2},{2,1},{3,0},{4,7},{5,6},{6,5},{7,4},{8,11},{9,10},{10,... | collective-permute-start | bytes 12296 | tf_op jit(solution)/shard_map/ppermute | solution.py:484
  61.8 2.1 %collective-permute-done.20.refs_2_ = f32[8,128]{1,0:T(8,128)S(1)} collective-permute-done((f32[8,128]{1,0:T(8,128)S(1)}, f32[8,128]{1,0:T(8,128)S(1)}, u32[]{:S(2)}, u32[]{:S(2)}) %collective-permute-start.20) | collective-permute-done | bytes 4128 | tf_op jit(solution)/shard_map/ppermute | solution.py:484
  (36 shorter events, 14.2 us)
Async XLA Ops:
  0.6 18.0 %copy-start = (f32[64,64]{1,0:T(8,128)S(1)}, f32[64,64]{1,0:T(8,128)}, u32[]{:S(2)}) copy-start(f32[64,64]{1,0:T(8,128)} %refs_4_.2) | copy-start | bytes 49156
  4.3 5.6 %collective-permute-start = (f32[168,128]{1,0:T(8,128)S(1)}, f32[168,128]{1,0:T(8,128)S(1)}, u32[]{:S(2)}, u32[]{:S(2)}) collective-permute-start(f32[168,128]{1,0:T(8,128)S(1)} %get-tuple-element.30), channel_id=1, source_target_pairs={{0,4},{4,0},{8,12},{12,8},{16,20},{20,16},{24,28},{28,24},{1,5},{5... | collective-permute-start | bytes 258056 | tf_op jit(solution)/shard_map/ppermute | solution.py:505
  7.4 7.2 %collective-permute-start.4 = (f32[136,128]{1,0:T(8,128)S(1)}, f32[136,128]{1,0:T(8,128)S(1)}, u32[]{:S(2)}, u32[]{:S(2)}) collective-permute-start(f32[136,128]{1,0:T(8,128)S(1)} %get-tuple-element.31), channel_id=1, source_target_pairs={{5,9},{7,11},{9,5},{11,7},{13,17},{15,19},{17,13},{19,15},{21,25},... | collective-permute-start | bytes 208904 | tf_op jit(solution)/shard_map/ppermute | solution.py:515
  9.9 5.8 %collective-permute-start.3 = (f32[32,128]{1,0:T(8,128)S(1)}, f32[32,128]{1,0:T(8,128)S(1)}, u32[]{:S(2)}, u32[]{:S(2)}) collective-permute-start(f32[32,128]{1,0:T(8,128)S(1)} %slice_add_fusion.2.refs_0_), channel_id=1, source_target_pairs={{0,24},{4,28},{8,16},{12,20},{16,8},{20,12},{24,0},{28,4},{1,25},{... | collective-permute-start | bytes 49160 | tf_op jit(solution)/shard_map/ppermute | solution.py:484
  14.0 4.6 %collective-permute-start.2 = (f32[32,128]{1,0:T(8,128)S(1)}, f32[32,128]{1,0:T(8,128)S(1)}, u32[]{:S(2)}, u32[]{:S(2)}) collective-permute-start(f32[32,128]{1,0:T(8,128)S(1)} %slice_add_fusion.2.refs_0_), channel_id=1, source_target_pairs={{0,16},{4,20},{8,24},{12,28},{16,0},{20,4},{24,8},{28,12},{1,17},{... | collective-permute-start | bytes 49160 | tf_op jit(solution)/shard_map/ppermute | solution.py:484
  14.0 4.6 %collective-permute-start.1 = (f32[32,128]{1,0:T(8,128)S(1)}, f32[32,128]{1,0:T(8,128)S(1)}, u32[]{:S(2)}, u32[]{:S(2)}) collective-permute-start(f32[32,128]{1,0:T(8,128)S(1)} %slice_add_fusion.2.refs_0_), channel_id=1, source_target_pairs={{0,8},{4,12},{8,0},{12,4},{16,24},{20,28},{24,16},{28,20},{1,9},{5... | collective-permute-start | bytes 49160 | tf_op jit(solution)/shard_map/ppermute | solution.py:484
  19.7 1.4 %collective-permute-start.5 = (f32[136,256]{1,0:T(8,128)S(1)}, f32[136,256]{1,0:T(8,128)S(1)}, u32[]{:S(2)}, u32[]{:S(2)}) collective-permute-start(f32[136,256]{1,0:T(8,128)S(1)} %shard_map.131), channel_id=1, source_target_pairs={{0,1},{1,0},{2,3},{3,2},{4,5},{5,4},{6,7},{7,6},{8,9},{9,8},{10,11... | collective-permute-start | bytes 417800 | tf_op jit(solution)/shard_map/ppermute | solution.py:491
  21.1 4.3 %collective-permute-start.6 = (f32[64,256]{1,0:T(8,128)S(1)}, f32[64,256]{1,0:T(8,128)S(1)}, u32[]{:S(2)}, u32[]{:S(2)}) collective-permute-start(f32[64,256]{1,0:T(8,128)S(1)} %slice_add_fusion.1.refs_0_), channel_id=1, source_target_pairs={{0,2},{1,3},{2,0},{3,1},{4,6},{5,7},{6,4},{7,5},{8,10},{9,11},{10,... | collective-permute-start | bytes 196616 | tf_op jit(solution)/shard_map/ppermute | solution.py:484
  27.1 4.2 %collective-permute-start.7 = (f32[104,128]{1,0:T(8,128)S(1)}, f32[104,128]{1,0:T(8,128)S(1)}, u32[]{:S(2)}, u32[]{:S(2)}) collective-permute-start(f32[104,128]{1,0:T(8,128)S(1)} %get-tuple-element.39.sent), channel_id=1, source_target_pairs={{0,4},{4,0},{8,12},{12,8},{16,20},{20,16},{24,28},{28,24},{1,5},{5... | collective-permute-start | bytes 159752 | tf_op jit(solution)/shard_map/ppermute | solution.py:505
  28.7 0.7 %collective-permute-start.8 = (f32[64,128]{1,0:T(8,128)S(1)}, f32[64,128]{1,0:T(8,128)S(1)}, u32[]{:S(2)}, u32[]{:S(2)}) collective-permute-start(f32[64,128]{1,0:T(8,128)S(1)} %get-tuple-element.40.edge), channel_id=1, source_target_pairs={{5,9},{7,11},{9,5},{11,7},{13,17},{15,19},{17,13},{19,15},{21,25},... | collective-permute-start | bytes 98312 | tf_op jit(solution)/shard_map/ppermute | solution.py:515
  31.4 5.6 %collective-permute-start.11 = (f32[40,128]{1,0:T(8,128)S(1)}, f32[40,128]{1,0:T(8,128)S(1)}, u32[]{:S(2)}, u32[]{:S(2)}) collective-permute-start(f32[40,128]{1,0:T(8,128)S(1)} %shard_map.133.refs_0_), channel_id=1, source_target_pairs={{0,24},{4,28},{8,16},{12,20},{16,8},{20,12},{24,0},{28,4},{1,25},{... | collective-permute-start | bytes 61448 | tf_op jit(solution)/shard_map/ppermute | solution.py:484
  33.0 4.7 %collective-permute-start.10 = (f32[40,128]{1,0:T(8,128)S(1)}, f32[40,128]{1,0:T(8,128)S(1)}, u32[]{:S(2)}, u32[]{:S(2)}) collective-permute-start(f32[40,128]{1,0:T(8,128)S(1)} %shard_map.133.refs_0_), channel_id=1, source_target_pairs={{0,16},{4,20},{8,24},{12,28},{16,0},{20,4},{24,8},{28,12},{1,17},{... | collective-permute-start | bytes 61448 | tf_op jit(solution)/shard_map/ppermute | solution.py:484
  33.6 4.7 %collective-permute-start.9 = (f32[40,128]{1,0:T(8,128)S(1)}, f32[40,128]{1,0:T(8,128)S(1)}, u32[]{:S(2)}, u32[]{:S(2)}) collective-permute-start(f32[40,128]{1,0:T(8,128)S(1)} %shard_map.133.refs_0_), channel_id=1, source_target_pairs={{0,8},{4,12},{8,0},{12,4},{16,24},{20,28},{24,16},{28,20},{1,9},{5... | collective-permute-start | bytes 61448 | tf_op jit(solution)/shard_map/ppermute | solution.py:484
  39.4 1.4 %collective-permute-start.12 = (f32[104,256]{1,0:T(8,128)S(1)}, f32[104,256]{1,0:T(8,128)S(1)}, u32[]{:S(2)}, u32[]{:S(2)}) collective-permute-start(f32[104,256]{1,0:T(8,128)S(1)} %get-tuple-element.41), channel_id=1, source_target_pairs={{0,1},{1,0},{2,3},{3,2},{4,5},{5,4},{6,7},{7,6},{8,9},{9,8},{10,11... | collective-permute-start | bytes 319496 | tf_op jit(solution)/shard_map/ppermute | solution.py:491
  40.8 4.4 %collective-permute-start.13 = (f32[72,256]{1,0:T(8,128)S(1)}, f32[72,256]{1,0:T(8,128)S(1)}, u32[]{:S(2)}, u32[]{:S(2)}) collective-permute-start(f32[72,256]{1,0:T(8,128)S(1)} %slice_add_fusion.refs_0_), channel_id=1, source_target_pairs={{0,2},{1,3},{2,0},{3,1},{4,6},{5,7},{6,4},{7,5},{8,10},{9,11},{10,... | collective-permute-start | bytes 221192 | tf_op jit(solution)/shard_map/ppermute | solution.py:484
  47.1 4.2 %collective-permute-start.14 = (f32[104,128]{1,0:T(8,128)S(1)}, f32[104,128]{1,0:T(8,128)S(1)}, u32[]{:S(2)}, u32[]{:S(2)}) collective-permute-start(f32[104,128]{1,0:T(8,128)S(1)} %get-tuple-element.48.sent), channel_id=1, source_target_pairs={{0,4},{4,0},{8,12},{12,8},{16,20},{20,16},{24,28},{28,24},{1,5},{5... | collective-permute-start | bytes 159752 | tf_op jit(solution)/shard_map/ppermute | solution.py:505
  48.3 0.7 %collective-permute-start.15 = (f32[64,128]{1,0:T(8,128)S(1)}, f32[64,128]{1,0:T(8,128)S(1)}, u32[]{:S(2)}, u32[]{:S(2)}) collective-permute-start(f32[64,128]{1,0:T(8,128)S(1)} %get-tuple-element.49.edge), channel_id=1, source_target_pairs={{5,9},{7,11},{9,5},{11,7},{13,17},{15,19},{17,13},{19,15},{21,25},... | collective-permute-start | bytes 98312 | tf_op jit(solution)/shard_map/ppermute | solution.py:515
  51.4 5.6 %collective-permute-start.18 = (f32[40,128]{1,0:T(8,128)S(1)}, f32[40,128]{1,0:T(8,128)S(1)}, u32[]{:S(2)}, u32[]{:S(2)}) collective-permute-start(f32[40,128]{1,0:T(8,128)S(1)} %shard_map.136.refs_0_), channel_id=1, source_target_pairs={{0,24},{4,28},{8,16},{12,20},{16,8},{20,12},{24,0},{28,4},{1,25},{... | collective-permute-start | bytes 61448 | tf_op jit(solution)/shard_map/ppermute | solution.py:484
  53.7 4.8 %collective-permute-start.17 = (f32[40,128]{1,0:T(8,128)S(1)}, f32[40,128]{1,0:T(8,128)S(1)}, u32[]{:S(2)}, u32[]{:S(2)}) collective-permute-start(f32[40,128]{1,0:T(8,128)S(1)} %shard_map.136.refs_0_), channel_id=1, source_target_pairs={{0,16},{4,20},{8,24},{12,28},{16,0},{20,4},{24,8},{28,12},{1,17},{... | collective-permute-start | bytes 61448 | tf_op jit(solution)/shard_map/ppermute | solution.py:484
  54.3 4.2 %collective-permute-start.16 = (f32[40,128]{1,0:T(8,128)S(1)}, f32[40,128]{1,0:T(8,128)S(1)}, u32[]{:S(2)}, u32[]{:S(2)}) collective-permute-start(f32[40,128]{1,0:T(8,128)S(1)} %shard_map.136.refs_0_), channel_id=1, source_target_pairs={{0,8},{4,12},{8,0},{12,4},{16,24},{20,28},{24,16},{28,20},{1,9},{5... | collective-permute-start | bytes 61448 | tf_op jit(solution)/shard_map/ppermute | solution.py:484
  58.6 5.3 %collective-permute-start.22 = (f32[64,128]{1,0:T(8,128)S(1)}, f32[64,128]{1,0:T(8,128)S(1)}, u32[]{:S(2)}, u32[]{:S(2)}) collective-permute-start(f32[64,128]{1,0:T(8,128)S(1)} %collective-permute-done.15.other.refs_11_), channel_id=1, source_target_pairs={{0,1},{1,0},{2,3},{3,2},{4,5},{5,4},{6,7},{7,6},{8,9},{9,8},{10,11... | collective-permute-start | bytes 98312 | tf_op jit(solution)/shard_map/ppermute | solution.py:491
  58.8 3.0 %collective-permute-start.21 = (f32[8,128]{1,0:T(8,128)S(1)}, f32[8,128]{1,0:T(8,128)S(1)}, u32[]{:S(2)}, u32[]{:S(2)}) collective-permute-start(f32[8,128]{1,0:T(8,128)S(1)} %get-tuple-element.50.refs_0_), channel_id=1, source_target_pairs={{0,3},{1,2},{2,1},{3,0},{4,7},{5,6},{6,5},{7,4},{8,11},{9,10},{10,... | collective-permute-start | bytes 12296 | tf_op jit(solution)/shard_map/ppermute | solution.py:484
  60.3 3.6 %collective-permute-start.20 = (f32[8,128]{1,0:T(8,128)S(1)}, f32[8,128]{1,0:T(8,128)S(1)}, u32[]{:S(2)}, u32[]{:S(2)}) collective-permute-start(f32[8,128]{1,0:T(8,128)S(1)} %get-tuple-element.50.refs_0_), channel_id=1, source_target_pairs={{0,2},{1,3},{2,0},{3,1},{4,6},{5,7},{6,4},{7,5},{8,10},{9,11},{10,... | collective-permute-start | bytes 12296 | tf_op jit(solution)/shard_map/ppermute | solution.py:484
  60.9 3.1 %collective-permute-start.19 = (f32[8,128]{1,0:T(8,128)S(1)}, f32[8,128]{1,0:T(8,128)S(1)}, u32[]{:S(2)}, u32[]{:S(2)}) collective-permute-start(f32[8,128]{1,0:T(8,128)S(1)} %get-tuple-element.50.refs_0_), channel_id=1, source_target_pairs={{0,1},{1,0},{2,3},{3,2},{4,5},{5,4},{6,7},{7,6},{8,9},{9,8},{10,11... | collective-permute-start | bytes 12296 | tf_op jit(solution)/shard_map/ppermute | solution.py:484

commit v6 on v5

--- a/solution.py
+++ b/solution.py
@@ -351,21 +351,23 @@
     out[top - 8 :, :] = sent[top - 8 : top, :] + came[top - 8 : top, :] + rows_of([0.0, 0.0, boundary])
 
 
-def first_gradient_body(count, *refs):
-    (start_multiplier, one, two, passed, linked_ref, kernel, plain, weighted_t,
-     adjoint_out, gradient, sent, edge, two_out) = refs[count:]
-    times, cells = adjoint_out.shape
+def start_back_body(start_multiplier, one, two, passed, linked, back, two_out):
+    times, cells = back.shape
     half = times // 2
     two = jnp.where(is_odd(), two[...], gathered(passed[times:, :], two.shape[0]))
     two_out[...] = two
-    linked = linked_ref[...]
-    total = summed(refs[:count])
     values = [[strip(start_multiplier[k], r) for r in range(cells // COLS)] for k in range(4)]
     above, below = beside(one[half + times : half + 2 * times, :], two[times : 2 * times, :])
-    field = total + gathered_jumps(values, above, below, linked)
+    back[...] = gathered_jumps(values, above, below, linked[...])
+
+
+def first_gradient_body(count, *refs):
+    back, linked, kernel, plain, weighted_t, adjoint_out, gradient, sent, edge = refs[count:]
+    total = summed(refs[:count])
+    field = total + back[...]
     adjoint_out[...] = total
     gradient[...] = field
-    response_of(field, kernel, plain, weighted_t, linked, sent, edge)
+    response_of(field, kernel, plain, weighted_t, linked[...], sent, edge)
 
 
 def second_adjoint_body(count, *refs):
@@ -385,8 +387,20 @@
     return norms[0, 0] / (scalars[0, 0] + (norms[1, 0] + scalars[1, 0]) + TINY)
 
 
+def both_jumps_body(model, gradient, one, two, grad_one, grad_two, passed, linked, model_jumps, grad_jumps):
+    times, cells = model.shape
+    half = times // 2
+    above, below = beside(one[half : half + times, :], two[:times, :])
+    from_other = jnp.where(is_odd(), grad_two[...], gathered(passed[times + 8 :, :], times))
+    halos = ((above, below), beside(grad_one[half + 8 :, :], from_other))
+    for field, (above, below), out in zip((model, gradient), halos, (model_jumps, grad_jumps)):
+        for k, strips in enumerate(jumps(field[...], above, below, linked[...])):
+            for r, values in enumerate(strips):
+                out[k, :, r * COLS : (r + 1) * COLS] = values
+
+
 def second_gradient_body(count, *refs):
-    (norms, adjoint_in, gradient_in, model, start_multiplier, threshold, one, two, grad_one, grad_two, passed, linked_ref,
+    (norms, adjoint_in, gradient_in, model, model_jumps, grad_jumps, start_multiplier, threshold, one, two, linked_ref,
      kernel, plain, weighted_t, model_out, jumps_out, multiplier_out, gradient_out, sent, edge) = refs[count:]
     times, cells = model.shape
     half = times // 2
@@ -396,9 +410,6 @@
     field, gradient = model[...], gradient_in[...]
     rows = cells // COLS
     above, below = beside(one[half:, :], two[...])
-    field_jumps = jumps(field, above[:times], below[:times], linked)
-    grad_two = jnp.where(is_odd(), grad_two[...], gathered(passed[times + 8 :, :], times))
-    grad_jumps = jumps(gradient, *beside(grad_one[half + 8 :, :], grad_two), linked)
 
     def advance(model_jumps, old_multiplier, limit):
         shifted = model_jumps + old_multiplier
@@ -411,10 +422,11 @@
         penalties.append([])
         new_jumps.append([])
         for r in range(rows):
-            new = field_jumps[k][r] - step * grad_jumps[k][r]
+            at = slice(r * COLS, (r + 1) * COLS)
+            new = model_jumps[k, :, at] - step * grad_jumps[k, :, at]
             multiplier, penalty = advance(new, strip(start_multiplier[k], r), strip(threshold[0:1], r))
-            jumps_out[k, :, r * COLS : (r + 1) * COLS] = new
-            multiplier_out[k, :, r * COLS : (r + 1) * COLS] = multiplier
+            jumps_out[k, :, at] = new
+            multiplier_out[k, :, at] = multiplier
             penalties[k].append(penalty)
             new_jumps[k].append(new)
     _, beside_above = advance(-new_jumps[2][0], above[times : 2 * times], above[2 * times : 2 * times + 1])
@@ -427,18 +439,21 @@
 
 
 def response_body(count, *refs):
-    out, norms = refs[count:]
+    two, out, passing, norms = refs[count:]
     total = summed(refs[:count])
     packed, squares = total[:-8], total[-8:]
-    out[...] = rows_of([square_sum(packed), squares[2:3, :] * (2.0 / lax.axis_size("sensor"))])
+    scalars = rows_of([square_sum(packed), squares[2:3, :] * (2.0 / lax.axis_size("sensor"))])
+    out[...] = scalars
+    passing[:8, :] = scalars
+    passing[8:, :] = two[...]
     norms[...] = squares
 
 
 def finish_body(count, *refs):
     (norms, gradient_in, model, model_jumps, multiplier, threshold, grad_one, grad_two, passed, linked,
      estimate_out, auxiliary_out, multiplier_out, estimate_here, auxiliary_here, multiplier_here, sems) = refs[count:]
-    step = step_of(norms, summed(refs[:count]))
-    grad_two = jnp.where(is_odd(), grad_two[...], passed[...])
+    step = step_of(norms, tree_sum([part[:8, :] for part in refs[:count]]))
+    grad_two = jnp.where(is_odd(), grad_two[...], passed[8:, :])
     half = gradient_in.shape[0] // 2
     gradient = gradient_in[...]
     copies = []
@@ -497,6 +512,19 @@
     return summing([total], "sensor", 2, stages_of(lax.axis_size("sensor") // 2, 2)), passed
 
 
+def last_sensor_parts(scalars, passing):
+    count = lax.axis_size("sensor")
+    near, far, across = (
+        lax.ppermute(array, "sensor", [(i, i ^ k) for i in range(count)])
+        for k, array in ((1, scalars), (2, scalars), (3, passing))
+    )
+    parts = [scalars, near, far, across]
+    if count > 4:
+        rows = scalars.shape[0]
+        parts = summing([tree_sum([part[:rows] for part in parts])], "sensor", 4, stages_of(count // 4, 4))
+    return parts, across
+
+
 def cell_parts(merged):
     return summing([merged], "cell", 2, stages_of(lax.axis_size("cell") // 2, 4, 4))
 
@@ -546,9 +574,10 @@
         *parts, observed, two, kernel, plain_t, weighted,
     )
     parts, passed = sensor_parts(back, times)
-    adjoint_one, gradient, sent, edge, two = call(
-        functools.partial(first_gradient_body, len(parts)), [field, field, message, side, shared],
-        *parts, start_multiplier, one, two, passed, linked, kernel, plain, weighted_t,
+    back, two = call(start_back_body, [field, shared], start_multiplier, one, two, passed, linked)
+    adjoint_one, gradient, sent, edge = call(
+        functools.partial(first_gradient_body, len(parts)), [field, field, message, side],
+        *parts, back, linked, kernel, plain, weighted_t,
     )
     grad_one, grad_two = from_partner(sent), from_other(edge)
     parts = cell_parts(call(merge_body, (half + 8, LANES), sent, grad_one, edge, grad_two, linked))
@@ -557,16 +586,20 @@
         *parts, grad_two, kernel, plain_t, weighted,
     )
     parts, passed = sensor_parts(back, times + 8)
+    model_jumps, grad_jumps = call(
+        both_jumps_body, [wide, wide], start_model, gradient, one, two, grad_one, grad_two, passed, linked
+    )
     model, model_jumps, multiplier, gradient, sent, edge = call(
         functools.partial(second_gradient_body, len(parts)), [field, wide, wide, field, message, side],
-        *parts, norms, adjoint_one, gradient, start_model, start_multiplier, threshold, one, two, grad_one, grad_two,
-        passed, linked, kernel, plain, weighted_t,
+        *parts, norms, adjoint_one, gradient, start_model, model_jumps, grad_jumps, start_multiplier, threshold,
+        one, two, linked, kernel, plain, weighted_t,
     )
     grad_one, grad_two = from_partner(sent), from_other(edge)
     parts = cell_parts(call(merge_body, (half + 8, LANES), sent, grad_one, edge, grad_two, linked))
-    scalars, norms = call(functools.partial(response_body, len(parts)), [(8, LANES), (8, LANES)], *parts)
-    passed = sensor_hop(lax.optimization_barrier((grad_two, norms))[0])
-    parts = summing([scalars], "sensor", 1, stages_of(lax.axis_size("sensor"), 4, 4))
+    scalars, passing, norms = call(
+        functools.partial(response_body, len(parts)), [(8, LANES), (8 + times, LANES), (8, LANES)], *parts, grad_two
+    )
+    parts, passed = last_sensor_parts(scalars, passing)
     return tuple(
         call(
             functools.partial(finish_body, len(parts)), [field, wide, wide],

time: 65.1 us -> 64.6 us (level)
    ppermute x14 -> x11, waiting for transfers between devices: 17.7 us -> 14.4 us  [summing(): lax.ppermute(total, axis, [(i, i ^ k * stride) for i in range(count)])]
    ppermute x0 -> x3, waiting for transfers between devices: none -> 2.93 us  [last_sensor_parts(): lax.ppermute(array, 'sensor', [(i, i ^ k) for i in range(count)])]
    ppermute x14 -> x11, starting transfers between devices: 18.8 us -> 16.7 us  [summing(): lax.ppermute(total, axis, [(i, i ^ k * stride) for i in range(count)])]
    ppermute x0 -> x3, starting transfers between devices: none -> 1.95 us  [last_sensor_parts(): lax.ppermute(array, 'sensor', [(i, i ^ k) for i in range(count)])]
    pallas_call x9 -> x11, Pallas kernels: 10.8 us -> 10.9 us  [call(): pl.pallas_call(body, out_shape=shapes, in_specs=[pl.BlockSpec(memory_spac...]
    ppermute x3 -> x2, waiting for transfers between devices: 2.55 us -> 2.54 us  [sensor_hop(): lax.ppermute(array, 'sensor', [(i, i ^ 1) for i in range(lax.axis_size('s...]
  transfers between devices with their start and end apart: 23 -> 22, of which waited for: 16 -> 15; matrix products, arithmetic and copies ran while one was open for 0% -> 0% of each run, Pallas kernels for 0% -> 0%
where the time goes in v6:
time: 64.6 us; the launch traced here: 64.4 us
  starting transfers between devices  26.6 us (41%)
  waiting for transfers between devices  26 us (40%)
  Pallas kernels  10.9 us (17%)
  between operations  0.78 us (1%)
    ppermute x11, starting transfers between devices, summing(): lax.ppermute(total, axis, [(i, i ^ k * stride) for i in range(count)])  16.7 us
    ppermute x11, waiting for transfers between devices, summing(): lax.ppermute(total, axis, [(i, i ^ k * stride) for i in range(count)])  14.4 us
    pallas_call x11, Pallas kernels, call(): pl.pallas_call(body, out_shape=shapes, in_specs=[pl.BlockSpec(memory_spac...  10.9 us
    ppermute x3, waiting for transfers between devices, from_partner(): lax.ppermute(array, 'cell', [(i, i ^ 1) for i in range(lax.axis_size('cel...  6.17 us
    ppermute x3, starting transfers between devices, from_partner(): lax.ppermute(array, 'cell', [(i, i ^ 1) for i in range(lax.axis_size('cel...  5.79 us
    ppermute x3, waiting for transfers between devices, last_sensor_parts(): lax.ppermute(array, 'sensor', [(i, i ^ k) for i in range(count)])  2.93 us
    ppermute x2, waiting for transfers between devices, sensor_hop(): lax.ppermute(array, 'sensor', [(i, i ^ 1) for i in range(lax.axis_size('s...  2.54 us
    ppermute x3, starting transfers between devices, from_other(): return lax.ppermute(array, ('cell', 'sensor'), pairs)  1.96 us
  transfers between devices with their start and end apart: 22, of which 15 were waited for; matrix products, arithmetic and copies ran while one was open for 0% of the time, Pallas kernels for 0%

profile of v6, /device:TPU:0, one launch (start us, length us, event | category | flops | bytes accessed | tf_op | source)
XLA Modules:
  0.0 64.4 jit_solution(16706229664053186692)
XLA Ops:
  0.6 3.7 %shard_map.130 = (f32[168,128]{1,0:T(8,128)S(1)}, f32[136,128]{1,0:T(8,128)S(1)}, f32[8,256]{1,0:T(8,128)S(1)}, f32[8,256]{1,0:T(8,128)S(1)}, bf16[2,65,64,256]{...) custom-call(bf16[2,65,64,256]{3,2,1,0:T(8,128)(2,1)} %refs_0_.1, ...), custom_call_target="tpu_custom_call" | custom-call | tf_op jit(solution)/shard_map/pallas_call | solution.py:201
  4.3 3.0 %collective-permute-start = (f32[168,128]{1,0:T(8,128)S(1)}, f32[168,128]{1,0:T(8,128)S(1)}, u32[]{:S(2)}, u32[]{:S(2)}) collective-permute-start(f32[168,128]{1,0:T(8,128)S(1)} %get-tuple-element.33), channel_id=1, source_target_pairs={{0,4},{4,0},{8,12},{12,8},{16,20},{20,16},{24,28},{28,24},{1,5},{5... | collective-permute-start | bytes 258056 | tf_op jit(solution)/shard_map/ppermute | solution.py:533
  8.0 1.9 %collective-permute-done.one.refs_10_ = f32[168,128]{1,0:T(8,128)S(1)} collective-permute-done((f32[168,128]{1,0:T(8,128)S(1)}, f32[168,128]{1,0:T(8,128)S(1)}, u32[]{:S(2)}, u32[]{:S(2)}) %collective-permute-start) | collective-permute-done | bytes 86048 | tf_op jit(solution)/shard_map/ppermute | solution.py:533
  9.9 4.0 %collective-permute-start.3 = (f32[32,128]{1,0:T(8,128)S(1)}, f32[32,128]{1,0:T(8,128)S(1)}, u32[]{:S(2)}, u32[]{:S(2)}) collective-permute-start(f32[32,128]{1,0:T(8,128)S(1)} %slice_add_fusion.2.refs_0_), channel_id=1, source_target_pairs={{0,24},{4,28},{8,16},{12,20},{16,8},{20,12},{24,0},{28,4},{1,25},{... | collective-permute-start | bytes 49160 | tf_op jit(solution)/shard_map/ppermute | solution.py:499
  15.7 2.9 %collective-permute-done.2.refs_2_ = f32[32,128]{1,0:T(8,128)S(1)} collective-permute-done((f32[32,128]{1,0:T(8,128)S(1)}, f32[32,128]{1,0:T(8,128)S(1)}, u32[]{:S(2)}, u32[]{:S(2)}) %collective-permute-start.2) | collective-permute-done | bytes 16416 | tf_op jit(solution)/shard_map/ppermute | solution.py:499
  19.7 1.3 %collective-permute-done.5.passed = f32[136,256]{1,0:T(8,128)S(1)} collective-permute-done((f32[136,256]{1,0:T(8,128)S(1)}, f32[136,256]{1,0:T(8,128)S(1)}, u32[]{:S(2)}, u32[]{:S(2)}) %collective-permute-start.5) | collective-permute-done | bytes 139296 | tf_op jit(solution)/shard_map/ppermute | solution.py:506
  21.1 1.6 %collective-permute-start.6 = (f32[64,256]{1,0:T(8,128)S(1)}, f32[64,256]{1,0:T(8,128)S(1)}, u32[]{:S(2)}, u32[]{:S(2)}) collective-permute-start(f32[64,256]{1,0:T(8,128)S(1)} %slice_add_fusion.1.refs_0_), channel_id=1, source_target_pairs={{0,2},{1,3},{2,0},{3,1},{4,6},{5,7},{6,4},{7,5},{8,10},{9,11},{10,... | collective-permute-start | bytes 196616 | tf_op jit(solution)/shard_map/ppermute | solution.py:499
  22.8 2.7 %collective-permute-done.6.refs_1_ = f32[64,256]{1,0:T(8,128)S(1)} collective-permute-done((f32[64,256]{1,0:T(8,128)S(1)}, f32[64,256]{1,0:T(8,128)S(1)}, u32[]{:S(2)}, u32[]{:S(2)}) %collective-permute-start.6) | collective-permute-done | bytes 65568 | tf_op jit(solution)/shard_map/ppermute | solution.py:499
  25.4 1.6 %shard_map.133 = (f32[64,256]{1,0:T(8,128)S(1)}, f32[64,256]{1,0:T(8,128)S(1)}, f32[104,128]{1,0:T(8,128)S(1)}, f32[64,128]{1,0:T(8,128)S(1)}) custom-call(f32[64,256]{1,0:T(8,128)S(1)} %slice_add_fusion.1.refs_0_, f32[64,256]{1,0:T(8,128)S(1)} %collective-permute-done.6.refs_1_, f32[64,256]{1,0:T(8,128)S(1)} %get-tuple-element.40.refs_2_, ...), custom_call_target="tpu_custom_call" | custom-call | tf_op jit(solution)/shard_map/pallas_call | solution.py:201
  27.0 1.6 %collective-permute-start.7 = (f32[104,128]{1,0:T(8,128)S(1)}, f32[104,128]{1,0:T(8,128)S(1)}, u32[]{:S(2)}, u32[]{:S(2)}) collective-permute-start(f32[104,128]{1,0:T(8,128)S(1)} %get-tuple-element.43.sent), channel_id=1, source_target_pairs={{0,4},{4,0},{8,12},{12,8},{16,20},{20,16},{24,28},{28,24},{1,5},{5... | collective-permute-start | bytes 159752 | tf_op jit(solution)/shard_map/ppermute | solution.py:533
  29.2 1.9 %collective-permute-done.7.came.grad_one = f32[104,128]{1,0:T(8,128)S(1)} collective-permute-done((f32[104,128]{1,0:T(8,128)S(1)}, f32[104,128]{1,0:T(8,128)S(1)}, u32[]{:S(2)}, u32[]{:S(2)}) %collective-permute-start.7) | collective-permute-done | bytes 53280 | tf_op jit(solution)/shard_map/ppermute | solution.py:533
  31.3 1.5 %collective-permute-start.11 = (f32[40,128]{1,0:T(8,128)S(1)}, f32[40,128]{1,0:T(8,128)S(1)}, u32[]{:S(2)}, u32[]{:S(2)}) collective-permute-start(f32[40,128]{1,0:T(8,128)S(1)} %shard_map.134.refs_0_), channel_id=1, source_target_pairs={{0,24},{4,28},{8,16},{12,20},{16,8},{20,12},{24,0},{28,4},{1,25},{... | collective-permute-start | bytes 61448 | tf_op jit(solution)/shard_map/ppermute | solution.py:499
  33.5 2.3 %collective-permute-start.9 = (f32[40,128]{1,0:T(8,128)S(1)}, f32[40,128]{1,0:T(8,128)S(1)}, u32[]{:S(2)}, u32[]{:S(2)}) collective-permute-start(f32[40,128]{1,0:T(8,128)S(1)} %shard_map.134.refs_0_), channel_id=1, source_target_pairs={{0,8},{4,12},{8,0},{12,4},{16,24},{20,28},{24,16},{28,20},{1,9},{5... | collective-permute-start | bytes 61448 | tf_op jit(solution)/shard_map/ppermute | solution.py:499
  35.8 1.2 %collective-permute-done.11.refs_3_ = f32[40,128]{1,0:T(8,128)S(1)} collective-permute-done((f32[40,128]{1,0:T(8,128)S(1)}, f32[40,128]{1,0:T(8,128)S(1)}, u32[]{:S(2)}, u32[]{:S(2)}) %collective-permute-start.11) | collective-permute-done | bytes 20512 | tf_op jit(solution)/shard_map/ppermute | solution.py:499
  39.5 1.2 %collective-permute-done.12.passed = f32[104,256]{1,0:T(8,128)S(1)} collective-permute-done((f32[104,256]{1,0:T(8,128)S(1)}, f32[104,256]{1,0:T(8,128)S(1)}, u32[]{:S(2)}, u32[]{:S(2)}) %collective-permute-start.12) | collective-permute-done | bytes 106528 | tf_op jit(solution)/shard_map/ppermute | solution.py:506
  40.7 1.6 %collective-permute-start.13 = (f32[72,256]{1,0:T(8,128)S(1)}, f32[72,256]{1,0:T(8,128)S(1)}, u32[]{:S(2)}, u32[]{:S(2)}) collective-permute-start(f32[72,256]{1,0:T(8,128)S(1)} %slice_add_fusion.refs_0_), channel_id=1, source_target_pairs={{0,2},{1,3},{2,0},{3,1},{4,6},{5,7},{6,4},{7,5},{8,10},{9,11},{10,... | collective-permute-start | bytes 221192 | tf_op jit(solution)/shard_map/ppermute | solution.py:499
  42.4 2.7 %collective-permute-done.13.refs_1_ = f32[72,256]{1,0:T(8,128)S(1)} collective-permute-done((f32[72,256]{1,0:T(8,128)S(1)}, f32[72,256]{1,0:T(8,128)S(1)}, u32[]{:S(2)}, u32[]{:S(2)}) %collective-permute-start.13) | collective-permute-done | bytes 73760 | tf_op jit(solution)/shard_map/ppermute | solution.py:499
  45.2 1.8 %shard_map.137 = (f32[64,256]{1,0:T(8,128)S(1)}, f32[4,64,256]{2,1,0:T(8,128)S(1)}, f32[4,64,256]{2,1,0:T(8,128)S(1)}, f32[64,256]{1,0:T(8,128)S(1)}, f32[104,128]{1,0:T(8,128)S(1)}, /*index=5*/f32[64,128]{1,0:T(8,128)S(1)}) custom-call(f32[72,256]{1,0:T(8,128)S(1)} %slice_add_fusion.refs_0_, f32[72,256]{1,0:T(8,128)S(1)} %collective-permute-done.13.refs_1_, ...), custom_call_target="tpu_custom_call" | custom-call | tf_op jit(solution)/shard_map/pallas_call | solution.py:201
  48.8 2.4 %collective-permute-done.14.came.refs_10_ = f32[104,128]{1,0:T(8,128)S(1)} collective-permute-done((f32[104,128]{1,0:T(8,128)S(1)}, f32[104,128]{1,0:T(8,128)S(1)}, u32[]{:S(2)}, u32[]{:S(2)}) %collective-permute-start.14) | collective-permute-done | bytes 53280 | tf_op jit(solution)/shard_map/ppermute | solution.py:533
  51.3 2.2 %collective-permute-start.18 = (f32[40,128]{1,0:T(8,128)S(1)}, f32[40,128]{1,0:T(8,128)S(1)}, u32[]{:S(2)}, u32[]{:S(2)}) collective-permute-start(f32[40,128]{1,0:T(8,128)S(1)} %shard_map.138.refs_0_), channel_id=1, source_target_pairs={{0,24},{4,28},{8,16},{12,20},{16,8},{20,12},{24,0},{28,4},{1,25},{... | collective-permute-start | bytes 61448 | tf_op jit(solution)/shard_map/ppermute | solution.py:499
  54.2 1.5 %collective-permute-start.16 = (f32[40,128]{1,0:T(8,128)S(1)}, f32[40,128]{1,0:T(8,128)S(1)}, u32[]{:S(2)}, u32[]{:S(2)}) collective-permute-start(f32[40,128]{1,0:T(8,128)S(1)} %shard_map.138.refs_0_), channel_id=1, source_target_pairs={{0,8},{4,12},{8,0},{12,4},{16,24},{20,28},{24,16},{28,20},{1,9},{5... | collective-permute-start | bytes 61448 | tf_op jit(solution)/shard_map/ppermute | solution.py:499
  57.0 1.4 %collective-permute-done.17.refs_2_ = f32[40,128]{1,0:T(8,128)S(1)} collective-permute-done((f32[40,128]{1,0:T(8,128)S(1)}, f32[40,128]{1,0:T(8,128)S(1)}, u32[]{:S(2)}, u32[]{:S(2)}) %collective-permute-start.17) | collective-permute-done | bytes 20512 | tf_op jit(solution)/shard_map/ppermute | solution.py:499
  58.5 1.3 %collective-permute-start.21 = (f32[72,128]{1,0:T(8,128)S(1)}, f32[72,128]{1,0:T(8,128)S(1)}, u32[]{:S(2)}, u32[]{:S(2)}) collective-permute-start(f32[72,128]{1,0:T(8,128)S(1)} %get-tuple-element.57), channel_id=1, source_target_pairs={{0,3},{1,2},{2,1},{3,0},{4,7},{5,6},{6,5},{7,4},{8,11},{9,10},{10,... | collective-permute-start | bytes 110600 | tf_op jit(solution)/shard_map/ppermute | solution.py:518
  60.5 2.9 %collective-permute-done.20.refs_2_ = f32[8,128]{1,0:T(8,128)S(1)} collective-permute-done((f32[8,128]{1,0:T(8,128)S(1)}, f32[8,128]{1,0:T(8,128)S(1)}, u32[]{:S(2)}, u32[]{:S(2)}) %collective-permute-start.20) | collective-permute-done | bytes 4128 | tf_op jit(solution)/shard_map/ppermute | solution.py:518
  (36 shorter events, 13.4 us)
Async XLA Ops:
  0.6 18.0 %copy-start = (f32[64,64]{1,0:T(8,128)S(1)}, f32[64,64]{1,0:T(8,128)}, u32[]{:S(2)}) copy-start(f32[64,64]{1,0:T(8,128)} %refs_4_.2) | copy-start | bytes 49156
  4.3 5.6 %collective-permute-start = (f32[168,128]{1,0:T(8,128)S(1)}, f32[168,128]{1,0:T(8,128)S(1)}, u32[]{:S(2)}, u32[]{:S(2)}) collective-permute-start(f32[168,128]{1,0:T(8,128)S(1)} %get-tuple-element.33), channel_id=1, source_target_pairs={{0,4},{4,0},{8,12},{12,8},{16,20},{20,16},{24,28},{28,24},{1,5},{5... | collective-permute-start | bytes 258056 | tf_op jit(solution)/shard_map/ppermute | solution.py:533
  7.4 7.2 %collective-permute-start.4 = (f32[136,128]{1,0:T(8,128)S(1)}, f32[136,128]{1,0:T(8,128)S(1)}, u32[]{:S(2)}, u32[]{:S(2)}) collective-permute-start(f32[136,128]{1,0:T(8,128)S(1)} %get-tuple-element.34), channel_id=1, source_target_pairs={{5,9},{7,11},{9,5},{11,7},{13,17},{15,19},{17,13},{19,15},{21,25},... | collective-permute-start | bytes 208904 | tf_op jit(solution)/shard_map/ppermute | solution.py:543
  9.9 5.8 %collective-permute-start.3 = (f32[32,128]{1,0:T(8,128)S(1)}, f32[32,128]{1,0:T(8,128)S(1)}, u32[]{:S(2)}, u32[]{:S(2)}) collective-permute-start(f32[32,128]{1,0:T(8,128)S(1)} %slice_add_fusion.2.refs_0_), channel_id=1, source_target_pairs={{0,24},{4,28},{8,16},{12,20},{16,8},{20,12},{24,0},{28,4},{1,25},{... | collective-permute-start | bytes 49160 | tf_op jit(solution)/shard_map/ppermute | solution.py:499
  14.0 4.6 %collective-permute-start.2 = (f32[32,128]{1,0:T(8,128)S(1)}, f32[32,128]{1,0:T(8,128)S(1)}, u32[]{:S(2)}, u32[]{:S(2)}) collective-permute-start(f32[32,128]{1,0:T(8,128)S(1)} %slice_add_fusion.2.refs_0_), channel_id=1, source_target_pairs={{0,16},{4,20},{8,24},{12,28},{16,0},{20,4},{24,8},{28,12},{1,17},{... | collective-permute-start | bytes 49160 | tf_op jit(solution)/shard_map/ppermute | solution.py:499
  14.0 4.6 %collective-permute-start.1 = (f32[32,128]{1,0:T(8,128)S(1)}, f32[32,128]{1,0:T(8,128)S(1)}, u32[]{:S(2)}, u32[]{:S(2)}) collective-permute-start(f32[32,128]{1,0:T(8,128)S(1)} %slice_add_fusion.2.refs_0_), channel_id=1, source_target_pairs={{0,8},{4,12},{8,0},{12,4},{16,24},{20,28},{24,16},{28,20},{1,9},{5... | collective-permute-start | bytes 49160 | tf_op jit(solution)/shard_map/ppermute | solution.py:499
  19.7 1.4 %collective-permute-start.5 = (f32[136,256]{1,0:T(8,128)S(1)}, f32[136,256]{1,0:T(8,128)S(1)}, u32[]{:S(2)}, u32[]{:S(2)}) collective-permute-start(f32[136,256]{1,0:T(8,128)S(1)} %shard_map.131), channel_id=1, source_target_pairs={{0,1},{1,0},{2,3},{3,2},{4,5},{5,4},{6,7},{7,6},{8,9},{9,8},{10,11... | collective-permute-start | bytes 417800 | tf_op jit(solution)/shard_map/ppermute | solution.py:506
  21.1 4.3 %collective-permute-start.6 = (f32[64,256]{1,0:T(8,128)S(1)}, f32[64,256]{1,0:T(8,128)S(1)}, u32[]{:S(2)}, u32[]{:S(2)}) collective-permute-start(f32[64,256]{1,0:T(8,128)S(1)} %slice_add_fusion.1.refs_0_), channel_id=1, source_target_pairs={{0,2},{1,3},{2,0},{3,1},{4,6},{5,7},{6,4},{7,5},{8,10},{9,11},{10,... | collective-permute-start | bytes 196616 | tf_op jit(solution)/shard_map/ppermute | solution.py:499
  27.0 4.2 %collective-permute-start.7 = (f32[104,128]{1,0:T(8,128)S(1)}, f32[104,128]{1,0:T(8,128)S(1)}, u32[]{:S(2)}, u32[]{:S(2)}) collective-permute-start(f32[104,128]{1,0:T(8,128)S(1)} %get-tuple-element.43.sent), channel_id=1, source_target_pairs={{0,4},{4,0},{8,12},{12,8},{16,20},{20,16},{24,28},{28,24},{1,5},{5... | collective-permute-start | bytes 159752 | tf_op jit(solution)/shard_map/ppermute | solution.py:533
  28.6 0.7 %collective-permute-start.8 = (f32[64,128]{1,0:T(8,128)S(1)}, f32[64,128]{1,0:T(8,128)S(1)}, u32[]{:S(2)}, u32[]{:S(2)}) collective-permute-start(f32[64,128]{1,0:T(8,128)S(1)} %get-tuple-element.44.edge), channel_id=1, source_target_pairs={{5,9},{7,11},{9,5},{11,7},{13,17},{15,19},{17,13},{19,15},{21,25},... | collective-permute-start | bytes 98312 | tf_op jit(solution)/shard_map/ppermute | solution.py:543
  31.3 5.6 %collective-permute-start.11 = (f32[40,128]{1,0:T(8,128)S(1)}, f32[40,128]{1,0:T(8,128)S(1)}, u32[]{:S(2)}, u32[]{:S(2)}) collective-permute-start(f32[40,128]{1,0:T(8,128)S(1)} %shard_map.134.refs_0_), channel_id=1, source_target_pairs={{0,24},{4,28},{8,16},{12,20},{16,8},{20,12},{24,0},{28,4},{1,25},{... | collective-permute-start | bytes 61448 | tf_op jit(solution)/shard_map/ppermute | solution.py:499
  32.9 4.7 %collective-permute-start.10 = (f32[40,128]{1,0:T(8,128)S(1)}, f32[40,128]{1,0:T(8,128)S(1)}, u32[]{:S(2)}, u32[]{:S(2)}) collective-permute-start(f32[40,128]{1,0:T(8,128)S(1)} %shard_map.134.refs_0_), channel_id=1, source_target_pairs={{0,16},{4,20},{8,24},{12,28},{16,0},{20,4},{24,8},{28,12},{1,17},{... | collective-permute-start | bytes 61448 | tf_op jit(solution)/shard_map/ppermute | solution.py:499
  33.5 4.7 %collective-permute-start.9 = (f32[40,128]{1,0:T(8,128)S(1)}, f32[40,128]{1,0:T(8,128)S(1)}, u32[]{:S(2)}, u32[]{:S(2)}) collective-permute-start(f32[40,128]{1,0:T(8,128)S(1)} %shard_map.134.refs_0_), channel_id=1, source_target_pairs={{0,8},{4,12},{8,0},{12,4},{16,24},{20,28},{24,16},{28,20},{1,9},{5... | collective-permute-start | bytes 61448 | tf_op jit(solution)/shard_map/ppermute | solution.py:499
  39.4 1.4 %collective-permute-start.12 = (f32[104,256]{1,0:T(8,128)S(1)}, f32[104,256]{1,0:T(8,128)S(1)}, u32[]{:S(2)}, u32[]{:S(2)}) collective-permute-start(f32[104,256]{1,0:T(8,128)S(1)} %get-tuple-element.45), channel_id=1, source_target_pairs={{0,1},{1,0},{2,3},{3,2},{4,5},{5,4},{6,7},{7,6},{8,9},{9,8},{10,11... | collective-permute-start | bytes 319496 | tf_op jit(solution)/shard_map/ppermute | solution.py:506
  40.7 4.4 %collective-permute-start.13 = (f32[72,256]{1,0:T(8,128)S(1)}, f32[72,256]{1,0:T(8,128)S(1)}, u32[]{:S(2)}, u32[]{:S(2)}) collective-permute-start(f32[72,256]{1,0:T(8,128)S(1)} %slice_add_fusion.refs_0_), channel_id=1, source_target_pairs={{0,2},{1,3},{2,0},{3,1},{4,6},{5,7},{6,4},{7,5},{8,10},{9,11},{10,... | collective-permute-start | bytes 221192 | tf_op jit(solution)/shard_map/ppermute | solution.py:499
  47.0 4.2 %collective-permute-start.14 = (f32[104,128]{1,0:T(8,128)S(1)}, f32[104,128]{1,0:T(8,128)S(1)}, u32[]{:S(2)}, u32[]{:S(2)}) collective-permute-start(f32[104,128]{1,0:T(8,128)S(1)} %get-tuple-element.54.sent), channel_id=1, source_target_pairs={{0,4},{4,0},{8,12},{12,8},{16,20},{20,16},{24,28},{28,24},{1,5},{5... | collective-permute-start | bytes 159752 | tf_op jit(solution)/shard_map/ppermute | solution.py:533
  48.1 0.7 %collective-permute-start.15 = (f32[64,128]{1,0:T(8,128)S(1)}, f32[64,128]{1,0:T(8,128)S(1)}, u32[]{:S(2)}, u32[]{:S(2)}) collective-permute-start(f32[64,128]{1,0:T(8,128)S(1)} %get-tuple-element.55.edge), channel_id=1, source_target_pairs={{5,9},{7,11},{9,5},{11,7},{13,17},{15,19},{17,13},{19,15},{21,25},... | collective-permute-start | bytes 98312 | tf_op jit(solution)/shard_map/ppermute | solution.py:543
  51.3 5.6 %collective-permute-start.18 = (f32[40,128]{1,0:T(8,128)S(1)}, f32[40,128]{1,0:T(8,128)S(1)}, u32[]{:S(2)}, u32[]{:S(2)}) collective-permute-start(f32[40,128]{1,0:T(8,128)S(1)} %shard_map.138.refs_0_), channel_id=1, source_target_pairs={{0,24},{4,28},{8,16},{12,20},{16,8},{20,12},{24,0},{28,4},{1,25},{... | collective-permute-start | bytes 61448 | tf_op jit(solution)/shard_map/ppermute | solution.py:499
  53.5 4.8 %collective-permute-start.17 = (f32[40,128]{1,0:T(8,128)S(1)}, f32[40,128]{1,0:T(8,128)S(1)}, u32[]{:S(2)}, u32[]{:S(2)}) collective-permute-start(f32[40,128]{1,0:T(8,128)S(1)} %shard_map.138.refs_0_), channel_id=1, source_target_pairs={{0,16},{4,20},{8,24},{12,28},{16,0},{20,4},{24,8},{28,12},{1,17},{... | collective-permute-start | bytes 61448 | tf_op jit(solution)/shard_map/ppermute | solution.py:499
  54.2 4.2 %collective-permute-start.16 = (f32[40,128]{1,0:T(8,128)S(1)}, f32[40,128]{1,0:T(8,128)S(1)}, u32[]{:S(2)}, u32[]{:S(2)}) collective-permute-start(f32[40,128]{1,0:T(8,128)S(1)} %shard_map.138.refs_0_), channel_id=1, source_target_pairs={{0,8},{4,12},{8,0},{12,4},{16,24},{20,28},{24,16},{28,20},{1,9},{5... | collective-permute-start | bytes 61448 | tf_op jit(solution)/shard_map/ppermute | solution.py:499
  58.5 4.9 %collective-permute-start.21 = (f32[72,128]{1,0:T(8,128)S(1)}, f32[72,128]{1,0:T(8,128)S(1)}, u32[]{:S(2)}, u32[]{:S(2)}) collective-permute-start(f32[72,128]{1,0:T(8,128)S(1)} %get-tuple-element.57), channel_id=1, source_target_pairs={{0,3},{1,2},{2,1},{3,0},{4,7},{5,6},{6,5},{7,4},{8,11},{9,10},{10,... | collective-permute-start | bytes 110600 | tf_op jit(solution)/shard_map/ppermute | solution.py:518
  59.8 3.6 %collective-permute-start.20 = (f32[8,128]{1,0:T(8,128)S(1)}, f32[8,128]{1,0:T(8,128)S(1)}, u32[]{:S(2)}, u32[]{:S(2)}) collective-permute-start(f32[8,128]{1,0:T(8,128)S(1)} %get-tuple-element.56.refs_0_), channel_id=1, source_target_pairs={{0,2},{1,3},{2,0},{3,1},{4,6},{5,7},{6,4},{7,5},{8,10},{9,11},{10,... | collective-permute-start | bytes 12296 | tf_op jit(solution)/shard_map/ppermute | solution.py:518
  60.3 3.1 %collective-permute-start.19 = (f32[8,128]{1,0:T(8,128)S(1)}, f32[8,128]{1,0:T(8,128)S(1)}, u32[]{:S(2)}, u32[]{:S(2)}) collective-permute-start(f32[8,128]{1,0:T(8,128)S(1)} %get-tuple-element.56.refs_0_), channel_id=1, source_target_pairs={{0,1},{1,0},{2,3},{3,2},{4,5},{5,4},{6,7},{7,6},{8,9},{9,8},{10,11... | collective-permute-start | bytes 12296 | tf_op jit(solution)/shard_map/ppermute | solution.py:518

commit v7 on v6

--- a/solution.py
+++ b/solution.py
@@ -11,7 +11,6 @@
 COLS = 128
 LANES = 128
 GROUP = 8
-CHUNK = 24
 SHRINK_SCALE = 0.4
 TINY = 1e-06
 VMEM = pltpu.VMEM
@@ -251,6 +250,11 @@
     return out
 
 
+def load_starts(freqs):
+    groups = -(-freqs // GROUP)
+    return sorted({0, groups * 4 // 9 * GROUP, groups * 7 // 9 * GROUP})
+
+
 def first_forward_body(*refs):
     loaded, (sent, edge, threshold, linked), kept, sems = refs[:10], refs[10:14], refs[14:24], refs[24]
     kernel, kernel_here = loaded[0], kept[0]
@@ -269,8 +273,9 @@
 
     early = [load(loaded[i], kept[i]) for i in (1, 3)]
     large = []
-    for start in range(0, freqs, CHUNK):
-        at = (slice(None), pl.ds(start, min(CHUNK, freqs - start)))
+    starts = load_starts(freqs)
+    for start, stop in zip(starts, starts[1:] + [freqs]):
+        at = (slice(None), pl.ds(start, stop - start))
         large.append(load(kernel.at[at], kernel_here.at[at]))
         if start == 0:
             small = [load(loaded[i], kept[i]) for i in (7, 8, 9, 2, 4)]
@@ -304,8 +309,8 @@
         edge[start : start + head.shape[0], :] = two
 
     def arrived(group):
-        if group * GROUP % CHUNK == 0:
-            large[group * GROUP // CHUNK].wait()
+        if group * GROUP in starts:
+            large[starts.index(group * GROUP)].wait()
 
     rows = forward_rows(spectra, kernel_here, arrived)
     sent[:half, :] = packed_series(rows, weighted_t[...], kernel.shape[2])
@@ -507,9 +512,11 @@
 
 
 def sensor_parts(array, rows):
+    count = lax.axis_size("sensor")
     passed = sensor_hop(array)
     total = array[:rows] + passed[:rows]
-    return summing([total], "sensor", 2, stages_of(lax.axis_size("sensor") // 2, 2)), passed
+    parts = [total, lax.ppermute(total, "sensor", [(i, i ^ 3) for i in range(count)])]
+    return summing(parts, "sensor", 4, stages_of(count // 4, 2)), passed
 
 
 def last_sensor_parts(scalars, passing):
@@ -562,7 +569,7 @@
         [(half + 2 * times + 8, LANES), (2 * times + 8, LANES), (8, cells), (8, cells)]
         + [jax.ShapeDtypeStruct(a.shape, a.dtype) for a in loads[:7]],
         *[pltpu.with_memory_space_constraint(a, HBM) for a in loads],
-        scratch=[VMEM(a.shape, a.dtype) for a in loads[7:]] + [pltpu.SemaphoreType.DMA((9 + -(-freqs // CHUNK),))],
+        scratch=[VMEM(a.shape, a.dtype) for a in loads[7:]] + [pltpu.SemaphoreType.DMA((9 + len(load_starts(freqs)),))],
         inputs=HBM,
     )
     one = from_partner(sent)

time: 64.6 us -> 65.8 us (1.019)
  starting transfers between devices: 26.6 us -> 28.5 us
  waiting for transfers between devices: 26 us -> 25.3 us
    ppermute x11 -> x9, waiting for transfers between devices: 14.4 us -> 8.57 us  [summing(): lax.ppermute(total, axis, [(i, i ^ k * stride) for i in range(count)])]
    ppermute x0 -> x2, waiting for transfers between devices: none -> 5.23 us  [sensor_parts(): lax.ppermute(total, 'sensor', [(i, i ^ 3) for i in range(count)])]
    ppermute x11 -> x9, starting transfers between devices: 16.7 us -> 13.6 us  [summing(): lax.ppermute(total, axis, [(i, i ^ k * stride) for i in range(count)])]
    ppermute x0 -> x2, starting transfers between devices: none -> 2.83 us  [sensor_parts(): lax.ppermute(total, 'sensor', [(i, i ^ 3) for i in range(count)])]
    ppermute x2, starting transfers between devices: 0.25 us -> 1.3 us  [sensor_hop(): lax.ppermute(array, 'sensor', [(i, i ^ 1) for i in range(lax.axis_size('s...]
    ppermute x3, starting transfers between devices: 1.95 us -> 2.98 us  [last_sensor_parts(): lax.ppermute(array, 'sensor', [(i, i ^ k) for i in range(count)])]
where the time goes in v7:
time: 65.8 us; the launch traced here: 65.7 us
  starting transfers between devices  28.5 us (43%)
  waiting for transfers between devices  25.3 us (38%)
  Pallas kernels  11.1 us (17%)
  between operations  0.78 us (1%)
    ppermute x9, starting transfers between devices, summing(): lax.ppermute(total, axis, [(i, i ^ k * stride) for i in range(count)])  13.6 us
    pallas_call x11, Pallas kernels, call(): pl.pallas_call(body, out_shape=shapes, in_specs=[pl.BlockSpec(memory_spac...  11.1 us
    ppermute x9, waiting for transfers between devices, summing(): lax.ppermute(total, axis, [(i, i ^ k * stride) for i in range(count)])  8.57 us
    ppermute x3, waiting for transfers between devices, from_partner(): lax.ppermute(array, 'cell', [(i, i ^ 1) for i in range(lax.axis_size('cel...  6.13 us
    ppermute x3, starting transfers between devices, from_partner(): lax.ppermute(array, 'cell', [(i, i ^ 1) for i in range(lax.axis_size('cel...  5.84 us
    ppermute x2, waiting for transfers between devices, sensor_parts(): lax.ppermute(total, 'sensor', [(i, i ^ 3) for i in range(count)])  5.23 us
    ppermute x3, waiting for transfers between devices, last_sensor_parts(): lax.ppermute(array, 'sensor', [(i, i ^ k) for i in range(count)])  3.07 us
    ppermute x3, starting transfers between devices, last_sensor_parts(): lax.ppermute(array, 'sensor', [(i, i ^ k) for i in range(count)])  2.98 us
  transfers between devices with their start and end apart: 22, of which 15 were waited for; matrix products, arithmetic and copies ran while one was open for 0% of the time, Pallas kernels for 0%

profile of v7, /device:TPU:0, one launch (start us, length us, event | category | flops | bytes accessed | tf_op | source)
XLA Modules:
  0.0 65.7 jit_solution(14924861483189485177)
XLA Ops:
  0.6 3.9 %shard_map.130 = (f32[168,128]{1,0:T(8,128)S(1)}, f32[136,128]{1,0:T(8,128)S(1)}, f32[8,256]{1,0:T(8,128)S(1)}, f32[8,256]{1,0:T(8,128)S(1)}, bf16[2,65,64,256]{...) custom-call(bf16[2,65,64,256]{3,2,1,0:T(8,128)(2,1)} %refs_0_.1, ...), custom_call_target="tpu_custom_call" | custom-call | tf_op jit(solution)/shard_map/pallas_call | solution.py:200
  4.5 3.0 %collective-permute-start = (f32[168,128]{1,0:T(8,128)S(1)}, f32[168,128]{1,0:T(8,128)S(1)}, u32[]{:S(2)}, u32[]{:S(2)}) collective-permute-start(f32[168,128]{1,0:T(8,128)S(1)} %get-tuple-element.33), channel_id=1, source_target_pairs={{0,4},{4,0},{8,12},{12,8},{16,20},{20,16},{24,28},{28,24},{1,5},{5... | collective-permute-start | bytes 258056 | tf_op jit(solution)/shard_map/ppermute | solution.py:540
  8.2 1.9 %collective-permute-done.one.refs_10_ = f32[168,128]{1,0:T(8,128)S(1)} collective-permute-done((f32[168,128]{1,0:T(8,128)S(1)}, f32[168,128]{1,0:T(8,128)S(1)}, u32[]{:S(2)}, u32[]{:S(2)}) %collective-permute-start) | collective-permute-done | bytes 86048 | tf_op jit(solution)/shard_map/ppermute | solution.py:540
  10.1 4.0 %collective-permute-start.3 = (f32[32,128]{1,0:T(8,128)S(1)}, f32[32,128]{1,0:T(8,128)S(1)}, u32[]{:S(2)}, u32[]{:S(2)}) collective-permute-start(f32[32,128]{1,0:T(8,128)S(1)} %slice_add_fusion.2.refs_0_), channel_id=1, source_target_pairs={{0,24},{4,28},{8,16},{12,20},{16,8},{20,12},{24,0},{28,4},{1,25},{... | collective-permute-start | bytes 49160 | tf_op jit(solution)/shard_map/ppermute | solution.py:504
  15.8 2.9 %collective-permute-done.2.refs_2_ = f32[32,128]{1,0:T(8,128)S(1)} collective-permute-done((f32[32,128]{1,0:T(8,128)S(1)}, f32[32,128]{1,0:T(8,128)S(1)}, u32[]{:S(2)}, u32[]{:S(2)}) %collective-permute-start.2) | collective-permute-done | bytes 16416 | tf_op jit(solution)/shard_map/ppermute | solution.py:504
  19.9 1.3 %collective-permute-done.5.passed = f32[136,256]{1,0:T(8,128)S(1)} collective-permute-done((f32[136,256]{1,0:T(8,128)S(1)}, f32[136,256]{1,0:T(8,128)S(1)}, u32[]{:S(2)}, u32[]{:S(2)}) %collective-permute-start.5) | collective-permute-done | bytes 139296 | tf_op jit(solution)/shard_map/ppermute | solution.py:511
  21.3 1.3 %collective-permute-start.6 = (f32[64,256]{1,0:T(8,128)S(1)}, f32[64,256]{1,0:T(8,128)S(1)}, u32[]{:S(2)}, u32[]{:S(2)}) collective-permute-start(f32[64,256]{1,0:T(8,128)S(1)} %slice_add_fusion.1.refs_0_), channel_id=1, source_target_pairs={{0,3},{1,2},{2,1},{3,0},{4,7},{5,6},{6,5},{7,4},{8,11},{9,10},{10,... | collective-permute-start | bytes 196616 | tf_op jit(solution)/shard_map/ppermute | solution.py:518
  22.7 2.7 %collective-permute-done.6.refs_1_ = f32[64,256]{1,0:T(8,128)S(1)} collective-permute-done((f32[64,256]{1,0:T(8,128)S(1)}, f32[64,256]{1,0:T(8,128)S(1)}, u32[]{:S(2)}, u32[]{:S(2)}) %collective-permute-start.6) | collective-permute-done | bytes 65568 | tf_op jit(solution)/shard_map/ppermute | solution.py:518
  25.4 1.6 %shard_map.133 = (f32[64,256]{1,0:T(8,128)S(1)}, f32[64,256]{1,0:T(8,128)S(1)}, f32[104,128]{1,0:T(8,128)S(1)}, f32[64,128]{1,0:T(8,128)S(1)}) custom-call(f32[64,256]{1,0:T(8,128)S(1)} %slice_add_fusion.1.refs_0_, f32[64,256]{1,0:T(8,128)S(1)} %collective-permute-done.6.refs_1_, f32[64,256]{1,0:T(8,128)S(1)} %get-tuple-element.40.refs_2_, ...), custom_call_target="tpu_custom_call" | custom-call | tf_op jit(solution)/shard_map/pallas_call | solution.py:200
  26.9 1.6 %collective-permute-start.7 = (f32[104,128]{1,0:T(8,128)S(1)}, f32[104,128]{1,0:T(8,128)S(1)}, u32[]{:S(2)}, u32[]{:S(2)}) collective-permute-start(f32[104,128]{1,0:T(8,128)S(1)} %get-tuple-element.43.sent), channel_id=1, source_target_pairs={{0,4},{4,0},{8,12},{12,8},{16,20},{20,16},{24,28},{28,24},{1,5},{5... | collective-permute-start | bytes 159752 | tf_op jit(solution)/shard_map/ppermute | solution.py:540
  29.2 1.9 %collective-permute-done.7.came.grad_one = f32[104,128]{1,0:T(8,128)S(1)} collective-permute-done((f32[104,128]{1,0:T(8,128)S(1)}, f32[104,128]{1,0:T(8,128)S(1)}, u32[]{:S(2)}, u32[]{:S(2)}) %collective-permute-start.7) | collective-permute-done | bytes 53280 | tf_op jit(solution)/shard_map/ppermute | solution.py:540
  31.3 1.5 %collective-permute-start.11 = (f32[40,128]{1,0:T(8,128)S(1)}, f32[40,128]{1,0:T(8,128)S(1)}, u32[]{:S(2)}, u32[]{:S(2)}) collective-permute-start(f32[40,128]{1,0:T(8,128)S(1)} %shard_map.134.refs_0_), channel_id=1, source_target_pairs={{0,24},{4,28},{8,16},{12,20},{16,8},{20,12},{24,0},{28,4},{1,25},{... | collective-permute-start | bytes 61448 | tf_op jit(solution)/shard_map/ppermute | solution.py:504
  33.5 2.3 %collective-permute-start.9 = (f32[40,128]{1,0:T(8,128)S(1)}, f32[40,128]{1,0:T(8,128)S(1)}, u32[]{:S(2)}, u32[]{:S(2)}) collective-permute-start(f32[40,128]{1,0:T(8,128)S(1)} %shard_map.134.refs_0_), channel_id=1, source_target_pairs={{0,8},{4,12},{8,0},{12,4},{16,24},{20,28},{24,16},{28,20},{1,9},{5... | collective-permute-start | bytes 61448 | tf_op jit(solution)/shard_map/ppermute | solution.py:504
  38.9 1.2 %collective-permute-start.12 = (f32[104,256]{1,0:T(8,128)S(1)}, f32[104,256]{1,0:T(8,128)S(1)}, u32[]{:S(2)}, u32[]{:S(2)}) collective-permute-start(f32[104,256]{1,0:T(8,128)S(1)} %get-tuple-element.45), channel_id=1, source_target_pairs={{0,1},{1,0},{2,3},{3,2},{4,5},{5,4},{6,7},{7,6},{8,9},{9,8},{10,11... | collective-permute-start | bytes 319496 | tf_op jit(solution)/shard_map/ppermute | solution.py:511
  41.1 1.5 %collective-permute-start.13 = (f32[72,256]{1,0:T(8,128)S(1)}, f32[72,256]{1,0:T(8,128)S(1)}, u32[]{:S(2)}, u32[]{:S(2)}) collective-permute-start(f32[72,256]{1,0:T(8,128)S(1)} %slice_add_fusion.refs_0_), channel_id=1, source_target_pairs={{0,3},{1,2},{2,1},{3,0},{4,7},{5,6},{6,5},{7,4},{8,11},{9,10},{10,... | collective-permute-start | bytes 221192 | tf_op jit(solution)/shard_map/ppermute | solution.py:518
  42.7 2.5 %collective-permute-done.13.refs_1_ = f32[72,256]{1,0:T(8,128)S(1)} collective-permute-done((f32[72,256]{1,0:T(8,128)S(1)}, f32[72,256]{1,0:T(8,128)S(1)}, u32[]{:S(2)}, u32[]{:S(2)}) %collective-permute-start.13) | collective-permute-done | bytes 73760 | tf_op jit(solution)/shard_map/ppermute | solution.py:518
  45.3 1.8 %shard_map.137 = (f32[64,256]{1,0:T(8,128)S(1)}, f32[4,64,256]{2,1,0:T(8,128)S(1)}, f32[4,64,256]{2,1,0:T(8,128)S(1)}, f32[64,256]{1,0:T(8,128)S(1)}, f32[104,128]{1,0:T(8,128)S(1)}, /*index=5*/f32[64,128]{1,0:T(8,128)S(1)}) custom-call(f32[72,256]{1,0:T(8,128)S(1)} %slice_add_fusion.refs_0_, f32[72,256]{1,0:T(8,128)S(1)} %collective-permute-done.13.refs_1_, ...), custom_call_target="tpu_custom_call" | custom-call | tf_op jit(solution)/shard_map/pallas_call | solution.py:200
  47.1 1.2 %collective-permute-start.14 = (f32[104,128]{1,0:T(8,128)S(1)}, f32[104,128]{1,0:T(8,128)S(1)}, u32[]{:S(2)}, u32[]{:S(2)}) collective-permute-start(f32[104,128]{1,0:T(8,128)S(1)} %get-tuple-element.54.sent), channel_id=1, source_target_pairs={{0,4},{4,0},{8,12},{12,8},{16,20},{20,16},{24,28},{28,24},{1,5},{5... | collective-permute-start | bytes 159752 | tf_op jit(solution)/shard_map/ppermute | solution.py:540
  49.0 2.3 %collective-permute-done.14.came.refs_10_ = f32[104,128]{1,0:T(8,128)S(1)} collective-permute-done((f32[104,128]{1,0:T(8,128)S(1)}, f32[104,128]{1,0:T(8,128)S(1)}, u32[]{:S(2)}, u32[]{:S(2)}) %collective-permute-start.14) | collective-permute-done | bytes 53280 | tf_op jit(solution)/shard_map/ppermute | solution.py:540
  51.4 2.4 %collective-permute-start.18 = (f32[40,128]{1,0:T(8,128)S(1)}, f32[40,128]{1,0:T(8,128)S(1)}, u32[]{:S(2)}, u32[]{:S(2)}) collective-permute-start(f32[40,128]{1,0:T(8,128)S(1)} %shard_map.138.refs_0_), channel_id=1, source_target_pairs={{0,24},{4,28},{8,16},{12,20},{16,8},{20,12},{24,0},{28,4},{1,25},{... | collective-permute-start | bytes 61448 | tf_op jit(solution)/shard_map/ppermute | solution.py:504
  54.1 1.8 %collective-permute-start.16 = (f32[40,128]{1,0:T(8,128)S(1)}, f32[40,128]{1,0:T(8,128)S(1)}, u32[]{:S(2)}, u32[]{:S(2)}) collective-permute-start(f32[40,128]{1,0:T(8,128)S(1)} %shard_map.138.refs_0_), channel_id=1, source_target_pairs={{0,8},{4,12},{8,0},{12,4},{16,24},{20,28},{24,16},{28,20},{1,9},{5... | collective-permute-start | bytes 61448 | tf_op jit(solution)/shard_map/ppermute | solution.py:504
  57.1 1.4 %collective-permute-done.17.refs_2_ = f32[40,128]{1,0:T(8,128)S(1)} collective-permute-done((f32[40,128]{1,0:T(8,128)S(1)}, f32[40,128]{1,0:T(8,128)S(1)}, u32[]{:S(2)}, u32[]{:S(2)}) %collective-permute-start.17) | collective-permute-done | bytes 20512 | tf_op jit(solution)/shard_map/ppermute | solution.py:504
  58.6 2.4 %collective-permute-start.21 = (f32[72,128]{1,0:T(8,128)S(1)}, f32[72,128]{1,0:T(8,128)S(1)}, u32[]{:S(2)}, u32[]{:S(2)}) collective-permute-start(f32[72,128]{1,0:T(8,128)S(1)} %get-tuple-element.57), channel_id=1, source_target_pairs={{0,3},{1,2},{2,1},{3,0},{4,7},{5,6},{6,5},{7,4},{8,11},{9,10},{10,... | collective-permute-start | bytes 110600 | tf_op jit(solution)/shard_map/ppermute | solution.py:525
  61.6 3.1 %collective-permute-done.20.refs_2_ = f32[8,128]{1,0:T(8,128)S(1)} collective-permute-done((f32[8,128]{1,0:T(8,128)S(1)}, f32[8,128]{1,0:T(8,128)S(1)}, u32[]{:S(2)}, u32[]{:S(2)}) %collective-permute-start.20) | collective-permute-done | bytes 4128 | tf_op jit(solution)/shard_map/ppermute | solution.py:525
  (36 shorter events, 13.2 us)
Async XLA Ops:
  0.6 18.1 %copy-start = (f32[64,64]{1,0:T(8,128)S(1)}, f32[64,64]{1,0:T(8,128)}, u32[]{:S(2)}) copy-start(f32[64,64]{1,0:T(8,128)} %refs_4_.2) | copy-start | bytes 49156
  4.5 5.6 %collective-permute-start = (f32[168,128]{1,0:T(8,128)S(1)}, f32[168,128]{1,0:T(8,128)S(1)}, u32[]{:S(2)}, u32[]{:S(2)}) collective-permute-start(f32[168,128]{1,0:T(8,128)S(1)} %get-tuple-element.33), channel_id=1, source_target_pairs={{0,4},{4,0},{8,12},{12,8},{16,20},{20,16},{24,28},{28,24},{1,5},{5... | collective-permute-start | bytes 258056 | tf_op jit(solution)/shard_map/ppermute | solution.py:540
  7.5 7.2 %collective-permute-start.4 = (f32[136,128]{1,0:T(8,128)S(1)}, f32[136,128]{1,0:T(8,128)S(1)}, u32[]{:S(2)}, u32[]{:S(2)}) collective-permute-start(f32[136,128]{1,0:T(8,128)S(1)} %get-tuple-element.34), channel_id=1, source_target_pairs={{5,9},{7,11},{9,5},{11,7},{13,17},{15,19},{17,13},{19,15},{21,25},... | collective-permute-start | bytes 208904 | tf_op jit(solution)/shard_map/ppermute | solution.py:550
  10.1 5.8 %collective-permute-start.3 = (f32[32,128]{1,0:T(8,128)S(1)}, f32[32,128]{1,0:T(8,128)S(1)}, u32[]{:S(2)}, u32[]{:S(2)}) collective-permute-start(f32[32,128]{1,0:T(8,128)S(1)} %slice_add_fusion.2.refs_0_), channel_id=1, source_target_pairs={{0,24},{4,28},{8,16},{12,20},{16,8},{20,12},{24,0},{28,4},{1,25},{... | collective-permute-start | bytes 49160 | tf_op jit(solution)/shard_map/ppermute | solution.py:504
  14.1 4.6 %collective-permute-start.2 = (f32[32,128]{1,0:T(8,128)S(1)}, f32[32,128]{1,0:T(8,128)S(1)}, u32[]{:S(2)}, u32[]{:S(2)}) collective-permute-start(f32[32,128]{1,0:T(8,128)S(1)} %slice_add_fusion.2.refs_0_), channel_id=1, source_target_pairs={{0,16},{4,20},{8,24},{12,28},{16,0},{20,4},{24,8},{28,12},{1,17},{... | collective-permute-start | bytes 49160 | tf_op jit(solution)/shard_map/ppermute | solution.py:504
  14.1 4.6 %collective-permute-start.1 = (f32[32,128]{1,0:T(8,128)S(1)}, f32[32,128]{1,0:T(8,128)S(1)}, u32[]{:S(2)}, u32[]{:S(2)}) collective-permute-start(f32[32,128]{1,0:T(8,128)S(1)} %slice_add_fusion.2.refs_0_), channel_id=1, source_target_pairs={{0,8},{4,12},{8,0},{12,4},{16,24},{20,28},{24,16},{28,20},{1,9},{5... | collective-permute-start | bytes 49160 | tf_op jit(solution)/shard_map/ppermute | solution.py:504
  19.8 1.4 %collective-permute-start.5 = (f32[136,256]{1,0:T(8,128)S(1)}, f32[136,256]{1,0:T(8,128)S(1)}, u32[]{:S(2)}, u32[]{:S(2)}) collective-permute-start(f32[136,256]{1,0:T(8,128)S(1)} %shard_map.131), channel_id=1, source_target_pairs={{0,1},{1,0},{2,3},{3,2},{4,5},{5,4},{6,7},{7,6},{8,9},{9,8},{10,11... | collective-permute-start | bytes 417800 | tf_op jit(solution)/shard_map/ppermute | solution.py:511
  21.3 4.1 %collective-permute-start.6 = (f32[64,256]{1,0:T(8,128)S(1)}, f32[64,256]{1,0:T(8,128)S(1)}, u32[]{:S(2)}, u32[]{:S(2)}) collective-permute-start(f32[64,256]{1,0:T(8,128)S(1)} %slice_add_fusion.1.refs_0_), channel_id=1, source_target_pairs={{0,3},{1,2},{2,1},{3,0},{4,7},{5,6},{6,5},{7,4},{8,11},{9,10},{10,... | collective-permute-start | bytes 196616 | tf_op jit(solution)/shard_map/ppermute | solution.py:518
  26.9 4.2 %collective-permute-start.7 = (f32[104,128]{1,0:T(8,128)S(1)}, f32[104,128]{1,0:T(8,128)S(1)}, u32[]{:S(2)}, u32[]{:S(2)}) collective-permute-start(f32[104,128]{1,0:T(8,128)S(1)} %get-tuple-element.43.sent), channel_id=1, source_target_pairs={{0,4},{4,0},{8,12},{12,8},{16,20},{20,16},{24,28},{28,24},{1,5},{5... | collective-permute-start | bytes 159752 | tf_op jit(solution)/shard_map/ppermute | solution.py:540
  28.5 0.7 %collective-permute-start.8 = (f32[64,128]{1,0:T(8,128)S(1)}, f32[64,128]{1,0:T(8,128)S(1)}, u32[]{:S(2)}, u32[]{:S(2)}) collective-permute-start(f32[64,128]{1,0:T(8,128)S(1)} %get-tuple-element.44.edge), channel_id=1, source_target_pairs={{5,9},{7,11},{9,5},{11,7},{13,17},{15,19},{17,13},{19,15},{21,25},... | collective-permute-start | bytes 98312 | tf_op jit(solution)/shard_map/ppermute | solution.py:550
  31.3 5.6 %collective-permute-start.11 = (f32[40,128]{1,0:T(8,128)S(1)}, f32[40,128]{1,0:T(8,128)S(1)}, u32[]{:S(2)}, u32[]{:S(2)}) collective-permute-start(f32[40,128]{1,0:T(8,128)S(1)} %shard_map.134.refs_0_), channel_id=1, source_target_pairs={{0,24},{4,28},{8,16},{12,20},{16,8},{20,12},{24,0},{28,4},{1,25},{... | collective-permute-start | bytes 61448 | tf_op jit(solution)/shard_map/ppermute | solution.py:504
  32.8 4.7 %collective-permute-start.10 = (f32[40,128]{1,0:T(8,128)S(1)}, f32[40,128]{1,0:T(8,128)S(1)}, u32[]{:S(2)}, u32[]{:S(2)}) collective-permute-start(f32[40,128]{1,0:T(8,128)S(1)} %shard_map.134.refs_0_), channel_id=1, source_target_pairs={{0,16},{4,20},{8,24},{12,28},{16,0},{20,4},{24,8},{28,12},{1,17},{... | collective-permute-start | bytes 61448 | tf_op jit(solution)/shard_map/ppermute | solution.py:504
  33.5 4.3 %collective-permute-start.9 = (f32[40,128]{1,0:T(8,128)S(1)}, f32[40,128]{1,0:T(8,128)S(1)}, u32[]{:S(2)}, u32[]{:S(2)}) collective-permute-start(f32[40,128]{1,0:T(8,128)S(1)} %shard_map.134.refs_0_), channel_id=1, source_target_pairs={{0,8},{4,12},{8,0},{12,4},{16,24},{20,28},{24,16},{28,20},{1,9},{5... | collective-permute-start | bytes 61448 | tf_op jit(solution)/shard_map/ppermute | solution.py:504
  38.9 2.2 %collective-permute-start.12 = (f32[104,256]{1,0:T(8,128)S(1)}, f32[104,256]{1,0:T(8,128)S(1)}, u32[]{:S(2)}, u32[]{:S(2)}) collective-permute-start(f32[104,256]{1,0:T(8,128)S(1)} %get-tuple-element.45), channel_id=1, source_target_pairs={{0,1},{1,0},{2,3},{3,2},{4,5},{5,4},{6,7},{7,6},{8,9},{9,8},{10,11... | collective-permute-start | bytes 319496 | tf_op jit(solution)/shard_map/ppermute | solution.py:511
  41.1 4.2 %collective-permute-start.13 = (f32[72,256]{1,0:T(8,128)S(1)}, f32[72,256]{1,0:T(8,128)S(1)}, u32[]{:S(2)}, u32[]{:S(2)}) collective-permute-start(f32[72,256]{1,0:T(8,128)S(1)} %slice_add_fusion.refs_0_), channel_id=1, source_target_pairs={{0,3},{1,2},{2,1},{3,0},{4,7},{5,6},{6,5},{7,4},{8,11},{9,10},{10,... | collective-permute-start | bytes 221192 | tf_op jit(solution)/shard_map/ppermute | solution.py:518
  47.1 4.2 %collective-permute-start.14 = (f32[104,128]{1,0:T(8,128)S(1)}, f32[104,128]{1,0:T(8,128)S(1)}, u32[]{:S(2)}, u32[]{:S(2)}) collective-permute-start(f32[104,128]{1,0:T(8,128)S(1)} %get-tuple-element.54.sent), channel_id=1, source_target_pairs={{0,4},{4,0},{8,12},{12,8},{16,20},{20,16},{24,28},{28,24},{1,5},{5... | collective-permute-start | bytes 159752 | tf_op jit(solution)/shard_map/ppermute | solution.py:540
  48.3 0.7 %collective-permute-start.15 = (f32[64,128]{1,0:T(8,128)S(1)}, f32[64,128]{1,0:T(8,128)S(1)}, u32[]{:S(2)}, u32[]{:S(2)}) collective-permute-start(f32[64,128]{1,0:T(8,128)S(1)} %get-tuple-element.55.edge), channel_id=1, source_target_pairs={{5,9},{7,11},{9,5},{11,7},{13,17},{15,19},{17,13},{19,15},{21,25},... | collective-permute-start | bytes 98312 | tf_op jit(solution)/shard_map/ppermute | solution.py:550
  51.4 5.6 %collective-permute-start.18 = (f32[40,128]{1,0:T(8,128)S(1)}, f32[40,128]{1,0:T(8,128)S(1)}, u32[]{:S(2)}, u32[]{:S(2)}) collective-permute-start(f32[40,128]{1,0:T(8,128)S(1)} %shard_map.138.refs_0_), channel_id=1, source_target_pairs={{0,24},{4,28},{8,16},{12,20},{16,8},{20,12},{24,0},{28,4},{1,25},{... | collective-permute-start | bytes 61448 | tf_op jit(solution)/shard_map/ppermute | solution.py:504
  53.8 4.7 %collective-permute-start.17 = (f32[40,128]{1,0:T(8,128)S(1)}, f32[40,128]{1,0:T(8,128)S(1)}, u32[]{:S(2)}, u32[]{:S(2)}) collective-permute-start(f32[40,128]{1,0:T(8,128)S(1)} %shard_map.138.refs_0_), channel_id=1, source_target_pairs={{0,16},{4,20},{8,24},{12,28},{16,0},{20,4},{24,8},{28,12},{1,17},{... | collective-permute-start | bytes 61448 | tf_op jit(solution)/shard_map/ppermute | solution.py:504
  54.1 4.4 %collective-permute-start.16 = (f32[40,128]{1,0:T(8,128)S(1)}, f32[40,128]{1,0:T(8,128)S(1)}, u32[]{:S(2)}, u32[]{:S(2)}) collective-permute-start(f32[40,128]{1,0:T(8,128)S(1)} %shard_map.138.refs_0_), channel_id=1, source_target_pairs={{0,8},{4,12},{8,0},{12,4},{16,24},{20,28},{24,16},{28,20},{1,9},{5... | collective-permute-start | bytes 61448 | tf_op jit(solution)/shard_map/ppermute | solution.py:504
  58.6 6.1 %collective-permute-start.21 = (f32[72,128]{1,0:T(8,128)S(1)}, f32[72,128]{1,0:T(8,128)S(1)}, u32[]{:S(2)}, u32[]{:S(2)}) collective-permute-start(f32[72,128]{1,0:T(8,128)S(1)} %get-tuple-element.57), channel_id=1, source_target_pairs={{0,3},{1,2},{2,1},{3,0},{4,7},{5,6},{6,5},{7,4},{8,11},{9,10},{10,... | collective-permute-start | bytes 110600 | tf_op jit(solution)/shard_map/ppermute | solution.py:525
  61.0 3.6 %collective-permute-start.20 = (f32[8,128]{1,0:T(8,128)S(1)}, f32[8,128]{1,0:T(8,128)S(1)}, u32[]{:S(2)}, u32[]{:S(2)}) collective-permute-start(f32[8,128]{1,0:T(8,128)S(1)} %get-tuple-element.56.refs_0_), channel_id=1, source_target_pairs={{0,2},{1,3},{2,0},{3,1},{4,6},{5,7},{6,4},{7,5},{8,10},{9,11},{10,... | collective-permute-start | bytes 12296 | tf_op jit(solution)/shard_map/ppermute | solution.py:525
  61.6 3.1 %collective-permute-start.19 = (f32[8,128]{1,0:T(8,128)S(1)}, f32[8,128]{1,0:T(8,128)S(1)}, u32[]{:S(2)}, u32[]{:S(2)}) collective-permute-start(f32[8,128]{1,0:T(8,128)S(1)} %get-tuple-element.56.refs_0_), channel_id=1, source_target_pairs={{0,1},{1,0},{2,3},{3,2},{4,5},{5,4},{6,7},{7,6},{8,9},{9,8},{10,11... | collective-permute-start | bytes 12296 | tf_op jit(solution)/shard_map/ppermute | solution.py:525

commit v8 on v6

--- a/solution.py
+++ b/solution.py
@@ -186,8 +186,12 @@
     return parts[0]
 
 
+def total_of(array):
+    return jnp.sum(array, axis=(0, 1), keepdims=True)
+
+
 def square_sum(array):
-    return jnp.sum(array * array)
+    return total_of(array * array)
 
 
 def block_of(scalar, rows=8):
@@ -243,11 +247,12 @@
     return jnp.concatenate([wide[:, :LANES], wide[: count - wide.shape[0], LANES:]])
 
 
-def rows_of(scalars):
+def rows_of(values):
     row = lax.broadcasted_iota(jnp.int32, (8, LANES), 0)
     out = jnp.zeros((8, LANES), jnp.float32)
-    for i, scalar in enumerate(scalars):
-        out = jnp.where(row == i, scalar, out)
+    for i, value in enumerate(values):
+        if value is not None:
+            out = jnp.where(row == i, jnp.broadcast_to(value, (8, LANES)), out)
     return out
 
 
@@ -335,7 +340,7 @@
             north = strip(linked[2:3], row) * (strip(field, row - 1) - here)
             squares.append(north * north)
     sent[:half, :] = forward(field, kernel, plain[...], weighted_t[...])
-    sent[half : half + 8, :] = rows_of([square_sum(field), 2.0 * jnp.sum(tree_sum(squares))])
+    sent[half : half + 8, :] = rows_of([square_sum(field), 2.0 * total_of(tree_sum(squares))])
     sent[half + 8 :, :] = one
     edge[...] = two
 
@@ -348,7 +353,7 @@
     beyond = to_other * (other[...] - edge[...])
     out[: top - 8, :] = sent[: top - 8, :] + came[: top - 8, :]
     boundary = 2.0 * square_sum(jnp.where(is_odd(), beyond, across))
-    out[top - 8 :, :] = sent[top - 8 : top, :] + came[top - 8 : top, :] + rows_of([0.0, 0.0, boundary])
+    out[top - 8 :, :] = sent[top - 8 : top, :] + came[top - 8 : top, :] + rows_of([None, None, boundary])
 
 
 def start_back_body(start_multiplier, one, two, passed, linked, back, two_out):
@@ -384,7 +389,7 @@
 
 
 def step_of(norms, scalars):
-    return norms[0, 0] / (scalars[0, 0] + (norms[1, 0] + scalars[1, 0]) + TINY)
+    return norms[0:1, :] / (scalars[0:1, :] + (norms[1:2, :] + scalars[1:2, :]) + TINY)
 
 
 def both_jumps_body(model, gradient, one, two, grad_one, grad_two, passed, linked, model_jumps, grad_jumps):
@@ -405,7 +410,7 @@
     times, cells = model.shape
     half = times // 2
     total = summed(refs[:count])
-    step = step_of(norms, total[times:])
+    step = step_of(norms, total[times:, :LANES])
     linked = linked_ref[...]
     field, gradient = model[...], gradient_in[...]
     rows = cells // COLS
@@ -432,8 +437,9 @@
     _, beside_above = advance(-new_jumps[2][0], above[times : 2 * times], above[2 * times : 2 * times + 1])
     _, beside_below = advance(-new_jumps[3][-1], below[times : 2 * times], below[2 * times : 2 * times + 1])
     back = gathered_jumps(penalties, beside_above, beside_below, linked)
-    model_out[...] = field - step * gradient
-    new_gradient = adjoint_in[...] - step * total[:times] + back
+    wide_step = jnp.concatenate([step] * rows, axis=1)
+    model_out[...] = field - wide_step * gradient
+    new_gradient = adjoint_in[...] - wide_step * total[:times] + back
     gradient_out[...] = new_gradient
     response_of(new_gradient, kernel, plain, weighted_t, linked, sent, edge)
 
@@ -463,7 +469,7 @@
         copy.start()
         copies.append(copy)
 
-    estimate_here[...] = model[...] - step * gradient
+    estimate_here[...] = model[...] - jnp.concatenate([step] * (gradient.shape[1] // COLS), axis=1) * gradient
     store(estimate_here, estimate_out)
     grad_jumps = jumps(gradient, *beside(grad_one[half + 8 :, :], grad_two), linked[...])
     for k in range(4):

time: 64.6 us -> 64.5 us (level)
  no operation moved by 1% of the time
where the time goes in v8:
time: 64.5 us; the launch traced here: 64.3 us
  starting transfers between devices  26.6 us (41%)
  waiting for transfers between devices  26 us (40%)
  Pallas kernels  10.8 us (17%)
  between operations  0.78 us (1%)
    ppermute x11, starting transfers between devices, summing(): lax.ppermute(total, axis, [(i, i ^ k * stride) for i in range(count)])  16.7 us
    ppermute x11, waiting for transfers between devices, summing(): lax.ppermute(total, axis, [(i, i ^ k * stride) for i in range(count)])  14.4 us
    pallas_call x11, Pallas kernels, call(): pl.pallas_call(body, out_shape=shapes, in_specs=[pl.BlockSpec(memory_spac...  10.8 us
    ppermute x3, waiting for transfers between devices, from_partner(): lax.ppermute(array, 'cell', [(i, i ^ 1) for i in range(lax.axis_size('cel...  6.17 us
    ppermute x3, starting transfers between devices, from_partner(): lax.ppermute(array, 'cell', [(i, i ^ 1) for i in range(lax.axis_size('cel...  5.79 us
    ppermute x3, waiting for transfers between devices, last_sensor_parts(): lax.ppermute(array, 'sensor', [(i, i ^ k) for i in range(count)])  2.93 us
    ppermute x2, waiting for transfers between devices, sensor_hop(): lax.ppermute(array, 'sensor', [(i, i ^ 1) for i in range(lax.axis_size('s...  2.54 us
    ppermute x3, starting transfers between devices, from_other(): return lax.ppermute(array, ('cell', 'sensor'), pairs)  1.96 us
  transfers between devices with their start and end apart: 22, of which 15 were waited for; matrix products, arithmetic and copies ran while one was open for 0% of the time, Pallas kernels for 0%

profile of v8, /device:TPU:0, one launch (start us, length us, event | category | flops | bytes accessed | tf_op | source)
XLA Modules:
  0.0 64.3 jit_solution(10704647004601788957)
XLA Ops:
  0.6 3.7 %shard_map.130 = (f32[168,128]{1,0:T(8,128)S(1)}, f32[136,128]{1,0:T(8,128)S(1)}, f32[8,256]{1,0:T(8,128)S(1)}, f32[8,256]{1,0:T(8,128)S(1)}, bf16[2,65,64,256]{...) custom-call(bf16[2,65,64,256]{3,2,1,0:T(8,128)(2,1)} %refs_0_.1, ...), custom_call_target="tpu_custom_call" | custom-call | tf_op jit(solution)/shard_map/pallas_call | solution.py:205
  4.3 3.0 %collective-permute-start = (f32[168,128]{1,0:T(8,128)S(1)}, f32[168,128]{1,0:T(8,128)S(1)}, u32[]{:S(2)}, u32[]{:S(2)}) collective-permute-start(f32[168,128]{1,0:T(8,128)S(1)} %get-tuple-element.33), channel_id=1, source_target_pairs={{0,4},{4,0},{8,12},{12,8},{16,20},{20,16},{24,28},{28,24},{1,5},{5... | collective-permute-start | bytes 258056 | tf_op jit(solution)/shard_map/ppermute | solution.py:539
  8.0 1.9 %collective-permute-done.one.refs_10_ = f32[168,128]{1,0:T(8,128)S(1)} collective-permute-done((f32[168,128]{1,0:T(8,128)S(1)}, f32[168,128]{1,0:T(8,128)S(1)}, u32[]{:S(2)}, u32[]{:S(2)}) %collective-permute-start) | collective-permute-done | bytes 86048 | tf_op jit(solution)/shard_map/ppermute | solution.py:539
  9.9 4.0 %collective-permute-start.3 = (f32[32,128]{1,0:T(8,128)S(1)}, f32[32,128]{1,0:T(8,128)S(1)}, u32[]{:S(2)}, u32[]{:S(2)}) collective-permute-start(f32[32,128]{1,0:T(8,128)S(1)} %slice_add_fusion.2.refs_0_), channel_id=1, source_target_pairs={{0,24},{4,28},{8,16},{12,20},{16,8},{20,12},{24,0},{28,4},{1,25},{... | collective-permute-start | bytes 49160 | tf_op jit(solution)/shard_map/ppermute | solution.py:505
  15.7 2.9 %collective-permute-done.2.refs_2_ = f32[32,128]{1,0:T(8,128)S(1)} collective-permute-done((f32[32,128]{1,0:T(8,128)S(1)}, f32[32,128]{1,0:T(8,128)S(1)}, u32[]{:S(2)}, u32[]{:S(2)}) %collective-permute-start.2) | collective-permute-done | bytes 16416 | tf_op jit(solution)/shard_map/ppermute | solution.py:505
  19.7 1.3 %collective-permute-done.5.passed = f32[136,256]{1,0:T(8,128)S(1)} collective-permute-done((f32[136,256]{1,0:T(8,128)S(1)}, f32[136,256]{1,0:T(8,128)S(1)}, u32[]{:S(2)}, u32[]{:S(2)}) %collective-permute-start.5) | collective-permute-done | bytes 139296 | tf_op jit(solution)/shard_map/ppermute | solution.py:512
  21.1 1.6 %collective-permute-start.6 = (f32[64,256]{1,0:T(8,128)S(1)}, f32[64,256]{1,0:T(8,128)S(1)}, u32[]{:S(2)}, u32[]{:S(2)}) collective-permute-start(f32[64,256]{1,0:T(8,128)S(1)} %slice_add_fusion.1.refs_0_), channel_id=1, source_target_pairs={{0,2},{1,3},{2,0},{3,1},{4,6},{5,7},{6,4},{7,5},{8,10},{9,11},{10,... | collective-permute-start | bytes 196616 | tf_op jit(solution)/shard_map/ppermute | solution.py:505
  22.8 2.7 %collective-permute-done.6.refs_1_ = f32[64,256]{1,0:T(8,128)S(1)} collective-permute-done((f32[64,256]{1,0:T(8,128)S(1)}, f32[64,256]{1,0:T(8,128)S(1)}, u32[]{:S(2)}, u32[]{:S(2)}) %collective-permute-start.6) | collective-permute-done | bytes 65568 | tf_op jit(solution)/shard_map/ppermute | solution.py:505
  25.4 1.6 %shard_map.133 = (f32[64,256]{1,0:T(8,128)S(1)}, f32[64,256]{1,0:T(8,128)S(1)}, f32[104,128]{1,0:T(8,128)S(1)}, f32[64,128]{1,0:T(8,128)S(1)}) custom-call(f32[64,256]{1,0:T(8,128)S(1)} %slice_add_fusion.1.refs_0_, f32[64,256]{1,0:T(8,128)S(1)} %collective-permute-done.6.refs_1_, f32[64,256]{1,0:T(8,128)S(1)} %get-tuple-element.40.refs_2_, ...), custom_call_target="tpu_custom_call" | custom-call | tf_op jit(solution)/shard_map/pallas_call | solution.py:205
  27.0 1.6 %collective-permute-start.7 = (f32[104,128]{1,0:T(8,128)S(1)}, f32[104,128]{1,0:T(8,128)S(1)}, u32[]{:S(2)}, u32[]{:S(2)}) collective-permute-start(f32[104,128]{1,0:T(8,128)S(1)} %get-tuple-element.43.sent), channel_id=1, source_target_pairs={{0,4},{4,0},{8,12},{12,8},{16,20},{20,16},{24,28},{28,24},{1,5},{5... | collective-permute-start | bytes 159752 | tf_op jit(solution)/shard_map/ppermute | solution.py:539
  29.2 1.9 %collective-permute-done.7.came.grad_one = f32[104,128]{1,0:T(8,128)S(1)} collective-permute-done((f32[104,128]{1,0:T(8,128)S(1)}, f32[104,128]{1,0:T(8,128)S(1)}, u32[]{:S(2)}, u32[]{:S(2)}) %collective-permute-start.7) | collective-permute-done | bytes 53280 | tf_op jit(solution)/shard_map/ppermute | solution.py:539
  31.3 1.5 %collective-permute-start.11 = (f32[40,128]{1,0:T(8,128)S(1)}, f32[40,128]{1,0:T(8,128)S(1)}, u32[]{:S(2)}, u32[]{:S(2)}) collective-permute-start(f32[40,128]{1,0:T(8,128)S(1)} %shard_map.134.refs_0_), channel_id=1, source_target_pairs={{0,24},{4,28},{8,16},{12,20},{16,8},{20,12},{24,0},{28,4},{1,25},{... | collective-permute-start | bytes 61448 | tf_op jit(solution)/shard_map/ppermute | solution.py:505
  33.5 2.3 %collective-permute-start.9 = (f32[40,128]{1,0:T(8,128)S(1)}, f32[40,128]{1,0:T(8,128)S(1)}, u32[]{:S(2)}, u32[]{:S(2)}) collective-permute-start(f32[40,128]{1,0:T(8,128)S(1)} %shard_map.134.refs_0_), channel_id=1, source_target_pairs={{0,8},{4,12},{8,0},{12,4},{16,24},{20,28},{24,16},{28,20},{1,9},{5... | collective-permute-start | bytes 61448 | tf_op jit(solution)/shard_map/ppermute | solution.py:505
  35.8 1.2 %collective-permute-done.11.refs_3_ = f32[40,128]{1,0:T(8,128)S(1)} collective-permute-done((f32[40,128]{1,0:T(8,128)S(1)}, f32[40,128]{1,0:T(8,128)S(1)}, u32[]{:S(2)}, u32[]{:S(2)}) %collective-permute-start.11) | collective-permute-done | bytes 20512 | tf_op jit(solution)/shard_map/ppermute | solution.py:505
  39.5 1.2 %collective-permute-done.12.passed = f32[104,256]{1,0:T(8,128)S(1)} collective-permute-done((f32[104,256]{1,0:T(8,128)S(1)}, f32[104,256]{1,0:T(8,128)S(1)}, u32[]{:S(2)}, u32[]{:S(2)}) %collective-permute-start.12) | collective-permute-done | bytes 106528 | tf_op jit(solution)/shard_map/ppermute | solution.py:512
  40.7 1.6 %collective-permute-start.13 = (f32[72,256]{1,0:T(8,128)S(1)}, f32[72,256]{1,0:T(8,128)S(1)}, u32[]{:S(2)}, u32[]{:S(2)}) collective-permute-start(f32[72,256]{1,0:T(8,128)S(1)} %slice_add_fusion.refs_0_), channel_id=1, source_target_pairs={{0,2},{1,3},{2,0},{3,1},{4,6},{5,7},{6,4},{7,5},{8,10},{9,11},{10,... | collective-permute-start | bytes 221192 | tf_op jit(solution)/shard_map/ppermute | solution.py:505
  42.4 2.7 %collective-permute-done.13.refs_1_ = f32[72,256]{1,0:T(8,128)S(1)} collective-permute-done((f32[72,256]{1,0:T(8,128)S(1)}, f32[72,256]{1,0:T(8,128)S(1)}, u32[]{:S(2)}, u32[]{:S(2)}) %collective-permute-start.13) | collective-permute-done | bytes 73760 | tf_op jit(solution)/shard_map/ppermute | solution.py:505
  45.2 1.7 %shard_map.137 = (f32[64,256]{1,0:T(8,128)S(1)}, f32[4,64,256]{2,1,0:T(8,128)S(1)}, f32[4,64,256]{2,1,0:T(8,128)S(1)}, f32[64,256]{1,0:T(8,128)S(1)}, f32[104,128]{1,0:T(8,128)S(1)}, /*index=5*/f32[64,128]{1,0:T(8,128)S(1)}) custom-call(f32[72,256]{1,0:T(8,128)S(1)} %slice_add_fusion.refs_0_, f32[72,256]{1,0:T(8,128)S(1)} %collective-permute-done.13.refs_1_, ...), custom_call_target="tpu_custom_call" | custom-call | tf_op jit(solution)/shard_map/pallas_call | solution.py:205
  48.7 2.4 %collective-permute-done.14.came.refs_10_ = f32[104,128]{1,0:T(8,128)S(1)} collective-permute-done((f32[104,128]{1,0:T(8,128)S(1)}, f32[104,128]{1,0:T(8,128)S(1)}, u32[]{:S(2)}, u32[]{:S(2)}) %collective-permute-start.14) | collective-permute-done | bytes 53280 | tf_op jit(solution)/shard_map/ppermute | solution.py:539
  51.2 2.2 %collective-permute-start.18 = (f32[40,128]{1,0:T(8,128)S(1)}, f32[40,128]{1,0:T(8,128)S(1)}, u32[]{:S(2)}, u32[]{:S(2)}) collective-permute-start(f32[40,128]{1,0:T(8,128)S(1)} %shard_map.138.refs_0_), channel_id=1, source_target_pairs={{0,24},{4,28},{8,16},{12,20},{16,8},{20,12},{24,0},{28,4},{1,25},{... | collective-permute-start | bytes 61448 | tf_op jit(solution)/shard_map/ppermute | solution.py:505
  54.1 1.5 %collective-permute-start.16 = (f32[40,128]{1,0:T(8,128)S(1)}, f32[40,128]{1,0:T(8,128)S(1)}, u32[]{:S(2)}, u32[]{:S(2)}) collective-permute-start(f32[40,128]{1,0:T(8,128)S(1)} %shard_map.138.refs_0_), channel_id=1, source_target_pairs={{0,8},{4,12},{8,0},{12,4},{16,24},{20,28},{24,16},{28,20},{1,9},{5... | collective-permute-start | bytes 61448 | tf_op jit(solution)/shard_map/ppermute | solution.py:505
  56.9 1.4 %collective-permute-done.17.refs_2_ = f32[40,128]{1,0:T(8,128)S(1)} collective-permute-done((f32[40,128]{1,0:T(8,128)S(1)}, f32[40,128]{1,0:T(8,128)S(1)}, u32[]{:S(2)}, u32[]{:S(2)}) %collective-permute-start.17) | collective-permute-done | bytes 20512 | tf_op jit(solution)/shard_map/ppermute | solution.py:505
  58.4 1.3 %collective-permute-start.21 = (f32[72,128]{1,0:T(8,128)S(1)}, f32[72,128]{1,0:T(8,128)S(1)}, u32[]{:S(2)}, u32[]{:S(2)}) collective-permute-start(f32[72,128]{1,0:T(8,128)S(1)} %get-tuple-element.57), channel_id=1, source_target_pairs={{0,3},{1,2},{2,1},{3,0},{4,7},{5,6},{6,5},{7,4},{8,11},{9,10},{10,... | collective-permute-start | bytes 110600 | tf_op jit(solution)/shard_map/ppermute | solution.py:524
  60.4 2.9 %collective-permute-done.20.refs_2_ = f32[8,128]{1,0:T(8,128)S(1)} collective-permute-done((f32[8,128]{1,0:T(8,128)S(1)}, f32[8,128]{1,0:T(8,128)S(1)}, u32[]{:S(2)}, u32[]{:S(2)}) %collective-permute-start.20) | collective-permute-done | bytes 4128 | tf_op jit(solution)/shard_map/ppermute | solution.py:524
  (36 shorter events, 13.4 us)
Async XLA Ops:
  0.6 18.0 %copy-start = (f32[64,64]{1,0:T(8,128)S(1)}, f32[64,64]{1,0:T(8,128)}, u32[]{:S(2)}) copy-start(f32[64,64]{1,0:T(8,128)} %refs_4_.2) | copy-start | bytes 49156
  4.3 5.6 %collective-permute-start = (f32[168,128]{1,0:T(8,128)S(1)}, f32[168,128]{1,0:T(8,128)S(1)}, u32[]{:S(2)}, u32[]{:S(2)}) collective-permute-start(f32[168,128]{1,0:T(8,128)S(1)} %get-tuple-element.33), channel_id=1, source_target_pairs={{0,4},{4,0},{8,12},{12,8},{16,20},{20,16},{24,28},{28,24},{1,5},{5... | collective-permute-start | bytes 258056 | tf_op jit(solution)/shard_map/ppermute | solution.py:539
  7.4 7.2 %collective-permute-start.4 = (f32[136,128]{1,0:T(8,128)S(1)}, f32[136,128]{1,0:T(8,128)S(1)}, u32[]{:S(2)}, u32[]{:S(2)}) collective-permute-start(f32[136,128]{1,0:T(8,128)S(1)} %get-tuple-element.34), channel_id=1, source_target_pairs={{5,9},{7,11},{9,5},{11,7},{13,17},{15,19},{17,13},{19,15},{21,25},... | collective-permute-start | bytes 208904 | tf_op jit(solution)/shard_map/ppermute | solution.py:549
  9.9 5.8 %collective-permute-start.3 = (f32[32,128]{1,0:T(8,128)S(1)}, f32[32,128]{1,0:T(8,128)S(1)}, u32[]{:S(2)}, u32[]{:S(2)}) collective-permute-start(f32[32,128]{1,0:T(8,128)S(1)} %slice_add_fusion.2.refs_0_), channel_id=1, source_target_pairs={{0,24},{4,28},{8,16},{12,20},{16,8},{20,12},{24,0},{28,4},{1,25},{... | collective-permute-start | bytes 49160 | tf_op jit(solution)/shard_map/ppermute | solution.py:505
  14.0 4.6 %collective-permute-start.2 = (f32[32,128]{1,0:T(8,128)S(1)}, f32[32,128]{1,0:T(8,128)S(1)}, u32[]{:S(2)}, u32[]{:S(2)}) collective-permute-start(f32[32,128]{1,0:T(8,128)S(1)} %slice_add_fusion.2.refs_0_), channel_id=1, source_target_pairs={{0,16},{4,20},{8,24},{12,28},{16,0},{20,4},{24,8},{28,12},{1,17},{... | collective-permute-start | bytes 49160 | tf_op jit(solution)/shard_map/ppermute | solution.py:505
  14.0 4.6 %collective-permute-start.1 = (f32[32,128]{1,0:T(8,128)S(1)}, f32[32,128]{1,0:T(8,128)S(1)}, u32[]{:S(2)}, u32[]{:S(2)}) collective-permute-start(f32[32,128]{1,0:T(8,128)S(1)} %slice_add_fusion.2.refs_0_), channel_id=1, source_target_pairs={{0,8},{4,12},{8,0},{12,4},{16,24},{20,28},{24,16},{28,20},{1,9},{5... | collective-permute-start | bytes 49160 | tf_op jit(solution)/shard_map/ppermute | solution.py:505
  19.7 1.4 %collective-permute-start.5 = (f32[136,256]{1,0:T(8,128)S(1)}, f32[136,256]{1,0:T(8,128)S(1)}, u32[]{:S(2)}, u32[]{:S(2)}) collective-permute-start(f32[136,256]{1,0:T(8,128)S(1)} %shard_map.131), channel_id=1, source_target_pairs={{0,1},{1,0},{2,3},{3,2},{4,5},{5,4},{6,7},{7,6},{8,9},{9,8},{10,11... | collective-permute-start | bytes 417800 | tf_op jit(solution)/shard_map/ppermute | solution.py:512
  21.1 4.3 %collective-permute-start.6 = (f32[64,256]{1,0:T(8,128)S(1)}, f32[64,256]{1,0:T(8,128)S(1)}, u32[]{:S(2)}, u32[]{:S(2)}) collective-permute-start(f32[64,256]{1,0:T(8,128)S(1)} %slice_add_fusion.1.refs_0_), channel_id=1, source_target_pairs={{0,2},{1,3},{2,0},{3,1},{4,6},{5,7},{6,4},{7,5},{8,10},{9,11},{10,... | collective-permute-start | bytes 196616 | tf_op jit(solution)/shard_map/ppermute | solution.py:505
  27.0 4.2 %collective-permute-start.7 = (f32[104,128]{1,0:T(8,128)S(1)}, f32[104,128]{1,0:T(8,128)S(1)}, u32[]{:S(2)}, u32[]{:S(2)}) collective-permute-start(f32[104,128]{1,0:T(8,128)S(1)} %get-tuple-element.43.sent), channel_id=1, source_target_pairs={{0,4},{4,0},{8,12},{12,8},{16,20},{20,16},{24,28},{28,24},{1,5},{5... | collective-permute-start | bytes 159752 | tf_op jit(solution)/shard_map/ppermute | solution.py:539
  28.6 0.7 %collective-permute-start.8 = (f32[64,128]{1,0:T(8,128)S(1)}, f32[64,128]{1,0:T(8,128)S(1)}, u32[]{:S(2)}, u32[]{:S(2)}) collective-permute-start(f32[64,128]{1,0:T(8,128)S(1)} %get-tuple-element.44.edge), channel_id=1, source_target_pairs={{5,9},{7,11},{9,5},{11,7},{13,17},{15,19},{17,13},{19,15},{21,25},... | collective-permute-start | bytes 98312 | tf_op jit(solution)/shard_map/ppermute | solution.py:549
  31.3 5.6 %collective-permute-start.11 = (f32[40,128]{1,0:T(8,128)S(1)}, f32[40,128]{1,0:T(8,128)S(1)}, u32[]{:S(2)}, u32[]{:S(2)}) collective-permute-start(f32[40,128]{1,0:T(8,128)S(1)} %shard_map.134.refs_0_), channel_id=1, source_target_pairs={{0,24},{4,28},{8,16},{12,20},{16,8},{20,12},{24,0},{28,4},{1,25},{... | collective-permute-start | bytes 61448 | tf_op jit(solution)/shard_map/ppermute | solution.py:505
  32.9 4.7 %collective-permute-start.10 = (f32[40,128]{1,0:T(8,128)S(1)}, f32[40,128]{1,0:T(8,128)S(1)}, u32[]{:S(2)}, u32[]{:S(2)}) collective-permute-start(f32[40,128]{1,0:T(8,128)S(1)} %shard_map.134.refs_0_), channel_id=1, source_target_pairs={{0,16},{4,20},{8,24},{12,28},{16,0},{20,4},{24,8},{28,12},{1,17},{... | collective-permute-start | bytes 61448 | tf_op jit(solution)/shard_map/ppermute | solution.py:505
  33.5 4.7 %collective-permute-start.9 = (f32[40,128]{1,0:T(8,128)S(1)}, f32[40,128]{1,0:T(8,128)S(1)}, u32[]{:S(2)}, u32[]{:S(2)}) collective-permute-start(f32[40,128]{1,0:T(8,128)S(1)} %shard_map.134.refs_0_), channel_id=1, source_target_pairs={{0,8},{4,12},{8,0},{12,4},{16,24},{20,28},{24,16},{28,20},{1,9},{5... | collective-permute-start | bytes 61448 | tf_op jit(solution)/shard_map/ppermute | solution.py:505
  39.4 1.4 %collective-permute-start.12 = (f32[104,256]{1,0:T(8,128)S(1)}, f32[104,256]{1,0:T(8,128)S(1)}, u32[]{:S(2)}, u32[]{:S(2)}) collective-permute-start(f32[104,256]{1,0:T(8,128)S(1)} %get-tuple-element.45), channel_id=1, source_target_pairs={{0,1},{1,0},{2,3},{3,2},{4,5},{5,4},{6,7},{7,6},{8,9},{9,8},{10,11... | collective-permute-start | bytes 319496 | tf_op jit(solution)/shard_map/ppermute | solution.py:512
  40.7 4.4 %collective-permute-start.13 = (f32[72,256]{1,0:T(8,128)S(1)}, f32[72,256]{1,0:T(8,128)S(1)}, u32[]{:S(2)}, u32[]{:S(2)}) collective-permute-start(f32[72,256]{1,0:T(8,128)S(1)} %slice_add_fusion.refs_0_), channel_id=1, source_target_pairs={{0,2},{1,3},{2,0},{3,1},{4,6},{5,7},{6,4},{7,5},{8,10},{9,11},{10,... | collective-permute-start | bytes 221192 | tf_op jit(solution)/shard_map/ppermute | solution.py:505
  46.9 4.2 %collective-permute-start.14 = (f32[104,128]{1,0:T(8,128)S(1)}, f32[104,128]{1,0:T(8,128)S(1)}, u32[]{:S(2)}, u32[]{:S(2)}) collective-permute-start(f32[104,128]{1,0:T(8,128)S(1)} %get-tuple-element.54.sent), channel_id=1, source_target_pairs={{0,4},{4,0},{8,12},{12,8},{16,20},{20,16},{24,28},{28,24},{1,5},{5... | collective-permute-start | bytes 159752 | tf_op jit(solution)/shard_map/ppermute | solution.py:539
  48.1 0.7 %collective-permute-start.15 = (f32[64,128]{1,0:T(8,128)S(1)}, f32[64,128]{1,0:T(8,128)S(1)}, u32[]{:S(2)}, u32[]{:S(2)}) collective-permute-start(f32[64,128]{1,0:T(8,128)S(1)} %get-tuple-element.55.edge), channel_id=1, source_target_pairs={{5,9},{7,11},{9,5},{11,7},{13,17},{15,19},{17,13},{19,15},{21,25},... | collective-permute-start | bytes 98312 | tf_op jit(solution)/shard_map/ppermute | solution.py:549
  51.2 5.6 %collective-permute-start.18 = (f32[40,128]{1,0:T(8,128)S(1)}, f32[40,128]{1,0:T(8,128)S(1)}, u32[]{:S(2)}, u32[]{:S(2)}) collective-permute-start(f32[40,128]{1,0:T(8,128)S(1)} %shard_map.138.refs_0_), channel_id=1, source_target_pairs={{0,24},{4,28},{8,16},{12,20},{16,8},{20,12},{24,0},{28,4},{1,25},{... | collective-permute-start | bytes 61448 | tf_op jit(solution)/shard_map/ppermute | solution.py:505
  53.5 4.8 %collective-permute-start.17 = (f32[40,128]{1,0:T(8,128)S(1)}, f32[40,128]{1,0:T(8,128)S(1)}, u32[]{:S(2)}, u32[]{:S(2)}) collective-permute-start(f32[40,128]{1,0:T(8,128)S(1)} %shard_map.138.refs_0_), channel_id=1, source_target_pairs={{0,16},{4,20},{8,24},{12,28},{16,0},{20,4},{24,8},{28,12},{1,17},{... | collective-permute-start | bytes 61448 | tf_op jit(solution)/shard_map/ppermute | solution.py:505
  54.1 4.2 %collective-permute-start.16 = (f32[40,128]{1,0:T(8,128)S(1)}, f32[40,128]{1,0:T(8,128)S(1)}, u32[]{:S(2)}, u32[]{:S(2)}) collective-permute-start(f32[40,128]{1,0:T(8,128)S(1)} %shard_map.138.refs_0_), channel_id=1, source_target_pairs={{0,8},{4,12},{8,0},{12,4},{16,24},{20,28},{24,16},{28,20},{1,9},{5... | collective-permute-start | bytes 61448 | tf_op jit(solution)/shard_map/ppermute | solution.py:505
  58.4 4.9 %collective-permute-start.21 = (f32[72,128]{1,0:T(8,128)S(1)}, f32[72,128]{1,0:T(8,128)S(1)}, u32[]{:S(2)}, u32[]{:S(2)}) collective-permute-start(f32[72,128]{1,0:T(8,128)S(1)} %get-tuple-element.57), channel_id=1, source_target_pairs={{0,3},{1,2},{2,1},{3,0},{4,7},{5,6},{6,5},{7,4},{8,11},{9,10},{10,... | collective-permute-start | bytes 110600 | tf_op jit(solution)/shard_map/ppermute | solution.py:524
  59.7 3.6 %collective-permute-start.20 = (f32[8,128]{1,0:T(8,128)S(1)}, f32[8,128]{1,0:T(8,128)S(1)}, u32[]{:S(2)}, u32[]{:S(2)}) collective-permute-start(f32[8,128]{1,0:T(8,128)S(1)} %get-tuple-element.56.refs_0_), channel_id=1, source_target_pairs={{0,2},{1,3},{2,0},{3,1},{4,6},{5,7},{6,4},{7,5},{8,10},{9,11},{10,... | collective-permute-start | bytes 12296 | tf_op jit(solution)/shard_map/ppermute | solution.py:524
  60.2 3.1 %collective-permute-start.19 = (f32[8,128]{1,0:T(8,128)S(1)}, f32[8,128]{1,0:T(8,128)S(1)}, u32[]{:S(2)}, u32[]{:S(2)}) collective-permute-start(f32[8,128]{1,0:T(8,128)S(1)} %get-tuple-element.56.refs_0_), channel_id=1, source_target_pairs={{0,1},{1,0},{2,3},{3,2},{4,5},{5,4},{6,7},{7,6},{8,9},{9,8},{10,11... | collective-permute-start | bytes 12296 | tf_op jit(solution)/shard_map/ppermute | solution.py:524

commit v9 on v8

--- a/solution.py
+++ b/solution.py
@@ -77,8 +77,25 @@
     return total + pltpu.roll(total, LANES // 2, 1)
 
 
-def forward(field, kernel_ref, plain, weighted_t):
-    return packed_series(forward_rows(table_dot(plain, field), kernel_ref), weighted_t, kernel_ref.shape[2])
+def forward(field, turned_ref, plain, weighted_t, sensors):
+    freqs = field.shape[0] + 1
+    spectra = table_dot(plain, field)
+    rows = []
+    for group in range(spectra.shape[0] // 16):
+        part = spectra[16 * group : 16 * group + 16]
+        width = min(GROUP, freqs - group * GROUP) * sensors
+        out = dot_nn(part.astype(jnp.bfloat16), turned_ref[0, group, :, :width])
+        out += dot_nn(turned(part), turned_ref[1, group, :, :width])
+        rows.append(fold_own(out, sensors))
+    return packed_series(jnp.concatenate(rows, axis=0), weighted_t, sensors)
+
+
+def fold_own(out, sensors):
+    width = out.shape[1]
+    out = jnp.where(own_block(width, sensors), out, 0.0)
+    if width < LANES:
+        out = jnp.concatenate([out, jnp.zeros((16, LANES - width), jnp.float32)], axis=1)
+    return fold(out)
 
 
 def forward_rows(spectra, kernel_ref, arrived=None):
@@ -90,11 +107,7 @@
             arrived(group)
         re_slab, im_slab = slab(kernel_ref, 0, group), slab(kernel_ref, 1, group)
         out = dot_nt(part.astype(jnp.bfloat16), re_slab) + dot_nt(turned(part), im_slab)
-        width = out.shape[1]
-        out = jnp.where(own_block(width, sensors), out, 0.0)
-        if width < LANES:
-            out = jnp.concatenate([out, jnp.zeros((16, LANES - width), jnp.float32)], axis=1)
-        rows.append(fold(out))
+        rows.append(fold_own(out, sensors))
     return jnp.concatenate(rows, axis=0)
 
 
@@ -199,7 +212,7 @@
 
 
 def call(body, out_shapes, *operands, scratch=(), inputs=VMEM, outputs=VMEM):
-    single = isinstance(out_shapes, tuple)
+    single = not isinstance(out_shapes, list)
     shapes = [out_shapes] if single else list(out_shapes)
     shapes = [s if isinstance(s, jax.ShapeDtypeStruct) else jax.ShapeDtypeStruct(s, jnp.float32) for s in shapes]
     out = pl.pallas_call(
@@ -318,8 +331,16 @@
         copy.wait()
 
 
+def turn_body(kernel, came, out):
+    freqs, sensors = kernel.shape[1:3]
+    for part in range(2):
+        for group in range(out.shape[1]):
+            width = min(GROUP, freqs - group * GROUP) * sensors
+            out[part, group, :, :width] = slab(kernel, part, group).T
+
+
 def first_adjoint_body(count, *refs):
-    observed, two, kernel, plain_t, weighted, out = refs[count:]
+    observed, two, kernel, plain_t, weighted, _, out = refs[count:]
     times = observed.shape[0]
     predicted = unpacked(summed(refs[:count]), kernel.shape[2])
     residual = predicted - jnp.concatenate([observed[...], observed[...]], axis=1)
@@ -327,7 +348,7 @@
     out[times:, :] = spread(two[...])
 
 
-def response_of(field, kernel, plain, weighted_t, linked, sent, edge):
+def response_of(field, turned_ref, plain, weighted_t, linked, sent, edge):
     half = field.shape[0] // 2
     rows = field.shape[1] // COLS
     one, two = edges(strip(field, 0), strip(field, rows - 1))
@@ -339,7 +360,8 @@
         if row > 0:
             north = strip(linked[2:3], row) * (strip(field, row - 1) - here)
             squares.append(north * north)
-    sent[:half, :] = forward(field, kernel, plain[...], weighted_t[...])
+    sensors = turned_ref.shape[3] // GROUP
+    sent[:half, :] = forward(field, turned_ref, plain[...], weighted_t[...], sensors)
     sent[half : half + 8, :] = rows_of([square_sum(field), 2.0 * total_of(tree_sum(squares))])
     sent[half + 8 :, :] = one
     edge[...] = two
@@ -574,16 +596,19 @@
     one = from_partner(sent)
     two = from_other(edge)
     parts = cell_parts(sent[:half] + one[:half])
+    across = call(
+        turn_body, jax.ShapeDtypeStruct((2, plain.shape[0] // 16, cells, GROUP * sensors), kernel.dtype), kernel, one
+    )
     message, side, shared = (half + 8 + times, LANES), (times, LANES), (2 * times + 8, LANES)
     back = call(
         functools.partial(first_adjoint_body, len(parts)), (2 * times + 8, cells),
-        *parts, observed, two, kernel, plain_t, weighted,
+        *parts, observed, two, kernel, plain_t, weighted, across,
     )
     parts, passed = sensor_parts(back, times)
     back, two = call(start_back_body, [field, shared], start_multiplier, one, two, passed, linked)
     adjoint_one, gradient, sent, edge = call(
         functools.partial(first_gradient_body, len(parts)), [field, field, message, side],
-        *parts, back, linked, kernel, plain, weighted_t,
+        *parts, back, linked, across, plain, weighted_t,
     )
     grad_one, grad_two = from_partner(sent), from_other(edge)
     parts = cell_parts(call(merge_body, (half + 8, LANES), sent, grad_one, edge, grad_two, linked))
@@ -598,7 +623,7 @@
     model, model_jumps, multiplier, gradient, sent, edge = call(
         functools.partial(second_gradient_body, len(parts)), [field, wide, wide, field, message, side],
         *parts, norms, adjoint_one, gradient, start_model, model_jumps, grad_jumps, start_multiplier, threshold,
-        one, two, linked, kernel, plain, weighted_t,
+        one, two, linked, across, plain, weighted_t,
     )
     grad_one, grad_two = from_partner(sent), from_other(edge)
     parts = cell_parts(call(merge_body, (half + 8, LANES), sent, grad_one, edge, grad_two, linked))

time: 64.5 us -> 63.4 us (0.983)
  waiting for transfers between devices: 26 us -> 24.9 us
    ppermute x11, waiting for transfers between devices: 14.4 us -> 13.2 us  [summing(): lax.ppermute(total, axis, [(i, i ^ k * stride) for i in range(count)])]
    pallas_call x11 -> x12, Pallas kernels: 10.8 us -> 10.9 us  [call(): pl.pallas_call(body, out_shape=shapes, in_specs=[pl.BlockSpec(memory_spac...]
  transfers between devices with their start and end apart: 22 -> 22, of which waited for: 15 -> 14; matrix products, arithmetic and copies ran while one was open for 0% -> 0% of each run, Pallas kernels for 0% -> 2%
where the time goes in v9:
time: 63.4 us; the launch traced here: 63.3 us
  starting transfers between devices  26.6 us (42%)
  waiting for transfers between devices  24.9 us (39%)
  Pallas kernels  10.9 us (17%)
  between operations  0.8 us (1%)
    ppermute x11, starting transfers between devices, summing(): lax.ppermute(total, axis, [(i, i ^ k * stride) for i in range(count)])  16.7 us
    ppermute x11, waiting for transfers between devices, summing(): lax.ppermute(total, axis, [(i, i ^ k * stride) for i in range(count)])  13.2 us
    pallas_call x12, Pallas kernels, call(): pl.pallas_call(body, out_shape=shapes, in_specs=[pl.BlockSpec(memory_spac...  10.9 us
    ppermute x3, waiting for transfers between devices, from_partner(): lax.ppermute(array, 'cell', [(i, i ^ 1) for i in range(lax.axis_size('cel...  6.17 us
    ppermute x3, starting transfers between devices, from_partner(): lax.ppermute(array, 'cell', [(i, i ^ 1) for i in range(lax.axis_size('cel...  5.79 us
    ppermute x3, waiting for transfers between devices, last_sensor_parts(): lax.ppermute(array, 'sensor', [(i, i ^ k) for i in range(count)])  2.93 us
    ppermute x2, waiting for transfers between devices, sensor_hop(): lax.ppermute(array, 'sensor', [(i, i ^ 1) for i in range(lax.axis_size('s...  2.54 us
    ppermute x3, starting transfers between devices, from_other(): return lax.ppermute(array, ('cell', 'sensor'), pairs)  1.96 us
  transfers between devices with their start and end apart: 22, of which 14 were waited for; matrix products, arithmetic and copies ran while one was open for 0% of the time, Pallas kernels for 2%

profile of v9, /device:TPU:0, one launch (start us, length us, event | category | flops | bytes accessed | tf_op | source)
XLA Modules:
  0.0 63.3 jit_solution(16664621246668363665)
XLA Ops:
  0.6 3.7 %shard_map.130 = (f32[168,128]{1,0:T(8,128)S(1)}, f32[136,128]{1,0:T(8,128)S(1)}, f32[8,256]{1,0:T(8,128)S(1)}, f32[8,256]{1,0:T(8,128)S(1)}, bf16[2,65,64,256]{...) custom-call(bf16[2,65,64,256]{3,2,1,0:T(8,128)(2,1)} %refs_0_.1, ...), custom_call_target="tpu_custom_call" | custom-call | tf_op jit(solution)/shard_map/pallas_call | solution.py:218
  4.3 3.0 %collective-permute-start = (f32[168,128]{1,0:T(8,128)S(1)}, f32[168,128]{1,0:T(8,128)S(1)}, u32[]{:S(2)}, u32[]{:S(2)}) collective-permute-start(f32[168,128]{1,0:T(8,128)S(1)} %get-tuple-element.33), channel_id=1, source_target_pairs={{0,4},{4,0},{8,12},{12,8},{16,20},{20,16},{24,28},{28,24},{1,5},{5... | collective-permute-start | bytes 258056 | tf_op jit(solution)/shard_map/ppermute | solution.py:561
  8.0 1.9 %collective-permute-done.came.one.refs_10_ = f32[168,128]{1,0:T(8,128)S(1)} collective-permute-done((f32[168,128]{1,0:T(8,128)S(1)}, f32[168,128]{1,0:T(8,128)S(1)}, u32[]{:S(2)}, u32[]{:S(2)}) %collective-permute-start) | collective-permute-done | bytes 86048 | tf_op jit(solution)/shard_map/ppermute | solution.py:561
  9.9 4.0 %collective-permute-start.3 = (f32[32,128]{1,0:T(8,128)S(1)}, f32[32,128]{1,0:T(8,128)S(1)}, u32[]{:S(2)}, u32[]{:S(2)}) collective-permute-start(f32[32,128]{1,0:T(8,128)S(1)} %slice_add_fusion.2.refs_0_), channel_id=1, source_target_pairs={{0,24},{4,28},{8,16},{12,20},{16,8},{20,12},{24,0},{28,4},{1,25},{... | collective-permute-start | bytes 49160 | tf_op jit(solution)/shard_map/ppermute | solution.py:527
  15.8 2.8 %collective-permute-done.2.refs_2_ = f32[32,128]{1,0:T(8,128)S(1)} collective-permute-done((f32[32,128]{1,0:T(8,128)S(1)}, f32[32,128]{1,0:T(8,128)S(1)}, u32[]{:S(2)}, u32[]{:S(2)}) %collective-permute-start.2) | collective-permute-done | bytes 16416 | tf_op jit(solution)/shard_map/ppermute | solution.py:527
  19.7 1.3 %collective-permute-done.5.passed = f32[136,256]{1,0:T(8,128)S(1)} collective-permute-done((f32[136,256]{1,0:T(8,128)S(1)}, f32[136,256]{1,0:T(8,128)S(1)}, u32[]{:S(2)}, u32[]{:S(2)}) %collective-permute-start.5) | collective-permute-done | bytes 139296 | tf_op jit(solution)/shard_map/ppermute | solution.py:534
  21.1 1.6 %collective-permute-start.6 = (f32[64,256]{1,0:T(8,128)S(1)}, f32[64,256]{1,0:T(8,128)S(1)}, u32[]{:S(2)}, u32[]{:S(2)}) collective-permute-start(f32[64,256]{1,0:T(8,128)S(1)} %slice_add_fusion.1.refs_0_), channel_id=1, source_target_pairs={{0,2},{1,3},{2,0},{3,1},{4,6},{5,7},{6,4},{7,5},{8,10},{9,11},{10,... | collective-permute-start | bytes 196616 | tf_op jit(solution)/shard_map/ppermute | solution.py:527
  22.8 2.7 %collective-permute-done.6.refs_1_ = f32[64,256]{1,0:T(8,128)S(1)} collective-permute-done((f32[64,256]{1,0:T(8,128)S(1)}, f32[64,256]{1,0:T(8,128)S(1)}, u32[]{:S(2)}, u32[]{:S(2)}) %collective-permute-start.6) | collective-permute-done | bytes 65568 | tf_op jit(solution)/shard_map/ppermute | solution.py:527
  26.5 1.6 %collective-permute-start.7 = (f32[104,128]{1,0:T(8,128)S(1)}, f32[104,128]{1,0:T(8,128)S(1)}, u32[]{:S(2)}, u32[]{:S(2)}) collective-permute-start(f32[104,128]{1,0:T(8,128)S(1)} %get-tuple-element.43.sent), channel_id=1, source_target_pairs={{0,4},{4,0},{8,12},{12,8},{16,20},{20,16},{24,28},{28,24},{1,5},{5... | collective-permute-start | bytes 159752 | tf_op jit(solution)/shard_map/ppermute | solution.py:561
  28.7 1.9 %collective-permute-done.7.came.grad_one = f32[104,128]{1,0:T(8,128)S(1)} collective-permute-done((f32[104,128]{1,0:T(8,128)S(1)}, f32[104,128]{1,0:T(8,128)S(1)}, u32[]{:S(2)}, u32[]{:S(2)}) %collective-permute-start.7) | collective-permute-done | bytes 53280 | tf_op jit(solution)/shard_map/ppermute | solution.py:561
  30.8 1.5 %collective-permute-start.11 = (f32[40,128]{1,0:T(8,128)S(1)}, f32[40,128]{1,0:T(8,128)S(1)}, u32[]{:S(2)}, u32[]{:S(2)}) collective-permute-start(f32[40,128]{1,0:T(8,128)S(1)} %shard_map.135.refs_0_), channel_id=1, source_target_pairs={{0,24},{4,28},{8,16},{12,20},{16,8},{20,12},{24,0},{28,4},{1,25},{... | collective-permute-start | bytes 61448 | tf_op jit(solution)/shard_map/ppermute | solution.py:527
  33.0 2.3 %collective-permute-start.9 = (f32[40,128]{1,0:T(8,128)S(1)}, f32[40,128]{1,0:T(8,128)S(1)}, u32[]{:S(2)}, u32[]{:S(2)}) collective-permute-start(f32[40,128]{1,0:T(8,128)S(1)} %shard_map.135.refs_0_), channel_id=1, source_target_pairs={{0,8},{4,12},{8,0},{12,4},{16,24},{20,28},{24,16},{28,20},{1,9},{5... | collective-permute-start | bytes 61448 | tf_op jit(solution)/shard_map/ppermute | solution.py:527
  35.3 1.2 %collective-permute-done.11.refs_3_ = f32[40,128]{1,0:T(8,128)S(1)} collective-permute-done((f32[40,128]{1,0:T(8,128)S(1)}, f32[40,128]{1,0:T(8,128)S(1)}, u32[]{:S(2)}, u32[]{:S(2)}) %collective-permute-start.11) | collective-permute-done | bytes 20512 | tf_op jit(solution)/shard_map/ppermute | solution.py:527
  39.0 1.2 %collective-permute-done.12.passed = f32[104,256]{1,0:T(8,128)S(1)} collective-permute-done((f32[104,256]{1,0:T(8,128)S(1)}, f32[104,256]{1,0:T(8,128)S(1)}, u32[]{:S(2)}, u32[]{:S(2)}) %collective-permute-start.12) | collective-permute-done | bytes 106528 | tf_op jit(solution)/shard_map/ppermute | solution.py:534
  40.2 1.6 %collective-permute-start.13 = (f32[72,256]{1,0:T(8,128)S(1)}, f32[72,256]{1,0:T(8,128)S(1)}, u32[]{:S(2)}, u32[]{:S(2)}) collective-permute-start(f32[72,256]{1,0:T(8,128)S(1)} %slice_add_fusion.refs_0_), channel_id=1, source_target_pairs={{0,2},{1,3},{2,0},{3,1},{4,6},{5,7},{6,4},{7,5},{8,10},{9,11},{10,... | collective-permute-start | bytes 221192 | tf_op jit(solution)/shard_map/ppermute | solution.py:527
  41.9 2.7 %collective-permute-done.13.refs_1_ = f32[72,256]{1,0:T(8,128)S(1)} collective-permute-done((f32[72,256]{1,0:T(8,128)S(1)}, f32[72,256]{1,0:T(8,128)S(1)}, u32[]{:S(2)}, u32[]{:S(2)}) %collective-permute-start.13) | collective-permute-done | bytes 73760 | tf_op jit(solution)/shard_map/ppermute | solution.py:527
  44.6 1.2 %shard_map.138 = (f32[64,256]{1,0:T(8,128)S(1)}, f32[4,64,256]{2,1,0:T(8,128)S(1)}, f32[4,64,256]{2,1,0:T(8,128)S(1)}, f32[64,256]{1,0:T(8,128)S(1)}, f32[104,128]{1,0:T(8,128)S(1)}, /*index=5*/f32[64,128]{1,0:T(8,128)S(1)}) custom-call(f32[72,256]{1,0:T(8,128)S(1)} %slice_add_fusion.refs_0_, f32[72,256]{1,0:T(8,128)S(1)} %collective-permute-done.13.refs_1_, ...), custom_call_target="tpu_custom_call" | custom-call | tf_op jit(solution)/shard_map/pallas_call | solution.py:218
  47.7 2.4 %collective-permute-done.14.came.refs_10_ = f32[104,128]{1,0:T(8,128)S(1)} collective-permute-done((f32[104,128]{1,0:T(8,128)S(1)}, f32[104,128]{1,0:T(8,128)S(1)}, u32[]{:S(2)}, u32[]{:S(2)}) %collective-permute-start.14) | collective-permute-done | bytes 53280 | tf_op jit(solution)/shard_map/ppermute | solution.py:561
  50.2 2.2 %collective-permute-start.18 = (f32[40,128]{1,0:T(8,128)S(1)}, f32[40,128]{1,0:T(8,128)S(1)}, u32[]{:S(2)}, u32[]{:S(2)}) collective-permute-start(f32[40,128]{1,0:T(8,128)S(1)} %shard_map.139.refs_0_), channel_id=1, source_target_pairs={{0,24},{4,28},{8,16},{12,20},{16,8},{20,12},{24,0},{28,4},{1,25},{... | collective-permute-start | bytes 61448 | tf_op jit(solution)/shard_map/ppermute | solution.py:527
  53.1 1.6 %collective-permute-start.16 = (f32[40,128]{1,0:T(8,128)S(1)}, f32[40,128]{1,0:T(8,128)S(1)}, u32[]{:S(2)}, u32[]{:S(2)}) collective-permute-start(f32[40,128]{1,0:T(8,128)S(1)} %shard_map.139.refs_0_), channel_id=1, source_target_pairs={{0,8},{4,12},{8,0},{12,4},{16,24},{20,28},{24,16},{28,20},{1,9},{5... | collective-permute-start | bytes 61448 | tf_op jit(solution)/shard_map/ppermute | solution.py:527
  54.7 1.2 %collective-permute-done.18.refs_3_ = f32[40,128]{1,0:T(8,128)S(1)} collective-permute-done((f32[40,128]{1,0:T(8,128)S(1)}, f32[40,128]{1,0:T(8,128)S(1)}, u32[]{:S(2)}, u32[]{:S(2)}) %collective-permute-start.18) | collective-permute-done | bytes 20512 | tf_op jit(solution)/shard_map/ppermute | solution.py:527
  55.9 1.4 %collective-permute-done.17.refs_2_ = f32[40,128]{1,0:T(8,128)S(1)} collective-permute-done((f32[40,128]{1,0:T(8,128)S(1)}, f32[40,128]{1,0:T(8,128)S(1)}, u32[]{:S(2)}, u32[]{:S(2)}) %collective-permute-start.17) | collective-permute-done | bytes 20512 | tf_op jit(solution)/shard_map/ppermute | solution.py:527
  57.4 1.3 %collective-permute-start.21 = (f32[72,128]{1,0:T(8,128)S(1)}, f32[72,128]{1,0:T(8,128)S(1)}, u32[]{:S(2)}, u32[]{:S(2)}) collective-permute-start(f32[72,128]{1,0:T(8,128)S(1)} %get-tuple-element.57), channel_id=1, source_target_pairs={{0,3},{1,2},{2,1},{3,0},{4,7},{5,6},{6,5},{7,4},{8,11},{9,10},{10,... | collective-permute-start | bytes 110600 | tf_op jit(solution)/shard_map/ppermute | solution.py:546
  59.4 2.9 %collective-permute-done.20.refs_2_ = f32[8,128]{1,0:T(8,128)S(1)} collective-permute-done((f32[8,128]{1,0:T(8,128)S(1)}, f32[8,128]{1,0:T(8,128)S(1)}, u32[]{:S(2)}, u32[]{:S(2)}) %collective-permute-start.20) | collective-permute-done | bytes 4128 | tf_op jit(solution)/shard_map/ppermute | solution.py:546
  (37 shorter events, 13.3 us)
Async XLA Ops:
  4.3 5.6 %collective-permute-start = (f32[168,128]{1,0:T(8,128)S(1)}, f32[168,128]{1,0:T(8,128)S(1)}, u32[]{:S(2)}, u32[]{:S(2)}) collective-permute-start(f32[168,128]{1,0:T(8,128)S(1)} %get-tuple-element.33), channel_id=1, source_target_pairs={{0,4},{4,0},{8,12},{12,8},{16,20},{20,16},{24,28},{28,24},{1,5},{5... | collective-permute-start | bytes 258056 | tf_op jit(solution)/shard_map/ppermute | solution.py:561
  7.4 8.4 %collective-permute-start.4 = (f32[136,128]{1,0:T(8,128)S(1)}, f32[136,128]{1,0:T(8,128)S(1)}, u32[]{:S(2)}, u32[]{:S(2)}) collective-permute-start(f32[136,128]{1,0:T(8,128)S(1)} %get-tuple-element.34), channel_id=1, source_target_pairs={{5,9},{7,11},{9,5},{11,7},{13,17},{15,19},{17,13},{19,15},{21,25},... | collective-permute-start | bytes 208904 | tf_op jit(solution)/shard_map/ppermute | solution.py:571
  9.9 5.9 %collective-permute-start.3 = (f32[32,128]{1,0:T(8,128)S(1)}, f32[32,128]{1,0:T(8,128)S(1)}, u32[]{:S(2)}, u32[]{:S(2)}) collective-permute-start(f32[32,128]{1,0:T(8,128)S(1)} %slice_add_fusion.2.refs_0_), channel_id=1, source_target_pairs={{0,24},{4,28},{8,16},{12,20},{16,8},{20,12},{24,0},{28,4},{1,25},{... | collective-permute-start | bytes 49160 | tf_op jit(solution)/shard_map/ppermute | solution.py:527
  13.9 4.6 %collective-permute-start.2 = (f32[32,128]{1,0:T(8,128)S(1)}, f32[32,128]{1,0:T(8,128)S(1)}, u32[]{:S(2)}, u32[]{:S(2)}) collective-permute-start(f32[32,128]{1,0:T(8,128)S(1)} %slice_add_fusion.2.refs_0_), channel_id=1, source_target_pairs={{0,16},{4,20},{8,24},{12,28},{16,0},{20,4},{24,8},{28,12},{1,17},{... | collective-permute-start | bytes 49160 | tf_op jit(solution)/shard_map/ppermute | solution.py:527
  13.9 4.6 %collective-permute-start.1 = (f32[32,128]{1,0:T(8,128)S(1)}, f32[32,128]{1,0:T(8,128)S(1)}, u32[]{:S(2)}, u32[]{:S(2)}) collective-permute-start(f32[32,128]{1,0:T(8,128)S(1)} %slice_add_fusion.2.refs_0_), channel_id=1, source_target_pairs={{0,8},{4,12},{8,0},{12,4},{16,24},{20,28},{24,16},{28,20},{1,9},{5... | collective-permute-start | bytes 49160 | tf_op jit(solution)/shard_map/ppermute | solution.py:527
  14.6 4.0 %copy-start = (f32[64,64]{1,0:T(8,128)S(1)}, f32[64,64]{1,0:T(8,128)}, u32[]{:S(2)}) copy-start(f32[64,64]{1,0:T(8,128)} %refs_4_.2) | copy-start | bytes 49156
  19.6 1.4 %collective-permute-start.5 = (f32[136,256]{1,0:T(8,128)S(1)}, f32[136,256]{1,0:T(8,128)S(1)}, u32[]{:S(2)}, u32[]{:S(2)}) collective-permute-start(f32[136,256]{1,0:T(8,128)S(1)} %shard_map.132), channel_id=1, source_target_pairs={{0,1},{1,0},{2,3},{3,2},{4,5},{5,4},{6,7},{7,6},{8,9},{9,8},{10,11... | collective-permute-start | bytes 417800 | tf_op jit(solution)/shard_map/ppermute | solution.py:534
  21.1 4.3 %collective-permute-start.6 = (f32[64,256]{1,0:T(8,128)S(1)}, f32[64,256]{1,0:T(8,128)S(1)}, u32[]{:S(2)}, u32[]{:S(2)}) collective-permute-start(f32[64,256]{1,0:T(8,128)S(1)} %slice_add_fusion.1.refs_0_), channel_id=1, source_target_pairs={{0,2},{1,3},{2,0},{3,1},{4,6},{5,7},{6,4},{7,5},{8,10},{9,11},{10,... | collective-permute-start | bytes 196616 | tf_op jit(solution)/shard_map/ppermute | solution.py:527
  26.5 4.2 %collective-permute-start.7 = (f32[104,128]{1,0:T(8,128)S(1)}, f32[104,128]{1,0:T(8,128)S(1)}, u32[]{:S(2)}, u32[]{:S(2)}) collective-permute-start(f32[104,128]{1,0:T(8,128)S(1)} %get-tuple-element.43.sent), channel_id=1, source_target_pairs={{0,4},{4,0},{8,12},{12,8},{16,20},{20,16},{24,28},{28,24},{1,5},{5... | collective-permute-start | bytes 159752 | tf_op jit(solution)/shard_map/ppermute | solution.py:561
  28.1 0.7 %collective-permute-start.8 = (f32[64,128]{1,0:T(8,128)S(1)}, f32[64,128]{1,0:T(8,128)S(1)}, u32[]{:S(2)}, u32[]{:S(2)}) collective-permute-start(f32[64,128]{1,0:T(8,128)S(1)} %get-tuple-element.44.edge), channel_id=1, source_target_pairs={{5,9},{7,11},{9,5},{11,7},{13,17},{15,19},{17,13},{19,15},{21,25},... | collective-permute-start | bytes 98312 | tf_op jit(solution)/shard_map/ppermute | solution.py:571
  30.8 5.6 %collective-permute-start.11 = (f32[40,128]{1,0:T(8,128)S(1)}, f32[40,128]{1,0:T(8,128)S(1)}, u32[]{:S(2)}, u32[]{:S(2)}) collective-permute-start(f32[40,128]{1,0:T(8,128)S(1)} %shard_map.135.refs_0_), channel_id=1, source_target_pairs={{0,24},{4,28},{8,16},{12,20},{16,8},{20,12},{24,0},{28,4},{1,25},{... | collective-permute-start | bytes 61448 | tf_op jit(solution)/shard_map/ppermute | solution.py:527
  32.4 4.7 %collective-permute-start.10 = (f32[40,128]{1,0:T(8,128)S(1)}, f32[40,128]{1,0:T(8,128)S(1)}, u32[]{:S(2)}, u32[]{:S(2)}) collective-permute-start(f32[40,128]{1,0:T(8,128)S(1)} %shard_map.135.refs_0_), channel_id=1, source_target_pairs={{0,16},{4,20},{8,24},{12,28},{16,0},{20,4},{24,8},{28,12},{1,17},{... | collective-permute-start | bytes 61448 | tf_op jit(solution)/shard_map/ppermute | solution.py:527
  33.0 4.7 %collective-permute-start.9 = (f32[40,128]{1,0:T(8,128)S(1)}, f32[40,128]{1,0:T(8,128)S(1)}, u32[]{:S(2)}, u32[]{:S(2)}) collective-permute-start(f32[40,128]{1,0:T(8,128)S(1)} %shard_map.135.refs_0_), channel_id=1, source_target_pairs={{0,8},{4,12},{8,0},{12,4},{16,24},{20,28},{24,16},{28,20},{1,9},{5... | collective-permute-start | bytes 61448 | tf_op jit(solution)/shard_map/ppermute | solution.py:527
  38.8 1.4 %collective-permute-start.12 = (f32[104,256]{1,0:T(8,128)S(1)}, f32[104,256]{1,0:T(8,128)S(1)}, u32[]{:S(2)}, u32[]{:S(2)}) collective-permute-start(f32[104,256]{1,0:T(8,128)S(1)} %get-tuple-element.45), channel_id=1, source_target_pairs={{0,1},{1,0},{2,3},{3,2},{4,5},{5,4},{6,7},{7,6},{8,9},{9,8},{10,11... | collective-permute-start | bytes 319496 | tf_op jit(solution)/shard_map/ppermute | solution.py:534
  40.2 4.4 %collective-permute-start.13 = (f32[72,256]{1,0:T(8,128)S(1)}, f32[72,256]{1,0:T(8,128)S(1)}, u32[]{:S(2)}, u32[]{:S(2)}) collective-permute-start(f32[72,256]{1,0:T(8,128)S(1)} %slice_add_fusion.refs_0_), channel_id=1, source_target_pairs={{0,2},{1,3},{2,0},{3,1},{4,6},{5,7},{6,4},{7,5},{8,10},{9,11},{10,... | collective-permute-start | bytes 221192 | tf_op jit(solution)/shard_map/ppermute | solution.py:527
  45.9 4.2 %collective-permute-start.14 = (f32[104,128]{1,0:T(8,128)S(1)}, f32[104,128]{1,0:T(8,128)S(1)}, u32[]{:S(2)}, u32[]{:S(2)}) collective-permute-start(f32[104,128]{1,0:T(8,128)S(1)} %get-tuple-element.54.sent), channel_id=1, source_target_pairs={{0,4},{4,0},{8,12},{12,8},{16,20},{20,16},{24,28},{28,24},{1,5},{5... | collective-permute-start | bytes 159752 | tf_op jit(solution)/shard_map/ppermute | solution.py:561
  47.0 0.7 %collective-permute-start.15 = (f32[64,128]{1,0:T(8,128)S(1)}, f32[64,128]{1,0:T(8,128)S(1)}, u32[]{:S(2)}, u32[]{:S(2)}) collective-permute-start(f32[64,128]{1,0:T(8,128)S(1)} %get-tuple-element.55.edge), channel_id=1, source_target_pairs={{5,9},{7,11},{9,5},{11,7},{13,17},{15,19},{17,13},{19,15},{21,25},... | collective-permute-start | bytes 98312 | tf_op jit(solution)/shard_map/ppermute | solution.py:571
  50.2 5.6 %collective-permute-start.18 = (f32[40,128]{1,0:T(8,128)S(1)}, f32[40,128]{1,0:T(8,128)S(1)}, u32[]{:S(2)}, u32[]{:S(2)}) collective-permute-start(f32[40,128]{1,0:T(8,128)S(1)} %shard_map.139.refs_0_), channel_id=1, source_target_pairs={{0,24},{4,28},{8,16},{12,20},{16,8},{20,12},{24,0},{28,4},{1,25},{... | collective-permute-start | bytes 61448 | tf_op jit(solution)/shard_map/ppermute | solution.py:527
  52.5 4.8 %collective-permute-start.17 = (f32[40,128]{1,0:T(8,128)S(1)}, f32[40,128]{1,0:T(8,128)S(1)}, u32[]{:S(2)}, u32[]{:S(2)}) collective-permute-start(f32[40,128]{1,0:T(8,128)S(1)} %shard_map.139.refs_0_), channel_id=1, source_target_pairs={{0,16},{4,20},{8,24},{12,28},{16,0},{20,4},{24,8},{28,12},{1,17},{... | collective-permute-start | bytes 61448 | tf_op jit(solution)/shard_map/ppermute | solution.py:527
  53.1 4.2 %collective-permute-start.16 = (f32[40,128]{1,0:T(8,128)S(1)}, f32[40,128]{1,0:T(8,128)S(1)}, u32[]{:S(2)}, u32[]{:S(2)}) collective-permute-start(f32[40,128]{1,0:T(8,128)S(1)} %shard_map.139.refs_0_), channel_id=1, source_target_pairs={{0,8},{4,12},{8,0},{12,4},{16,24},{20,28},{24,16},{28,20},{1,9},{5... | collective-permute-start | bytes 61448 | tf_op jit(solution)/shard_map/ppermute | solution.py:527
  57.4 4.9 %collective-permute-start.21 = (f32[72,128]{1,0:T(8,128)S(1)}, f32[72,128]{1,0:T(8,128)S(1)}, u32[]{:S(2)}, u32[]{:S(2)}) collective-permute-start(f32[72,128]{1,0:T(8,128)S(1)} %get-tuple-element.57), channel_id=1, source_target_pairs={{0,3},{1,2},{2,1},{3,0},{4,7},{5,6},{6,5},{7,4},{8,11},{9,10},{10,... | collective-permute-start | bytes 110600 | tf_op jit(solution)/shard_map/ppermute | solution.py:546
  58.7 3.6 %collective-permute-start.20 = (f32[8,128]{1,0:T(8,128)S(1)}, f32[8,128]{1,0:T(8,128)S(1)}, u32[]{:S(2)}, u32[]{:S(2)}) collective-permute-start(f32[8,128]{1,0:T(8,128)S(1)} %get-tuple-element.56.refs_0_), channel_id=1, source_target_pairs={{0,2},{1,3},{2,0},{3,1},{4,6},{5,7},{6,4},{7,5},{8,10},{9,11},{10,... | collective-permute-start | bytes 12296 | tf_op jit(solution)/shard_map/ppermute | solution.py:546
  59.2 3.1 %collective-permute-start.19 = (f32[8,128]{1,0:T(8,128)S(1)}, f32[8,128]{1,0:T(8,128)S(1)}, u32[]{:S(2)}, u32[]{:S(2)}) collective-permute-start(f32[8,128]{1,0:T(8,128)S(1)} %get-tuple-element.56.refs_0_), channel_id=1, source_target_pairs={{0,1},{1,0},{2,3},{3,2},{4,5},{5,4},{6,7},{7,6},{8,9},{9,8},{10,11... | collective-permute-start | bytes 12296 | tf_op jit(solution)/shard_map/ppermute | solution.py:546

commit v10 on v9

--- a/solution.py
+++ b/solution.py
@@ -11,7 +11,7 @@
 COLS = 128
 LANES = 128
 GROUP = 8
-CHUNK = 24
+CHUNK = 32
 SHRINK_SCALE = 0.4
 TINY = 1e-06
 VMEM = pltpu.VMEM
@@ -279,17 +279,17 @@
     half = times // 2
     copies = []
 
-    def load(source, target):
+    def load(source, target, priority=0):
         copy = pltpu.make_async_copy(source, target, sems.at[len(copies)])
-        copy.start()
+        copy.start(priority=priority)
         copies.append(copy)
         return copy
 
-    early = [load(loaded[i], kept[i]) for i in (1, 3)]
+    early = [load(loaded[i], kept[i], 1) for i in (1, 3)]
     large = []
     for start in range(0, freqs, CHUNK):
         at = (slice(None), pl.ds(start, min(CHUNK, freqs - start)))
-        large.append(load(kernel.at[at], kernel_here.at[at]))
+        large.append(load(kernel.at[at], kernel_here.at[at], 1 if start == 0 else 0))
         if start == 0:
             small = [load(loaded[i], kept[i]) for i in (7, 8, 9, 2, 4)]
     late = [load(loaded[i], kept[i]) for i in (5, 6)]
@@ -477,13 +477,22 @@
     norms[...] = squares
 
 
+def before_finish_body(gradient, model_jumps, multiplier, linked, sum_out, jumps_out):
+    field = gradient[...]
+    sum_out[...] = model_jumps[...] + multiplier[...]
+    nothing = jnp.zeros((field.shape[0], COLS), jnp.float32)
+    for k, strips in enumerate(jumps(field, nothing, nothing, linked[...])):
+        for r, values in enumerate(strips):
+            jumps_out[k, :, r * COLS : (r + 1) * COLS] = values
+
+
 def finish_body(count, *refs):
-    (norms, gradient_in, model, model_jumps, multiplier, threshold, grad_one, grad_two, passed, linked,
+    (norms, gradient_in, model, sums, inner_jumps, threshold, grad_one, grad_two, passed, linked,
      estimate_out, auxiliary_out, multiplier_out, estimate_here, auxiliary_here, multiplier_here, sems) = refs[count:]
     step = step_of(norms, tree_sum([part[:8, :] for part in refs[:count]]))
-    grad_two = jnp.where(is_odd(), grad_two[...], passed[8:, :])
     half = gradient_in.shape[0] // 2
     gradient = gradient_in[...]
+    rows = gradient.shape[1] // COLS
     copies = []
 
     def store(source, target):
@@ -491,18 +500,22 @@
         copy.start()
         copies.append(copy)
 
-    estimate_here[...] = model[...] - jnp.concatenate([step] * (gradient.shape[1] // COLS), axis=1) * gradient
-    store(estimate_here, estimate_out)
-    grad_jumps = jumps(gradient, *beside(grad_one[half + 8 :, :], grad_two), linked[...])
+    above, below = beside(grad_one[half + 8 :, :], jnp.where(is_odd(), grad_two[...], passed[8:, :]))
+    outer = {
+        (2, 0): linked[2:3, :COLS] * (above - strip(gradient, 0)),
+        (3, rows - 1): linked[3:4, (rows - 1) * COLS :] * (below - strip(gradient, rows - 1)),
+    }
     for k in range(4):
-        for r in range(gradient.shape[1] // COLS):
+        for r in range(rows):
             at = slice(r * COLS, (r + 1) * COLS)
-            shifted = model_jumps[k, :, at] - step * grad_jumps[k][r] + multiplier[k, :, at]
+            shifted = sums[k, :, at] - step * outer.get((k, r), inner_jumps[k, :, at])
             auxiliary = shrunk(shifted, threshold[0:1, at])
             auxiliary_here[k, :, at] = auxiliary
             multiplier_here[k, :, at] = shifted - auxiliary
         store(auxiliary_here.at[k], auxiliary_out.at[k])
         store(multiplier_here.at[k], multiplier_out.at[k])
+    estimate_here[...] = model[...] - jnp.concatenate([step] * rows, axis=1) * gradient
+    store(estimate_here, estimate_out)
     for copy in copies:
         copy.wait()
 
@@ -627,6 +640,7 @@
     )
     grad_one, grad_two = from_partner(sent), from_other(edge)
     parts = cell_parts(call(merge_body, (half + 8, LANES), sent, grad_one, edge, grad_two, linked))
+    sums, inner_jumps = call(before_finish_body, [wide, wide], gradient, model_jumps, multiplier, linked)
     scalars, passing, norms = call(
         functools.partial(response_body, len(parts)), [(8, LANES), (8 + times, LANES), (8, LANES)], *parts, grad_two
     )
@@ -634,7 +648,7 @@
     return tuple(
         call(
             functools.partial(finish_body, len(parts)), [field, wide, wide],
-            *parts, norms, gradient, model, model_jumps, multiplier, threshold, grad_one, grad_two, passed, linked,
+            *parts, norms, gradient, model, sums, inner_jumps, threshold, grad_one, grad_two, passed, linked,
             scratch=[VMEM(shape, jnp.float32) for shape in (field, wide, wide)] + [pltpu.SemaphoreType.DMA((9,))],
             outputs=HBM,
         )

time: 63.4 us -> 64.2 us (1.013)
  Pallas kernels: 10.9 us -> 11.8 us
    pallas_call x12 -> x13, Pallas kernels: 10.9 us -> 11.8 us  [call(): pl.pallas_call(body, out_shape=shapes, in_specs=[pl.BlockSpec(memory_spac...]
where the time goes in v10:
time: 64.2 us; the launch traced here: 64 us
  starting transfers between devices  26.6 us (41%)
  waiting for transfers between devices  24.7 us (38%)
  Pallas kernels  11.8 us (18%)
  between operations  0.8 us (1%)
    ppermute x11, starting transfers between devices, summing(): lax.ppermute(total, axis, [(i, i ^ k * stride) for i in range(count)])  16.7 us
    ppermute x11, waiting for transfers between devices, summing(): lax.ppermute(total, axis, [(i, i ^ k * stride) for i in range(count)])  13.2 us
    pallas_call x13, Pallas kernels, call(): pl.pallas_call(body, out_shape=shapes, in_specs=[pl.BlockSpec(memory_spac...  11.8 us
    ppermute x3, waiting for transfers between devices, from_partner(): lax.ppermute(array, 'cell', [(i, i ^ 1) for i in range(lax.axis_size('cel...  6.17 us
    ppermute x3, starting transfers between devices, from_partner(): lax.ppermute(array, 'cell', [(i, i ^ 1) for i in range(lax.axis_size('cel...  5.8 us
    ppermute x3, waiting for transfers between devices, last_sensor_parts(): lax.ppermute(array, 'sensor', [(i, i ^ k) for i in range(count)])  2.82 us
    ppermute x2, waiting for transfers between devices, sensor_hop(): lax.ppermute(array, 'sensor', [(i, i ^ 1) for i in range(lax.axis_size('s...  2.54 us
    ppermute x3, starting transfers between devices, from_other(): return lax.ppermute(array, ('cell', 'sensor'), pairs)  1.96 us
  transfers between devices with their start and end apart: 22, of which 14 were waited for; matrix products, arithmetic and copies ran while one was open for 0% of the time, Pallas kernels for 2%

profile of v10, /device:TPU:0, one launch (start us, length us, event | category | flops | bytes accessed | tf_op | source)
XLA Modules:
  0.0 64.0 jit_solution(2456669955278069848)
XLA Ops:
  0.6 4.5 %shard_map.130 = (f32[168,128]{1,0:T(8,128)S(1)}, f32[136,128]{1,0:T(8,128)S(1)}, f32[8,256]{1,0:T(8,128)S(1)}, f32[8,256]{1,0:T(8,128)S(1)}, bf16[2,65,64,256]{...) custom-call(bf16[2,65,64,256]{3,2,1,0:T(8,128)(2,1)} %refs_0_.1, ...), custom_call_target="tpu_custom_call" | custom-call | tf_op jit(solution)/shard_map/pallas_call | solution.py:218
  5.1 3.0 %collective-permute-start = (f32[168,128]{1,0:T(8,128)S(1)}, f32[168,128]{1,0:T(8,128)S(1)}, u32[]{:S(2)}, u32[]{:S(2)}) collective-permute-start(f32[168,128]{1,0:T(8,128)S(1)} %get-tuple-element.35), channel_id=1, source_target_pairs={{0,4},{4,0},{8,12},{12,8},{16,20},{20,16},{24,28},{28,24},{1,5},{5... | collective-permute-start | bytes 258056 | tf_op jit(solution)/shard_map/ppermute | solution.py:574
  8.8 1.9 %collective-permute-done.came.one.refs_10_ = f32[168,128]{1,0:T(8,128)S(1)} collective-permute-done((f32[168,128]{1,0:T(8,128)S(1)}, f32[168,128]{1,0:T(8,128)S(1)}, u32[]{:S(2)}, u32[]{:S(2)}) %collective-permute-start) | collective-permute-done | bytes 86048 | tf_op jit(solution)/shard_map/ppermute | solution.py:574
  10.7 4.0 %collective-permute-start.3 = (f32[32,128]{1,0:T(8,128)S(1)}, f32[32,128]{1,0:T(8,128)S(1)}, u32[]{:S(2)}, u32[]{:S(2)}) collective-permute-start(f32[32,128]{1,0:T(8,128)S(1)} %slice_add_fusion.2.refs_0_), channel_id=1, source_target_pairs={{0,24},{4,28},{8,16},{12,20},{16,8},{20,12},{24,0},{28,4},{1,25},{... | collective-permute-start | bytes 49160 | tf_op jit(solution)/shard_map/ppermute | solution.py:540
  16.6 2.8 %collective-permute-done.2.refs_2_ = f32[32,128]{1,0:T(8,128)S(1)} collective-permute-done((f32[32,128]{1,0:T(8,128)S(1)}, f32[32,128]{1,0:T(8,128)S(1)}, u32[]{:S(2)}, u32[]{:S(2)}) %collective-permute-start.2) | collective-permute-done | bytes 16416 | tf_op jit(solution)/shard_map/ppermute | solution.py:540
  20.5 1.3 %collective-permute-done.5.passed = f32[136,256]{1,0:T(8,128)S(1)} collective-permute-done((f32[136,256]{1,0:T(8,128)S(1)}, f32[136,256]{1,0:T(8,128)S(1)}, u32[]{:S(2)}, u32[]{:S(2)}) %collective-permute-start.5) | collective-permute-done | bytes 139296 | tf_op jit(solution)/shard_map/ppermute | solution.py:547
  21.9 1.6 %collective-permute-start.6 = (f32[64,256]{1,0:T(8,128)S(1)}, f32[64,256]{1,0:T(8,128)S(1)}, u32[]{:S(2)}, u32[]{:S(2)}) collective-permute-start(f32[64,256]{1,0:T(8,128)S(1)} %slice_add_fusion.1.refs_0_), channel_id=1, source_target_pairs={{0,2},{1,3},{2,0},{3,1},{4,6},{5,7},{6,4},{7,5},{8,10},{9,11},{10,... | collective-permute-start | bytes 196616 | tf_op jit(solution)/shard_map/ppermute | solution.py:540
  23.5 2.7 %collective-permute-done.6.refs_1_ = f32[64,256]{1,0:T(8,128)S(1)} collective-permute-done((f32[64,256]{1,0:T(8,128)S(1)}, f32[64,256]{1,0:T(8,128)S(1)}, u32[]{:S(2)}, u32[]{:S(2)}) %collective-permute-start.6) | collective-permute-done | bytes 65568 | tf_op jit(solution)/shard_map/ppermute | solution.py:540
  27.3 1.6 %collective-permute-start.7 = (f32[104,128]{1,0:T(8,128)S(1)}, f32[104,128]{1,0:T(8,128)S(1)}, u32[]{:S(2)}, u32[]{:S(2)}) collective-permute-start(f32[104,128]{1,0:T(8,128)S(1)} %get-tuple-element.45.sent), channel_id=1, source_target_pairs={{0,4},{4,0},{8,12},{12,8},{16,20},{20,16},{24,28},{28,24},{1,5},{5... | collective-permute-start | bytes 159752 | tf_op jit(solution)/shard_map/ppermute | solution.py:574
  29.5 1.9 %collective-permute-done.7.came.grad_one = f32[104,128]{1,0:T(8,128)S(1)} collective-permute-done((f32[104,128]{1,0:T(8,128)S(1)}, f32[104,128]{1,0:T(8,128)S(1)}, u32[]{:S(2)}, u32[]{:S(2)}) %collective-permute-start.7) | collective-permute-done | bytes 53280 | tf_op jit(solution)/shard_map/ppermute | solution.py:574
  31.6 1.5 %collective-permute-start.11 = (f32[40,128]{1,0:T(8,128)S(1)}, f32[40,128]{1,0:T(8,128)S(1)}, u32[]{:S(2)}, u32[]{:S(2)}) collective-permute-start(f32[40,128]{1,0:T(8,128)S(1)} %shard_map.135.refs_0_), channel_id=1, source_target_pairs={{0,24},{4,28},{8,16},{12,20},{16,8},{20,12},{24,0},{28,4},{1,25},{... | collective-permute-start | bytes 61448 | tf_op jit(solution)/shard_map/ppermute | solution.py:540
  33.8 2.3 %collective-permute-start.9 = (f32[40,128]{1,0:T(8,128)S(1)}, f32[40,128]{1,0:T(8,128)S(1)}, u32[]{:S(2)}, u32[]{:S(2)}) collective-permute-start(f32[40,128]{1,0:T(8,128)S(1)} %shard_map.135.refs_0_), channel_id=1, source_target_pairs={{0,8},{4,12},{8,0},{12,4},{16,24},{20,28},{24,16},{28,20},{1,9},{5... | collective-permute-start | bytes 61448 | tf_op jit(solution)/shard_map/ppermute | solution.py:540
  36.1 1.2 %collective-permute-done.11.refs_3_ = f32[40,128]{1,0:T(8,128)S(1)} collective-permute-done((f32[40,128]{1,0:T(8,128)S(1)}, f32[40,128]{1,0:T(8,128)S(1)}, u32[]{:S(2)}, u32[]{:S(2)}) %collective-permute-start.11) | collective-permute-done | bytes 20512 | tf_op jit(solution)/shard_map/ppermute | solution.py:540
  39.8 1.2 %collective-permute-done.12.passed = f32[104,256]{1,0:T(8,128)S(1)} collective-permute-done((f32[104,256]{1,0:T(8,128)S(1)}, f32[104,256]{1,0:T(8,128)S(1)}, u32[]{:S(2)}, u32[]{:S(2)}) %collective-permute-start.12) | collective-permute-done | bytes 106528 | tf_op jit(solution)/shard_map/ppermute | solution.py:547
  41.0 1.6 %collective-permute-start.13 = (f32[72,256]{1,0:T(8,128)S(1)}, f32[72,256]{1,0:T(8,128)S(1)}, u32[]{:S(2)}, u32[]{:S(2)}) collective-permute-start(f32[72,256]{1,0:T(8,128)S(1)} %slice_add_fusion.refs_0_), channel_id=1, source_target_pairs={{0,2},{1,3},{2,0},{3,1},{4,6},{5,7},{6,4},{7,5},{8,10},{9,11},{10,... | collective-permute-start | bytes 221192 | tf_op jit(solution)/shard_map/ppermute | solution.py:540
  42.7 2.7 %collective-permute-done.13.refs_1_ = f32[72,256]{1,0:T(8,128)S(1)} collective-permute-done((f32[72,256]{1,0:T(8,128)S(1)}, f32[72,256]{1,0:T(8,128)S(1)}, u32[]{:S(2)}, u32[]{:S(2)}) %collective-permute-start.13) | collective-permute-done | bytes 73760 | tf_op jit(solution)/shard_map/ppermute | solution.py:540
  45.4 1.2 %shard_map.138 = (f32[64,256]{1,0:T(8,128)S(1)}, f32[4,64,256]{2,1,0:T(8,128)S(1)}, f32[4,64,256]{2,1,0:T(8,128)S(1)}, f32[64,256]{1,0:T(8,128)S(1)}, f32[104,128]{1,0:T(8,128)S(1)}, /*index=5*/f32[64,128]{1,0:T(8,128)S(1)}) custom-call(f32[72,256]{1,0:T(8,128)S(1)} %slice_add_fusion.refs_0_, f32[72,256]{1,0:T(8,128)S(1)} %collective-permute-done.13.refs_1_, ...), custom_call_target="tpu_custom_call" | custom-call | tf_op jit(solution)/shard_map/pallas_call | solution.py:218
  48.5 2.4 %collective-permute-done.14.came.refs_10_ = f32[104,128]{1,0:T(8,128)S(1)} collective-permute-done((f32[104,128]{1,0:T(8,128)S(1)}, f32[104,128]{1,0:T(8,128)S(1)}, u32[]{:S(2)}, u32[]{:S(2)}) %collective-permute-start.14) | collective-permute-done | bytes 53280 | tf_op jit(solution)/shard_map/ppermute | solution.py:574
  51.0 2.2 %collective-permute-start.18 = (f32[40,128]{1,0:T(8,128)S(1)}, f32[40,128]{1,0:T(8,128)S(1)}, u32[]{:S(2)}, u32[]{:S(2)}) collective-permute-start(f32[40,128]{1,0:T(8,128)S(1)} %shard_map.139.refs_0_), channel_id=1, source_target_pairs={{0,24},{4,28},{8,16},{12,20},{16,8},{20,12},{24,0},{28,4},{1,25},{... | collective-permute-start | bytes 61448 | tf_op jit(solution)/shard_map/ppermute | solution.py:540
  53.9 1.5 %collective-permute-start.16 = (f32[40,128]{1,0:T(8,128)S(1)}, f32[40,128]{1,0:T(8,128)S(1)}, u32[]{:S(2)}, u32[]{:S(2)}) collective-permute-start(f32[40,128]{1,0:T(8,128)S(1)} %shard_map.139.refs_0_), channel_id=1, source_target_pairs={{0,8},{4,12},{8,0},{12,4},{16,24},{20,28},{24,16},{28,20},{1,9},{5... | collective-permute-start | bytes 61448 | tf_op jit(solution)/shard_map/ppermute | solution.py:540
  55.5 1.2 %collective-permute-done.18.refs_3_ = f32[40,128]{1,0:T(8,128)S(1)} collective-permute-done((f32[40,128]{1,0:T(8,128)S(1)}, f32[40,128]{1,0:T(8,128)S(1)}, u32[]{:S(2)}, u32[]{:S(2)}) %collective-permute-start.18) | collective-permute-done | bytes 20512 | tf_op jit(solution)/shard_map/ppermute | solution.py:540
  56.7 1.4 %collective-permute-done.17.refs_2_ = f32[40,128]{1,0:T(8,128)S(1)} collective-permute-done((f32[40,128]{1,0:T(8,128)S(1)}, f32[40,128]{1,0:T(8,128)S(1)}, u32[]{:S(2)}, u32[]{:S(2)}) %collective-permute-start.17) | collective-permute-done | bytes 20512 | tf_op jit(solution)/shard_map/ppermute | solution.py:540
  58.2 1.3 %collective-permute-start.21 = (f32[72,128]{1,0:T(8,128)S(1)}, f32[72,128]{1,0:T(8,128)S(1)}, u32[]{:S(2)}, u32[]{:S(2)}) collective-permute-start(f32[72,128]{1,0:T(8,128)S(1)} %get-tuple-element.59), channel_id=1, source_target_pairs={{0,3},{1,2},{2,1},{3,0},{4,7},{5,6},{6,5},{7,4},{8,11},{9,10},{10,... | collective-permute-start | bytes 110600 | tf_op jit(solution)/shard_map/ppermute | solution.py:559
  60.3 2.8 %collective-permute-done.20.refs_2_ = f32[8,128]{1,0:T(8,128)S(1)} collective-permute-done((f32[8,128]{1,0:T(8,128)S(1)}, f32[8,128]{1,0:T(8,128)S(1)}, u32[]{:S(2)}, u32[]{:S(2)}) %collective-permute-start.20) | collective-permute-done | bytes 4128 | tf_op jit(solution)/shard_map/ppermute | solution.py:559
  (38 shorter events, 13.4 us)
Async XLA Ops:
  5.1 5.6 %collective-permute-start = (f32[168,128]{1,0:T(8,128)S(1)}, f32[168,128]{1,0:T(8,128)S(1)}, u32[]{:S(2)}, u32[]{:S(2)}) collective-permute-start(f32[168,128]{1,0:T(8,128)S(1)} %get-tuple-element.35), channel_id=1, source_target_pairs={{0,4},{4,0},{8,12},{12,8},{16,20},{20,16},{24,28},{28,24},{1,5},{5... | collective-permute-start | bytes 258056 | tf_op jit(solution)/shard_map/ppermute | solution.py:574
  8.2 8.4 %collective-permute-start.4 = (f32[136,128]{1,0:T(8,128)S(1)}, f32[136,128]{1,0:T(8,128)S(1)}, u32[]{:S(2)}, u32[]{:S(2)}) collective-permute-start(f32[136,128]{1,0:T(8,128)S(1)} %get-tuple-element.36), channel_id=1, source_target_pairs={{5,9},{7,11},{9,5},{11,7},{13,17},{15,19},{17,13},{19,15},{21,25},... | collective-permute-start | bytes 208904 | tf_op jit(solution)/shard_map/ppermute | solution.py:584
  10.7 5.9 %collective-permute-start.3 = (f32[32,128]{1,0:T(8,128)S(1)}, f32[32,128]{1,0:T(8,128)S(1)}, u32[]{:S(2)}, u32[]{:S(2)}) collective-permute-start(f32[32,128]{1,0:T(8,128)S(1)} %slice_add_fusion.2.refs_0_), channel_id=1, source_target_pairs={{0,24},{4,28},{8,16},{12,20},{16,8},{20,12},{24,0},{28,4},{1,25},{... | collective-permute-start | bytes 49160 | tf_op jit(solution)/shard_map/ppermute | solution.py:540
  14.7 4.6 %collective-permute-start.2 = (f32[32,128]{1,0:T(8,128)S(1)}, f32[32,128]{1,0:T(8,128)S(1)}, u32[]{:S(2)}, u32[]{:S(2)}) collective-permute-start(f32[32,128]{1,0:T(8,128)S(1)} %slice_add_fusion.2.refs_0_), channel_id=1, source_target_pairs={{0,16},{4,20},{8,24},{12,28},{16,0},{20,4},{24,8},{28,12},{1,17},{... | collective-permute-start | bytes 49160 | tf_op jit(solution)/shard_map/ppermute | solution.py:540
  14.7 4.6 %collective-permute-start.1 = (f32[32,128]{1,0:T(8,128)S(1)}, f32[32,128]{1,0:T(8,128)S(1)}, u32[]{:S(2)}, u32[]{:S(2)}) collective-permute-start(f32[32,128]{1,0:T(8,128)S(1)} %slice_add_fusion.2.refs_0_), channel_id=1, source_target_pairs={{0,8},{4,12},{8,0},{12,4},{16,24},{20,28},{24,16},{28,20},{1,9},{5... | collective-permute-start | bytes 49160 | tf_op jit(solution)/shard_map/ppermute | solution.py:540
  15.4 4.0 %copy-start = (f32[64,64]{1,0:T(8,128)S(1)}, f32[64,64]{1,0:T(8,128)}, u32[]{:S(2)}) copy-start(f32[64,64]{1,0:T(8,128)} %refs_4_.2) | copy-start | bytes 49156
  20.4 1.4 %collective-permute-start.5 = (f32[136,256]{1,0:T(8,128)S(1)}, f32[136,256]{1,0:T(8,128)S(1)}, u32[]{:S(2)}, u32[]{:S(2)}) collective-permute-start(f32[136,256]{1,0:T(8,128)S(1)} %shard_map.132), channel_id=1, source_target_pairs={{0,1},{1,0},{2,3},{3,2},{4,5},{5,4},{6,7},{7,6},{8,9},{9,8},{10,11... | collective-permute-start | bytes 417800 | tf_op jit(solution)/shard_map/ppermute | solution.py:547
  21.9 4.3 %collective-permute-start.6 = (f32[64,256]{1,0:T(8,128)S(1)}, f32[64,256]{1,0:T(8,128)S(1)}, u32[]{:S(2)}, u32[]{:S(2)}) collective-permute-start(f32[64,256]{1,0:T(8,128)S(1)} %slice_add_fusion.1.refs_0_), channel_id=1, source_target_pairs={{0,2},{1,3},{2,0},{3,1},{4,6},{5,7},{6,4},{7,5},{8,10},{9,11},{10,... | collective-permute-start | bytes 196616 | tf_op jit(solution)/shard_map/ppermute | solution.py:540
  27.3 4.2 %collective-permute-start.7 = (f32[104,128]{1,0:T(8,128)S(1)}, f32[104,128]{1,0:T(8,128)S(1)}, u32[]{:S(2)}, u32[]{:S(2)}) collective-permute-start(f32[104,128]{1,0:T(8,128)S(1)} %get-tuple-element.45.sent), channel_id=1, source_target_pairs={{0,4},{4,0},{8,12},{12,8},{16,20},{20,16},{24,28},{28,24},{1,5},{5... | collective-permute-start | bytes 159752 | tf_op jit(solution)/shard_map/ppermute | solution.py:574
  28.9 0.7 %collective-permute-start.8 = (f32[64,128]{1,0:T(8,128)S(1)}, f32[64,128]{1,0:T(8,128)S(1)}, u32[]{:S(2)}, u32[]{:S(2)}) collective-permute-start(f32[64,128]{1,0:T(8,128)S(1)} %get-tuple-element.46.edge), channel_id=1, source_target_pairs={{5,9},{7,11},{9,5},{11,7},{13,17},{15,19},{17,13},{19,15},{21,25},... | collective-permute-start | bytes 98312 | tf_op jit(solution)/shard_map/ppermute | solution.py:584
  31.6 5.6 %collective-permute-start.11 = (f32[40,128]{1,0:T(8,128)S(1)}, f32[40,128]{1,0:T(8,128)S(1)}, u32[]{:S(2)}, u32[]{:S(2)}) collective-permute-start(f32[40,128]{1,0:T(8,128)S(1)} %shard_map.135.refs_0_), channel_id=1, source_target_pairs={{0,24},{4,28},{8,16},{12,20},{16,8},{20,12},{24,0},{28,4},{1,25},{... | collective-permute-start | bytes 61448 | tf_op jit(solution)/shard_map/ppermute | solution.py:540
  33.1 4.7 %collective-permute-start.10 = (f32[40,128]{1,0:T(8,128)S(1)}, f32[40,128]{1,0:T(8,128)S(1)}, u32[]{:S(2)}, u32[]{:S(2)}) collective-permute-start(f32[40,128]{1,0:T(8,128)S(1)} %shard_map.135.refs_0_), channel_id=1, source_target_pairs={{0,16},{4,20},{8,24},{12,28},{16,0},{20,4},{24,8},{28,12},{1,17},{... | collective-permute-start | bytes 61448 | tf_op jit(solution)/shard_map/ppermute | solution.py:540
  33.8 4.7 %collective-permute-start.9 = (f32[40,128]{1,0:T(8,128)S(1)}, f32[40,128]{1,0:T(8,128)S(1)}, u32[]{:S(2)}, u32[]{:S(2)}) collective-permute-start(f32[40,128]{1,0:T(8,128)S(1)} %shard_map.135.refs_0_), channel_id=1, source_target_pairs={{0,8},{4,12},{8,0},{12,4},{16,24},{20,28},{24,16},{28,20},{1,9},{5... | collective-permute-start | bytes 61448 | tf_op jit(solution)/shard_map/ppermute | solution.py:540
  39.6 1.4 %collective-permute-start.12 = (f32[104,256]{1,0:T(8,128)S(1)}, f32[104,256]{1,0:T(8,128)S(1)}, u32[]{:S(2)}, u32[]{:S(2)}) collective-permute-start(f32[104,256]{1,0:T(8,128)S(1)} %get-tuple-element.47), channel_id=1, source_target_pairs={{0,1},{1,0},{2,3},{3,2},{4,5},{5,4},{6,7},{7,6},{8,9},{9,8},{10,11... | collective-permute-start | bytes 319496 | tf_op jit(solution)/shard_map/ppermute | solution.py:547
  41.0 4.4 %collective-permute-start.13 = (f32[72,256]{1,0:T(8,128)S(1)}, f32[72,256]{1,0:T(8,128)S(1)}, u32[]{:S(2)}, u32[]{:S(2)}) collective-permute-start(f32[72,256]{1,0:T(8,128)S(1)} %slice_add_fusion.refs_0_), channel_id=1, source_target_pairs={{0,2},{1,3},{2,0},{3,1},{4,6},{5,7},{6,4},{7,5},{8,10},{9,11},{10,... | collective-permute-start | bytes 221192 | tf_op jit(solution)/shard_map/ppermute | solution.py:540
  46.7 4.2 %collective-permute-start.14 = (f32[104,128]{1,0:T(8,128)S(1)}, f32[104,128]{1,0:T(8,128)S(1)}, u32[]{:S(2)}, u32[]{:S(2)}) collective-permute-start(f32[104,128]{1,0:T(8,128)S(1)} %get-tuple-element.56.sent), channel_id=1, source_target_pairs={{0,4},{4,0},{8,12},{12,8},{16,20},{20,16},{24,28},{28,24},{1,5},{5... | collective-permute-start | bytes 159752 | tf_op jit(solution)/shard_map/ppermute | solution.py:574
  47.8 0.7 %collective-permute-start.15 = (f32[64,128]{1,0:T(8,128)S(1)}, f32[64,128]{1,0:T(8,128)S(1)}, u32[]{:S(2)}, u32[]{:S(2)}) collective-permute-start(f32[64,128]{1,0:T(8,128)S(1)} %get-tuple-element.57.edge), channel_id=1, source_target_pairs={{5,9},{7,11},{9,5},{11,7},{13,17},{15,19},{17,13},{19,15},{21,25},... | collective-permute-start | bytes 98312 | tf_op jit(solution)/shard_map/ppermute | solution.py:584
  51.0 5.6 %collective-permute-start.18 = (f32[40,128]{1,0:T(8,128)S(1)}, f32[40,128]{1,0:T(8,128)S(1)}, u32[]{:S(2)}, u32[]{:S(2)}) collective-permute-start(f32[40,128]{1,0:T(8,128)S(1)} %shard_map.139.refs_0_), channel_id=1, source_target_pairs={{0,24},{4,28},{8,16},{12,20},{16,8},{20,12},{24,0},{28,4},{1,25},{... | collective-permute-start | bytes 61448 | tf_op jit(solution)/shard_map/ppermute | solution.py:540
  53.3 4.8 %collective-permute-start.17 = (f32[40,128]{1,0:T(8,128)S(1)}, f32[40,128]{1,0:T(8,128)S(1)}, u32[]{:S(2)}, u32[]{:S(2)}) collective-permute-start(f32[40,128]{1,0:T(8,128)S(1)} %shard_map.139.refs_0_), channel_id=1, source_target_pairs={{0,16},{4,20},{8,24},{12,28},{16,0},{20,4},{24,8},{28,12},{1,17},{... | collective-permute-start | bytes 61448 | tf_op jit(solution)/shard_map/ppermute | solution.py:540
  53.9 4.2 %collective-permute-start.16 = (f32[40,128]{1,0:T(8,128)S(1)}, f32[40,128]{1,0:T(8,128)S(1)}, u32[]{:S(2)}, u32[]{:S(2)}) collective-permute-start(f32[40,128]{1,0:T(8,128)S(1)} %shard_map.139.refs_0_), channel_id=1, source_target_pairs={{0,8},{4,12},{8,0},{12,4},{16,24},{20,28},{24,16},{28,20},{1,9},{5... | collective-permute-start | bytes 61448 | tf_op jit(solution)/shard_map/ppermute | solution.py:540
  58.2 4.9 %collective-permute-start.21 = (f32[72,128]{1,0:T(8,128)S(1)}, f32[72,128]{1,0:T(8,128)S(1)}, u32[]{:S(2)}, u32[]{:S(2)}) collective-permute-start(f32[72,128]{1,0:T(8,128)S(1)} %get-tuple-element.59), channel_id=1, source_target_pairs={{0,3},{1,2},{2,1},{3,0},{4,7},{5,6},{6,5},{7,4},{8,11},{9,10},{10,... | collective-permute-start | bytes 110600 | tf_op jit(solution)/shard_map/ppermute | solution.py:559
  59.5 3.6 %collective-permute-start.20 = (f32[8,128]{1,0:T(8,128)S(1)}, f32[8,128]{1,0:T(8,128)S(1)}, u32[]{:S(2)}, u32[]{:S(2)}) collective-permute-start(f32[8,128]{1,0:T(8,128)S(1)} %get-tuple-element.58.refs_0_), channel_id=1, source_target_pairs={{0,2},{1,3},{2,0},{3,1},{4,6},{5,7},{6,4},{7,5},{8,10},{9,11},{10,... | collective-permute-start | bytes 12296 | tf_op jit(solution)/shard_map/ppermute | solution.py:559
  60.0 3.1 %collective-permute-start.19 = (f32[8,128]{1,0:T(8,128)S(1)}, f32[8,128]{1,0:T(8,128)S(1)}, u32[]{:S(2)}, u32[]{:S(2)}) collective-permute-start(f32[8,128]{1,0:T(8,128)S(1)} %get-tuple-element.58.refs_0_), channel_id=1, source_target_pairs={{0,1},{1,0},{2,3},{3,2},{4,5},{5,4},{6,7},{7,6},{8,9},{9,8},{10,11... | collective-permute-start | bytes 12296 | tf_op jit(solution)/shard_map/ppermute | solution.py:559

commit v11 on v10

--- a/solution.py
+++ b/solution.py
@@ -11,7 +11,7 @@
 COLS = 128
 LANES = 128
 GROUP = 8
-CHUNK = 32
+CHUNK = 16
 SHRINK_SCALE = 0.4
 TINY = 1e-06
 VMEM = pltpu.VMEM
@@ -279,17 +279,17 @@
     half = times // 2
     copies = []
 
-    def load(source, target, priority=0):
+    def load(source, target):
         copy = pltpu.make_async_copy(source, target, sems.at[len(copies)])
-        copy.start(priority=priority)
+        copy.start()
         copies.append(copy)
         return copy
 
-    early = [load(loaded[i], kept[i], 1) for i in (1, 3)]
+    early = [load(loaded[i], kept[i]) for i in (1, 3)]
     large = []
     for start in range(0, freqs, CHUNK):
         at = (slice(None), pl.ds(start, min(CHUNK, freqs - start)))
-        large.append(load(kernel.at[at], kernel_here.at[at], 1 if start == 0 else 0))
+        large.append(load(kernel.at[at], kernel_here.at[at]))
         if start == 0:
             small = [load(loaded[i], kept[i]) for i in (7, 8, 9, 2, 4)]
     late = [load(loaded[i], kept[i]) for i in (5, 6)]

time: 64.2 us -> 63.6 us (level)
  no operation moved by 1% of the time
where the time goes in v11:
time: 63.6 us; the launch traced here: 63.5 us
  starting transfers between devices  26.6 us (42%)
  waiting for transfers between devices  24.7 us (39%)
  Pallas kernels  11.2 us (18%)
  between operations  0.8 us (1%)
    ppermute x11, starting transfers between devices, summing(): lax.ppermute(total, axis, [(i, i ^ k * stride) for i in range(count)])  16.7 us
    ppermute x11, waiting for transfers between devices, summing(): lax.ppermute(total, axis, [(i, i ^ k * stride) for i in range(count)])  13.2 us
    pallas_call x13, Pallas kernels, call(): pl.pallas_call(body, out_shape=shapes, in_specs=[pl.BlockSpec(memory_spac...  11.2 us
    ppermute x3, waiting for transfers between devices, from_partner(): lax.ppermute(array, 'cell', [(i, i ^ 1) for i in range(lax.axis_size('cel...  6.17 us
    ppermute x3, starting transfers between devices, from_partner(): lax.ppermute(array, 'cell', [(i, i ^ 1) for i in range(lax.axis_size('cel...  5.8 us
    ppermute x3, waiting for transfers between devices, last_sensor_parts(): lax.ppermute(array, 'sensor', [(i, i ^ k) for i in range(count)])  2.82 us
    ppermute x2, waiting for transfers between devices, sensor_hop(): lax.ppermute(array, 'sensor', [(i, i ^ 1) for i in range(lax.axis_size('s...  2.54 us
    ppermute x3, starting transfers between devices, from_other(): return lax.ppermute(array, ('cell', 'sensor'), pairs)  1.96 us
  transfers between devices with their start and end apart: 22, of which 14 were waited for; matrix products, arithmetic and copies ran while one was open for 0% of the time, Pallas kernels for 2%

profile of v11, /device:TPU:0, one launch (start us, length us, event | category | flops | bytes accessed | tf_op | source)
XLA Modules:
  0.0 63.5 jit_solution(6533684734707912763)
XLA Ops:
  0.6 3.9 %shard_map.130 = (f32[168,128]{1,0:T(8,128)S(1)}, f32[136,128]{1,0:T(8,128)S(1)}, f32[8,256]{1,0:T(8,128)S(1)}, f32[8,256]{1,0:T(8,128)S(1)}, bf16[2,65,64,256]{...) custom-call(bf16[2,65,64,256]{3,2,1,0:T(8,128)(2,1)} %refs_0_.1, ...), custom_call_target="tpu_custom_call" | custom-call | tf_op jit(solution)/shard_map/pallas_call | solution.py:218
  4.6 3.0 %collective-permute-start = (f32[168,128]{1,0:T(8,128)S(1)}, f32[168,128]{1,0:T(8,128)S(1)}, u32[]{:S(2)}, u32[]{:S(2)}) collective-permute-start(f32[168,128]{1,0:T(8,128)S(1)} %get-tuple-element.35), channel_id=1, source_target_pairs={{0,4},{4,0},{8,12},{12,8},{16,20},{20,16},{24,28},{28,24},{1,5},{5... | collective-permute-start | bytes 258056 | tf_op jit(solution)/shard_map/ppermute | solution.py:574
  8.3 1.9 %collective-permute-done.came.one.refs_10_ = f32[168,128]{1,0:T(8,128)S(1)} collective-permute-done((f32[168,128]{1,0:T(8,128)S(1)}, f32[168,128]{1,0:T(8,128)S(1)}, u32[]{:S(2)}, u32[]{:S(2)}) %collective-permute-start) | collective-permute-done | bytes 86048 | tf_op jit(solution)/shard_map/ppermute | solution.py:574
  10.1 4.0 %collective-permute-start.3 = (f32[32,128]{1,0:T(8,128)S(1)}, f32[32,128]{1,0:T(8,128)S(1)}, u32[]{:S(2)}, u32[]{:S(2)}) collective-permute-start(f32[32,128]{1,0:T(8,128)S(1)} %slice_add_fusion.2.refs_0_), channel_id=1, source_target_pairs={{0,24},{4,28},{8,16},{12,20},{16,8},{20,12},{24,0},{28,4},{1,25},{... | collective-permute-start | bytes 49160 | tf_op jit(solution)/shard_map/ppermute | solution.py:540
  16.0 2.8 %collective-permute-done.2.refs_2_ = f32[32,128]{1,0:T(8,128)S(1)} collective-permute-done((f32[32,128]{1,0:T(8,128)S(1)}, f32[32,128]{1,0:T(8,128)S(1)}, u32[]{:S(2)}, u32[]{:S(2)}) %collective-permute-start.2) | collective-permute-done | bytes 16416 | tf_op jit(solution)/shard_map/ppermute | solution.py:540
  20.0 1.3 %collective-permute-done.5.passed = f32[136,256]{1,0:T(8,128)S(1)} collective-permute-done((f32[136,256]{1,0:T(8,128)S(1)}, f32[136,256]{1,0:T(8,128)S(1)}, u32[]{:S(2)}, u32[]{:S(2)}) %collective-permute-start.5) | collective-permute-done | bytes 139296 | tf_op jit(solution)/shard_map/ppermute | solution.py:547
  21.3 1.6 %collective-permute-start.6 = (f32[64,256]{1,0:T(8,128)S(1)}, f32[64,256]{1,0:T(8,128)S(1)}, u32[]{:S(2)}, u32[]{:S(2)}) collective-permute-start(f32[64,256]{1,0:T(8,128)S(1)} %slice_add_fusion.1.refs_0_), channel_id=1, source_target_pairs={{0,2},{1,3},{2,0},{3,1},{4,6},{5,7},{6,4},{7,5},{8,10},{9,11},{10,... | collective-permute-start | bytes 196616 | tf_op jit(solution)/shard_map/ppermute | solution.py:540
  23.0 2.7 %collective-permute-done.6.refs_1_ = f32[64,256]{1,0:T(8,128)S(1)} collective-permute-done((f32[64,256]{1,0:T(8,128)S(1)}, f32[64,256]{1,0:T(8,128)S(1)}, u32[]{:S(2)}, u32[]{:S(2)}) %collective-permute-start.6) | collective-permute-done | bytes 65568 | tf_op jit(solution)/shard_map/ppermute | solution.py:540
  26.7 1.6 %collective-permute-start.7 = (f32[104,128]{1,0:T(8,128)S(1)}, f32[104,128]{1,0:T(8,128)S(1)}, u32[]{:S(2)}, u32[]{:S(2)}) collective-permute-start(f32[104,128]{1,0:T(8,128)S(1)} %get-tuple-element.45.sent), channel_id=1, source_target_pairs={{0,4},{4,0},{8,12},{12,8},{16,20},{20,16},{24,28},{28,24},{1,5},{5... | collective-permute-start | bytes 159752 | tf_op jit(solution)/shard_map/ppermute | solution.py:574
  29.0 1.9 %collective-permute-done.7.came.grad_one = f32[104,128]{1,0:T(8,128)S(1)} collective-permute-done((f32[104,128]{1,0:T(8,128)S(1)}, f32[104,128]{1,0:T(8,128)S(1)}, u32[]{:S(2)}, u32[]{:S(2)}) %collective-permute-start.7) | collective-permute-done | bytes 53280 | tf_op jit(solution)/shard_map/ppermute | solution.py:574
  31.1 1.5 %collective-permute-start.11 = (f32[40,128]{1,0:T(8,128)S(1)}, f32[40,128]{1,0:T(8,128)S(1)}, u32[]{:S(2)}, u32[]{:S(2)}) collective-permute-start(f32[40,128]{1,0:T(8,128)S(1)} %shard_map.135.refs_0_), channel_id=1, source_target_pairs={{0,24},{4,28},{8,16},{12,20},{16,8},{20,12},{24,0},{28,4},{1,25},{... | collective-permute-start | bytes 61448 | tf_op jit(solution)/shard_map/ppermute | solution.py:540
  33.2 2.3 %collective-permute-start.9 = (f32[40,128]{1,0:T(8,128)S(1)}, f32[40,128]{1,0:T(8,128)S(1)}, u32[]{:S(2)}, u32[]{:S(2)}) collective-permute-start(f32[40,128]{1,0:T(8,128)S(1)} %shard_map.135.refs_0_), channel_id=1, source_target_pairs={{0,8},{4,12},{8,0},{12,4},{16,24},{20,28},{24,16},{28,20},{1,9},{5... | collective-permute-start | bytes 61448 | tf_op jit(solution)/shard_map/ppermute | solution.py:540
  35.5 1.2 %collective-permute-done.11.refs_3_ = f32[40,128]{1,0:T(8,128)S(1)} collective-permute-done((f32[40,128]{1,0:T(8,128)S(1)}, f32[40,128]{1,0:T(8,128)S(1)}, u32[]{:S(2)}, u32[]{:S(2)}) %collective-permute-start.11) | collective-permute-done | bytes 20512 | tf_op jit(solution)/shard_map/ppermute | solution.py:540
  39.3 1.2 %collective-permute-done.12.passed = f32[104,256]{1,0:T(8,128)S(1)} collective-permute-done((f32[104,256]{1,0:T(8,128)S(1)}, f32[104,256]{1,0:T(8,128)S(1)}, u32[]{:S(2)}, u32[]{:S(2)}) %collective-permute-start.12) | collective-permute-done | bytes 106528 | tf_op jit(solution)/shard_map/ppermute | solution.py:547
  40.5 1.6 %collective-permute-start.13 = (f32[72,256]{1,0:T(8,128)S(1)}, f32[72,256]{1,0:T(8,128)S(1)}, u32[]{:S(2)}, u32[]{:S(2)}) collective-permute-start(f32[72,256]{1,0:T(8,128)S(1)} %slice_add_fusion.refs_0_), channel_id=1, source_target_pairs={{0,2},{1,3},{2,0},{3,1},{4,6},{5,7},{6,4},{7,5},{8,10},{9,11},{10,... | collective-permute-start | bytes 221192 | tf_op jit(solution)/shard_map/ppermute | solution.py:540
  42.2 2.7 %collective-permute-done.13.refs_1_ = f32[72,256]{1,0:T(8,128)S(1)} collective-permute-done((f32[72,256]{1,0:T(8,128)S(1)}, f32[72,256]{1,0:T(8,128)S(1)}, u32[]{:S(2)}, u32[]{:S(2)}) %collective-permute-start.13) | collective-permute-done | bytes 73760 | tf_op jit(solution)/shard_map/ppermute | solution.py:540
  44.9 1.2 %shard_map.138 = (f32[64,256]{1,0:T(8,128)S(1)}, f32[4,64,256]{2,1,0:T(8,128)S(1)}, f32[4,64,256]{2,1,0:T(8,128)S(1)}, f32[64,256]{1,0:T(8,128)S(1)}, f32[104,128]{1,0:T(8,128)S(1)}, /*index=5*/f32[64,128]{1,0:T(8,128)S(1)}) custom-call(f32[72,256]{1,0:T(8,128)S(1)} %slice_add_fusion.refs_0_, f32[72,256]{1,0:T(8,128)S(1)} %collective-permute-done.13.refs_1_, ...), custom_call_target="tpu_custom_call" | custom-call | tf_op jit(solution)/shard_map/pallas_call | solution.py:218
  48.0 2.4 %collective-permute-done.14.came.refs_10_ = f32[104,128]{1,0:T(8,128)S(1)} collective-permute-done((f32[104,128]{1,0:T(8,128)S(1)}, f32[104,128]{1,0:T(8,128)S(1)}, u32[]{:S(2)}, u32[]{:S(2)}) %collective-permute-start.14) | collective-permute-done | bytes 53280 | tf_op jit(solution)/shard_map/ppermute | solution.py:574
  50.5 2.2 %collective-permute-start.18 = (f32[40,128]{1,0:T(8,128)S(1)}, f32[40,128]{1,0:T(8,128)S(1)}, u32[]{:S(2)}, u32[]{:S(2)}) collective-permute-start(f32[40,128]{1,0:T(8,128)S(1)} %shard_map.139.refs_0_), channel_id=1, source_target_pairs={{0,24},{4,28},{8,16},{12,20},{16,8},{20,12},{24,0},{28,4},{1,25},{... | collective-permute-start | bytes 61448 | tf_op jit(solution)/shard_map/ppermute | solution.py:540
  53.4 1.5 %collective-permute-start.16 = (f32[40,128]{1,0:T(8,128)S(1)}, f32[40,128]{1,0:T(8,128)S(1)}, u32[]{:S(2)}, u32[]{:S(2)}) collective-permute-start(f32[40,128]{1,0:T(8,128)S(1)} %shard_map.139.refs_0_), channel_id=1, source_target_pairs={{0,8},{4,12},{8,0},{12,4},{16,24},{20,28},{24,16},{28,20},{1,9},{5... | collective-permute-start | bytes 61448 | tf_op jit(solution)/shard_map/ppermute | solution.py:540
  54.9 1.2 %collective-permute-done.18.refs_3_ = f32[40,128]{1,0:T(8,128)S(1)} collective-permute-done((f32[40,128]{1,0:T(8,128)S(1)}, f32[40,128]{1,0:T(8,128)S(1)}, u32[]{:S(2)}, u32[]{:S(2)}) %collective-permute-start.18) | collective-permute-done | bytes 20512 | tf_op jit(solution)/shard_map/ppermute | solution.py:540
  56.1 1.4 %collective-permute-done.17.refs_2_ = f32[40,128]{1,0:T(8,128)S(1)} collective-permute-done((f32[40,128]{1,0:T(8,128)S(1)}, f32[40,128]{1,0:T(8,128)S(1)}, u32[]{:S(2)}, u32[]{:S(2)}) %collective-permute-start.17) | collective-permute-done | bytes 20512 | tf_op jit(solution)/shard_map/ppermute | solution.py:540
  57.7 1.3 %collective-permute-start.21 = (f32[72,128]{1,0:T(8,128)S(1)}, f32[72,128]{1,0:T(8,128)S(1)}, u32[]{:S(2)}, u32[]{:S(2)}) collective-permute-start(f32[72,128]{1,0:T(8,128)S(1)} %get-tuple-element.59), channel_id=1, source_target_pairs={{0,3},{1,2},{2,1},{3,0},{4,7},{5,6},{6,5},{7,4},{8,11},{9,10},{10,... | collective-permute-start | bytes 110600 | tf_op jit(solution)/shard_map/ppermute | solution.py:559
  59.7 2.8 %collective-permute-done.20.refs_2_ = f32[8,128]{1,0:T(8,128)S(1)} collective-permute-done((f32[8,128]{1,0:T(8,128)S(1)}, f32[8,128]{1,0:T(8,128)S(1)}, u32[]{:S(2)}, u32[]{:S(2)}) %collective-permute-start.20) | collective-permute-done | bytes 4128 | tf_op jit(solution)/shard_map/ppermute | solution.py:559
  (38 shorter events, 13.4 us)
Async XLA Ops:
  4.6 5.6 %collective-permute-start = (f32[168,128]{1,0:T(8,128)S(1)}, f32[168,128]{1,0:T(8,128)S(1)}, u32[]{:S(2)}, u32[]{:S(2)}) collective-permute-start(f32[168,128]{1,0:T(8,128)S(1)} %get-tuple-element.35), channel_id=1, source_target_pairs={{0,4},{4,0},{8,12},{12,8},{16,20},{20,16},{24,28},{28,24},{1,5},{5... | collective-permute-start | bytes 258056 | tf_op jit(solution)/shard_map/ppermute | solution.py:574
  7.6 8.4 %collective-permute-start.4 = (f32[136,128]{1,0:T(8,128)S(1)}, f32[136,128]{1,0:T(8,128)S(1)}, u32[]{:S(2)}, u32[]{:S(2)}) collective-permute-start(f32[136,128]{1,0:T(8,128)S(1)} %get-tuple-element.36), channel_id=1, source_target_pairs={{5,9},{7,11},{9,5},{11,7},{13,17},{15,19},{17,13},{19,15},{21,25},... | collective-permute-start | bytes 208904 | tf_op jit(solution)/shard_map/ppermute | solution.py:584
  10.1 5.9 %collective-permute-start.3 = (f32[32,128]{1,0:T(8,128)S(1)}, f32[32,128]{1,0:T(8,128)S(1)}, u32[]{:S(2)}, u32[]{:S(2)}) collective-permute-start(f32[32,128]{1,0:T(8,128)S(1)} %slice_add_fusion.2.refs_0_), channel_id=1, source_target_pairs={{0,24},{4,28},{8,16},{12,20},{16,8},{20,12},{24,0},{28,4},{1,25},{... | collective-permute-start | bytes 49160 | tf_op jit(solution)/shard_map/ppermute | solution.py:540
  14.2 4.6 %collective-permute-start.2 = (f32[32,128]{1,0:T(8,128)S(1)}, f32[32,128]{1,0:T(8,128)S(1)}, u32[]{:S(2)}, u32[]{:S(2)}) collective-permute-start(f32[32,128]{1,0:T(8,128)S(1)} %slice_add_fusion.2.refs_0_), channel_id=1, source_target_pairs={{0,16},{4,20},{8,24},{12,28},{16,0},{20,4},{24,8},{28,12},{1,17},{... | collective-permute-start | bytes 49160 | tf_op jit(solution)/shard_map/ppermute | solution.py:540
  14.2 4.6 %collective-permute-start.1 = (f32[32,128]{1,0:T(8,128)S(1)}, f32[32,128]{1,0:T(8,128)S(1)}, u32[]{:S(2)}, u32[]{:S(2)}) collective-permute-start(f32[32,128]{1,0:T(8,128)S(1)} %slice_add_fusion.2.refs_0_), channel_id=1, source_target_pairs={{0,8},{4,12},{8,0},{12,4},{16,24},{20,28},{24,16},{28,20},{1,9},{5... | collective-permute-start | bytes 49160 | tf_op jit(solution)/shard_map/ppermute | solution.py:540
  14.8 4.0 %copy-start = (f32[64,64]{1,0:T(8,128)S(1)}, f32[64,64]{1,0:T(8,128)}, u32[]{:S(2)}) copy-start(f32[64,64]{1,0:T(8,128)} %refs_4_.2) | copy-start | bytes 49156
  19.9 1.4 %collective-permute-start.5 = (f32[136,256]{1,0:T(8,128)S(1)}, f32[136,256]{1,0:T(8,128)S(1)}, u32[]{:S(2)}, u32[]{:S(2)}) collective-permute-start(f32[136,256]{1,0:T(8,128)S(1)} %shard_map.132), channel_id=1, source_target_pairs={{0,1},{1,0},{2,3},{3,2},{4,5},{5,4},{6,7},{7,6},{8,9},{9,8},{10,11... | collective-permute-start | bytes 417800 | tf_op jit(solution)/shard_map/ppermute | solution.py:547
  21.3 4.3 %collective-permute-start.6 = (f32[64,256]{1,0:T(8,128)S(1)}, f32[64,256]{1,0:T(8,128)S(1)}, u32[]{:S(2)}, u32[]{:S(2)}) collective-permute-start(f32[64,256]{1,0:T(8,128)S(1)} %slice_add_fusion.1.refs_0_), channel_id=1, source_target_pairs={{0,2},{1,3},{2,0},{3,1},{4,6},{5,7},{6,4},{7,5},{8,10},{9,11},{10,... | collective-permute-start | bytes 196616 | tf_op jit(solution)/shard_map/ppermute | solution.py:540
  26.7 4.2 %collective-permute-start.7 = (f32[104,128]{1,0:T(8,128)S(1)}, f32[104,128]{1,0:T(8,128)S(1)}, u32[]{:S(2)}, u32[]{:S(2)}) collective-permute-start(f32[104,128]{1,0:T(8,128)S(1)} %get-tuple-element.45.sent), channel_id=1, source_target_pairs={{0,4},{4,0},{8,12},{12,8},{16,20},{20,16},{24,28},{28,24},{1,5},{5... | collective-permute-start | bytes 159752 | tf_op jit(solution)/shard_map/ppermute | solution.py:574
  28.3 0.7 %collective-permute-start.8 = (f32[64,128]{1,0:T(8,128)S(1)}, f32[64,128]{1,0:T(8,128)S(1)}, u32[]{:S(2)}, u32[]{:S(2)}) collective-permute-start(f32[64,128]{1,0:T(8,128)S(1)} %get-tuple-element.46.edge), channel_id=1, source_target_pairs={{5,9},{7,11},{9,5},{11,7},{13,17},{15,19},{17,13},{19,15},{21,25},... | collective-permute-start | bytes 98312 | tf_op jit(solution)/shard_map/ppermute | solution.py:584
  31.1 5.6 %collective-permute-start.11 = (f32[40,128]{1,0:T(8,128)S(1)}, f32[40,128]{1,0:T(8,128)S(1)}, u32[]{:S(2)}, u32[]{:S(2)}) collective-permute-start(f32[40,128]{1,0:T(8,128)S(1)} %shard_map.135.refs_0_), channel_id=1, source_target_pairs={{0,24},{4,28},{8,16},{12,20},{16,8},{20,12},{24,0},{28,4},{1,25},{... | collective-permute-start | bytes 61448 | tf_op jit(solution)/shard_map/ppermute | solution.py:540
  32.6 4.7 %collective-permute-start.10 = (f32[40,128]{1,0:T(8,128)S(1)}, f32[40,128]{1,0:T(8,128)S(1)}, u32[]{:S(2)}, u32[]{:S(2)}) collective-permute-start(f32[40,128]{1,0:T(8,128)S(1)} %shard_map.135.refs_0_), channel_id=1, source_target_pairs={{0,16},{4,20},{8,24},{12,28},{16,0},{20,4},{24,8},{28,12},{1,17},{... | collective-permute-start | bytes 61448 | tf_op jit(solution)/shard_map/ppermute | solution.py:540
  33.2 4.7 %collective-permute-start.9 = (f32[40,128]{1,0:T(8,128)S(1)}, f32[40,128]{1,0:T(8,128)S(1)}, u32[]{:S(2)}, u32[]{:S(2)}) collective-permute-start(f32[40,128]{1,0:T(8,128)S(1)} %shard_map.135.refs_0_), channel_id=1, source_target_pairs={{0,8},{4,12},{8,0},{12,4},{16,24},{20,28},{24,16},{28,20},{1,9},{5... | collective-permute-start | bytes 61448 | tf_op jit(solution)/shard_map/ppermute | solution.py:540
  39.1 1.4 %collective-permute-start.12 = (f32[104,256]{1,0:T(8,128)S(1)}, f32[104,256]{1,0:T(8,128)S(1)}, u32[]{:S(2)}, u32[]{:S(2)}) collective-permute-start(f32[104,256]{1,0:T(8,128)S(1)} %get-tuple-element.47), channel_id=1, source_target_pairs={{0,1},{1,0},{2,3},{3,2},{4,5},{5,4},{6,7},{7,6},{8,9},{9,8},{10,11... | collective-permute-start | bytes 319496 | tf_op jit(solution)/shard_map/ppermute | solution.py:547
  40.5 4.4 %collective-permute-start.13 = (f32[72,256]{1,0:T(8,128)S(1)}, f32[72,256]{1,0:T(8,128)S(1)}, u32[]{:S(2)}, u32[]{:S(2)}) collective-permute-start(f32[72,256]{1,0:T(8,128)S(1)} %slice_add_fusion.refs_0_), channel_id=1, source_target_pairs={{0,2},{1,3},{2,0},{3,1},{4,6},{5,7},{6,4},{7,5},{8,10},{9,11},{10,... | collective-permute-start | bytes 221192 | tf_op jit(solution)/shard_map/ppermute | solution.py:540
  46.1 4.2 %collective-permute-start.14 = (f32[104,128]{1,0:T(8,128)S(1)}, f32[104,128]{1,0:T(8,128)S(1)}, u32[]{:S(2)}, u32[]{:S(2)}) collective-permute-start(f32[104,128]{1,0:T(8,128)S(1)} %get-tuple-element.56.sent), channel_id=1, source_target_pairs={{0,4},{4,0},{8,12},{12,8},{16,20},{20,16},{24,28},{28,24},{1,5},{5... | collective-permute-start | bytes 159752 | tf_op jit(solution)/shard_map/ppermute | solution.py:574
  47.3 0.7 %collective-permute-start.15 = (f32[64,128]{1,0:T(8,128)S(1)}, f32[64,128]{1,0:T(8,128)S(1)}, u32[]{:S(2)}, u32[]{:S(2)}) collective-permute-start(f32[64,128]{1,0:T(8,128)S(1)} %get-tuple-element.57.edge), channel_id=1, source_target_pairs={{5,9},{7,11},{9,5},{11,7},{13,17},{15,19},{17,13},{19,15},{21,25},... | collective-permute-start | bytes 98312 | tf_op jit(solution)/shard_map/ppermute | solution.py:584
  50.5 5.6 %collective-permute-start.18 = (f32[40,128]{1,0:T(8,128)S(1)}, f32[40,128]{1,0:T(8,128)S(1)}, u32[]{:S(2)}, u32[]{:S(2)}) collective-permute-start(f32[40,128]{1,0:T(8,128)S(1)} %shard_map.139.refs_0_), channel_id=1, source_target_pairs={{0,24},{4,28},{8,16},{12,20},{16,8},{20,12},{24,0},{28,4},{1,25},{... | collective-permute-start | bytes 61448 | tf_op jit(solution)/shard_map/ppermute | solution.py:540
  52.7 4.8 %collective-permute-start.17 = (f32[40,128]{1,0:T(8,128)S(1)}, f32[40,128]{1,0:T(8,128)S(1)}, u32[]{:S(2)}, u32[]{:S(2)}) collective-permute-start(f32[40,128]{1,0:T(8,128)S(1)} %shard_map.139.refs_0_), channel_id=1, source_target_pairs={{0,16},{4,20},{8,24},{12,28},{16,0},{20,4},{24,8},{28,12},{1,17},{... | collective-permute-start | bytes 61448 | tf_op jit(solution)/shard_map/ppermute | solution.py:540
  53.4 4.2 %collective-permute-start.16 = (f32[40,128]{1,0:T(8,128)S(1)}, f32[40,128]{1,0:T(8,128)S(1)}, u32[]{:S(2)}, u32[]{:S(2)}) collective-permute-start(f32[40,128]{1,0:T(8,128)S(1)} %shard_map.139.refs_0_), channel_id=1, source_target_pairs={{0,8},{4,12},{8,0},{12,4},{16,24},{20,28},{24,16},{28,20},{1,9},{5... | collective-permute-start | bytes 61448 | tf_op jit(solution)/shard_map/ppermute | solution.py:540
  57.7 4.9 %collective-permute-start.21 = (f32[72,128]{1,0:T(8,128)S(1)}, f32[72,128]{1,0:T(8,128)S(1)}, u32[]{:S(2)}, u32[]{:S(2)}) collective-permute-start(f32[72,128]{1,0:T(8,128)S(1)} %get-tuple-element.59), channel_id=1, source_target_pairs={{0,3},{1,2},{2,1},{3,0},{4,7},{5,6},{6,5},{7,4},{8,11},{9,10},{10,... | collective-permute-start | bytes 110600 | tf_op jit(solution)/shard_map/ppermute | solution.py:559
  58.9 3.6 %collective-permute-start.20 = (f32[8,128]{1,0:T(8,128)S(1)}, f32[8,128]{1,0:T(8,128)S(1)}, u32[]{:S(2)}, u32[]{:S(2)}) collective-permute-start(f32[8,128]{1,0:T(8,128)S(1)} %get-tuple-element.58.refs_0_), channel_id=1, source_target_pairs={{0,2},{1,3},{2,0},{3,1},{4,6},{5,7},{6,4},{7,5},{8,10},{9,11},{10,... | collective-permute-start | bytes 12296 | tf_op jit(solution)/shard_map/ppermute | solution.py:559
  59.5 3.1 %collective-permute-start.19 = (f32[8,128]{1,0:T(8,128)S(1)}, f32[8,128]{1,0:T(8,128)S(1)}, u32[]{:S(2)}, u32[]{:S(2)}) collective-permute-start(f32[8,128]{1,0:T(8,128)S(1)} %get-tuple-element.58.refs_0_), channel_id=1, source_target_pairs={{0,1},{1,0},{2,3},{3,2},{4,5},{5,4},{6,7},{7,6},{8,9},{9,8},{10,11... | collective-permute-start | bytes 12296 | tf_op jit(solution)/shard_map/ppermute | solution.py:559

commit v12 on v11

--- a/solution.py
+++ b/solution.py
@@ -11,7 +11,7 @@
 COLS = 128
 LANES = 128
 GROUP = 8
-CHUNK = 16
+CHUNK = 24
 SHRINK_SCALE = 0.4
 TINY = 1e-06
 VMEM = pltpu.VMEM

time: 63.6 us -> 63.4 us (level)
  no operation moved by 1% of the time
where the time goes in v12:
time: 63.4 us; the launch traced here: 63.2 us
  starting transfers between devices  26.6 us (42%)
  waiting for transfers between devices  24.8 us (39%)
  Pallas kernels  11 us (17%)
  between operations  0.8 us (1%)
    ppermute x11, starting transfers between devices, summing(): lax.ppermute(total, axis, [(i, i ^ k * stride) for i in range(count)])  16.7 us
    ppermute x11, waiting for transfers between devices, summing(): lax.ppermute(total, axis, [(i, i ^ k * stride) for i in range(count)])  13.2 us
    pallas_call x13, Pallas kernels, call(): pl.pallas_call(body, out_shape=shapes, in_specs=[pl.BlockSpec(memory_spac...  11 us
    ppermute x3, waiting for transfers between devices, from_partner(): lax.ppermute(array, 'cell', [(i, i ^ 1) for i in range(lax.axis_size('cel...  6.16 us
    ppermute x3, starting transfers between devices, from_partner(): lax.ppermute(array, 'cell', [(i, i ^ 1) for i in range(lax.axis_size('cel...  5.8 us
    ppermute x3, waiting for transfers between devices, last_sensor_parts(): lax.ppermute(array, 'sensor', [(i, i ^ k) for i in range(count)])  2.83 us
    ppermute x2, waiting for transfers between devices, sensor_hop(): lax.ppermute(array, 'sensor', [(i, i ^ 1) for i in range(lax.axis_size('s...  2.54 us
    ppermute x3, starting transfers between devices, from_other(): return lax.ppermute(array, ('cell', 'sensor'), pairs)  1.96 us
  transfers between devices with their start and end apart: 22, of which 14 were waited for; matrix products, arithmetic and copies ran while one was open for 0% of the time, Pallas kernels for 2%

profile of v12, /device:TPU:0, one launch (start us, length us, event | category | flops | bytes accessed | tf_op | source)
XLA Modules:
  0.0 63.2 jit_solution(881775012566156083)
XLA Ops:
  0.6 3.7 %shard_map.130 = (f32[168,128]{1,0:T(8,128)S(1)}, f32[136,128]{1,0:T(8,128)S(1)}, f32[8,256]{1,0:T(8,128)S(1)}, f32[8,256]{1,0:T(8,128)S(1)}, bf16[2,65,64,256]{...) custom-call(bf16[2,65,64,256]{3,2,1,0:T(8,128)(2,1)} %refs_0_.1, ...), custom_call_target="tpu_custom_call" | custom-call | tf_op jit(solution)/shard_map/pallas_call | solution.py:218
  4.3 3.0 %collective-permute-start = (f32[168,128]{1,0:T(8,128)S(1)}, f32[168,128]{1,0:T(8,128)S(1)}, u32[]{:S(2)}, u32[]{:S(2)}) collective-permute-start(f32[168,128]{1,0:T(8,128)S(1)} %get-tuple-element.35), channel_id=1, source_target_pairs={{0,4},{4,0},{8,12},{12,8},{16,20},{20,16},{24,28},{28,24},{1,5},{5... | collective-permute-start | bytes 258056 | tf_op jit(solution)/shard_map/ppermute | solution.py:574
  8.0 1.9 %collective-permute-done.came.one.refs_10_ = f32[168,128]{1,0:T(8,128)S(1)} collective-permute-done((f32[168,128]{1,0:T(8,128)S(1)}, f32[168,128]{1,0:T(8,128)S(1)}, u32[]{:S(2)}, u32[]{:S(2)}) %collective-permute-start) | collective-permute-done | bytes 86048 | tf_op jit(solution)/shard_map/ppermute | solution.py:574
  9.9 4.0 %collective-permute-start.3 = (f32[32,128]{1,0:T(8,128)S(1)}, f32[32,128]{1,0:T(8,128)S(1)}, u32[]{:S(2)}, u32[]{:S(2)}) collective-permute-start(f32[32,128]{1,0:T(8,128)S(1)} %slice_add_fusion.2.refs_0_), channel_id=1, source_target_pairs={{0,24},{4,28},{8,16},{12,20},{16,8},{20,12},{24,0},{28,4},{1,25},{... | collective-permute-start | bytes 49160 | tf_op jit(solution)/shard_map/ppermute | solution.py:540
  15.8 2.8 %collective-permute-done.2.refs_2_ = f32[32,128]{1,0:T(8,128)S(1)} collective-permute-done((f32[32,128]{1,0:T(8,128)S(1)}, f32[32,128]{1,0:T(8,128)S(1)}, u32[]{:S(2)}, u32[]{:S(2)}) %collective-permute-start.2) | collective-permute-done | bytes 16416 | tf_op jit(solution)/shard_map/ppermute | solution.py:540
  19.7 1.3 %collective-permute-done.5.passed = f32[136,256]{1,0:T(8,128)S(1)} collective-permute-done((f32[136,256]{1,0:T(8,128)S(1)}, f32[136,256]{1,0:T(8,128)S(1)}, u32[]{:S(2)}, u32[]{:S(2)}) %collective-permute-start.5) | collective-permute-done | bytes 139296 | tf_op jit(solution)/shard_map/ppermute | solution.py:547
  21.1 1.6 %collective-permute-start.6 = (f32[64,256]{1,0:T(8,128)S(1)}, f32[64,256]{1,0:T(8,128)S(1)}, u32[]{:S(2)}, u32[]{:S(2)}) collective-permute-start(f32[64,256]{1,0:T(8,128)S(1)} %slice_add_fusion.1.refs_0_), channel_id=1, source_target_pairs={{0,2},{1,3},{2,0},{3,1},{4,6},{5,7},{6,4},{7,5},{8,10},{9,11},{10,... | collective-permute-start | bytes 196616 | tf_op jit(solution)/shard_map/ppermute | solution.py:540
  22.8 2.7 %collective-permute-done.6.refs_1_ = f32[64,256]{1,0:T(8,128)S(1)} collective-permute-done((f32[64,256]{1,0:T(8,128)S(1)}, f32[64,256]{1,0:T(8,128)S(1)}, u32[]{:S(2)}, u32[]{:S(2)}) %collective-permute-start.6) | collective-permute-done | bytes 65568 | tf_op jit(solution)/shard_map/ppermute | solution.py:540
  26.5 1.6 %collective-permute-start.7 = (f32[104,128]{1,0:T(8,128)S(1)}, f32[104,128]{1,0:T(8,128)S(1)}, u32[]{:S(2)}, u32[]{:S(2)}) collective-permute-start(f32[104,128]{1,0:T(8,128)S(1)} %get-tuple-element.45.sent), channel_id=1, source_target_pairs={{0,4},{4,0},{8,12},{12,8},{16,20},{20,16},{24,28},{28,24},{1,5},{5... | collective-permute-start | bytes 159752 | tf_op jit(solution)/shard_map/ppermute | solution.py:574
  28.7 1.9 %collective-permute-done.7.came.grad_one = f32[104,128]{1,0:T(8,128)S(1)} collective-permute-done((f32[104,128]{1,0:T(8,128)S(1)}, f32[104,128]{1,0:T(8,128)S(1)}, u32[]{:S(2)}, u32[]{:S(2)}) %collective-permute-start.7) | collective-permute-done | bytes 53280 | tf_op jit(solution)/shard_map/ppermute | solution.py:574
  30.8 1.5 %collective-permute-start.11 = (f32[40,128]{1,0:T(8,128)S(1)}, f32[40,128]{1,0:T(8,128)S(1)}, u32[]{:S(2)}, u32[]{:S(2)}) collective-permute-start(f32[40,128]{1,0:T(8,128)S(1)} %shard_map.135.refs_0_), channel_id=1, source_target_pairs={{0,24},{4,28},{8,16},{12,20},{16,8},{20,12},{24,0},{28,4},{1,25},{... | collective-permute-start | bytes 61448 | tf_op jit(solution)/shard_map/ppermute | solution.py:540
  33.0 2.3 %collective-permute-start.9 = (f32[40,128]{1,0:T(8,128)S(1)}, f32[40,128]{1,0:T(8,128)S(1)}, u32[]{:S(2)}, u32[]{:S(2)}) collective-permute-start(f32[40,128]{1,0:T(8,128)S(1)} %shard_map.135.refs_0_), channel_id=1, source_target_pairs={{0,8},{4,12},{8,0},{12,4},{16,24},{20,28},{24,16},{28,20},{1,9},{5... | collective-permute-start | bytes 61448 | tf_op jit(solution)/shard_map/ppermute | solution.py:540
  35.3 1.2 %collective-permute-done.11.refs_3_ = f32[40,128]{1,0:T(8,128)S(1)} collective-permute-done((f32[40,128]{1,0:T(8,128)S(1)}, f32[40,128]{1,0:T(8,128)S(1)}, u32[]{:S(2)}, u32[]{:S(2)}) %collective-permute-start.11) | collective-permute-done | bytes 20512 | tf_op jit(solution)/shard_map/ppermute | solution.py:540
  39.0 1.2 %collective-permute-done.12.passed = f32[104,256]{1,0:T(8,128)S(1)} collective-permute-done((f32[104,256]{1,0:T(8,128)S(1)}, f32[104,256]{1,0:T(8,128)S(1)}, u32[]{:S(2)}, u32[]{:S(2)}) %collective-permute-start.12) | collective-permute-done | bytes 106528 | tf_op jit(solution)/shard_map/ppermute | solution.py:547
  40.2 1.6 %collective-permute-start.13 = (f32[72,256]{1,0:T(8,128)S(1)}, f32[72,256]{1,0:T(8,128)S(1)}, u32[]{:S(2)}, u32[]{:S(2)}) collective-permute-start(f32[72,256]{1,0:T(8,128)S(1)} %slice_add_fusion.refs_0_), channel_id=1, source_target_pairs={{0,2},{1,3},{2,0},{3,1},{4,6},{5,7},{6,4},{7,5},{8,10},{9,11},{10,... | collective-permute-start | bytes 221192 | tf_op jit(solution)/shard_map/ppermute | solution.py:540
  41.9 2.7 %collective-permute-done.13.refs_1_ = f32[72,256]{1,0:T(8,128)S(1)} collective-permute-done((f32[72,256]{1,0:T(8,128)S(1)}, f32[72,256]{1,0:T(8,128)S(1)}, u32[]{:S(2)}, u32[]{:S(2)}) %collective-permute-start.13) | collective-permute-done | bytes 73760 | tf_op jit(solution)/shard_map/ppermute | solution.py:540
  44.6 1.2 %shard_map.138 = (f32[64,256]{1,0:T(8,128)S(1)}, f32[4,64,256]{2,1,0:T(8,128)S(1)}, f32[4,64,256]{2,1,0:T(8,128)S(1)}, f32[64,256]{1,0:T(8,128)S(1)}, f32[104,128]{1,0:T(8,128)S(1)}, /*index=5*/f32[64,128]{1,0:T(8,128)S(1)}) custom-call(f32[72,256]{1,0:T(8,128)S(1)} %slice_add_fusion.refs_0_, f32[72,256]{1,0:T(8,128)S(1)} %collective-permute-done.13.refs_1_, ...), custom_call_target="tpu_custom_call" | custom-call | tf_op jit(solution)/shard_map/pallas_call | solution.py:218
  47.7 2.4 %collective-permute-done.14.came.refs_10_ = f32[104,128]{1,0:T(8,128)S(1)} collective-permute-done((f32[104,128]{1,0:T(8,128)S(1)}, f32[104,128]{1,0:T(8,128)S(1)}, u32[]{:S(2)}, u32[]{:S(2)}) %collective-permute-start.14) | collective-permute-done | bytes 53280 | tf_op jit(solution)/shard_map/ppermute | solution.py:574
  50.2 2.2 %collective-permute-start.18 = (f32[40,128]{1,0:T(8,128)S(1)}, f32[40,128]{1,0:T(8,128)S(1)}, u32[]{:S(2)}, u32[]{:S(2)}) collective-permute-start(f32[40,128]{1,0:T(8,128)S(1)} %shard_map.139.refs_0_), channel_id=1, source_target_pairs={{0,24},{4,28},{8,16},{12,20},{16,8},{20,12},{24,0},{28,4},{1,25},{... | collective-permute-start | bytes 61448 | tf_op jit(solution)/shard_map/ppermute | solution.py:540
  53.1 1.6 %collective-permute-start.16 = (f32[40,128]{1,0:T(8,128)S(1)}, f32[40,128]{1,0:T(8,128)S(1)}, u32[]{:S(2)}, u32[]{:S(2)}) collective-permute-start(f32[40,128]{1,0:T(8,128)S(1)} %shard_map.139.refs_0_), channel_id=1, source_target_pairs={{0,8},{4,12},{8,0},{12,4},{16,24},{20,28},{24,16},{28,20},{1,9},{5... | collective-permute-start | bytes 61448 | tf_op jit(solution)/shard_map/ppermute | solution.py:540
  54.7 1.2 %collective-permute-done.18.refs_3_ = f32[40,128]{1,0:T(8,128)S(1)} collective-permute-done((f32[40,128]{1,0:T(8,128)S(1)}, f32[40,128]{1,0:T(8,128)S(1)}, u32[]{:S(2)}, u32[]{:S(2)}) %collective-permute-start.18) | collective-permute-done | bytes 20512 | tf_op jit(solution)/shard_map/ppermute | solution.py:540
  55.9 1.4 %collective-permute-done.17.refs_2_ = f32[40,128]{1,0:T(8,128)S(1)} collective-permute-done((f32[40,128]{1,0:T(8,128)S(1)}, f32[40,128]{1,0:T(8,128)S(1)}, u32[]{:S(2)}, u32[]{:S(2)}) %collective-permute-start.17) | collective-permute-done | bytes 20512 | tf_op jit(solution)/shard_map/ppermute | solution.py:540
  57.4 1.3 %collective-permute-start.21 = (f32[72,128]{1,0:T(8,128)S(1)}, f32[72,128]{1,0:T(8,128)S(1)}, u32[]{:S(2)}, u32[]{:S(2)}) collective-permute-start(f32[72,128]{1,0:T(8,128)S(1)} %get-tuple-element.59), channel_id=1, source_target_pairs={{0,3},{1,2},{2,1},{3,0},{4,7},{5,6},{6,5},{7,4},{8,11},{9,10},{10,... | collective-permute-start | bytes 110600 | tf_op jit(solution)/shard_map/ppermute | solution.py:559
  59.5 2.8 %collective-permute-done.20.refs_2_ = f32[8,128]{1,0:T(8,128)S(1)} collective-permute-done((f32[8,128]{1,0:T(8,128)S(1)}, f32[8,128]{1,0:T(8,128)S(1)}, u32[]{:S(2)}, u32[]{:S(2)}) %collective-permute-start.20) | collective-permute-done | bytes 4128 | tf_op jit(solution)/shard_map/ppermute | solution.py:559
  (38 shorter events, 13.3 us)
Async XLA Ops:
  4.3 5.6 %collective-permute-start = (f32[168,128]{1,0:T(8,128)S(1)}, f32[168,128]{1,0:T(8,128)S(1)}, u32[]{:S(2)}, u32[]{:S(2)}) collective-permute-start(f32[168,128]{1,0:T(8,128)S(1)} %get-tuple-element.35), channel_id=1, source_target_pairs={{0,4},{4,0},{8,12},{12,8},{16,20},{20,16},{24,28},{28,24},{1,5},{5... | collective-permute-start | bytes 258056 | tf_op jit(solution)/shard_map/ppermute | solution.py:574
  7.4 8.4 %collective-permute-start.4 = (f32[136,128]{1,0:T(8,128)S(1)}, f32[136,128]{1,0:T(8,128)S(1)}, u32[]{:S(2)}, u32[]{:S(2)}) collective-permute-start(f32[136,128]{1,0:T(8,128)S(1)} %get-tuple-element.36), channel_id=1, source_target_pairs={{5,9},{7,11},{9,5},{11,7},{13,17},{15,19},{17,13},{19,15},{21,25},... | collective-permute-start | bytes 208904 | tf_op jit(solution)/shard_map/ppermute | solution.py:584
  9.9 5.9 %collective-permute-start.3 = (f32[32,128]{1,0:T(8,128)S(1)}, f32[32,128]{1,0:T(8,128)S(1)}, u32[]{:S(2)}, u32[]{:S(2)}) collective-permute-start(f32[32,128]{1,0:T(8,128)S(1)} %slice_add_fusion.2.refs_0_), channel_id=1, source_target_pairs={{0,24},{4,28},{8,16},{12,20},{16,8},{20,12},{24,0},{28,4},{1,25},{... | collective-permute-start | bytes 49160 | tf_op jit(solution)/shard_map/ppermute | solution.py:540
  13.9 4.6 %collective-permute-start.2 = (f32[32,128]{1,0:T(8,128)S(1)}, f32[32,128]{1,0:T(8,128)S(1)}, u32[]{:S(2)}, u32[]{:S(2)}) collective-permute-start(f32[32,128]{1,0:T(8,128)S(1)} %slice_add_fusion.2.refs_0_), channel_id=1, source_target_pairs={{0,16},{4,20},{8,24},{12,28},{16,0},{20,4},{24,8},{28,12},{1,17},{... | collective-permute-start | bytes 49160 | tf_op jit(solution)/shard_map/ppermute | solution.py:540
  13.9 4.6 %collective-permute-start.1 = (f32[32,128]{1,0:T(8,128)S(1)}, f32[32,128]{1,0:T(8,128)S(1)}, u32[]{:S(2)}, u32[]{:S(2)}) collective-permute-start(f32[32,128]{1,0:T(8,128)S(1)} %slice_add_fusion.2.refs_0_), channel_id=1, source_target_pairs={{0,8},{4,12},{8,0},{12,4},{16,24},{20,28},{24,16},{28,20},{1,9},{5... | collective-permute-start | bytes 49160 | tf_op jit(solution)/shard_map/ppermute | solution.py:540
  14.6 4.0 %copy-start = (f32[64,64]{1,0:T(8,128)S(1)}, f32[64,64]{1,0:T(8,128)}, u32[]{:S(2)}) copy-start(f32[64,64]{1,0:T(8,128)} %refs_4_.2) | copy-start | bytes 49156
  19.6 1.4 %collective-permute-start.5 = (f32[136,256]{1,0:T(8,128)S(1)}, f32[136,256]{1,0:T(8,128)S(1)}, u32[]{:S(2)}, u32[]{:S(2)}) collective-permute-start(f32[136,256]{1,0:T(8,128)S(1)} %shard_map.132), channel_id=1, source_target_pairs={{0,1},{1,0},{2,3},{3,2},{4,5},{5,4},{6,7},{7,6},{8,9},{9,8},{10,11... | collective-permute-start | bytes 417800 | tf_op jit(solution)/shard_map/ppermute | solution.py:547
  21.1 4.3 %collective-permute-start.6 = (f32[64,256]{1,0:T(8,128)S(1)}, f32[64,256]{1,0:T(8,128)S(1)}, u32[]{:S(2)}, u32[]{:S(2)}) collective-permute-start(f32[64,256]{1,0:T(8,128)S(1)} %slice_add_fusion.1.refs_0_), channel_id=1, source_target_pairs={{0,2},{1,3},{2,0},{3,1},{4,6},{5,7},{6,4},{7,5},{8,10},{9,11},{10,... | collective-permute-start | bytes 196616 | tf_op jit(solution)/shard_map/ppermute | solution.py:540
  26.5 4.2 %collective-permute-start.7 = (f32[104,128]{1,0:T(8,128)S(1)}, f32[104,128]{1,0:T(8,128)S(1)}, u32[]{:S(2)}, u32[]{:S(2)}) collective-permute-start(f32[104,128]{1,0:T(8,128)S(1)} %get-tuple-element.45.sent), channel_id=1, source_target_pairs={{0,4},{4,0},{8,12},{12,8},{16,20},{20,16},{24,28},{28,24},{1,5},{5... | collective-permute-start | bytes 159752 | tf_op jit(solution)/shard_map/ppermute | solution.py:574
  28.1 0.7 %collective-permute-start.8 = (f32[64,128]{1,0:T(8,128)S(1)}, f32[64,128]{1,0:T(8,128)S(1)}, u32[]{:S(2)}, u32[]{:S(2)}) collective-permute-start(f32[64,128]{1,0:T(8,128)S(1)} %get-tuple-element.46.edge), channel_id=1, source_target_pairs={{5,9},{7,11},{9,5},{11,7},{13,17},{15,19},{17,13},{19,15},{21,25},... | collective-permute-start | bytes 98312 | tf_op jit(solution)/shard_map/ppermute | solution.py:584
  30.8 5.6 %collective-permute-start.11 = (f32[40,128]{1,0:T(8,128)S(1)}, f32[40,128]{1,0:T(8,128)S(1)}, u32[]{:S(2)}, u32[]{:S(2)}) collective-permute-start(f32[40,128]{1,0:T(8,128)S(1)} %shard_map.135.refs_0_), channel_id=1, source_target_pairs={{0,24},{4,28},{8,16},{12,20},{16,8},{20,12},{24,0},{28,4},{1,25},{... | collective-permute-start | bytes 61448 | tf_op jit(solution)/shard_map/ppermute | solution.py:540
  32.4 4.7 %collective-permute-start.10 = (f32[40,128]{1,0:T(8,128)S(1)}, f32[40,128]{1,0:T(8,128)S(1)}, u32[]{:S(2)}, u32[]{:S(2)}) collective-permute-start(f32[40,128]{1,0:T(8,128)S(1)} %shard_map.135.refs_0_), channel_id=1, source_target_pairs={{0,16},{4,20},{8,24},{12,28},{16,0},{20,4},{24,8},{28,12},{1,17},{... | collective-permute-start | bytes 61448 | tf_op jit(solution)/shard_map/ppermute | solution.py:540
  33.0 4.7 %collective-permute-start.9 = (f32[40,128]{1,0:T(8,128)S(1)}, f32[40,128]{1,0:T(8,128)S(1)}, u32[]{:S(2)}, u32[]{:S(2)}) collective-permute-start(f32[40,128]{1,0:T(8,128)S(1)} %shard_map.135.refs_0_), channel_id=1, source_target_pairs={{0,8},{4,12},{8,0},{12,4},{16,24},{20,28},{24,16},{28,20},{1,9},{5... | collective-permute-start | bytes 61448 | tf_op jit(solution)/shard_map/ppermute | solution.py:540
  38.8 1.4 %collective-permute-start.12 = (f32[104,256]{1,0:T(8,128)S(1)}, f32[104,256]{1,0:T(8,128)S(1)}, u32[]{:S(2)}, u32[]{:S(2)}) collective-permute-start(f32[104,256]{1,0:T(8,128)S(1)} %get-tuple-element.47), channel_id=1, source_target_pairs={{0,1},{1,0},{2,3},{3,2},{4,5},{5,4},{6,7},{7,6},{8,9},{9,8},{10,11... | collective-permute-start | bytes 319496 | tf_op jit(solution)/shard_map/ppermute | solution.py:547
  40.2 4.4 %collective-permute-start.13 = (f32[72,256]{1,0:T(8,128)S(1)}, f32[72,256]{1,0:T(8,128)S(1)}, u32[]{:S(2)}, u32[]{:S(2)}) collective-permute-start(f32[72,256]{1,0:T(8,128)S(1)} %slice_add_fusion.refs_0_), channel_id=1, source_target_pairs={{0,2},{1,3},{2,0},{3,1},{4,6},{5,7},{6,4},{7,5},{8,10},{9,11},{10,... | collective-permute-start | bytes 221192 | tf_op jit(solution)/shard_map/ppermute | solution.py:540
  45.9 4.2 %collective-permute-start.14 = (f32[104,128]{1,0:T(8,128)S(1)}, f32[104,128]{1,0:T(8,128)S(1)}, u32[]{:S(2)}, u32[]{:S(2)}) collective-permute-start(f32[104,128]{1,0:T(8,128)S(1)} %get-tuple-element.56.sent), channel_id=1, source_target_pairs={{0,4},{4,0},{8,12},{12,8},{16,20},{20,16},{24,28},{28,24},{1,5},{5... | collective-permute-start | bytes 159752 | tf_op jit(solution)/shard_map/ppermute | solution.py:574
  47.1 0.7 %collective-permute-start.15 = (f32[64,128]{1,0:T(8,128)S(1)}, f32[64,128]{1,0:T(8,128)S(1)}, u32[]{:S(2)}, u32[]{:S(2)}) collective-permute-start(f32[64,128]{1,0:T(8,128)S(1)} %get-tuple-element.57.edge), channel_id=1, source_target_pairs={{5,9},{7,11},{9,5},{11,7},{13,17},{15,19},{17,13},{19,15},{21,25},... | collective-permute-start | bytes 98312 | tf_op jit(solution)/shard_map/ppermute | solution.py:584
  50.2 5.6 %collective-permute-start.18 = (f32[40,128]{1,0:T(8,128)S(1)}, f32[40,128]{1,0:T(8,128)S(1)}, u32[]{:S(2)}, u32[]{:S(2)}) collective-permute-start(f32[40,128]{1,0:T(8,128)S(1)} %shard_map.139.refs_0_), channel_id=1, source_target_pairs={{0,24},{4,28},{8,16},{12,20},{16,8},{20,12},{24,0},{28,4},{1,25},{... | collective-permute-start | bytes 61448 | tf_op jit(solution)/shard_map/ppermute | solution.py:540
  52.5 4.8 %collective-permute-start.17 = (f32[40,128]{1,0:T(8,128)S(1)}, f32[40,128]{1,0:T(8,128)S(1)}, u32[]{:S(2)}, u32[]{:S(2)}) collective-permute-start(f32[40,128]{1,0:T(8,128)S(1)} %shard_map.139.refs_0_), channel_id=1, source_target_pairs={{0,16},{4,20},{8,24},{12,28},{16,0},{20,4},{24,8},{28,12},{1,17},{... | collective-permute-start | bytes 61448 | tf_op jit(solution)/shard_map/ppermute | solution.py:540
  53.1 4.2 %collective-permute-start.16 = (f32[40,128]{1,0:T(8,128)S(1)}, f32[40,128]{1,0:T(8,128)S(1)}, u32[]{:S(2)}, u32[]{:S(2)}) collective-permute-start(f32[40,128]{1,0:T(8,128)S(1)} %shard_map.139.refs_0_), channel_id=1, source_target_pairs={{0,8},{4,12},{8,0},{12,4},{16,24},{20,28},{24,16},{28,20},{1,9},{5... | collective-permute-start | bytes 61448 | tf_op jit(solution)/shard_map/ppermute | solution.py:540
  57.4 4.9 %collective-permute-start.21 = (f32[72,128]{1,0:T(8,128)S(1)}, f32[72,128]{1,0:T(8,128)S(1)}, u32[]{:S(2)}, u32[]{:S(2)}) collective-permute-start(f32[72,128]{1,0:T(8,128)S(1)} %get-tuple-element.59), channel_id=1, source_target_pairs={{0,3},{1,2},{2,1},{3,0},{4,7},{5,6},{6,5},{7,4},{8,11},{9,10},{10,... | collective-permute-start | bytes 110600 | tf_op jit(solution)/shard_map/ppermute | solution.py:559
  58.7 3.6 %collective-permute-start.20 = (f32[8,128]{1,0:T(8,128)S(1)}, f32[8,128]{1,0:T(8,128)S(1)}, u32[]{:S(2)}, u32[]{:S(2)}) collective-permute-start(f32[8,128]{1,0:T(8,128)S(1)} %get-tuple-element.58.refs_0_), channel_id=1, source_target_pairs={{0,2},{1,3},{2,0},{3,1},{4,6},{5,7},{6,4},{7,5},{8,10},{9,11},{10,... | collective-permute-start | bytes 12296 | tf_op jit(solution)/shard_map/ppermute | solution.py:559
  59.2 3.1 %collective-permute-start.19 = (f32[8,128]{1,0:T(8,128)S(1)}, f32[8,128]{1,0:T(8,128)S(1)}, u32[]{:S(2)}, u32[]{:S(2)}) collective-permute-start(f32[8,128]{1,0:T(8,128)S(1)} %get-tuple-element.58.refs_0_), channel_id=1, source_target_pairs={{0,1},{1,0},{2,3},{3,2},{4,5},{5,4},{6,7},{7,6},{8,9},{9,8},{10,11... | collective-permute-start | bytes 12296 | tf_op jit(solution)/shard_map/ppermute | solution.py:559

commit v13 on v12

--- a/solution.py
+++ b/solution.py
@@ -548,9 +548,11 @@
 
 
 def sensor_parts(array, rows):
-    passed = sensor_hop(array)
-    total = array[:rows] + passed[:rows]
-    return summing([total], "sensor", 2, stages_of(lax.axis_size("sensor") // 2, 2)), passed
+    count = lax.axis_size("sensor")
+    own, passed = array[:rows], sensor_hop(array)
+    far = [lax.ppermute(own, "sensor", [(i, i ^ k) for i in range(count)]) for k in (2, 3)]
+    parts = [own, passed[:rows]] + far
+    return summing(parts, "sensor", 4, stages_of(count // 4, 4)), passed
 
 
 def last_sensor_parts(scalars, passing):

time: 63.4 us -> 64.7 us (1.021)
  starting transfers between devices: 26.6 us -> 27.7 us
    ppermute x0 -> x4, waiting for transfers between devices: none -> 7.6 us  [sensor_parts(): lax.ppermute(own, 'sensor', [(i, i ^ k) for i in range(count)])]
    ppermute x11 -> x9, waiting for transfers between devices: 13.2 us -> 8.12 us  [summing(): lax.ppermute(total, axis, [(i, i ^ k * stride) for i in range(count)])]
    ppermute x0 -> x4, starting transfers between devices: none -> 4.16 us  [sensor_parts(): lax.ppermute(own, 'sensor', [(i, i ^ k) for i in range(count)])]
    ppermute x11 -> x9, starting transfers between devices: 16.7 us -> 13.6 us  [summing(): lax.ppermute(total, axis, [(i, i ^ k * stride) for i in range(count)])]
    ppermute x2, waiting for transfers between devices: 2.54 us -> 0.01 us  [sensor_hop(): lax.ppermute(array, 'sensor', [(i, i ^ 1) for i in range(lax.axis_size('s...]
  transfers between devices with their start and end apart: 22 -> 24, of which waited for: 14 -> 14; matrix products, arithmetic and copies ran while one was open for 0% -> 0% of each run, Pallas kernels for 2% -> 2%
where the time goes in v13:
time: 64.7 us; the launch traced here: 64.5 us
  starting transfers between devices  27.7 us (43%)
  waiting for transfers between devices  24.9 us (38%)
  Pallas kernels  11 us (17%)
  between operations  0.81 us (1%)
    ppermute x9, starting transfers between devices, summing(): lax.ppermute(total, axis, [(i, i ^ k * stride) for i in range(count)])  13.6 us
    pallas_call x13, Pallas kernels, call(): pl.pallas_call(body, out_shape=shapes, in_specs=[pl.BlockSpec(memory_spac...  11 us
    ppermute x9, waiting for transfers between devices, summing(): lax.ppermute(total, axis, [(i, i ^ k * stride) for i in range(count)])  8.12 us
    ppermute x4, waiting for transfers between devices, sensor_parts(): lax.ppermute(own, 'sensor', [(i, i ^ k) for i in range(count)])  7.6 us
    ppermute x3, waiting for transfers between devices, from_partner(): lax.ppermute(array, 'cell', [(i, i ^ 1) for i in range(lax.axis_size('cel...  6.12 us
    ppermute x3, starting transfers between devices, from_partner(): lax.ppermute(array, 'cell', [(i, i ^ 1) for i in range(lax.axis_size('cel...  5.84 us
    ppermute x4, starting transfers between devices, sensor_parts(): lax.ppermute(own, 'sensor', [(i, i ^ k) for i in range(count)])  4.16 us
    ppermute x3, waiting for transfers between devices, last_sensor_parts(): lax.ppermute(array, 'sensor', [(i, i ^ k) for i in range(count)])  3.09 us
  transfers between devices with their start and end apart: 24, of which 14 were waited for; matrix products, arithmetic and copies ran while one was open for 0% of the time, Pallas kernels for 2%

profile of v13, /device:TPU:0, one launch (start us, length us, event | category | flops | bytes accessed | tf_op | source)
XLA Modules:
  0.0 64.5 jit_solution(829282767821743359)
XLA Ops:
  0.6 3.7 %shard_map.130 = (f32[168,128]{1,0:T(8,128)S(1)}, f32[136,128]{1,0:T(8,128)S(1)}, f32[8,256]{1,0:T(8,128)S(1)}, f32[8,256]{1,0:T(8,128)S(1)}, bf16[2,65,64,256]{...) custom-call(bf16[2,65,64,256]{3,2,1,0:T(8,128)(2,1)} %refs_0_.1, ...), custom_call_target="tpu_custom_call" | custom-call | tf_op jit(solution)/shard_map/pallas_call | solution.py:218
  4.3 3.0 %collective-permute-start = (f32[168,128]{1,0:T(8,128)S(1)}, f32[168,128]{1,0:T(8,128)S(1)}, u32[]{:S(2)}, u32[]{:S(2)}) collective-permute-start(f32[168,128]{1,0:T(8,128)S(1)} %get-tuple-element.35), channel_id=1, source_target_pairs={{0,4},{4,0},{8,12},{12,8},{16,20},{20,16},{24,28},{28,24},{1,5},{5... | collective-permute-start | bytes 258056 | tf_op jit(solution)/shard_map/ppermute | solution.py:576
  8.0 1.9 %collective-permute-done.came.one.refs_12_ = f32[168,128]{1,0:T(8,128)S(1)} collective-permute-done((f32[168,128]{1,0:T(8,128)S(1)}, f32[168,128]{1,0:T(8,128)S(1)}, u32[]{:S(2)}, u32[]{:S(2)}) %collective-permute-start) | collective-permute-done | bytes 86048 | tf_op jit(solution)/shard_map/ppermute | solution.py:576
  9.9 4.0 %collective-permute-start.3 = (f32[32,128]{1,0:T(8,128)S(1)}, f32[32,128]{1,0:T(8,128)S(1)}, u32[]{:S(2)}, u32[]{:S(2)}) collective-permute-start(f32[32,128]{1,0:T(8,128)S(1)} %slice_add_fusion.refs_0_), channel_id=1, source_target_pairs={{0,24},{4,28},{8,16},{12,20},{16,8},{20,12},{24,0},{28,4},{1,25},{... | collective-permute-start | bytes 49160 | tf_op jit(solution)/shard_map/ppermute | solution.py:540
  15.8 2.8 %collective-permute-done.2.refs_2_ = f32[32,128]{1,0:T(8,128)S(1)} collective-permute-done((f32[32,128]{1,0:T(8,128)S(1)}, f32[32,128]{1,0:T(8,128)S(1)}, u32[]{:S(2)}, u32[]{:S(2)}) %collective-permute-start.2) | collective-permute-done | bytes 16416 | tf_op jit(solution)/shard_map/ppermute | solution.py:540
  19.7 1.6 %collective-permute-start.7 = (f32[64,256]{1,0:T(8,128)S(1)}, f32[64,256]{1,0:T(8,128)S(1)}, u32[]{:S(2)}, u32[]{:S(2)}) collective-permute-start(f32[64,256]{1,0:T(8,128)S(1)} %slice.25.refs_0_), channel_id=1, source_target_pairs={{0,3},{1,2},{2,1},{3,0},{4,7},{5,6},{6,5},{7,4},{8,11},{9,10},{10,... | collective-permute-start | bytes 196616 | tf_op jit(solution)/shard_map/ppermute | solution.py:553
  22.0 1.8 %collective-permute-done.7.refs_3_ = f32[64,256]{1,0:T(8,128)S(1)} collective-permute-done((f32[64,256]{1,0:T(8,128)S(1)}, f32[64,256]{1,0:T(8,128)S(1)}, u32[]{:S(2)}, u32[]{:S(2)}) %collective-permute-start.7) | collective-permute-done | bytes 65568 | tf_op jit(solution)/shard_map/ppermute | solution.py:553
  23.8 1.8 %collective-permute-done.6.refs_2_ = f32[64,256]{1,0:T(8,128)S(1)} collective-permute-done((f32[64,256]{1,0:T(8,128)S(1)}, f32[64,256]{1,0:T(8,128)S(1)}, u32[]{:S(2)}, u32[]{:S(2)}) %collective-permute-start.6) | collective-permute-done | bytes 65568 | tf_op jit(solution)/shard_map/ppermute | solution.py:553
  26.7 1.6 %collective-permute-start.8 = (f32[104,128]{1,0:T(8,128)S(1)}, f32[104,128]{1,0:T(8,128)S(1)}, u32[]{:S(2)}, u32[]{:S(2)}) collective-permute-start(f32[104,128]{1,0:T(8,128)S(1)} %get-tuple-element.45.sent), channel_id=1, source_target_pairs={{0,4},{4,0},{8,12},{12,8},{16,20},{20,16},{24,28},{28,24},{1,5},{5... | collective-permute-start | bytes 159752 | tf_op jit(solution)/shard_map/ppermute | solution.py:576
  28.9 1.9 %collective-permute-done.8.came.grad_one = f32[104,128]{1,0:T(8,128)S(1)} collective-permute-done((f32[104,128]{1,0:T(8,128)S(1)}, f32[104,128]{1,0:T(8,128)S(1)}, u32[]{:S(2)}, u32[]{:S(2)}) %collective-permute-start.8) | collective-permute-done | bytes 53280 | tf_op jit(solution)/shard_map/ppermute | solution.py:576
  31.0 1.5 %collective-permute-start.12 = (f32[40,128]{1,0:T(8,128)S(1)}, f32[40,128]{1,0:T(8,128)S(1)}, u32[]{:S(2)}, u32[]{:S(2)}) collective-permute-start(f32[40,128]{1,0:T(8,128)S(1)} %shard_map.135.refs_0_), channel_id=1, source_target_pairs={{0,24},{4,28},{8,16},{12,20},{16,8},{20,12},{24,0},{28,4},{1,25},{... | collective-permute-start | bytes 61448 | tf_op jit(solution)/shard_map/ppermute | solution.py:540
  33.2 2.3 %collective-permute-start.10 = (f32[40,128]{1,0:T(8,128)S(1)}, f32[40,128]{1,0:T(8,128)S(1)}, u32[]{:S(2)}, u32[]{:S(2)}) collective-permute-start(f32[40,128]{1,0:T(8,128)S(1)} %shard_map.135.refs_0_), channel_id=1, source_target_pairs={{0,8},{4,12},{8,0},{12,4},{16,24},{20,28},{24,16},{28,20},{1,9},{5... | collective-permute-start | bytes 61448 | tf_op jit(solution)/shard_map/ppermute | solution.py:540
  35.5 1.2 %collective-permute-done.12.refs_3_ = f32[40,128]{1,0:T(8,128)S(1)} collective-permute-done((f32[40,128]{1,0:T(8,128)S(1)}, f32[40,128]{1,0:T(8,128)S(1)}, u32[]{:S(2)}, u32[]{:S(2)}) %collective-permute-start.12) | collective-permute-done | bytes 20512 | tf_op jit(solution)/shard_map/ppermute | solution.py:540
  39.1 1.3 %collective-permute-start.15 = (f32[72,256]{1,0:T(8,128)S(1)}, f32[72,256]{1,0:T(8,128)S(1)}, u32[]{:S(2)}, u32[]{:S(2)}) collective-permute-start(f32[72,256]{1,0:T(8,128)S(1)} %slice.22.refs_0_), channel_id=1, source_target_pairs={{0,3},{1,2},{2,1},{3,0},{4,7},{5,6},{6,5},{7,4},{8,11},{9,10},{10,... | collective-permute-start | bytes 221192 | tf_op jit(solution)/shard_map/ppermute | solution.py:553
  41.3 1.9 %collective-permute-done.15.refs_3_ = f32[72,256]{1,0:T(8,128)S(1)} collective-permute-done((f32[72,256]{1,0:T(8,128)S(1)}, f32[72,256]{1,0:T(8,128)S(1)}, u32[]{:S(2)}, u32[]{:S(2)}) %collective-permute-start.15) | collective-permute-done | bytes 73760 | tf_op jit(solution)/shard_map/ppermute | solution.py:553
  43.2 2.1 %collective-permute-done.14.refs_2_ = f32[72,256]{1,0:T(8,128)S(1)} collective-permute-done((f32[72,256]{1,0:T(8,128)S(1)}, f32[72,256]{1,0:T(8,128)S(1)}, u32[]{:S(2)}, u32[]{:S(2)}) %collective-permute-start.14) | collective-permute-done | bytes 73760 | tf_op jit(solution)/shard_map/ppermute | solution.py:553
  45.3 1.2 %shard_map.138 = (f32[64,256]{1,0:T(8,128)S(1)}, f32[4,64,256]{2,1,0:T(8,128)S(1)}, f32[4,64,256]{2,1,0:T(8,128)S(1)}, f32[64,256]{1,0:T(8,128)S(1)}, f32[104,128]{1,0:T(8,128)S(1)}, /*index=5*/f32[64,128]{1,0:T(8,128)S(1)}) custom-call(f32[72,256]{1,0:T(8,128)S(1)} %slice.22.refs_0_, f32[72,256]{1,0:T(8,128)S(1)} %slice.27.refs_1_, ...), custom_call_target="tpu_custom_call" | custom-call | tf_op jit(solution)/shard_map/pallas_call | solution.py:218
  46.5 1.2 %collective-permute-start.16 = (f32[104,128]{1,0:T(8,128)S(1)}, f32[104,128]{1,0:T(8,128)S(1)}, u32[]{:S(2)}, u32[]{:S(2)}) collective-permute-start(f32[104,128]{1,0:T(8,128)S(1)} %get-tuple-element.56.sent), channel_id=1, source_target_pairs={{0,4},{4,0},{8,12},{12,8},{16,20},{20,16},{24,28},{28,24},{1,5},{5... | collective-permute-start | bytes 159752 | tf_op jit(solution)/shard_map/ppermute | solution.py:576
  48.4 2.3 %collective-permute-done.16.came.refs_10_ = f32[104,128]{1,0:T(8,128)S(1)} collective-permute-done((f32[104,128]{1,0:T(8,128)S(1)}, f32[104,128]{1,0:T(8,128)S(1)}, u32[]{:S(2)}, u32[]{:S(2)}) %collective-permute-start.16) | collective-permute-done | bytes 53280 | tf_op jit(solution)/shard_map/ppermute | solution.py:576
  50.9 2.5 %collective-permute-start.20 = (f32[40,128]{1,0:T(8,128)S(1)}, f32[40,128]{1,0:T(8,128)S(1)}, u32[]{:S(2)}, u32[]{:S(2)}) collective-permute-start(f32[40,128]{1,0:T(8,128)S(1)} %shard_map.139.refs_0_), channel_id=1, source_target_pairs={{0,24},{4,28},{8,16},{12,20},{16,8},{20,12},{24,0},{28,4},{1,25},{... | collective-permute-start | bytes 61448 | tf_op jit(solution)/shard_map/ppermute | solution.py:540
  53.8 1.5 %collective-permute-start.18 = (f32[40,128]{1,0:T(8,128)S(1)}, f32[40,128]{1,0:T(8,128)S(1)}, u32[]{:S(2)}, u32[]{:S(2)}) collective-permute-start(f32[40,128]{1,0:T(8,128)S(1)} %shard_map.139.refs_0_), channel_id=1, source_target_pairs={{0,8},{4,12},{8,0},{12,4},{16,24},{20,28},{24,16},{28,20},{1,9},{5... | collective-permute-start | bytes 61448 | tf_op jit(solution)/shard_map/ppermute | solution.py:540
  56.5 1.8 %collective-permute-done.19.refs_2_ = f32[40,128]{1,0:T(8,128)S(1)} collective-permute-done((f32[40,128]{1,0:T(8,128)S(1)}, f32[40,128]{1,0:T(8,128)S(1)}, u32[]{:S(2)}, u32[]{:S(2)}) %collective-permute-start.19) | collective-permute-done | bytes 20512 | tf_op jit(solution)/shard_map/ppermute | solution.py:540
  58.5 1.5 %collective-permute-start.23 = (f32[72,128]{1,0:T(8,128)S(1)}, f32[72,128]{1,0:T(8,128)S(1)}, u32[]{:S(2)}, u32[]{:S(2)}) collective-permute-start(f32[72,128]{1,0:T(8,128)S(1)} %get-tuple-element.59), channel_id=1, source_target_pairs={{0,3},{1,2},{2,1},{3,0},{4,7},{5,6},{6,5},{7,4},{8,11},{9,10},{10,... | collective-permute-start | bytes 110600 | tf_op jit(solution)/shard_map/ppermute | solution.py:561
  60.5 3.1 %collective-permute-done.22.refs_2_ = f32[8,128]{1,0:T(8,128)S(1)} collective-permute-done((f32[8,128]{1,0:T(8,128)S(1)}, f32[8,128]{1,0:T(8,128)S(1)}, u32[]{:S(2)}, u32[]{:S(2)}) %collective-permute-start.22) | collective-permute-done | bytes 4128 | tf_op jit(solution)/shard_map/ppermute | solution.py:561
  (44 shorter events, 14.0 us)
Async XLA Ops:
  4.3 5.6 %collective-permute-start = (f32[168,128]{1,0:T(8,128)S(1)}, f32[168,128]{1,0:T(8,128)S(1)}, u32[]{:S(2)}, u32[]{:S(2)}) collective-permute-start(f32[168,128]{1,0:T(8,128)S(1)} %get-tuple-element.35), channel_id=1, source_target_pairs={{0,4},{4,0},{8,12},{12,8},{16,20},{20,16},{24,28},{28,24},{1,5},{5... | collective-permute-start | bytes 258056 | tf_op jit(solution)/shard_map/ppermute | solution.py:576
  7.4 8.4 %collective-permute-start.4 = (f32[136,128]{1,0:T(8,128)S(1)}, f32[136,128]{1,0:T(8,128)S(1)}, u32[]{:S(2)}, u32[]{:S(2)}) collective-permute-start(f32[136,128]{1,0:T(8,128)S(1)} %get-tuple-element.36), channel_id=1, source_target_pairs={{5,9},{7,11},{9,5},{11,7},{13,17},{15,19},{17,13},{19,15},{21,25},... | collective-permute-start | bytes 208904 | tf_op jit(solution)/shard_map/ppermute | solution.py:586
  9.9 5.9 %collective-permute-start.3 = (f32[32,128]{1,0:T(8,128)S(1)}, f32[32,128]{1,0:T(8,128)S(1)}, u32[]{:S(2)}, u32[]{:S(2)}) collective-permute-start(f32[32,128]{1,0:T(8,128)S(1)} %slice_add_fusion.refs_0_), channel_id=1, source_target_pairs={{0,24},{4,28},{8,16},{12,20},{16,8},{20,12},{24,0},{28,4},{1,25},{... | collective-permute-start | bytes 49160 | tf_op jit(solution)/shard_map/ppermute | solution.py:540
  13.9 4.6 %collective-permute-start.2 = (f32[32,128]{1,0:T(8,128)S(1)}, f32[32,128]{1,0:T(8,128)S(1)}, u32[]{:S(2)}, u32[]{:S(2)}) collective-permute-start(f32[32,128]{1,0:T(8,128)S(1)} %slice_add_fusion.refs_0_), channel_id=1, source_target_pairs={{0,16},{4,20},{8,24},{12,28},{16,0},{20,4},{24,8},{28,12},{1,17},{... | collective-permute-start | bytes 49160 | tf_op jit(solution)/shard_map/ppermute | solution.py:540
  13.9 4.6 %collective-permute-start.1 = (f32[32,128]{1,0:T(8,128)S(1)}, f32[32,128]{1,0:T(8,128)S(1)}, u32[]{:S(2)}, u32[]{:S(2)}) collective-permute-start(f32[32,128]{1,0:T(8,128)S(1)} %slice_add_fusion.refs_0_), channel_id=1, source_target_pairs={{0,8},{4,12},{8,0},{12,4},{16,24},{20,28},{24,16},{28,20},{1,9},{5... | collective-permute-start | bytes 49160 | tf_op jit(solution)/shard_map/ppermute | solution.py:540
  19.6 2.2 %collective-permute-start.5 = (f32[136,256]{1,0:T(8,128)S(1)}, f32[136,256]{1,0:T(8,128)S(1)}, u32[]{:S(2)}, u32[]{:S(2)}) collective-permute-start(f32[136,256]{1,0:T(8,128)S(1)} %shard_map.132), channel_id=1, source_target_pairs={{0,1},{1,0},{2,3},{3,2},{4,5},{5,4},{6,7},{7,6},{8,9},{9,8},{10,11... | collective-permute-start | bytes 417800 | tf_op jit(solution)/shard_map/ppermute | solution.py:547
  19.7 4.0 %collective-permute-start.7 = (f32[64,256]{1,0:T(8,128)S(1)}, f32[64,256]{1,0:T(8,128)S(1)}, u32[]{:S(2)}, u32[]{:S(2)}) collective-permute-start(f32[64,256]{1,0:T(8,128)S(1)} %slice.25.refs_0_), channel_id=1, source_target_pairs={{0,3},{1,2},{2,1},{3,0},{4,7},{5,6},{6,5},{7,4},{8,11},{9,10},{10,... | collective-permute-start | bytes 196616 | tf_op jit(solution)/shard_map/ppermute | solution.py:553
  21.3 4.3 %collective-permute-start.6 = (f32[64,256]{1,0:T(8,128)S(1)}, f32[64,256]{1,0:T(8,128)S(1)}, u32[]{:S(2)}, u32[]{:S(2)}) collective-permute-start(f32[64,256]{1,0:T(8,128)S(1)} %slice.25.refs_0_), channel_id=1, source_target_pairs={{0,2},{1,3},{2,0},{3,1},{4,6},{5,7},{6,4},{7,5},{8,10},{9,11},{10,... | collective-permute-start | bytes 196616 | tf_op jit(solution)/shard_map/ppermute | solution.py:553
  26.7 4.2 %collective-permute-start.8 = (f32[104,128]{1,0:T(8,128)S(1)}, f32[104,128]{1,0:T(8,128)S(1)}, u32[]{:S(2)}, u32[]{:S(2)}) collective-permute-start(f32[104,128]{1,0:T(8,128)S(1)} %get-tuple-element.45.sent), channel_id=1, source_target_pairs={{0,4},{4,0},{8,12},{12,8},{16,20},{20,16},{24,28},{28,24},{1,5},{5... | collective-permute-start | bytes 159752 | tf_op jit(solution)/shard_map/ppermute | solution.py:576
  28.3 0.7 %collective-permute-start.9 = (f32[64,128]{1,0:T(8,128)S(1)}, f32[64,128]{1,0:T(8,128)S(1)}, u32[]{:S(2)}, u32[]{:S(2)}) collective-permute-start(f32[64,128]{1,0:T(8,128)S(1)} %get-tuple-element.46.edge), channel_id=1, source_target_pairs={{5,9},{7,11},{9,5},{11,7},{13,17},{15,19},{17,13},{19,15},{21,25},... | collective-permute-start | bytes 98312 | tf_op jit(solution)/shard_map/ppermute | solution.py:586
  31.0 5.6 %collective-permute-start.12 = (f32[40,128]{1,0:T(8,128)S(1)}, f32[40,128]{1,0:T(8,128)S(1)}, u32[]{:S(2)}, u32[]{:S(2)}) collective-permute-start(f32[40,128]{1,0:T(8,128)S(1)} %shard_map.135.refs_0_), channel_id=1, source_target_pairs={{0,24},{4,28},{8,16},{12,20},{16,8},{20,12},{24,0},{28,4},{1,25},{... | collective-permute-start | bytes 61448 | tf_op jit(solution)/shard_map/ppermute | solution.py:540
  32.5 4.7 %collective-permute-start.11 = (f32[40,128]{1,0:T(8,128)S(1)}, f32[40,128]{1,0:T(8,128)S(1)}, u32[]{:S(2)}, u32[]{:S(2)}) collective-permute-start(f32[40,128]{1,0:T(8,128)S(1)} %shard_map.135.refs_0_), channel_id=1, source_target_pairs={{0,16},{4,20},{8,24},{12,28},{16,0},{20,4},{24,8},{28,12},{1,17},{... | collective-permute-start | bytes 61448 | tf_op jit(solution)/shard_map/ppermute | solution.py:540
  33.2 4.6 %collective-permute-start.10 = (f32[40,128]{1,0:T(8,128)S(1)}, f32[40,128]{1,0:T(8,128)S(1)}, u32[]{:S(2)}, u32[]{:S(2)}) collective-permute-start(f32[40,128]{1,0:T(8,128)S(1)} %shard_map.135.refs_0_), channel_id=1, source_target_pairs={{0,8},{4,12},{8,0},{12,4},{16,24},{20,28},{24,16},{28,20},{1,9},{5... | collective-permute-start | bytes 61448 | tf_op jit(solution)/shard_map/ppermute | solution.py:540
  38.9 2.2 %collective-permute-start.13 = (f32[104,256]{1,0:T(8,128)S(1)}, f32[104,256]{1,0:T(8,128)S(1)}, u32[]{:S(2)}, u32[]{:S(2)}) collective-permute-start(f32[104,256]{1,0:T(8,128)S(1)} %get-tuple-element.47), channel_id=1, source_target_pairs={{0,1},{1,0},{2,3},{3,2},{4,5},{5,4},{6,7},{7,6},{8,9},{9,8},{10,11... | collective-permute-start | bytes 319496 | tf_op jit(solution)/shard_map/ppermute | solution.py:547
  39.1 4.1 %collective-permute-start.15 = (f32[72,256]{1,0:T(8,128)S(1)}, f32[72,256]{1,0:T(8,128)S(1)}, u32[]{:S(2)}, u32[]{:S(2)}) collective-permute-start(f32[72,256]{1,0:T(8,128)S(1)} %slice.22.refs_0_), channel_id=1, source_target_pairs={{0,3},{1,2},{2,1},{3,0},{4,7},{5,6},{6,5},{7,4},{8,11},{9,10},{10,... | collective-permute-start | bytes 221192 | tf_op jit(solution)/shard_map/ppermute | solution.py:553
  40.4 4.9 %collective-permute-start.14 = (f32[72,256]{1,0:T(8,128)S(1)}, f32[72,256]{1,0:T(8,128)S(1)}, u32[]{:S(2)}, u32[]{:S(2)}) collective-permute-start(f32[72,256]{1,0:T(8,128)S(1)} %slice.22.refs_0_), channel_id=1, source_target_pairs={{0,2},{1,3},{2,0},{3,1},{4,6},{5,7},{6,4},{7,5},{8,10},{9,11},{10,... | collective-permute-start | bytes 221192 | tf_op jit(solution)/shard_map/ppermute | solution.py:553
  46.5 4.2 %collective-permute-start.16 = (f32[104,128]{1,0:T(8,128)S(1)}, f32[104,128]{1,0:T(8,128)S(1)}, u32[]{:S(2)}, u32[]{:S(2)}) collective-permute-start(f32[104,128]{1,0:T(8,128)S(1)} %get-tuple-element.56.sent), channel_id=1, source_target_pairs={{0,4},{4,0},{8,12},{12,8},{16,20},{20,16},{24,28},{28,24},{1,5},{5... | collective-permute-start | bytes 159752 | tf_op jit(solution)/shard_map/ppermute | solution.py:576
  47.7 0.7 %collective-permute-start.17 = (f32[64,128]{1,0:T(8,128)S(1)}, f32[64,128]{1,0:T(8,128)S(1)}, u32[]{:S(2)}, u32[]{:S(2)}) collective-permute-start(f32[64,128]{1,0:T(8,128)S(1)} %get-tuple-element.57.edge), channel_id=1, source_target_pairs={{5,9},{7,11},{9,5},{11,7},{13,17},{15,19},{17,13},{19,15},{21,25},... | collective-permute-start | bytes 98312 | tf_op jit(solution)/shard_map/ppermute | solution.py:586
  50.9 5.6 %collective-permute-start.20 = (f32[40,128]{1,0:T(8,128)S(1)}, f32[40,128]{1,0:T(8,128)S(1)}, u32[]{:S(2)}, u32[]{:S(2)}) collective-permute-start(f32[40,128]{1,0:T(8,128)S(1)} %shard_map.139.refs_0_), channel_id=1, source_target_pairs={{0,24},{4,28},{8,16},{12,20},{16,8},{20,12},{24,0},{28,4},{1,25},{... | collective-permute-start | bytes 61448 | tf_op jit(solution)/shard_map/ppermute | solution.py:540
  53.4 5.0 %collective-permute-start.19 = (f32[40,128]{1,0:T(8,128)S(1)}, f32[40,128]{1,0:T(8,128)S(1)}, u32[]{:S(2)}, u32[]{:S(2)}) collective-permute-start(f32[40,128]{1,0:T(8,128)S(1)} %shard_map.139.refs_0_), channel_id=1, source_target_pairs={{0,16},{4,20},{8,24},{12,28},{16,0},{20,4},{24,8},{28,12},{1,17},{... | collective-permute-start | bytes 61448 | tf_op jit(solution)/shard_map/ppermute | solution.py:540
  53.8 4.5 %collective-permute-start.18 = (f32[40,128]{1,0:T(8,128)S(1)}, f32[40,128]{1,0:T(8,128)S(1)}, u32[]{:S(2)}, u32[]{:S(2)}) collective-permute-start(f32[40,128]{1,0:T(8,128)S(1)} %shard_map.139.refs_0_), channel_id=1, source_target_pairs={{0,8},{4,12},{8,0},{12,4},{16,24},{20,28},{24,16},{28,20},{1,9},{5... | collective-permute-start | bytes 61448 | tf_op jit(solution)/shard_map/ppermute | solution.py:540
  58.5 5.1 %collective-permute-start.23 = (f32[72,128]{1,0:T(8,128)S(1)}, f32[72,128]{1,0:T(8,128)S(1)}, u32[]{:S(2)}, u32[]{:S(2)}) collective-permute-start(f32[72,128]{1,0:T(8,128)S(1)} %get-tuple-element.59), channel_id=1, source_target_pairs={{0,3},{1,2},{2,1},{3,0},{4,7},{5,6},{6,5},{7,4},{8,11},{9,10},{10,... | collective-permute-start | bytes 110600 | tf_op jit(solution)/shard_map/ppermute | solution.py:561
  60.0 3.6 %collective-permute-start.22 = (f32[8,128]{1,0:T(8,128)S(1)}, f32[8,128]{1,0:T(8,128)S(1)}, u32[]{:S(2)}, u32[]{:S(2)}) collective-permute-start(f32[8,128]{1,0:T(8,128)S(1)} %get-tuple-element.58.refs_0_), channel_id=1, source_target_pairs={{0,2},{1,3},{2,0},{3,1},{4,6},{5,7},{6,4},{7,5},{8,10},{9,11},{10,... | collective-permute-start | bytes 12296 | tf_op jit(solution)/shard_map/ppermute | solution.py:561
  60.3 3.3 %collective-permute-start.21 = (f32[8,128]{1,0:T(8,128)S(1)}, f32[8,128]{1,0:T(8,128)S(1)}, u32[]{:S(2)}, u32[]{:S(2)}) collective-permute-start(f32[8,128]{1,0:T(8,128)S(1)} %get-tuple-element.58.refs_0_), channel_id=1, source_target_pairs={{0,1},{1,0},{2,3},{3,2},{4,5},{5,4},{6,7},{7,6},{8,9},{9,8},{10,11... | collective-permute-start | bytes 12296 | tf_op jit(solution)/shard_map/ppermute | solution.py:561
  (1 other events, 4.0 us)

commit v14 on v12

--- a/solution.py
+++ b/solution.py
@@ -11,7 +11,7 @@
 COLS = 128
 LANES = 128
 GROUP = 8
-CHUNK = 24
+CHUNK = 40
 SHRINK_SCALE = 0.4
 TINY = 1e-06
 VMEM = pltpu.VMEM

time: 63.4 us -> 63.5 us (level)
  no operation moved by 1% of the time
where the time goes in v14:
time: 63.5 us; the launch traced here: 63.3 us
  starting transfers between devices  26.6 us (42%)
  waiting for transfers between devices  24.7 us (39%)
  Pallas kernels  11.1 us (17%)
  between operations  0.8 us (1%)
    ppermute x11, starting transfers between devices, summing(): lax.ppermute(total, axis, [(i, i ^ k * stride) for i in range(count)])  16.7 us
    ppermute x11, waiting for transfers between devices, summing(): lax.ppermute(total, axis, [(i, i ^ k * stride) for i in range(count)])  13.2 us
    pallas_call x13, Pallas kernels, call(): pl.pallas_call(body, out_shape=shapes, in_specs=[pl.BlockSpec(memory_spac...  11.1 us
    ppermute x3, waiting for transfers between devices, from_partner(): lax.ppermute(array, 'cell', [(i, i ^ 1) for i in range(lax.axis_size('cel...  6.16 us
    ppermute x3, starting transfers between devices, from_partner(): lax.ppermute(array, 'cell', [(i, i ^ 1) for i in range(lax.axis_size('cel...  5.8 us
    ppermute x3, waiting for transfers between devices, last_sensor_parts(): lax.ppermute(array, 'sensor', [(i, i ^ k) for i in range(count)])  2.82 us
    ppermute x2, waiting for transfers between devices, sensor_hop(): lax.ppermute(array, 'sensor', [(i, i ^ 1) for i in range(lax.axis_size('s...  2.54 us
    ppermute x3, starting transfers between devices, from_other(): return lax.ppermute(array, ('cell', 'sensor'), pairs)  1.96 us
  transfers between devices with their start and end apart: 22, of which 14 were waited for; matrix products, arithmetic and copies ran while one was open for 0% of the time, Pallas kernels for 2%

profile of v14, /device:TPU:0, one launch (start us, length us, event | category | flops | bytes accessed | tf_op | source)
XLA Modules:
  0.0 63.3 jit_solution(10811712509992650779)
XLA Ops:
  0.6 3.8 %shard_map.130 = (f32[168,128]{1,0:T(8,128)S(1)}, f32[136,128]{1,0:T(8,128)S(1)}, f32[8,256]{1,0:T(8,128)S(1)}, f32[8,256]{1,0:T(8,128)S(1)}, bf16[2,65,64,256]{...) custom-call(bf16[2,65,64,256]{3,2,1,0:T(8,128)(2,1)} %refs_0_.1, ...), custom_call_target="tpu_custom_call" | custom-call | tf_op jit(solution)/shard_map/pallas_call | solution.py:218
  4.5 3.0 %collective-permute-start = (f32[168,128]{1,0:T(8,128)S(1)}, f32[168,128]{1,0:T(8,128)S(1)}, u32[]{:S(2)}, u32[]{:S(2)}) collective-permute-start(f32[168,128]{1,0:T(8,128)S(1)} %get-tuple-element.35), channel_id=1, source_target_pairs={{0,4},{4,0},{8,12},{12,8},{16,20},{20,16},{24,28},{28,24},{1,5},{5... | collective-permute-start | bytes 258056 | tf_op jit(solution)/shard_map/ppermute | solution.py:574
  8.1 1.9 %collective-permute-done.came.one.refs_10_ = f32[168,128]{1,0:T(8,128)S(1)} collective-permute-done((f32[168,128]{1,0:T(8,128)S(1)}, f32[168,128]{1,0:T(8,128)S(1)}, u32[]{:S(2)}, u32[]{:S(2)}) %collective-permute-start) | collective-permute-done | bytes 86048 | tf_op jit(solution)/shard_map/ppermute | solution.py:574
  10.0 4.0 %collective-permute-start.3 = (f32[32,128]{1,0:T(8,128)S(1)}, f32[32,128]{1,0:T(8,128)S(1)}, u32[]{:S(2)}, u32[]{:S(2)}) collective-permute-start(f32[32,128]{1,0:T(8,128)S(1)} %slice_add_fusion.2.refs_0_), channel_id=1, source_target_pairs={{0,24},{4,28},{8,16},{12,20},{16,8},{20,12},{24,0},{28,4},{1,25},{... | collective-permute-start | bytes 49160 | tf_op jit(solution)/shard_map/ppermute | solution.py:540
  15.9 2.8 %collective-permute-done.2.refs_2_ = f32[32,128]{1,0:T(8,128)S(1)} collective-permute-done((f32[32,128]{1,0:T(8,128)S(1)}, f32[32,128]{1,0:T(8,128)S(1)}, u32[]{:S(2)}, u32[]{:S(2)}) %collective-permute-start.2) | collective-permute-done | bytes 16416 | tf_op jit(solution)/shard_map/ppermute | solution.py:540
  19.8 1.3 %collective-permute-done.5.passed = f32[136,256]{1,0:T(8,128)S(1)} collective-permute-done((f32[136,256]{1,0:T(8,128)S(1)}, f32[136,256]{1,0:T(8,128)S(1)}, u32[]{:S(2)}, u32[]{:S(2)}) %collective-permute-start.5) | collective-permute-done | bytes 139296 | tf_op jit(solution)/shard_map/ppermute | solution.py:547
  21.2 1.6 %collective-permute-start.6 = (f32[64,256]{1,0:T(8,128)S(1)}, f32[64,256]{1,0:T(8,128)S(1)}, u32[]{:S(2)}, u32[]{:S(2)}) collective-permute-start(f32[64,256]{1,0:T(8,128)S(1)} %slice_add_fusion.1.refs_0_), channel_id=1, source_target_pairs={{0,2},{1,3},{2,0},{3,1},{4,6},{5,7},{6,4},{7,5},{8,10},{9,11},{10,... | collective-permute-start | bytes 196616 | tf_op jit(solution)/shard_map/ppermute | solution.py:540
  22.9 2.7 %collective-permute-done.6.refs_1_ = f32[64,256]{1,0:T(8,128)S(1)} collective-permute-done((f32[64,256]{1,0:T(8,128)S(1)}, f32[64,256]{1,0:T(8,128)S(1)}, u32[]{:S(2)}, u32[]{:S(2)}) %collective-permute-start.6) | collective-permute-done | bytes 65568 | tf_op jit(solution)/shard_map/ppermute | solution.py:540
  26.6 1.6 %collective-permute-start.7 = (f32[104,128]{1,0:T(8,128)S(1)}, f32[104,128]{1,0:T(8,128)S(1)}, u32[]{:S(2)}, u32[]{:S(2)}) collective-permute-start(f32[104,128]{1,0:T(8,128)S(1)} %get-tuple-element.45.sent), channel_id=1, source_target_pairs={{0,4},{4,0},{8,12},{12,8},{16,20},{20,16},{24,28},{28,24},{1,5},{5... | collective-permute-start | bytes 159752 | tf_op jit(solution)/shard_map/ppermute | solution.py:574
  28.9 1.9 %collective-permute-done.7.came.grad_one = f32[104,128]{1,0:T(8,128)S(1)} collective-permute-done((f32[104,128]{1,0:T(8,128)S(1)}, f32[104,128]{1,0:T(8,128)S(1)}, u32[]{:S(2)}, u32[]{:S(2)}) %collective-permute-start.7) | collective-permute-done | bytes 53280 | tf_op jit(solution)/shard_map/ppermute | solution.py:574
  30.9 1.5 %collective-permute-start.11 = (f32[40,128]{1,0:T(8,128)S(1)}, f32[40,128]{1,0:T(8,128)S(1)}, u32[]{:S(2)}, u32[]{:S(2)}) collective-permute-start(f32[40,128]{1,0:T(8,128)S(1)} %shard_map.135.refs_0_), channel_id=1, source_target_pairs={{0,24},{4,28},{8,16},{12,20},{16,8},{20,12},{24,0},{28,4},{1,25},{... | collective-permute-start | bytes 61448 | tf_op jit(solution)/shard_map/ppermute | solution.py:540
  33.1 2.3 %collective-permute-start.9 = (f32[40,128]{1,0:T(8,128)S(1)}, f32[40,128]{1,0:T(8,128)S(1)}, u32[]{:S(2)}, u32[]{:S(2)}) collective-permute-start(f32[40,128]{1,0:T(8,128)S(1)} %shard_map.135.refs_0_), channel_id=1, source_target_pairs={{0,8},{4,12},{8,0},{12,4},{16,24},{20,28},{24,16},{28,20},{1,9},{5... | collective-permute-start | bytes 61448 | tf_op jit(solution)/shard_map/ppermute | solution.py:540
  35.4 1.2 %collective-permute-done.11.refs_3_ = f32[40,128]{1,0:T(8,128)S(1)} collective-permute-done((f32[40,128]{1,0:T(8,128)S(1)}, f32[40,128]{1,0:T(8,128)S(1)}, u32[]{:S(2)}, u32[]{:S(2)}) %collective-permute-start.11) | collective-permute-done | bytes 20512 | tf_op jit(solution)/shard_map/ppermute | solution.py:540
  39.1 1.2 %collective-permute-done.12.passed = f32[104,256]{1,0:T(8,128)S(1)} collective-permute-done((f32[104,256]{1,0:T(8,128)S(1)}, f32[104,256]{1,0:T(8,128)S(1)}, u32[]{:S(2)}, u32[]{:S(2)}) %collective-permute-start.12) | collective-permute-done | bytes 106528 | tf_op jit(solution)/shard_map/ppermute | solution.py:547
  40.3 1.6 %collective-permute-start.13 = (f32[72,256]{1,0:T(8,128)S(1)}, f32[72,256]{1,0:T(8,128)S(1)}, u32[]{:S(2)}, u32[]{:S(2)}) collective-permute-start(f32[72,256]{1,0:T(8,128)S(1)} %slice_add_fusion.refs_0_), channel_id=1, source_target_pairs={{0,2},{1,3},{2,0},{3,1},{4,6},{5,7},{6,4},{7,5},{8,10},{9,11},{10,... | collective-permute-start | bytes 221192 | tf_op jit(solution)/shard_map/ppermute | solution.py:540
  42.0 2.7 %collective-permute-done.13.refs_1_ = f32[72,256]{1,0:T(8,128)S(1)} collective-permute-done((f32[72,256]{1,0:T(8,128)S(1)}, f32[72,256]{1,0:T(8,128)S(1)}, u32[]{:S(2)}, u32[]{:S(2)}) %collective-permute-start.13) | collective-permute-done | bytes 73760 | tf_op jit(solution)/shard_map/ppermute | solution.py:540
  44.8 1.2 %shard_map.138 = (f32[64,256]{1,0:T(8,128)S(1)}, f32[4,64,256]{2,1,0:T(8,128)S(1)}, f32[4,64,256]{2,1,0:T(8,128)S(1)}, f32[64,256]{1,0:T(8,128)S(1)}, f32[104,128]{1,0:T(8,128)S(1)}, /*index=5*/f32[64,128]{1,0:T(8,128)S(1)}) custom-call(f32[72,256]{1,0:T(8,128)S(1)} %slice_add_fusion.refs_0_, f32[72,256]{1,0:T(8,128)S(1)} %collective-permute-done.13.refs_1_, ...), custom_call_target="tpu_custom_call" | custom-call | tf_op jit(solution)/shard_map/pallas_call | solution.py:218
  47.8 2.4 %collective-permute-done.14.came.refs_10_ = f32[104,128]{1,0:T(8,128)S(1)} collective-permute-done((f32[104,128]{1,0:T(8,128)S(1)}, f32[104,128]{1,0:T(8,128)S(1)}, u32[]{:S(2)}, u32[]{:S(2)}) %collective-permute-start.14) | collective-permute-done | bytes 53280 | tf_op jit(solution)/shard_map/ppermute | solution.py:574
  50.3 2.2 %collective-permute-start.18 = (f32[40,128]{1,0:T(8,128)S(1)}, f32[40,128]{1,0:T(8,128)S(1)}, u32[]{:S(2)}, u32[]{:S(2)}) collective-permute-start(f32[40,128]{1,0:T(8,128)S(1)} %shard_map.139.refs_0_), channel_id=1, source_target_pairs={{0,24},{4,28},{8,16},{12,20},{16,8},{20,12},{24,0},{28,4},{1,25},{... | collective-permute-start | bytes 61448 | tf_op jit(solution)/shard_map/ppermute | solution.py:540
  53.3 1.5 %collective-permute-start.16 = (f32[40,128]{1,0:T(8,128)S(1)}, f32[40,128]{1,0:T(8,128)S(1)}, u32[]{:S(2)}, u32[]{:S(2)}) collective-permute-start(f32[40,128]{1,0:T(8,128)S(1)} %shard_map.139.refs_0_), channel_id=1, source_target_pairs={{0,8},{4,12},{8,0},{12,4},{16,24},{20,28},{24,16},{28,20},{1,9},{5... | collective-permute-start | bytes 61448 | tf_op jit(solution)/shard_map/ppermute | solution.py:540
  54.8 1.2 %collective-permute-done.18.refs_3_ = f32[40,128]{1,0:T(8,128)S(1)} collective-permute-done((f32[40,128]{1,0:T(8,128)S(1)}, f32[40,128]{1,0:T(8,128)S(1)}, u32[]{:S(2)}, u32[]{:S(2)}) %collective-permute-start.18) | collective-permute-done | bytes 20512 | tf_op jit(solution)/shard_map/ppermute | solution.py:540
  56.0 1.4 %collective-permute-done.17.refs_2_ = f32[40,128]{1,0:T(8,128)S(1)} collective-permute-done((f32[40,128]{1,0:T(8,128)S(1)}, f32[40,128]{1,0:T(8,128)S(1)}, u32[]{:S(2)}, u32[]{:S(2)}) %collective-permute-start.17) | collective-permute-done | bytes 20512 | tf_op jit(solution)/shard_map/ppermute | solution.py:540
  57.5 1.3 %collective-permute-start.21 = (f32[72,128]{1,0:T(8,128)S(1)}, f32[72,128]{1,0:T(8,128)S(1)}, u32[]{:S(2)}, u32[]{:S(2)}) collective-permute-start(f32[72,128]{1,0:T(8,128)S(1)} %get-tuple-element.59), channel_id=1, source_target_pairs={{0,3},{1,2},{2,1},{3,0},{4,7},{5,6},{6,5},{7,4},{8,11},{9,10},{10,... | collective-permute-start | bytes 110600 | tf_op jit(solution)/shard_map/ppermute | solution.py:559
  59.6 2.8 %collective-permute-done.20.refs_2_ = f32[8,128]{1,0:T(8,128)S(1)} collective-permute-done((f32[8,128]{1,0:T(8,128)S(1)}, f32[8,128]{1,0:T(8,128)S(1)}, u32[]{:S(2)}, u32[]{:S(2)}) %collective-permute-start.20) | collective-permute-done | bytes 4128 | tf_op jit(solution)/shard_map/ppermute | solution.py:559
  (38 shorter events, 13.4 us)
Async XLA Ops:
  4.5 5.6 %collective-permute-start = (f32[168,128]{1,0:T(8,128)S(1)}, f32[168,128]{1,0:T(8,128)S(1)}, u32[]{:S(2)}, u32[]{:S(2)}) collective-permute-start(f32[168,128]{1,0:T(8,128)S(1)} %get-tuple-element.35), channel_id=1, source_target_pairs={{0,4},{4,0},{8,12},{12,8},{16,20},{20,16},{24,28},{28,24},{1,5},{5... | collective-permute-start | bytes 258056 | tf_op jit(solution)/shard_map/ppermute | solution.py:574
  7.5 8.4 %collective-permute-start.4 = (f32[136,128]{1,0:T(8,128)S(1)}, f32[136,128]{1,0:T(8,128)S(1)}, u32[]{:S(2)}, u32[]{:S(2)}) collective-permute-start(f32[136,128]{1,0:T(8,128)S(1)} %get-tuple-element.36), channel_id=1, source_target_pairs={{5,9},{7,11},{9,5},{11,7},{13,17},{15,19},{17,13},{19,15},{21,25},... | collective-permute-start | bytes 208904 | tf_op jit(solution)/shard_map/ppermute | solution.py:584
  10.0 5.9 %collective-permute-start.3 = (f32[32,128]{1,0:T(8,128)S(1)}, f32[32,128]{1,0:T(8,128)S(1)}, u32[]{:S(2)}, u32[]{:S(2)}) collective-permute-start(f32[32,128]{1,0:T(8,128)S(1)} %slice_add_fusion.2.refs_0_), channel_id=1, source_target_pairs={{0,24},{4,28},{8,16},{12,20},{16,8},{20,12},{24,0},{28,4},{1,25},{... | collective-permute-start | bytes 49160 | tf_op jit(solution)/shard_map/ppermute | solution.py:540
  14.1 4.6 %collective-permute-start.2 = (f32[32,128]{1,0:T(8,128)S(1)}, f32[32,128]{1,0:T(8,128)S(1)}, u32[]{:S(2)}, u32[]{:S(2)}) collective-permute-start(f32[32,128]{1,0:T(8,128)S(1)} %slice_add_fusion.2.refs_0_), channel_id=1, source_target_pairs={{0,16},{4,20},{8,24},{12,28},{16,0},{20,4},{24,8},{28,12},{1,17},{... | collective-permute-start | bytes 49160 | tf_op jit(solution)/shard_map/ppermute | solution.py:540
  14.1 4.6 %collective-permute-start.1 = (f32[32,128]{1,0:T(8,128)S(1)}, f32[32,128]{1,0:T(8,128)S(1)}, u32[]{:S(2)}, u32[]{:S(2)}) collective-permute-start(f32[32,128]{1,0:T(8,128)S(1)} %slice_add_fusion.2.refs_0_), channel_id=1, source_target_pairs={{0,8},{4,12},{8,0},{12,4},{16,24},{20,28},{24,16},{28,20},{1,9},{5... | collective-permute-start | bytes 49160 | tf_op jit(solution)/shard_map/ppermute | solution.py:540
  14.7 4.0 %copy-start = (f32[64,64]{1,0:T(8,128)S(1)}, f32[64,64]{1,0:T(8,128)}, u32[]{:S(2)}) copy-start(f32[64,64]{1,0:T(8,128)} %refs_4_.2) | copy-start | bytes 49156
  19.8 1.4 %collective-permute-start.5 = (f32[136,256]{1,0:T(8,128)S(1)}, f32[136,256]{1,0:T(8,128)S(1)}, u32[]{:S(2)}, u32[]{:S(2)}) collective-permute-start(f32[136,256]{1,0:T(8,128)S(1)} %shard_map.132), channel_id=1, source_target_pairs={{0,1},{1,0},{2,3},{3,2},{4,5},{5,4},{6,7},{7,6},{8,9},{9,8},{10,11... | collective-permute-start | bytes 417800 | tf_op jit(solution)/shard_map/ppermute | solution.py:547
  21.2 4.3 %collective-permute-start.6 = (f32[64,256]{1,0:T(8,128)S(1)}, f32[64,256]{1,0:T(8,128)S(1)}, u32[]{:S(2)}, u32[]{:S(2)}) collective-permute-start(f32[64,256]{1,0:T(8,128)S(1)} %slice_add_fusion.1.refs_0_), channel_id=1, source_target_pairs={{0,2},{1,3},{2,0},{3,1},{4,6},{5,7},{6,4},{7,5},{8,10},{9,11},{10,... | collective-permute-start | bytes 196616 | tf_op jit(solution)/shard_map/ppermute | solution.py:540
  26.6 4.2 %collective-permute-start.7 = (f32[104,128]{1,0:T(8,128)S(1)}, f32[104,128]{1,0:T(8,128)S(1)}, u32[]{:S(2)}, u32[]{:S(2)}) collective-permute-start(f32[104,128]{1,0:T(8,128)S(1)} %get-tuple-element.45.sent), channel_id=1, source_target_pairs={{0,4},{4,0},{8,12},{12,8},{16,20},{20,16},{24,28},{28,24},{1,5},{5... | collective-permute-start | bytes 159752 | tf_op jit(solution)/shard_map/ppermute | solution.py:574
  28.2 0.7 %collective-permute-start.8 = (f32[64,128]{1,0:T(8,128)S(1)}, f32[64,128]{1,0:T(8,128)S(1)}, u32[]{:S(2)}, u32[]{:S(2)}) collective-permute-start(f32[64,128]{1,0:T(8,128)S(1)} %get-tuple-element.46.edge), channel_id=1, source_target_pairs={{5,9},{7,11},{9,5},{11,7},{13,17},{15,19},{17,13},{19,15},{21,25},... | collective-permute-start | bytes 98312 | tf_op jit(solution)/shard_map/ppermute | solution.py:584
  30.9 5.6 %collective-permute-start.11 = (f32[40,128]{1,0:T(8,128)S(1)}, f32[40,128]{1,0:T(8,128)S(1)}, u32[]{:S(2)}, u32[]{:S(2)}) collective-permute-start(f32[40,128]{1,0:T(8,128)S(1)} %shard_map.135.refs_0_), channel_id=1, source_target_pairs={{0,24},{4,28},{8,16},{12,20},{16,8},{20,12},{24,0},{28,4},{1,25},{... | collective-permute-start | bytes 61448 | tf_op jit(solution)/shard_map/ppermute | solution.py:540
  32.5 4.7 %collective-permute-start.10 = (f32[40,128]{1,0:T(8,128)S(1)}, f32[40,128]{1,0:T(8,128)S(1)}, u32[]{:S(2)}, u32[]{:S(2)}) collective-permute-start(f32[40,128]{1,0:T(8,128)S(1)} %shard_map.135.refs_0_), channel_id=1, source_target_pairs={{0,16},{4,20},{8,24},{12,28},{16,0},{20,4},{24,8},{28,12},{1,17},{... | collective-permute-start | bytes 61448 | tf_op jit(solution)/shard_map/ppermute | solution.py:540
  33.1 4.7 %collective-permute-start.9 = (f32[40,128]{1,0:T(8,128)S(1)}, f32[40,128]{1,0:T(8,128)S(1)}, u32[]{:S(2)}, u32[]{:S(2)}) collective-permute-start(f32[40,128]{1,0:T(8,128)S(1)} %shard_map.135.refs_0_), channel_id=1, source_target_pairs={{0,8},{4,12},{8,0},{12,4},{16,24},{20,28},{24,16},{28,20},{1,9},{5... | collective-permute-start | bytes 61448 | tf_op jit(solution)/shard_map/ppermute | solution.py:540
  39.0 1.4 %collective-permute-start.12 = (f32[104,256]{1,0:T(8,128)S(1)}, f32[104,256]{1,0:T(8,128)S(1)}, u32[]{:S(2)}, u32[]{:S(2)}) collective-permute-start(f32[104,256]{1,0:T(8,128)S(1)} %get-tuple-element.47), channel_id=1, source_target_pairs={{0,1},{1,0},{2,3},{3,2},{4,5},{5,4},{6,7},{7,6},{8,9},{9,8},{10,11... | collective-permute-start | bytes 319496 | tf_op jit(solution)/shard_map/ppermute | solution.py:547
  40.3 4.4 %collective-permute-start.13 = (f32[72,256]{1,0:T(8,128)S(1)}, f32[72,256]{1,0:T(8,128)S(1)}, u32[]{:S(2)}, u32[]{:S(2)}) collective-permute-start(f32[72,256]{1,0:T(8,128)S(1)} %slice_add_fusion.refs_0_), channel_id=1, source_target_pairs={{0,2},{1,3},{2,0},{3,1},{4,6},{5,7},{6,4},{7,5},{8,10},{9,11},{10,... | collective-permute-start | bytes 221192 | tf_op jit(solution)/shard_map/ppermute | solution.py:540
  46.0 4.2 %collective-permute-start.14 = (f32[104,128]{1,0:T(8,128)S(1)}, f32[104,128]{1,0:T(8,128)S(1)}, u32[]{:S(2)}, u32[]{:S(2)}) collective-permute-start(f32[104,128]{1,0:T(8,128)S(1)} %get-tuple-element.56.sent), channel_id=1, source_target_pairs={{0,4},{4,0},{8,12},{12,8},{16,20},{20,16},{24,28},{28,24},{1,5},{5... | collective-permute-start | bytes 159752 | tf_op jit(solution)/shard_map/ppermute | solution.py:574
  47.2 0.7 %collective-permute-start.15 = (f32[64,128]{1,0:T(8,128)S(1)}, f32[64,128]{1,0:T(8,128)S(1)}, u32[]{:S(2)}, u32[]{:S(2)}) collective-permute-start(f32[64,128]{1,0:T(8,128)S(1)} %get-tuple-element.57.edge), channel_id=1, source_target_pairs={{5,9},{7,11},{9,5},{11,7},{13,17},{15,19},{17,13},{19,15},{21,25},... | collective-permute-start | bytes 98312 | tf_op jit(solution)/shard_map/ppermute | solution.py:584
  50.3 5.6 %collective-permute-start.18 = (f32[40,128]{1,0:T(8,128)S(1)}, f32[40,128]{1,0:T(8,128)S(1)}, u32[]{:S(2)}, u32[]{:S(2)}) collective-permute-start(f32[40,128]{1,0:T(8,128)S(1)} %shard_map.139.refs_0_), channel_id=1, source_target_pairs={{0,24},{4,28},{8,16},{12,20},{16,8},{20,12},{24,0},{28,4},{1,25},{... | collective-permute-start | bytes 61448 | tf_op jit(solution)/shard_map/ppermute | solution.py:540
  52.6 4.8 %collective-permute-start.17 = (f32[40,128]{1,0:T(8,128)S(1)}, f32[40,128]{1,0:T(8,128)S(1)}, u32[]{:S(2)}, u32[]{:S(2)}) collective-permute-start(f32[40,128]{1,0:T(8,128)S(1)} %shard_map.139.refs_0_), channel_id=1, source_target_pairs={{0,16},{4,20},{8,24},{12,28},{16,0},{20,4},{24,8},{28,12},{1,17},{... | collective-permute-start | bytes 61448 | tf_op jit(solution)/shard_map/ppermute | solution.py:540
  53.3 4.2 %collective-permute-start.16 = (f32[40,128]{1,0:T(8,128)S(1)}, f32[40,128]{1,0:T(8,128)S(1)}, u32[]{:S(2)}, u32[]{:S(2)}) collective-permute-start(f32[40,128]{1,0:T(8,128)S(1)} %shard_map.139.refs_0_), channel_id=1, source_target_pairs={{0,8},{4,12},{8,0},{12,4},{16,24},{20,28},{24,16},{28,20},{1,9},{5... | collective-permute-start | bytes 61448 | tf_op jit(solution)/shard_map/ppermute | solution.py:540
  57.5 4.9 %collective-permute-start.21 = (f32[72,128]{1,0:T(8,128)S(1)}, f32[72,128]{1,0:T(8,128)S(1)}, u32[]{:S(2)}, u32[]{:S(2)}) collective-permute-start(f32[72,128]{1,0:T(8,128)S(1)} %get-tuple-element.59), channel_id=1, source_target_pairs={{0,3},{1,2},{2,1},{3,0},{4,7},{5,6},{6,5},{7,4},{8,11},{9,10},{10,... | collective-permute-start | bytes 110600 | tf_op jit(solution)/shard_map/ppermute | solution.py:559
  58.8 3.6 %collective-permute-start.20 = (f32[8,128]{1,0:T(8,128)S(1)}, f32[8,128]{1,0:T(8,128)S(1)}, u32[]{:S(2)}, u32[]{:S(2)}) collective-permute-start(f32[8,128]{1,0:T(8,128)S(1)} %get-tuple-element.58.refs_0_), channel_id=1, source_target_pairs={{0,2},{1,3},{2,0},{3,1},{4,6},{5,7},{6,4},{7,5},{8,10},{9,11},{10,... | collective-permute-start | bytes 12296 | tf_op jit(solution)/shard_map/ppermute | solution.py:559
  59.3 3.1 %collective-permute-start.19 = (f32[8,128]{1,0:T(8,128)S(1)}, f32[8,128]{1,0:T(8,128)S(1)}, u32[]{:S(2)}, u32[]{:S(2)}) collective-permute-start(f32[8,128]{1,0:T(8,128)S(1)} %get-tuple-element.58.refs_0_), channel_id=1, source_target_pairs={{0,1},{1,0},{2,3},{3,2},{4,5},{5,4},{6,7},{7,6},{8,9},{9,8},{10,11... | collective-permute-start | bytes 12296 | tf_op jit(solution)/shard_map/ppermute | solution.py:559

commit v15 on v12

--- a/solution.py
+++ b/solution.py
@@ -428,7 +428,7 @@
 
 def second_gradient_body(count, *refs):
     (norms, adjoint_in, gradient_in, model, model_jumps, grad_jumps, start_multiplier, threshold, one, two, linked_ref,
-     kernel, plain, weighted_t, model_out, jumps_out, multiplier_out, gradient_out, sent, edge) = refs[count:]
+     kernel, plain, weighted_t, model_out, sum_out, gradient_out, sent, edge) = refs[count:]
     times, cells = model.shape
     half = times // 2
     total = summed(refs[:count])
@@ -452,8 +452,7 @@
             at = slice(r * COLS, (r + 1) * COLS)
             new = model_jumps[k, :, at] - step * grad_jumps[k, :, at]
             multiplier, penalty = advance(new, strip(start_multiplier[k], r), strip(threshold[0:1], r))
-            jumps_out[k, :, at] = new
-            multiplier_out[k, :, at] = multiplier
+            sum_out[k, :, at] = new + multiplier
             penalties[k].append(penalty)
             new_jumps[k].append(new)
     _, beside_above = advance(-new_jumps[2][0], above[times : 2 * times], above[2 * times : 2 * times + 1])
@@ -477,9 +476,8 @@
     norms[...] = squares
 
 
-def before_finish_body(gradient, model_jumps, multiplier, linked, sum_out, jumps_out):
+def before_finish_body(gradient, linked, jumps_out):
     field = gradient[...]
-    sum_out[...] = model_jumps[...] + multiplier[...]
     nothing = jnp.zeros((field.shape[0], COLS), jnp.float32)
     for k, strips in enumerate(jumps(field, nothing, nothing, linked[...])):
         for r, values in enumerate(strips):
@@ -633,14 +631,14 @@
     model_jumps, grad_jumps = call(
         both_jumps_body, [wide, wide], start_model, gradient, one, two, grad_one, grad_two, passed, linked
     )
-    model, model_jumps, multiplier, gradient, sent, edge = call(
-        functools.partial(second_gradient_body, len(parts)), [field, wide, wide, field, message, side],
+    model, sums, gradient, sent, edge = call(
+        functools.partial(second_gradient_body, len(parts)), [field, wide, field, message, side],
         *parts, norms, adjoint_one, gradient, start_model, model_jumps, grad_jumps, start_multiplier, threshold,
         one, two, linked, across, plain, weighted_t,
     )
     grad_one, grad_two = from_partner(sent), from_other(edge)
     parts = cell_parts(call(merge_body, (half + 8, LANES), sent, grad_one, edge, grad_two, linked))
-    sums, inner_jumps = call(before_finish_body, [wide, wide], gradient, model_jumps, multiplier, linked)
+    inner_jumps = call(before_finish_body, wide, gradient, linked)
     scalars, passing, norms = call(
         functools.partial(response_body, len(parts)), [(8, LANES), (8 + times, LANES), (8, LANES)], *parts, grad_two
     )

time: 63.4 us -> 63.4 us (level)
  no operation moved by 1% of the time
where the time goes in v15:
time: 63.4 us; the launch traced here: 63.2 us
  starting transfers between devices  26.6 us (42%)
  waiting for transfers between devices  24.8 us (39%)
  Pallas kernels  11 us (17%)
  between operations  0.81 us (1%)
    ppermute x11, starting transfers between devices, summing(): lax.ppermute(total, axis, [(i, i ^ k * stride) for i in range(count)])  16.7 us
    ppermute x11, waiting for transfers between devices, summing(): lax.ppermute(total, axis, [(i, i ^ k * stride) for i in range(count)])  13.2 us
    pallas_call x13, Pallas kernels, call(): pl.pallas_call(body, out_shape=shapes, in_specs=[pl.BlockSpec(memory_spac...  11 us
    ppermute x3, waiting for transfers between devices, from_partner(): lax.ppermute(array, 'cell', [(i, i ^ 1) for i in range(lax.axis_size('cel...  6.17 us
    ppermute x3, starting transfers between devices, from_partner(): lax.ppermute(array, 'cell', [(i, i ^ 1) for i in range(lax.axis_size('cel...  5.79 us
    ppermute x3, waiting for transfers between devices, last_sensor_parts(): lax.ppermute(array, 'sensor', [(i, i ^ k) for i in range(count)])  2.83 us
    ppermute x2, waiting for transfers between devices, sensor_hop(): lax.ppermute(array, 'sensor', [(i, i ^ 1) for i in range(lax.axis_size('s...  2.54 us
    ppermute x3, starting transfers between devices, from_other(): return lax.ppermute(array, ('cell', 'sensor'), pairs)  1.96 us
  transfers between devices with their start and end apart: 22, of which 14 were waited for; matrix products, arithmetic and copies ran while one was open for 0% of the time, Pallas kernels for 2%

profile of v15, /device:TPU:0, one launch (start us, length us, event | category | flops | bytes accessed | tf_op | source)
XLA Modules:
  0.0 63.2 jit_solution(14014044251367540910)
XLA Ops:
  0.6 3.7 %shard_map.130 = (f32[168,128]{1,0:T(8,128)S(1)}, f32[136,128]{1,0:T(8,128)S(1)}, f32[8,256]{1,0:T(8,128)S(1)}, f32[8,256]{1,0:T(8,128)S(1)}, bf16[2,65,64,256]{...) custom-call(bf16[2,65,64,256]{3,2,1,0:T(8,128)(2,1)} %refs_0_.1, ...), custom_call_target="tpu_custom_call" | custom-call | tf_op jit(solution)/shard_map/pallas_call | solution.py:218
  4.3 3.0 %collective-permute-start = (f32[168,128]{1,0:T(8,128)S(1)}, f32[168,128]{1,0:T(8,128)S(1)}, u32[]{:S(2)}, u32[]{:S(2)}) collective-permute-start(f32[168,128]{1,0:T(8,128)S(1)} %get-tuple-element.32), channel_id=1, source_target_pairs={{0,4},{4,0},{8,12},{12,8},{16,20},{20,16},{24,28},{28,24},{1,5},{5... | collective-permute-start | bytes 258056 | tf_op jit(solution)/shard_map/ppermute | solution.py:572
  8.0 1.9 %collective-permute-done.came.one.refs_10_ = f32[168,128]{1,0:T(8,128)S(1)} collective-permute-done((f32[168,128]{1,0:T(8,128)S(1)}, f32[168,128]{1,0:T(8,128)S(1)}, u32[]{:S(2)}, u32[]{:S(2)}) %collective-permute-start) | collective-permute-done | bytes 86048 | tf_op jit(solution)/shard_map/ppermute | solution.py:572
  9.9 4.0 %collective-permute-start.3 = (f32[32,128]{1,0:T(8,128)S(1)}, f32[32,128]{1,0:T(8,128)S(1)}, u32[]{:S(2)}, u32[]{:S(2)}) collective-permute-start(f32[32,128]{1,0:T(8,128)S(1)} %slice_add_fusion.2.refs_0_), channel_id=1, source_target_pairs={{0,24},{4,28},{8,16},{12,20},{16,8},{20,12},{24,0},{28,4},{1,25},{... | collective-permute-start | bytes 49160 | tf_op jit(solution)/shard_map/ppermute | solution.py:538
  15.8 2.8 %collective-permute-done.2.refs_2_ = f32[32,128]{1,0:T(8,128)S(1)} collective-permute-done((f32[32,128]{1,0:T(8,128)S(1)}, f32[32,128]{1,0:T(8,128)S(1)}, u32[]{:S(2)}, u32[]{:S(2)}) %collective-permute-start.2) | collective-permute-done | bytes 16416 | tf_op jit(solution)/shard_map/ppermute | solution.py:538
  19.7 1.3 %collective-permute-done.5.passed = f32[136,256]{1,0:T(8,128)S(1)} collective-permute-done((f32[136,256]{1,0:T(8,128)S(1)}, f32[136,256]{1,0:T(8,128)S(1)}, u32[]{:S(2)}, u32[]{:S(2)}) %collective-permute-start.5) | collective-permute-done | bytes 139296 | tf_op jit(solution)/shard_map/ppermute | solution.py:545
  21.1 1.6 %collective-permute-start.6 = (f32[64,256]{1,0:T(8,128)S(1)}, f32[64,256]{1,0:T(8,128)S(1)}, u32[]{:S(2)}, u32[]{:S(2)}) collective-permute-start(f32[64,256]{1,0:T(8,128)S(1)} %slice_add_fusion.1.refs_0_), channel_id=1, source_target_pairs={{0,2},{1,3},{2,0},{3,1},{4,6},{5,7},{6,4},{7,5},{8,10},{9,11},{10,... | collective-permute-start | bytes 196616 | tf_op jit(solution)/shard_map/ppermute | solution.py:538
  22.8 2.7 %collective-permute-done.6.refs_1_ = f32[64,256]{1,0:T(8,128)S(1)} collective-permute-done((f32[64,256]{1,0:T(8,128)S(1)}, f32[64,256]{1,0:T(8,128)S(1)}, u32[]{:S(2)}, u32[]{:S(2)}) %collective-permute-start.6) | collective-permute-done | bytes 65568 | tf_op jit(solution)/shard_map/ppermute | solution.py:538
  26.5 1.6 %collective-permute-start.7 = (f32[104,128]{1,0:T(8,128)S(1)}, f32[104,128]{1,0:T(8,128)S(1)}, u32[]{:S(2)}, u32[]{:S(2)}) collective-permute-start(f32[104,128]{1,0:T(8,128)S(1)} %get-tuple-element.42.sent), channel_id=1, source_target_pairs={{0,4},{4,0},{8,12},{12,8},{16,20},{20,16},{24,28},{28,24},{1,5},{5... | collective-permute-start | bytes 159752 | tf_op jit(solution)/shard_map/ppermute | solution.py:572
  28.7 1.9 %collective-permute-done.7.came.grad_one = f32[104,128]{1,0:T(8,128)S(1)} collective-permute-done((f32[104,128]{1,0:T(8,128)S(1)}, f32[104,128]{1,0:T(8,128)S(1)}, u32[]{:S(2)}, u32[]{:S(2)}) %collective-permute-start.7) | collective-permute-done | bytes 53280 | tf_op jit(solution)/shard_map/ppermute | solution.py:572
  30.8 1.5 %collective-permute-start.11 = (f32[40,128]{1,0:T(8,128)S(1)}, f32[40,128]{1,0:T(8,128)S(1)}, u32[]{:S(2)}, u32[]{:S(2)}) collective-permute-start(f32[40,128]{1,0:T(8,128)S(1)} %shard_map.135.refs_0_), channel_id=1, source_target_pairs={{0,24},{4,28},{8,16},{12,20},{16,8},{20,12},{24,0},{28,4},{1,25},{... | collective-permute-start | bytes 61448 | tf_op jit(solution)/shard_map/ppermute | solution.py:538
  33.0 2.3 %collective-permute-start.9 = (f32[40,128]{1,0:T(8,128)S(1)}, f32[40,128]{1,0:T(8,128)S(1)}, u32[]{:S(2)}, u32[]{:S(2)}) collective-permute-start(f32[40,128]{1,0:T(8,128)S(1)} %shard_map.135.refs_0_), channel_id=1, source_target_pairs={{0,8},{4,12},{8,0},{12,4},{16,24},{20,28},{24,16},{28,20},{1,9},{5... | collective-permute-start | bytes 61448 | tf_op jit(solution)/shard_map/ppermute | solution.py:538
  35.3 1.2 %collective-permute-done.11.refs_3_ = f32[40,128]{1,0:T(8,128)S(1)} collective-permute-done((f32[40,128]{1,0:T(8,128)S(1)}, f32[40,128]{1,0:T(8,128)S(1)}, u32[]{:S(2)}, u32[]{:S(2)}) %collective-permute-start.11) | collective-permute-done | bytes 20512 | tf_op jit(solution)/shard_map/ppermute | solution.py:538
  39.0 1.2 %collective-permute-done.12.passed = f32[104,256]{1,0:T(8,128)S(1)} collective-permute-done((f32[104,256]{1,0:T(8,128)S(1)}, f32[104,256]{1,0:T(8,128)S(1)}, u32[]{:S(2)}, u32[]{:S(2)}) %collective-permute-start.12) | collective-permute-done | bytes 106528 | tf_op jit(solution)/shard_map/ppermute | solution.py:545
  40.2 1.6 %collective-permute-start.13 = (f32[72,256]{1,0:T(8,128)S(1)}, f32[72,256]{1,0:T(8,128)S(1)}, u32[]{:S(2)}, u32[]{:S(2)}) collective-permute-start(f32[72,256]{1,0:T(8,128)S(1)} %slice_add_fusion.refs_0_), channel_id=1, source_target_pairs={{0,2},{1,3},{2,0},{3,1},{4,6},{5,7},{6,4},{7,5},{8,10},{9,11},{10,... | collective-permute-start | bytes 221192 | tf_op jit(solution)/shard_map/ppermute | solution.py:538
  41.9 2.7 %collective-permute-done.13.refs_1_ = f32[72,256]{1,0:T(8,128)S(1)} collective-permute-done((f32[72,256]{1,0:T(8,128)S(1)}, f32[72,256]{1,0:T(8,128)S(1)}, u32[]{:S(2)}, u32[]{:S(2)}) %collective-permute-start.13) | collective-permute-done | bytes 73760 | tf_op jit(solution)/shard_map/ppermute | solution.py:538
  44.6 1.2 %shard_map.138 = (f32[64,256]{1,0:T(8,128)S(1)}, f32[4,64,256]{2,1,0:T(8,128)S(1)}, f32[64,256]{1,0:T(8,128)S(1)}, f32[104,128]{1,0:T(8,128)S(1)}, f32[64,128]{1,0:T(8,128)S(1)}) custom-call(f32[72,256]{1,0:T(8,128)S(1)} %slice_add_fusion.refs_0_, f32[72,256]{1,0:T(8,128)S(1)} %collective-permute-done.13.refs_1_, f32[8,128]{1,0:T(8,128)S(1)} %get-tuple-element.45.refs_2_, ...), custom_call_target="tpu_custom_call" | custom-call | tf_op jit(solution)/shard_map/pallas_call | solution.py:218
  47.7 2.4 %collective-permute-done.14.came.refs_10_ = f32[104,128]{1,0:T(8,128)S(1)} collective-permute-done((f32[104,128]{1,0:T(8,128)S(1)}, f32[104,128]{1,0:T(8,128)S(1)}, u32[]{:S(2)}, u32[]{:S(2)}) %collective-permute-start.14) | collective-permute-done | bytes 53280 | tf_op jit(solution)/shard_map/ppermute | solution.py:572
  50.2 2.2 %collective-permute-start.18 = (f32[40,128]{1,0:T(8,128)S(1)}, f32[40,128]{1,0:T(8,128)S(1)}, u32[]{:S(2)}, u32[]{:S(2)}) collective-permute-start(f32[40,128]{1,0:T(8,128)S(1)} %shard_map.139.refs_0_), channel_id=1, source_target_pairs={{0,24},{4,28},{8,16},{12,20},{16,8},{20,12},{24,0},{28,4},{1,25},{... | collective-permute-start | bytes 61448 | tf_op jit(solution)/shard_map/ppermute | solution.py:538
  53.1 1.6 %collective-permute-start.16 = (f32[40,128]{1,0:T(8,128)S(1)}, f32[40,128]{1,0:T(8,128)S(1)}, u32[]{:S(2)}, u32[]{:S(2)}) collective-permute-start(f32[40,128]{1,0:T(8,128)S(1)} %shard_map.139.refs_0_), channel_id=1, source_target_pairs={{0,8},{4,12},{8,0},{12,4},{16,24},{20,28},{24,16},{28,20},{1,9},{5... | collective-permute-start | bytes 61448 | tf_op jit(solution)/shard_map/ppermute | solution.py:538
  54.7 1.2 %collective-permute-done.18.refs_3_ = f32[40,128]{1,0:T(8,128)S(1)} collective-permute-done((f32[40,128]{1,0:T(8,128)S(1)}, f32[40,128]{1,0:T(8,128)S(1)}, u32[]{:S(2)}, u32[]{:S(2)}) %collective-permute-start.18) | collective-permute-done | bytes 20512 | tf_op jit(solution)/shard_map/ppermute | solution.py:538
  55.9 1.4 %collective-permute-done.17.refs_2_ = f32[40,128]{1,0:T(8,128)S(1)} collective-permute-done((f32[40,128]{1,0:T(8,128)S(1)}, f32[40,128]{1,0:T(8,128)S(1)}, u32[]{:S(2)}, u32[]{:S(2)}) %collective-permute-start.17) | collective-permute-done | bytes 20512 | tf_op jit(solution)/shard_map/ppermute | solution.py:538
  57.4 1.3 %collective-permute-start.21 = (f32[72,128]{1,0:T(8,128)S(1)}, f32[72,128]{1,0:T(8,128)S(1)}, u32[]{:S(2)}, u32[]{:S(2)}) collective-permute-start(f32[72,128]{1,0:T(8,128)S(1)} %get-tuple-element.56), channel_id=1, source_target_pairs={{0,3},{1,2},{2,1},{3,0},{4,7},{5,6},{6,5},{7,4},{8,11},{9,10},{10,... | collective-permute-start | bytes 110600 | tf_op jit(solution)/shard_map/ppermute | solution.py:557
  59.5 2.8 %collective-permute-done.20.refs_2_ = f32[8,128]{1,0:T(8,128)S(1)} collective-permute-done((f32[8,128]{1,0:T(8,128)S(1)}, f32[8,128]{1,0:T(8,128)S(1)}, u32[]{:S(2)}, u32[]{:S(2)}) %collective-permute-start.20) | collective-permute-done | bytes 4128 | tf_op jit(solution)/shard_map/ppermute | solution.py:557
  (38 shorter events, 13.3 us)
Async XLA Ops:
  4.3 5.6 %collective-permute-start = (f32[168,128]{1,0:T(8,128)S(1)}, f32[168,128]{1,0:T(8,128)S(1)}, u32[]{:S(2)}, u32[]{:S(2)}) collective-permute-start(f32[168,128]{1,0:T(8,128)S(1)} %get-tuple-element.32), channel_id=1, source_target_pairs={{0,4},{4,0},{8,12},{12,8},{16,20},{20,16},{24,28},{28,24},{1,5},{5... | collective-permute-start | bytes 258056 | tf_op jit(solution)/shard_map/ppermute | solution.py:572
  7.4 8.4 %collective-permute-start.4 = (f32[136,128]{1,0:T(8,128)S(1)}, f32[136,128]{1,0:T(8,128)S(1)}, u32[]{:S(2)}, u32[]{:S(2)}) collective-permute-start(f32[136,128]{1,0:T(8,128)S(1)} %get-tuple-element.33), channel_id=1, source_target_pairs={{5,9},{7,11},{9,5},{11,7},{13,17},{15,19},{17,13},{19,15},{21,25},... | collective-permute-start | bytes 208904 | tf_op jit(solution)/shard_map/ppermute | solution.py:582
  9.9 5.9 %collective-permute-start.3 = (f32[32,128]{1,0:T(8,128)S(1)}, f32[32,128]{1,0:T(8,128)S(1)}, u32[]{:S(2)}, u32[]{:S(2)}) collective-permute-start(f32[32,128]{1,0:T(8,128)S(1)} %slice_add_fusion.2.refs_0_), channel_id=1, source_target_pairs={{0,24},{4,28},{8,16},{12,20},{16,8},{20,12},{24,0},{28,4},{1,25},{... | collective-permute-start | bytes 49160 | tf_op jit(solution)/shard_map/ppermute | solution.py:538
  13.9 4.6 %collective-permute-start.2 = (f32[32,128]{1,0:T(8,128)S(1)}, f32[32,128]{1,0:T(8,128)S(1)}, u32[]{:S(2)}, u32[]{:S(2)}) collective-permute-start(f32[32,128]{1,0:T(8,128)S(1)} %slice_add_fusion.2.refs_0_), channel_id=1, source_target_pairs={{0,16},{4,20},{8,24},{12,28},{16,0},{20,4},{24,8},{28,12},{1,17},{... | collective-permute-start | bytes 49160 | tf_op jit(solution)/shard_map/ppermute | solution.py:538
  13.9 4.6 %collective-permute-start.1 = (f32[32,128]{1,0:T(8,128)S(1)}, f32[32,128]{1,0:T(8,128)S(1)}, u32[]{:S(2)}, u32[]{:S(2)}) collective-permute-start(f32[32,128]{1,0:T(8,128)S(1)} %slice_add_fusion.2.refs_0_), channel_id=1, source_target_pairs={{0,8},{4,12},{8,0},{12,4},{16,24},{20,28},{24,16},{28,20},{1,9},{5... | collective-permute-start | bytes 49160 | tf_op jit(solution)/shard_map/ppermute | solution.py:538
  14.6 4.0 %copy-start = (f32[64,64]{1,0:T(8,128)S(1)}, f32[64,64]{1,0:T(8,128)}, u32[]{:S(2)}) copy-start(f32[64,64]{1,0:T(8,128)} %refs_4_.2) | copy-start | bytes 49156
  19.6 1.4 %collective-permute-start.5 = (f32[136,256]{1,0:T(8,128)S(1)}, f32[136,256]{1,0:T(8,128)S(1)}, u32[]{:S(2)}, u32[]{:S(2)}) collective-permute-start(f32[136,256]{1,0:T(8,128)S(1)} %shard_map.132), channel_id=1, source_target_pairs={{0,1},{1,0},{2,3},{3,2},{4,5},{5,4},{6,7},{7,6},{8,9},{9,8},{10,11... | collective-permute-start | bytes 417800 | tf_op jit(solution)/shard_map/ppermute | solution.py:545
  21.1 4.3 %collective-permute-start.6 = (f32[64,256]{1,0:T(8,128)S(1)}, f32[64,256]{1,0:T(8,128)S(1)}, u32[]{:S(2)}, u32[]{:S(2)}) collective-permute-start(f32[64,256]{1,0:T(8,128)S(1)} %slice_add_fusion.1.refs_0_), channel_id=1, source_target_pairs={{0,2},{1,3},{2,0},{3,1},{4,6},{5,7},{6,4},{7,5},{8,10},{9,11},{10,... | collective-permute-start | bytes 196616 | tf_op jit(solution)/shard_map/ppermute | solution.py:538
  26.5 4.2 %collective-permute-start.7 = (f32[104,128]{1,0:T(8,128)S(1)}, f32[104,128]{1,0:T(8,128)S(1)}, u32[]{:S(2)}, u32[]{:S(2)}) collective-permute-start(f32[104,128]{1,0:T(8,128)S(1)} %get-tuple-element.42.sent), channel_id=1, source_target_pairs={{0,4},{4,0},{8,12},{12,8},{16,20},{20,16},{24,28},{28,24},{1,5},{5... | collective-permute-start | bytes 159752 | tf_op jit(solution)/shard_map/ppermute | solution.py:572
  28.1 0.7 %collective-permute-start.8 = (f32[64,128]{1,0:T(8,128)S(1)}, f32[64,128]{1,0:T(8,128)S(1)}, u32[]{:S(2)}, u32[]{:S(2)}) collective-permute-start(f32[64,128]{1,0:T(8,128)S(1)} %get-tuple-element.43.edge), channel_id=1, source_target_pairs={{5,9},{7,11},{9,5},{11,7},{13,17},{15,19},{17,13},{19,15},{21,25},... | collective-permute-start | bytes 98312 | tf_op jit(solution)/shard_map/ppermute | solution.py:582
  30.8 5.6 %collective-permute-start.11 = (f32[40,128]{1,0:T(8,128)S(1)}, f32[40,128]{1,0:T(8,128)S(1)}, u32[]{:S(2)}, u32[]{:S(2)}) collective-permute-start(f32[40,128]{1,0:T(8,128)S(1)} %shard_map.135.refs_0_), channel_id=1, source_target_pairs={{0,24},{4,28},{8,16},{12,20},{16,8},{20,12},{24,0},{28,4},{1,25},{... | collective-permute-start | bytes 61448 | tf_op jit(solution)/shard_map/ppermute | solution.py:538
  32.4 4.7 %collective-permute-start.10 = (f32[40,128]{1,0:T(8,128)S(1)}, f32[40,128]{1,0:T(8,128)S(1)}, u32[]{:S(2)}, u32[]{:S(2)}) collective-permute-start(f32[40,128]{1,0:T(8,128)S(1)} %shard_map.135.refs_0_), channel_id=1, source_target_pairs={{0,16},{4,20},{8,24},{12,28},{16,0},{20,4},{24,8},{28,12},{1,17},{... | collective-permute-start | bytes 61448 | tf_op jit(solution)/shard_map/ppermute | solution.py:538
  33.0 4.7 %collective-permute-start.9 = (f32[40,128]{1,0:T(8,128)S(1)}, f32[40,128]{1,0:T(8,128)S(1)}, u32[]{:S(2)}, u32[]{:S(2)}) collective-permute-start(f32[40,128]{1,0:T(8,128)S(1)} %shard_map.135.refs_0_), channel_id=1, source_target_pairs={{0,8},{4,12},{8,0},{12,4},{16,24},{20,28},{24,16},{28,20},{1,9},{5... | collective-permute-start | bytes 61448 | tf_op jit(solution)/shard_map/ppermute | solution.py:538
  38.8 1.4 %collective-permute-start.12 = (f32[104,256]{1,0:T(8,128)S(1)}, f32[104,256]{1,0:T(8,128)S(1)}, u32[]{:S(2)}, u32[]{:S(2)}) collective-permute-start(f32[104,256]{1,0:T(8,128)S(1)} %get-tuple-element.44), channel_id=1, source_target_pairs={{0,1},{1,0},{2,3},{3,2},{4,5},{5,4},{6,7},{7,6},{8,9},{9,8},{10,11... | collective-permute-start | bytes 319496 | tf_op jit(solution)/shard_map/ppermute | solution.py:545
  40.2 4.4 %collective-permute-start.13 = (f32[72,256]{1,0:T(8,128)S(1)}, f32[72,256]{1,0:T(8,128)S(1)}, u32[]{:S(2)}, u32[]{:S(2)}) collective-permute-start(f32[72,256]{1,0:T(8,128)S(1)} %slice_add_fusion.refs_0_), channel_id=1, source_target_pairs={{0,2},{1,3},{2,0},{3,1},{4,6},{5,7},{6,4},{7,5},{8,10},{9,11},{10,... | collective-permute-start | bytes 221192 | tf_op jit(solution)/shard_map/ppermute | solution.py:538
  45.9 4.2 %collective-permute-start.14 = (f32[104,128]{1,0:T(8,128)S(1)}, f32[104,128]{1,0:T(8,128)S(1)}, u32[]{:S(2)}, u32[]{:S(2)}) collective-permute-start(f32[104,128]{1,0:T(8,128)S(1)} %get-tuple-element.53.sent), channel_id=1, source_target_pairs={{0,4},{4,0},{8,12},{12,8},{16,20},{20,16},{24,28},{28,24},{1,5},{5... | collective-permute-start | bytes 159752 | tf_op jit(solution)/shard_map/ppermute | solution.py:572
  47.1 0.7 %collective-permute-start.15 = (f32[64,128]{1,0:T(8,128)S(1)}, f32[64,128]{1,0:T(8,128)S(1)}, u32[]{:S(2)}, u32[]{:S(2)}) collective-permute-start(f32[64,128]{1,0:T(8,128)S(1)} %get-tuple-element.54.edge), channel_id=1, source_target_pairs={{5,9},{7,11},{9,5},{11,7},{13,17},{15,19},{17,13},{19,15},{21,25},... | collective-permute-start | bytes 98312 | tf_op jit(solution)/shard_map/ppermute | solution.py:582
  50.2 5.6 %collective-permute-start.18 = (f32[40,128]{1,0:T(8,128)S(1)}, f32[40,128]{1,0:T(8,128)S(1)}, u32[]{:S(2)}, u32[]{:S(2)}) collective-permute-start(f32[40,128]{1,0:T(8,128)S(1)} %shard_map.139.refs_0_), channel_id=1, source_target_pairs={{0,24},{4,28},{8,16},{12,20},{16,8},{20,12},{24,0},{28,4},{1,25},{... | collective-permute-start | bytes 61448 | tf_op jit(solution)/shard_map/ppermute | solution.py:538
  52.5 4.8 %collective-permute-start.17 = (f32[40,128]{1,0:T(8,128)S(1)}, f32[40,128]{1,0:T(8,128)S(1)}, u32[]{:S(2)}, u32[]{:S(2)}) collective-permute-start(f32[40,128]{1,0:T(8,128)S(1)} %shard_map.139.refs_0_), channel_id=1, source_target_pairs={{0,16},{4,20},{8,24},{12,28},{16,0},{20,4},{24,8},{28,12},{1,17},{... | collective-permute-start | bytes 61448 | tf_op jit(solution)/shard_map/ppermute | solution.py:538
  53.1 4.2 %collective-permute-start.16 = (f32[40,128]{1,0:T(8,128)S(1)}, f32[40,128]{1,0:T(8,128)S(1)}, u32[]{:S(2)}, u32[]{:S(2)}) collective-permute-start(f32[40,128]{1,0:T(8,128)S(1)} %shard_map.139.refs_0_), channel_id=1, source_target_pairs={{0,8},{4,12},{8,0},{12,4},{16,24},{20,28},{24,16},{28,20},{1,9},{5... | collective-permute-start | bytes 61448 | tf_op jit(solution)/shard_map/ppermute | solution.py:538
  57.4 4.9 %collective-permute-start.21 = (f32[72,128]{1,0:T(8,128)S(1)}, f32[72,128]{1,0:T(8,128)S(1)}, u32[]{:S(2)}, u32[]{:S(2)}) collective-permute-start(f32[72,128]{1,0:T(8,128)S(1)} %get-tuple-element.56), channel_id=1, source_target_pairs={{0,3},{1,2},{2,1},{3,0},{4,7},{5,6},{6,5},{7,4},{8,11},{9,10},{10,... | collective-permute-start | bytes 110600 | tf_op jit(solution)/shard_map/ppermute | solution.py:557
  58.7 3.6 %collective-permute-start.20 = (f32[8,128]{1,0:T(8,128)S(1)}, f32[8,128]{1,0:T(8,128)S(1)}, u32[]{:S(2)}, u32[]{:S(2)}) collective-permute-start(f32[8,128]{1,0:T(8,128)S(1)} %get-tuple-element.55.refs_0_), channel_id=1, source_target_pairs={{0,2},{1,3},{2,0},{3,1},{4,6},{5,7},{6,4},{7,5},{8,10},{9,11},{10,... | collective-permute-start | bytes 12296 | tf_op jit(solution)/shard_map/ppermute | solution.py:557
  59.2 3.1 %collective-permute-start.19 = (f32[8,128]{1,0:T(8,128)S(1)}, f32[8,128]{1,0:T(8,128)S(1)}, u32[]{:S(2)}, u32[]{:S(2)}) collective-permute-start(f32[8,128]{1,0:T(8,128)S(1)} %get-tuple-element.55.refs_0_), channel_id=1, source_target_pairs={{0,1},{1,0},{2,3},{3,2},{4,5},{5,4},{6,7},{7,6},{8,9},{9,8},{10,11... | collective-permute-start | bytes 12296 | tf_op jit(solution)/shard_map/ppermute | solution.py:557

commit v16 on v15

--- a/solution.py
+++ b/solution.py
@@ -286,12 +286,11 @@
         return copy
 
     early = [load(loaded[i], kept[i]) for i in (1, 3)]
+    small = [load(loaded[i], kept[i]) for i in (7, 8, 9, 2, 4)]
     large = []
     for start in range(0, freqs, CHUNK):
         at = (slice(None), pl.ds(start, min(CHUNK, freqs - start)))
         large.append(load(kernel.at[at], kernel_here.at[at]))
-        if start == 0:
-            small = [load(loaded[i], kept[i]) for i in (7, 8, 9, 2, 4)]
     late = [load(loaded[i], kept[i]) for i in (5, 6)]
     for copy in early:
         copy.wait()

time: 63.4 us -> 63.3 us (level)
  no operation moved by 1% of the time
where the time goes in v16:
time: 63.3 us; the launch traced here: 63.1 us
  starting transfers between devices  26.6 us (42%)
  waiting for transfers between devices  24.7 us (39%)
  Pallas kernels  10.9 us (17%)
  between operations  0.81 us (1%)
    ppermute x11, starting transfers between devices, summing(): lax.ppermute(total, axis, [(i, i ^ k * stride) for i in range(count)])  16.7 us
    ppermute x11, waiting for transfers between devices, summing(): lax.ppermute(total, axis, [(i, i ^ k * stride) for i in range(count)])  13.2 us
    pallas_call x13, Pallas kernels, call(): pl.pallas_call(body, out_shape=shapes, in_specs=[pl.BlockSpec(memory_spac...  10.9 us
    ppermute x3, waiting for transfers between devices, from_partner(): lax.ppermute(array, 'cell', [(i, i ^ 1) for i in range(lax.axis_size('cel...  6.17 us
    ppermute x3, starting transfers between devices, from_partner(): lax.ppermute(array, 'cell', [(i, i ^ 1) for i in range(lax.axis_size('cel...  5.8 us
    ppermute x3, waiting for transfers between devices, last_sensor_parts(): lax.ppermute(array, 'sensor', [(i, i ^ k) for i in range(count)])  2.82 us
    ppermute x2, waiting for transfers between devices, sensor_hop(): lax.ppermute(array, 'sensor', [(i, i ^ 1) for i in range(lax.axis_size('s...  2.54 us
    ppermute x3, starting transfers between devices, from_other(): return lax.ppermute(array, ('cell', 'sensor'), pairs)  1.96 us
  transfers between devices with their start and end apart: 22, of which 14 were waited for; matrix products, arithmetic and copies ran while one was open for 0% of the time, Pallas kernels for 2%

profile of v16, /device:TPU:0, one launch (start us, length us, event | category | flops | bytes accessed | tf_op | source)
XLA Modules:
  0.0 63.1 jit_solution(13732940319051215335)
XLA Ops:
  0.6 3.6 %shard_map.130 = (f32[168,128]{1,0:T(8,128)S(1)}, f32[136,128]{1,0:T(8,128)S(1)}, f32[8,256]{1,0:T(8,128)S(1)}, f32[8,256]{1,0:T(8,128)S(1)}, bf16[2,65,64,256]{...) custom-call(bf16[2,65,64,256]{3,2,1,0:T(8,128)(2,1)} %refs_0_.1, ...), custom_call_target="tpu_custom_call" | custom-call | tf_op jit(solution)/shard_map/pallas_call | solution.py:218
  4.3 3.0 %collective-permute-start = (f32[168,128]{1,0:T(8,128)S(1)}, f32[168,128]{1,0:T(8,128)S(1)}, u32[]{:S(2)}, u32[]{:S(2)}) collective-permute-start(f32[168,128]{1,0:T(8,128)S(1)} %get-tuple-element.32), channel_id=1, source_target_pairs={{0,4},{4,0},{8,12},{12,8},{16,20},{20,16},{24,28},{28,24},{1,5},{5... | collective-permute-start | bytes 258056 | tf_op jit(solution)/shard_map/ppermute | solution.py:571
  8.0 1.9 %collective-permute-done.came.one.refs_10_ = f32[168,128]{1,0:T(8,128)S(1)} collective-permute-done((f32[168,128]{1,0:T(8,128)S(1)}, f32[168,128]{1,0:T(8,128)S(1)}, u32[]{:S(2)}, u32[]{:S(2)}) %collective-permute-start) | collective-permute-done | bytes 86048 | tf_op jit(solution)/shard_map/ppermute | solution.py:571
  9.8 4.0 %collective-permute-start.3 = (f32[32,128]{1,0:T(8,128)S(1)}, f32[32,128]{1,0:T(8,128)S(1)}, u32[]{:S(2)}, u32[]{:S(2)}) collective-permute-start(f32[32,128]{1,0:T(8,128)S(1)} %slice_add_fusion.2.refs_0_), channel_id=1, source_target_pairs={{0,24},{4,28},{8,16},{12,20},{16,8},{20,12},{24,0},{28,4},{1,25},{... | collective-permute-start | bytes 49160 | tf_op jit(solution)/shard_map/ppermute | solution.py:537
  15.7 2.8 %collective-permute-done.2.refs_2_ = f32[32,128]{1,0:T(8,128)S(1)} collective-permute-done((f32[32,128]{1,0:T(8,128)S(1)}, f32[32,128]{1,0:T(8,128)S(1)}, u32[]{:S(2)}, u32[]{:S(2)}) %collective-permute-start.2) | collective-permute-done | bytes 16416 | tf_op jit(solution)/shard_map/ppermute | solution.py:537
  19.6 1.3 %collective-permute-done.5.passed = f32[136,256]{1,0:T(8,128)S(1)} collective-permute-done((f32[136,256]{1,0:T(8,128)S(1)}, f32[136,256]{1,0:T(8,128)S(1)}, u32[]{:S(2)}, u32[]{:S(2)}) %collective-permute-start.5) | collective-permute-done | bytes 139296 | tf_op jit(solution)/shard_map/ppermute | solution.py:544
  21.0 1.6 %collective-permute-start.6 = (f32[64,256]{1,0:T(8,128)S(1)}, f32[64,256]{1,0:T(8,128)S(1)}, u32[]{:S(2)}, u32[]{:S(2)}) collective-permute-start(f32[64,256]{1,0:T(8,128)S(1)} %slice_add_fusion.1.refs_0_), channel_id=1, source_target_pairs={{0,2},{1,3},{2,0},{3,1},{4,6},{5,7},{6,4},{7,5},{8,10},{9,11},{10,... | collective-permute-start | bytes 196616 | tf_op jit(solution)/shard_map/ppermute | solution.py:537
  22.7 2.7 %collective-permute-done.6.refs_1_ = f32[64,256]{1,0:T(8,128)S(1)} collective-permute-done((f32[64,256]{1,0:T(8,128)S(1)}, f32[64,256]{1,0:T(8,128)S(1)}, u32[]{:S(2)}, u32[]{:S(2)}) %collective-permute-start.6) | collective-permute-done | bytes 65568 | tf_op jit(solution)/shard_map/ppermute | solution.py:537
  26.4 1.6 %collective-permute-start.7 = (f32[104,128]{1,0:T(8,128)S(1)}, f32[104,128]{1,0:T(8,128)S(1)}, u32[]{:S(2)}, u32[]{:S(2)}) collective-permute-start(f32[104,128]{1,0:T(8,128)S(1)} %get-tuple-element.42.sent), channel_id=1, source_target_pairs={{0,4},{4,0},{8,12},{12,8},{16,20},{20,16},{24,28},{28,24},{1,5},{5... | collective-permute-start | bytes 159752 | tf_op jit(solution)/shard_map/ppermute | solution.py:571
  28.7 1.9 %collective-permute-done.7.came.grad_one = f32[104,128]{1,0:T(8,128)S(1)} collective-permute-done((f32[104,128]{1,0:T(8,128)S(1)}, f32[104,128]{1,0:T(8,128)S(1)}, u32[]{:S(2)}, u32[]{:S(2)}) %collective-permute-start.7) | collective-permute-done | bytes 53280 | tf_op jit(solution)/shard_map/ppermute | solution.py:571
  30.7 1.5 %collective-permute-start.11 = (f32[40,128]{1,0:T(8,128)S(1)}, f32[40,128]{1,0:T(8,128)S(1)}, u32[]{:S(2)}, u32[]{:S(2)}) collective-permute-start(f32[40,128]{1,0:T(8,128)S(1)} %shard_map.135.refs_0_), channel_id=1, source_target_pairs={{0,24},{4,28},{8,16},{12,20},{16,8},{20,12},{24,0},{28,4},{1,25},{... | collective-permute-start | bytes 61448 | tf_op jit(solution)/shard_map/ppermute | solution.py:537
  32.9 2.3 %collective-permute-start.9 = (f32[40,128]{1,0:T(8,128)S(1)}, f32[40,128]{1,0:T(8,128)S(1)}, u32[]{:S(2)}, u32[]{:S(2)}) collective-permute-start(f32[40,128]{1,0:T(8,128)S(1)} %shard_map.135.refs_0_), channel_id=1, source_target_pairs={{0,8},{4,12},{8,0},{12,4},{16,24},{20,28},{24,16},{28,20},{1,9},{5... | collective-permute-start | bytes 61448 | tf_op jit(solution)/shard_map/ppermute | solution.py:537
  35.2 1.2 %collective-permute-done.11.refs_3_ = f32[40,128]{1,0:T(8,128)S(1)} collective-permute-done((f32[40,128]{1,0:T(8,128)S(1)}, f32[40,128]{1,0:T(8,128)S(1)}, u32[]{:S(2)}, u32[]{:S(2)}) %collective-permute-start.11) | collective-permute-done | bytes 20512 | tf_op jit(solution)/shard_map/ppermute | solution.py:537
  38.9 1.2 %collective-permute-done.12.passed = f32[104,256]{1,0:T(8,128)S(1)} collective-permute-done((f32[104,256]{1,0:T(8,128)S(1)}, f32[104,256]{1,0:T(8,128)S(1)}, u32[]{:S(2)}, u32[]{:S(2)}) %collective-permute-start.12) | collective-permute-done | bytes 106528 | tf_op jit(solution)/shard_map/ppermute | solution.py:544
  40.1 1.6 %collective-permute-start.13 = (f32[72,256]{1,0:T(8,128)S(1)}, f32[72,256]{1,0:T(8,128)S(1)}, u32[]{:S(2)}, u32[]{:S(2)}) collective-permute-start(f32[72,256]{1,0:T(8,128)S(1)} %slice_add_fusion.refs_0_), channel_id=1, source_target_pairs={{0,2},{1,3},{2,0},{3,1},{4,6},{5,7},{6,4},{7,5},{8,10},{9,11},{10,... | collective-permute-start | bytes 221192 | tf_op jit(solution)/shard_map/ppermute | solution.py:537
  41.8 2.7 %collective-permute-done.13.refs_1_ = f32[72,256]{1,0:T(8,128)S(1)} collective-permute-done((f32[72,256]{1,0:T(8,128)S(1)}, f32[72,256]{1,0:T(8,128)S(1)}, u32[]{:S(2)}, u32[]{:S(2)}) %collective-permute-start.13) | collective-permute-done | bytes 73760 | tf_op jit(solution)/shard_map/ppermute | solution.py:537
  44.6 1.2 %shard_map.138 = (f32[64,256]{1,0:T(8,128)S(1)}, f32[4,64,256]{2,1,0:T(8,128)S(1)}, f32[64,256]{1,0:T(8,128)S(1)}, f32[104,128]{1,0:T(8,128)S(1)}, f32[64,128]{1,0:T(8,128)S(1)}) custom-call(f32[72,256]{1,0:T(8,128)S(1)} %slice_add_fusion.refs_0_, f32[72,256]{1,0:T(8,128)S(1)} %collective-permute-done.13.refs_1_, f32[8,128]{1,0:T(8,128)S(1)} %get-tuple-element.45.refs_2_, ...), custom_call_target="tpu_custom_call" | custom-call | tf_op jit(solution)/shard_map/pallas_call | solution.py:218
  47.7 2.4 %collective-permute-done.14.came.refs_10_ = f32[104,128]{1,0:T(8,128)S(1)} collective-permute-done((f32[104,128]{1,0:T(8,128)S(1)}, f32[104,128]{1,0:T(8,128)S(1)}, u32[]{:S(2)}, u32[]{:S(2)}) %collective-permute-start.14) | collective-permute-done | bytes 53280 | tf_op jit(solution)/shard_map/ppermute | solution.py:571
  50.2 2.2 %collective-permute-start.18 = (f32[40,128]{1,0:T(8,128)S(1)}, f32[40,128]{1,0:T(8,128)S(1)}, u32[]{:S(2)}, u32[]{:S(2)}) collective-permute-start(f32[40,128]{1,0:T(8,128)S(1)} %shard_map.139.refs_0_), channel_id=1, source_target_pairs={{0,24},{4,28},{8,16},{12,20},{16,8},{20,12},{24,0},{28,4},{1,25},{... | collective-permute-start | bytes 61448 | tf_op jit(solution)/shard_map/ppermute | solution.py:537
  53.1 1.5 %collective-permute-start.16 = (f32[40,128]{1,0:T(8,128)S(1)}, f32[40,128]{1,0:T(8,128)S(1)}, u32[]{:S(2)}, u32[]{:S(2)}) collective-permute-start(f32[40,128]{1,0:T(8,128)S(1)} %shard_map.139.refs_0_), channel_id=1, source_target_pairs={{0,8},{4,12},{8,0},{12,4},{16,24},{20,28},{24,16},{28,20},{1,9},{5... | collective-permute-start | bytes 61448 | tf_op jit(solution)/shard_map/ppermute | solution.py:537
  54.6 1.2 %collective-permute-done.18.refs_3_ = f32[40,128]{1,0:T(8,128)S(1)} collective-permute-done((f32[40,128]{1,0:T(8,128)S(1)}, f32[40,128]{1,0:T(8,128)S(1)}, u32[]{:S(2)}, u32[]{:S(2)}) %collective-permute-start.18) | collective-permute-done | bytes 20512 | tf_op jit(solution)/shard_map/ppermute | solution.py:537
  55.8 1.4 %collective-permute-done.17.refs_2_ = f32[40,128]{1,0:T(8,128)S(1)} collective-permute-done((f32[40,128]{1,0:T(8,128)S(1)}, f32[40,128]{1,0:T(8,128)S(1)}, u32[]{:S(2)}, u32[]{:S(2)}) %collective-permute-start.17) | collective-permute-done | bytes 20512 | tf_op jit(solution)/shard_map/ppermute | solution.py:537
  57.4 1.3 %collective-permute-start.21 = (f32[72,128]{1,0:T(8,128)S(1)}, f32[72,128]{1,0:T(8,128)S(1)}, u32[]{:S(2)}, u32[]{:S(2)}) collective-permute-start(f32[72,128]{1,0:T(8,128)S(1)} %get-tuple-element.56), channel_id=1, source_target_pairs={{0,3},{1,2},{2,1},{3,0},{4,7},{5,6},{6,5},{7,4},{8,11},{9,10},{10,... | collective-permute-start | bytes 110600 | tf_op jit(solution)/shard_map/ppermute | solution.py:556
  59.4 2.8 %collective-permute-done.20.refs_2_ = f32[8,128]{1,0:T(8,128)S(1)} collective-permute-done((f32[8,128]{1,0:T(8,128)S(1)}, f32[8,128]{1,0:T(8,128)S(1)}, u32[]{:S(2)}, u32[]{:S(2)}) %collective-permute-start.20) | collective-permute-done | bytes 4128 | tf_op jit(solution)/shard_map/ppermute | solution.py:556
  (38 shorter events, 13.3 us)
Async XLA Ops:
  4.3 5.6 %collective-permute-start = (f32[168,128]{1,0:T(8,128)S(1)}, f32[168,128]{1,0:T(8,128)S(1)}, u32[]{:S(2)}, u32[]{:S(2)}) collective-permute-start(f32[168,128]{1,0:T(8,128)S(1)} %get-tuple-element.32), channel_id=1, source_target_pairs={{0,4},{4,0},{8,12},{12,8},{16,20},{20,16},{24,28},{28,24},{1,5},{5... | collective-permute-start | bytes 258056 | tf_op jit(solution)/shard_map/ppermute | solution.py:571
  7.3 8.4 %collective-permute-start.4 = (f32[136,128]{1,0:T(8,128)S(1)}, f32[136,128]{1,0:T(8,128)S(1)}, u32[]{:S(2)}, u32[]{:S(2)}) collective-permute-start(f32[136,128]{1,0:T(8,128)S(1)} %get-tuple-element.33), channel_id=1, source_target_pairs={{5,9},{7,11},{9,5},{11,7},{13,17},{15,19},{17,13},{19,15},{21,25},... | collective-permute-start | bytes 208904 | tf_op jit(solution)/shard_map/ppermute | solution.py:581
  9.8 5.9 %collective-permute-start.3 = (f32[32,128]{1,0:T(8,128)S(1)}, f32[32,128]{1,0:T(8,128)S(1)}, u32[]{:S(2)}, u32[]{:S(2)}) collective-permute-start(f32[32,128]{1,0:T(8,128)S(1)} %slice_add_fusion.2.refs_0_), channel_id=1, source_target_pairs={{0,24},{4,28},{8,16},{12,20},{16,8},{20,12},{24,0},{28,4},{1,25},{... | collective-permute-start | bytes 49160 | tf_op jit(solution)/shard_map/ppermute | solution.py:537
  13.9 4.6 %collective-permute-start.2 = (f32[32,128]{1,0:T(8,128)S(1)}, f32[32,128]{1,0:T(8,128)S(1)}, u32[]{:S(2)}, u32[]{:S(2)}) collective-permute-start(f32[32,128]{1,0:T(8,128)S(1)} %slice_add_fusion.2.refs_0_), channel_id=1, source_target_pairs={{0,16},{4,20},{8,24},{12,28},{16,0},{20,4},{24,8},{28,12},{1,17},{... | collective-permute-start | bytes 49160 | tf_op jit(solution)/shard_map/ppermute | solution.py:537
  13.9 4.6 %collective-permute-start.1 = (f32[32,128]{1,0:T(8,128)S(1)}, f32[32,128]{1,0:T(8,128)S(1)}, u32[]{:S(2)}, u32[]{:S(2)}) collective-permute-start(f32[32,128]{1,0:T(8,128)S(1)} %slice_add_fusion.2.refs_0_), channel_id=1, source_target_pairs={{0,8},{4,12},{8,0},{12,4},{16,24},{20,28},{24,16},{28,20},{1,9},{5... | collective-permute-start | bytes 49160 | tf_op jit(solution)/shard_map/ppermute | solution.py:537
  14.5 4.0 %copy-start = (f32[64,64]{1,0:T(8,128)S(1)}, f32[64,64]{1,0:T(8,128)}, u32[]{:S(2)}) copy-start(f32[64,64]{1,0:T(8,128)} %refs_4_.2) | copy-start | bytes 49156
  19.6 1.4 %collective-permute-start.5 = (f32[136,256]{1,0:T(8,128)S(1)}, f32[136,256]{1,0:T(8,128)S(1)}, u32[]{:S(2)}, u32[]{:S(2)}) collective-permute-start(f32[136,256]{1,0:T(8,128)S(1)} %shard_map.132), channel_id=1, source_target_pairs={{0,1},{1,0},{2,3},{3,2},{4,5},{5,4},{6,7},{7,6},{8,9},{9,8},{10,11... | collective-permute-start | bytes 417800 | tf_op jit(solution)/shard_map/ppermute | solution.py:544
  21.0 4.3 %collective-permute-start.6 = (f32[64,256]{1,0:T(8,128)S(1)}, f32[64,256]{1,0:T(8,128)S(1)}, u32[]{:S(2)}, u32[]{:S(2)}) collective-permute-start(f32[64,256]{1,0:T(8,128)S(1)} %slice_add_fusion.1.refs_0_), channel_id=1, source_target_pairs={{0,2},{1,3},{2,0},{3,1},{4,6},{5,7},{6,4},{7,5},{8,10},{9,11},{10,... | collective-permute-start | bytes 196616 | tf_op jit(solution)/shard_map/ppermute | solution.py:537
  26.4 4.2 %collective-permute-start.7 = (f32[104,128]{1,0:T(8,128)S(1)}, f32[104,128]{1,0:T(8,128)S(1)}, u32[]{:S(2)}, u32[]{:S(2)}) collective-permute-start(f32[104,128]{1,0:T(8,128)S(1)} %get-tuple-element.42.sent), channel_id=1, source_target_pairs={{0,4},{4,0},{8,12},{12,8},{16,20},{20,16},{24,28},{28,24},{1,5},{5... | collective-permute-start | bytes 159752 | tf_op jit(solution)/shard_map/ppermute | solution.py:571
  28.0 0.7 %collective-permute-start.8 = (f32[64,128]{1,0:T(8,128)S(1)}, f32[64,128]{1,0:T(8,128)S(1)}, u32[]{:S(2)}, u32[]{:S(2)}) collective-permute-start(f32[64,128]{1,0:T(8,128)S(1)} %get-tuple-element.43.edge), channel_id=1, source_target_pairs={{5,9},{7,11},{9,5},{11,7},{13,17},{15,19},{17,13},{19,15},{21,25},... | collective-permute-start | bytes 98312 | tf_op jit(solution)/shard_map/ppermute | solution.py:581
  30.7 5.6 %collective-permute-start.11 = (f32[40,128]{1,0:T(8,128)S(1)}, f32[40,128]{1,0:T(8,128)S(1)}, u32[]{:S(2)}, u32[]{:S(2)}) collective-permute-start(f32[40,128]{1,0:T(8,128)S(1)} %shard_map.135.refs_0_), channel_id=1, source_target_pairs={{0,24},{4,28},{8,16},{12,20},{16,8},{20,12},{24,0},{28,4},{1,25},{... | collective-permute-start | bytes 61448 | tf_op jit(solution)/shard_map/ppermute | solution.py:537
  32.3 4.7 %collective-permute-start.10 = (f32[40,128]{1,0:T(8,128)S(1)}, f32[40,128]{1,0:T(8,128)S(1)}, u32[]{:S(2)}, u32[]{:S(2)}) collective-permute-start(f32[40,128]{1,0:T(8,128)S(1)} %shard_map.135.refs_0_), channel_id=1, source_target_pairs={{0,16},{4,20},{8,24},{12,28},{16,0},{20,4},{24,8},{28,12},{1,17},{... | collective-permute-start | bytes 61448 | tf_op jit(solution)/shard_map/ppermute | solution.py:537
  32.9 4.7 %collective-permute-start.9 = (f32[40,128]{1,0:T(8,128)S(1)}, f32[40,128]{1,0:T(8,128)S(1)}, u32[]{:S(2)}, u32[]{:S(2)}) collective-permute-start(f32[40,128]{1,0:T(8,128)S(1)} %shard_map.135.refs_0_), channel_id=1, source_target_pairs={{0,8},{4,12},{8,0},{12,4},{16,24},{20,28},{24,16},{28,20},{1,9},{5... | collective-permute-start | bytes 61448 | tf_op jit(solution)/shard_map/ppermute | solution.py:537
  38.8 1.4 %collective-permute-start.12 = (f32[104,256]{1,0:T(8,128)S(1)}, f32[104,256]{1,0:T(8,128)S(1)}, u32[]{:S(2)}, u32[]{:S(2)}) collective-permute-start(f32[104,256]{1,0:T(8,128)S(1)} %get-tuple-element.44), channel_id=1, source_target_pairs={{0,1},{1,0},{2,3},{3,2},{4,5},{5,4},{6,7},{7,6},{8,9},{9,8},{10,11... | collective-permute-start | bytes 319496 | tf_op jit(solution)/shard_map/ppermute | solution.py:544
  40.1 4.4 %collective-permute-start.13 = (f32[72,256]{1,0:T(8,128)S(1)}, f32[72,256]{1,0:T(8,128)S(1)}, u32[]{:S(2)}, u32[]{:S(2)}) collective-permute-start(f32[72,256]{1,0:T(8,128)S(1)} %slice_add_fusion.refs_0_), channel_id=1, source_target_pairs={{0,2},{1,3},{2,0},{3,1},{4,6},{5,7},{6,4},{7,5},{8,10},{9,11},{10,... | collective-permute-start | bytes 221192 | tf_op jit(solution)/shard_map/ppermute | solution.py:537
  45.8 4.2 %collective-permute-start.14 = (f32[104,128]{1,0:T(8,128)S(1)}, f32[104,128]{1,0:T(8,128)S(1)}, u32[]{:S(2)}, u32[]{:S(2)}) collective-permute-start(f32[104,128]{1,0:T(8,128)S(1)} %get-tuple-element.53.sent), channel_id=1, source_target_pairs={{0,4},{4,0},{8,12},{12,8},{16,20},{20,16},{24,28},{28,24},{1,5},{5... | collective-permute-start | bytes 159752 | tf_op jit(solution)/shard_map/ppermute | solution.py:571
  47.0 0.7 %collective-permute-start.15 = (f32[64,128]{1,0:T(8,128)S(1)}, f32[64,128]{1,0:T(8,128)S(1)}, u32[]{:S(2)}, u32[]{:S(2)}) collective-permute-start(f32[64,128]{1,0:T(8,128)S(1)} %get-tuple-element.54.edge), channel_id=1, source_target_pairs={{5,9},{7,11},{9,5},{11,7},{13,17},{15,19},{17,13},{19,15},{21,25},... | collective-permute-start | bytes 98312 | tf_op jit(solution)/shard_map/ppermute | solution.py:581
  50.2 5.6 %collective-permute-start.18 = (f32[40,128]{1,0:T(8,128)S(1)}, f32[40,128]{1,0:T(8,128)S(1)}, u32[]{:S(2)}, u32[]{:S(2)}) collective-permute-start(f32[40,128]{1,0:T(8,128)S(1)} %shard_map.139.refs_0_), channel_id=1, source_target_pairs={{0,24},{4,28},{8,16},{12,20},{16,8},{20,12},{24,0},{28,4},{1,25},{... | collective-permute-start | bytes 61448 | tf_op jit(solution)/shard_map/ppermute | solution.py:537
  52.4 4.8 %collective-permute-start.17 = (f32[40,128]{1,0:T(8,128)S(1)}, f32[40,128]{1,0:T(8,128)S(1)}, u32[]{:S(2)}, u32[]{:S(2)}) collective-permute-start(f32[40,128]{1,0:T(8,128)S(1)} %shard_map.139.refs_0_), channel_id=1, source_target_pairs={{0,16},{4,20},{8,24},{12,28},{16,0},{20,4},{24,8},{28,12},{1,17},{... | collective-permute-start | bytes 61448 | tf_op jit(solution)/shard_map/ppermute | solution.py:537
  53.1 4.2 %collective-permute-start.16 = (f32[40,128]{1,0:T(8,128)S(1)}, f32[40,128]{1,0:T(8,128)S(1)}, u32[]{:S(2)}, u32[]{:S(2)}) collective-permute-start(f32[40,128]{1,0:T(8,128)S(1)} %shard_map.139.refs_0_), channel_id=1, source_target_pairs={{0,8},{4,12},{8,0},{12,4},{16,24},{20,28},{24,16},{28,20},{1,9},{5... | collective-permute-start | bytes 61448 | tf_op jit(solution)/shard_map/ppermute | solution.py:537
  57.4 4.9 %collective-permute-start.21 = (f32[72,128]{1,0:T(8,128)S(1)}, f32[72,128]{1,0:T(8,128)S(1)}, u32[]{:S(2)}, u32[]{:S(2)}) collective-permute-start(f32[72,128]{1,0:T(8,128)S(1)} %get-tuple-element.56), channel_id=1, source_target_pairs={{0,3},{1,2},{2,1},{3,0},{4,7},{5,6},{6,5},{7,4},{8,11},{9,10},{10,... | collective-permute-start | bytes 110600 | tf_op jit(solution)/shard_map/ppermute | solution.py:556
  58.6 3.6 %collective-permute-start.20 = (f32[8,128]{1,0:T(8,128)S(1)}, f32[8,128]{1,0:T(8,128)S(1)}, u32[]{:S(2)}, u32[]{:S(2)}) collective-permute-start(f32[8,128]{1,0:T(8,128)S(1)} %get-tuple-element.55.refs_0_), channel_id=1, source_target_pairs={{0,2},{1,3},{2,0},{3,1},{4,6},{5,7},{6,4},{7,5},{8,10},{9,11},{10,... | collective-permute-start | bytes 12296 | tf_op jit(solution)/shard_map/ppermute | solution.py:556
  59.2 3.1 %collective-permute-start.19 = (f32[8,128]{1,0:T(8,128)S(1)}, f32[8,128]{1,0:T(8,128)S(1)}, u32[]{:S(2)}, u32[]{:S(2)}) collective-permute-start(f32[8,128]{1,0:T(8,128)S(1)} %get-tuple-element.55.refs_0_), channel_id=1, source_target_pairs={{0,1},{1,0},{2,3},{3,2},{4,5},{5,4},{6,7},{7,6},{8,9},{9,8},{10,11... | collective-permute-start | bytes 12296 | tf_op jit(solution)/shard_map/ppermute | solution.py:556
